TPU v7x, 32 devices: a whole 2x2x4 slice. The times are simulated.
32 devices in a mesh: seq: 8 (over z, y), fsdp: 4 (over x, core).
Axes of the slice: x: 2, y: 2, z: 4, core: 2. Of those that a mesh axis runs over, the one named last changes fastest.
Arguments:
- tokens: bfloat16 [4, 1024, 2304], P('fsdp', 'seq'), may hold values from -6 to 6
- doc_ids: int32 [4, 1024], P('fsdp', 'seq'), may hold values from 0 to 64, as said below
- padding: int32 [4, 1024], P('fsdp', 'seq'), may hold values from 0 to 1, as said below
- token_order: int32 [4, 1024], P('fsdp', 'seq'), may hold values from 0 to 1023, as said below
- query_code: bfloat16 [2304, 2048], P(None, 'fsdp'), may hold values from -128 to 127, as said below
- key_value_code: bfloat16 [2304, 2048], P(None, 'fsdp'), may hold values from -128 to 127, as said below
- output_code: bfloat16 [2048, 2304], P(None, 'fsdp'), may hold values from -128 to 127, as said below
- gate_up_code: bfloat16 [2304, 18432], P(None, 'fsdp'), may hold values from -128 to 127, as said below
- down_code: bfloat16 [9216, 2304], P(None, 'fsdp'), may hold values from -128 to 127, as said below
- query_scale: float32 [2048], replicated, may hold values from 0.00015 to 0.0007
- key_value_scale: float32 [2048], replicated, may hold values from 0.00015 to 0.0007
- output_scale: float32 [2304], replicated, may hold values from 0.0001 to 0.001
- gate_up_scale: float32 [18432], replicated, may hold values from 0.00012 to 0.0006
- down_scale: float32 [2304], replicated, may hold values from 5e-05 to 0.0005
- norm_gains: float32 [4, 2304], replicated, may hold values from -0.5 to 0.5
- cotangent: bfloat16 [4, 1024, 2304], P('fsdp', 'seq'), may hold values from -6 to 6
Outputs:
- block_out: bfloat16 [4, 1024, 2304], P('fsdp', 'seq')
- grad_tokens: float32 [4, 1024, 2304], P('fsdp', 'seq')
- grad_query_code: float32 [2304, 2048], P('seq', 'fsdp')
- grad_key_value_code: float32 [2304, 2048], P('seq', 'fsdp')
- grad_output_code: float32 [2048, 2304], P('seq', 'fsdp')
- grad_gate_up_code: float32 [2304, 18432], P('seq', 'fsdp')
- grad_down_code: float32 [9216, 2304], P('seq', 'fsdp')
- grad_query_scale: float32 [2048], replicated
- grad_key_value_scale: float32 [2048], replicated
- grad_output_scale: float32 [2304], replicated
- grad_gate_up_scale: float32 [18432], replicated
- grad_down_scale: float32 [2304], replicated
- grad_norm_gains: float32 [4, 2304], replicated
Inputs may be any that keep to these rules, and one draw needn't show every extreme that they name: `doc_ids`: along positions (token_order) of a pack the ids never fall; equal ids mark one document. In every pack one document has rows on every device of seq, and the last document of every pack has id 128 / 2. `padding`: padding rows are the last positions of a pack. `token_order`: within each pack, a permutation of the positions 0 to 1023; runs of 64 stored rows hold runs of consecutive positions. `query_code`: whole numbers. `key_value_code`: whole numbers. `output_code`: whole numbers. `gate_up_code`: whole numbers. `down_code`: whole numbers.
All inputs are finite; a program needn't handle non-finite values.
Results may differ from a plain program's by a relative error of at most 0.02.
Values may be sent and summed in bfloat16 or wider, within the bound.
A program may use at most 256 MiB of HBM per device.

v0:
```python
import jax
import jax.numpy as jnp
from jax import lax
from jax.sharding import PartitionSpec as P

HQ = 8
HK = 4
DH = 256
FF = 9216


EPSILON = 1e-06
CAP = 50.0
BASE = 10000.0
FLOOR_SCORE = -1e30


def normalize(value):
    return value * lax.rsqrt(jnp.mean(value * value, axis=-1, keepdims=True) + EPSILON)


def norm_back(value, normed, upstream):
    inverse = lax.rsqrt(jnp.mean(value * value, axis=-1, keepdims=True) + EPSILON)
    return inverse * (upstream - normed * jnp.mean(upstream * normed, axis=-1, keepdims=True))


def angles(positions):
    half = DH // 2
    rates = BASE ** (-2.0 * jnp.arange(half).astype(jnp.float32) / DH)
    turn = positions.astype(jnp.float32)[:, None] * rates[None, :]
    return (jnp.cos(turn), jnp.sin(turn))


def rotate(value, cosine, sine):
    half = DH // 2
    first = value[..., :half]
    second = value[..., half:]
    cosine = cosine[:, None, :]
    sine = sine[:, None, :]
    return jnp.concatenate(
        [first * cosine - second * sine, second * cosine + first * sine], axis=-1
    )


def gelu_tanh(value):
    return jax.nn.gelu(value, approximate=True)


def contract_last(left, right):
    return lax.dot_general(
        left, right, (((1,), (1,)), ((), ())), preferred_element_type=jnp.float32
    )


def contract_first(left, right):
    return lax.dot_general(
        left, right, (((0,), (0,)), ((), ())), preferred_element_type=jnp.float32
    )


def code_levels(code, step):
    levels = code.astype(jnp.float32)
    if step > 1.0:
        levels = jnp.floor(levels / step) * step + step / 2.0
    return levels.astype(jnp.bfloat16)


def group_rows(value):
    return lax.all_gather(value, "fsdp", axis=0, tiled=True)


def column_product(gathered, weight):
    return lax.all_to_all(
        jnp.dot(gathered, weight, preferred_element_type=jnp.float32),
        "fsdp",
        split_axis=0,
        concat_axis=1,
        tiled=True,
    )


def to_columns(grad):
    return lax.all_to_all(grad, "fsdp", split_axis=1, concat_axis=0, tiled=True)


def input_sum(grad_cols, weight):
    return lax.psum_scatter(
        contract_last(grad_cols, weight), "fsdp", scatter_dimension=0, tiled=True
    )


def weight_sum(gathered, grad_cols):
    return lax.psum_scatter(
        contract_first(gathered, grad_cols), "seq", scatter_dimension=0, tiled=True
    )


def score_block(query, keys, row_document, row_place, key_document, key_real, key_place):
    raw = jnp.einsum("tagd,kad->tagk", query, keys, preferred_element_type=jnp.float32)
    squash = jnp.tanh(raw * DH ** (-0.5) / CAP)
    allowed = (row_document[:, None] == key_document[None, :]) & (
        key_place[None, :] <= row_place[:, None]
    ) & (key_real[None, :] == 1) | (key_place[None, :] == row_place[:, None])
    return (CAP * squash, squash, allowed[:, None, None, :])


def forward_update(query, row_document, row_place, state, part):
    keys, values, key_document, key_real, key_place = part
    highest, total, summed = state
    capped, squash, allowed = score_block(
        query, keys, row_document, row_place, key_document, key_real, key_place
    )
    newest = jnp.maximum(highest, jnp.max(jnp.where(allowed, capped, FLOOR_SCORE), axis=-1))
    fade = jnp.exp(highest - newest)
    mass = jnp.where(allowed, jnp.exp(capped - newest[..., None]), 0.0)
    total = total * fade + jnp.sum(mass, axis=-1)
    summed = summed * fade[..., None] + jnp.einsum(
        "tagk,kad->tagd", mass.astype(jnp.bfloat16), values, preferred_element_type=jnp.float32
    )
    return (newest, total, summed)


def backward_update(
    query, row_document, row_place, highest, total, grad_mixed, delta, state, part, start
):
    keys, values, key_document, key_real, key_place = part
    grad_query, grad_pairs = state
    capped, squash, allowed = score_block(
        query, keys, row_document, row_place, key_document, key_real, key_place
    )
    share = jnp.where(allowed, jnp.exp(capped - highest[..., None]), 0.0) / total[..., None]
    grad_share = jnp.einsum(
        "tagd,kad->tagk", grad_mixed, values, preferred_element_type=jnp.float32
    )
    grad_raw = (
        share * (grad_share - delta[..., None]) * (1.0 - squash * squash) * DH ** (-0.5)
    ).astype(jnp.bfloat16)
    grad_query = grad_query + jnp.einsum(
        "tagk,kad->tagd", grad_raw, keys, preferred_element_type=jnp.float32
    )
    grad_keys = jnp.einsum("tagk,tagd->kad", grad_raw, query, preferred_element_type=jnp.float32)
    grad_values = jnp.einsum(
        "tagk,tagd->kad", share.astype(jnp.bfloat16), grad_mixed, preferred_element_type=jnp.float32
    )
    count = keys.shape[0]
    fresh = jnp.concatenate(
        [grad_keys.reshape(count, HK * DH), grad_values.reshape(count, HK * DH)], axis=1
    )
    grad_pairs = lax.dynamic_update_slice_in_dim(grad_pairs, fresh, start, 0)
    return (grad_query, grad_pairs)


def over_blocks(update, state, piece):
    count = piece[0].shape[0]
    size = 1024

    def step(index, carried):
        offset = index * size
        part = tuple((lax.dynamic_slice_in_dim(item, offset, size, 0) for item in piece))
        return update(carried, part, offset)

    return lax.fori_loop(0, count // size, step, state)


def per_device(
    tokens,
    doc_ids,
    padding,
    token_order,
    query_code,
    key_value_code,
    output_code,
    gate_up_code,
    down_code,
    query_scale,
    key_value_scale,
    output_scale,
    gate_up_scale,
    down_scale,
    norm_gains,
    cotangent,
):
    inputs = tokens[0].astype(jnp.float32)
    rows = inputs.shape[0]
    group = HQ // HK
    groups = lax.axis_size("fsdp")
    row_document = doc_ids[0]
    row_real = padding[0]
    row_place = token_order[0]
    query_local = code_levels(query_code, 1.0)
    pair_local = code_levels(key_value_code, 1.0)
    output_local = code_levels(output_code, 1.0)
    gate_local = code_levels(gate_up_code, 16.0)
    down_local = code_levels(down_code, 64.0)
    q_width = query_local.shape[1]
    attention_in = jnp.concatenate([query_local, pair_local], axis=1)
    cosine, sine = angles(row_place)
    first = normalize(inputs)
    first_input = (first * (1.0 + norm_gains[0])).astype(jnp.bfloat16)
    first_rows = group_rows(first_input)
    projected = column_product(first_rows, attention_in).reshape(rows, groups, -1)
    query_raw = projected[:, :, :q_width].reshape(rows, HQ * DH)
    pair_raw = projected[:, :, q_width:].reshape(rows, 2 * HK * DH)
    query_plain = query_raw * query_scale[None, :]
    pair_plain = pair_raw * key_value_scale[None, :]
    query = (
        rotate(query_plain.reshape(rows, HQ, DH), cosine, sine)
        .astype(jnp.bfloat16)
        .reshape(rows, HK, group, DH)
    )
    keys = rotate(pair_plain[:, : HK * DH].reshape(rows, HK, DH), cosine, sine).astype(jnp.bfloat16)
    values = pair_plain[:, HK * DH :].reshape(rows, HK, DH).astype(jnp.bfloat16)
    start_state = (
        jnp.full((rows, HK, group), FLOOR_SCORE, jnp.float32),
        jnp.zeros((rows, HK, group), jnp.float32),
        jnp.zeros((rows, HK, group, DH), jnp.float32),
    )

    def forward_piece(state, part, start):
        return forward_update(query, row_document, row_place, state, part)

    highest, total, summed = over_blocks(
        forward_piece,
        start_state,
        (
            lax.all_gather(keys, "seq", axis=0, tiled=True),
            lax.all_gather(values, "seq", axis=0, tiled=True),
            lax.all_gather(row_document, "seq", axis=0, tiled=True),
            lax.all_gather(row_real, "seq", axis=0, tiled=True),
            lax.all_gather(row_place, "seq", axis=0, tiled=True),
        ),
    )
    mixed = summed / total[..., None]
    mixed_low = mixed.reshape(rows, HQ * DH).astype(jnp.bfloat16)
    mixed_rows = group_rows(mixed_low)
    branch_raw = column_product(mixed_rows, output_local)
    branch = branch_raw * output_scale[None, :]
    second = normalize(branch)
    middle = inputs + second * (1.0 + norm_gains[1])
    third = normalize(middle)
    second_input = (third * (1.0 + norm_gains[2])).astype(jnp.bfloat16)
    second_rows = group_rows(second_input)
    gate_raw = column_product(second_rows, gate_local)
    gate_up = gate_raw * gate_up_scale[None, :]
    activated, gelu_back = jax.vjp(gelu_tanh, gate_up[:, :FF])
    hidden = (activated * gate_up[:, FF:]).astype(jnp.bfloat16)
    hidden_rows = group_rows(hidden)
    down_raw = column_product(hidden_rows, down_local)
    down = down_raw * down_scale[None, :]
    fourth = normalize(down)
    result = middle + fourth * (1.0 + norm_gains[3])
    grad_result = cotangent[0].astype(jnp.float32)
    gain_four = jnp.sum(grad_result * fourth, axis=0)
    grad_down_full = norm_back(down, fourth, grad_result * (1.0 + norm_gains[3]))
    scale_down = jnp.sum(down_raw * grad_down_full, axis=0)
    grad_down = (grad_down_full * down_scale[None, :]).astype(jnp.bfloat16)
    down_cols = to_columns(grad_down)
    grad_hidden = input_sum(down_cols, down_local)
    grad_gate = gelu_back(grad_hidden * gate_up[:, FF:])[0]
    grad_up = grad_hidden * activated
    grad_gate_full = jnp.concatenate([grad_gate, grad_up], axis=1)
    scale_gate = jnp.sum(gate_raw * grad_gate_full, axis=0)
    grad_gate_up = (grad_gate_full * gate_up_scale[None, :]).astype(jnp.bfloat16)
    gate_cols = to_columns(grad_gate_up)
    grad_second_input = input_sum(gate_cols, gate_local)
    gain_three = jnp.sum(grad_second_input * third, axis=0)
    grad_middle = grad_result + norm_back(middle, third, grad_second_input * (1.0 + norm_gains[2]))
    gain_two = jnp.sum(grad_middle * second, axis=0)
    grad_branch_full = norm_back(branch, second, grad_middle * (1.0 + norm_gains[1]))
    scale_output = jnp.sum(branch_raw * grad_branch_full, axis=0)
    grad_branch = (grad_branch_full * output_scale[None, :]).astype(jnp.bfloat16)
    branch_cols = to_columns(grad_branch)
    grad_mixed = (
        input_sum(branch_cols, output_local).astype(jnp.bfloat16).reshape(rows, HK, group, DH)
    )
    delta = jnp.sum(grad_mixed.astype(jnp.float32) * mixed, axis=-1)
    back_state = (
        jnp.zeros((rows, HK, group, DH), jnp.float32),
        jnp.zeros((rows * lax.axis_size("seq"), 2 * HK * DH), jnp.float32),
    )

    def backward_piece(state, part, start):
        return backward_update(
            query, row_document, row_place, highest, total, grad_mixed, delta, state, part, start
        )

    grad_query, grad_pairs = over_blocks(
        backward_piece,
        back_state,
        (
            lax.all_gather(keys, "seq", axis=0, tiled=True),
            lax.all_gather(values, "seq", axis=0, tiled=True),
            lax.all_gather(row_document, "seq", axis=0, tiled=True),
            lax.all_gather(row_real, "seq", axis=0, tiled=True),
            lax.all_gather(row_place, "seq", axis=0, tiled=True),
        ),
    )
    grad_own = lax.psum_scatter(grad_pairs, "seq", scatter_dimension=0, tiled=True)
    grad_query_full = rotate(grad_query.reshape(rows, HQ, DH), cosine, -sine).reshape(rows, HQ * DH)
    scale_query = jnp.sum(query_raw * grad_query_full, axis=0)
    grad_query_low = (grad_query_full * query_scale[None, :]).astype(jnp.bfloat16)
    grad_keys_turned = rotate(grad_own[:, : HK * DH].reshape(rows, HK, DH), cosine, -sine).reshape(
        rows, HK * DH
    )
    grad_pair_full = jnp.concatenate([grad_keys_turned, grad_own[:, HK * DH :]], axis=1)
    scale_pair = jnp.sum(pair_raw * grad_pair_full, axis=0)
    grad_pair_low = (grad_pair_full * key_value_scale[None, :]).astype(jnp.bfloat16)
    joined = jnp.concatenate(
        [grad_query_low.reshape(rows, groups, -1), grad_pair_low.reshape(rows, groups, -1)], axis=2
    ).reshape(rows, -1)
    attention_cols = to_columns(joined)
    grad_first_input = input_sum(attention_cols, attention_in)
    gain_one = jnp.sum(grad_first_input * first, axis=0)
    grad_inputs = grad_middle + norm_back(inputs, first, grad_first_input * (1.0 + norm_gains[0]))
    attention_block = weight_sum(first_rows, attention_cols)
    output_sum = weight_sum(mixed_rows, branch_cols)
    gate_sum = weight_sum(second_rows, gate_cols)
    down_sum = lax.psum_scatter(
        contract_first(hidden_rows, down_cols), "seq", scatter_dimension=0, tiled=True
    )
    query_sum = attention_block[:, :q_width]
    pair_sum = attention_block[:, q_width:]
    gains_total, total_query, total_pair, total_output, total_gate, total_down = lax.psum(
        (
            jnp.stack([gain_one, gain_two, gain_three, gain_four]),
            scale_query,
            scale_pair,
            scale_output,
            scale_gate,
            scale_down,
        ),
        ("seq", "fsdp"),
    )
    return (
        result.astype(jnp.bfloat16)[None],
        grad_inputs[None],
        query_sum,
        pair_sum,
        output_sum,
        gate_sum,
        down_sum,
        total_query,
        total_pair,
        total_output,
        total_gate,
        total_down,
        gains_total,
    )


def solution(mesh):
    return jax.shard_map(
        per_device,
        mesh=mesh,
        in_specs=(
            P("fsdp", "seq", None),
            P("fsdp", "seq"),
            P("fsdp", "seq"),
            P("fsdp", "seq"),
            P(None, "fsdp"),
            P(None, "fsdp"),
            P(None, "fsdp"),
            P(None, "fsdp"),
            P(None, "fsdp"),
            P(),
            P(),
            P(),
            P(),
            P(),
            P(),
            P("fsdp", "seq", None),
        ),
        out_specs=(
            P("fsdp", "seq", None),
            P("fsdp", "seq", None),
            P("seq", "fsdp"),
            P("seq", "fsdp"),
            P("seq", "fsdp"),
            P("seq", "fsdp"),
            P("seq", "fsdp"),
            P(),
            P(),
            P(),
            P(),
            P(),
            P(),
        ),
        check_vma=False,
    )
```

profile of v0, /device:TPU:0, one launch (start us, length us, event | category | flops | bytes accessed | tf_op | source)
XLA Modules:
  0.0 2724.5 jit_solution(6197462338610222381)
XLA Ops:
  13.0 3.4 constant_dynamic-update-slice_fusion.1
  18.0 22.0 all-gather.10.cloned.1.call-done
  39.9 7.0 fusion.113
  46.9 2.9 copy.82
  49.8 4.5 all-to-all-start
  55.3 24.7 all-to-all-done
  94.7 20.4 all-gather.1
  115.1 16.5 all-gather.2
  131.6 18.4 all-gather
  154.2 2.7 fusion.14
  160.0 31.8 %all-gather.14.cloned.1.call-done = bf16[1024,4,256]{0,2,1:T(8,128)(2,1)} async-done(((bf16[128,4,256]{0,2,1:T(8,128)(2,1)}), bf16[1024,4,256]{0,2,1:T(8,128)(2,1)}) %all-gather.14.cloned.1.call-update) | async-done | bytes 2097168 | tf_op jit(solution)/shard_map/all_gather | solution.py:227
  191.8 5.5 fusion.112
  197.3 21.2 all-gather.16.cloned.1.call-done
  218.5 3.0 convolution_bitcast_fusion
  222.6 4.4 all-to-all-start.1
  227.1 15.8 all-to-all-done.1
  244.6 2.7 copy.92
  251.3 24.0 all-gather.18.cloned.1.call-done
  275.2 18.4 fusion.1
  293.7 108.5 %all_to_all.146 = f32[4,128,4608]{2,1,0:T(8,128)S(1)} all-to-all(f32[4,128,4608]{2,1,0:T(8,128)} %bitcast.277), channel_id=1, replica_groups=mesh['seq'=8,'fsdp'=4] {'fsdp'}, dimensions={0} | all-to-all | bytes 18874368 | tf_op jit(solution)/shard_map/all_to_all | solution.py:73
  402.2 4.6 copy.141
  408.9 4.6 broadcast_multiply_fusion
  413.5 3.6 copy-done.2
  417.1 2.6 multiply_convert_fusion.1
  419.8 64.4 %all-gather.20.cloned.1.call-done = bf16[512,9216]{1,0:T(8,128)(2,1)} async-done(((bf16[128,9216]{1,0:T(8,128)(2,1)}), bf16[512,9216]{1,0:T(8,128)(2,1)}) %all-gather.20.cloned.1.call-update) | async-done | bytes 9437200 | tf_op jit(solution)/shard_map/all_gather | solution.py:69
  484.2 11.2 fusion.38
  496.5 3.5 all-to-all-start.3
  504.9 10.9 all-to-all-done.3
  520.9 2.8 fusion.62
  523.7 11.9 all_to_all.147
  536.4 14.0 fusion.3
  551.4 138.7 %reduce-scatter.10.cloned.1.call-done = f32[128,9216]{1,0:T(8,128)} async-done(((f32[512,9216]{1,0:T(8,128)}), f32[128,9216]{1,0:T(8,128)}) %reduce-scatter.10.cloned.1.call-update) | async-done | bytes 4718608 | tf_op jit(solution)/shard_map/reduce_scatter | solution.py:87
  690.1 6.9 fusion.27
  699.4 2.5 bitcast_dynamic-update-slice_fusion
  701.9 11.4 fusion.2
  713.4 57.8 %all_to_all.148 = bf16[128,4,4608]{2,0,1:T(8,128)(2,1)S(1)} all-to-all(bf16[128,4,4608]{2,0,1:T(8,128)(2,1)} %get-tuple-element.126), channel_id=1, replica_groups=mesh['seq'=8,'fsdp'=4] {'fsdp'}, dimensions={1} | all-to-all | bytes 9437184 | tf_op jit(solution)/shard_map/all_to_all | solution.py:83
  773.3 15.9 fusion
  789.3 47.9 %reduce-scatter.12.cloned.1.call-done = f32[128,2304]{1,0:T(8,128)} async-done(((f32[512,2304]{1,0:T(8,128)}), f32[128,2304]{1,0:T(8,128)}) %reduce-scatter.12.cloned.1.call-update) | async-done | bytes 1179664 | tf_op jit(solution)/shard_map/reduce_scatter | solution.py:87
  837.2 2.6 multiply_reduce_fusion
  845.6 11.9 all_to_all.149
  857.5 3.8 fusion.74
  861.6 44.4 %reduce-scatter.14.cloned.1.call-done = f32[128,2048]{1,0:T(8,128)} async-done(((f32[512,2048]{1,0:T(8,128)}), f32[128,2048]{1,0:T(8,128)}) %reduce-scatter.14.cloned.1.call-update) | async-done | bytes 1048592 | tf_op jit(solution)/shard_map/reduce_scatter | solution.py:87
  910.8 4.0 fusion.24
  915.0 2.8 fusion.12
  919.9 4.1 pad_maximum_fusion
  926.0 3.1 fusion.20
  930.4 143.3 %reduce-scatter.16.cloned.1.call-done = f32[128,2048]{0,1:T(8,128)} async-done(((f32[1024,2048]{0,1:T(8,128)}), f32[128,2048]{0,1:T(8,128)}) %reduce-scatter.16.cloned.1.call-update) | async-done | bytes 1048592 | tf_op jit(solution)/shard_map/reduce_scatter | solution.py:298
  1080.6 3.4 multiply_reduce_fusion.7
  1084.1 17.6 all_to_all.150
  1104.0 7.4 fusion.114
  1111.7 9.2 fusion.115
  1122.7 13.8 fusion.76
  1136.6 5.3 fusion.72
  1144.5 13.0 reduce-scatter.18.cloned.1.call-done
  1160.8 21.8 fusion.116
  1182.6 2.8 copy.91
  1186.8 3.3 fusion.58
  1190.7 2.5 fusion.54
  1193.3 131.6 %reduce-scatter.20.cloned.1.call-done = f32[288,1024]{1,0:T(8,128)} async-done(((f32[2304,1024]{1,0:T(8,128)}), f32[288,1024]{1,0:T(8,128)}) %reduce-scatter.20.cloned.1.call-update) | async-done | bytes 1179664 | tf_op jit(solution)/shard_map/reduce_scatter | solution.py:93
  1327.2 121.7 %all-reduce.4.cloned.1.call-done = f32[18432]{0:T(1024)} async-done(((f32[18432]{0:T(1024)}), f32[18432]{0:T(1024)}) %all-reduce.4.cloned.1.call-update) | async-done | bytes 73744 | tf_op jit(solution)/shard_map/psum | solution.py:323
  1448.9 353.9 %reduce-scatter.26.cloned.1.call-done = f32[1152,576]{0,1:T(8,128)} async-done(((f32[9216,576]{0,1:T(8,128)}), f32[1152,576]{0,1:T(8,128)}) %reduce-scatter.26.cloned.1.call-update) | async-done | bytes 2654224 | tf_op jit(solution)/shard_map/reduce_scatter | solution.py:318
  1802.8 99.1 %reduce-scatter.22.cloned.1.call-done = f32[256,576]{0,1:T(8,128)} async-done(((f32[2048,576]{0,1:T(8,128)}), f32[256,576]{0,1:T(8,128)}) %reduce-scatter.22.cloned.1.call-update) | async-done | bytes 589840 | tf_op jit(solution)/shard_map/reduce_scatter | solution.py:93
  1901.9 128.5 %all-reduce.6.cloned.1.call-done = (f32[2048]{0:T(1024)}, f32[2048]{0:T(1024)}, f32[2304]{0:T(1024)}, f32[2304]{0:T(1024)}, f32[4,2304]{1,0:T(4,128)}) async-done(((f32[2048]{0:T(1024)}, f32[2048]{0:T(1024)}, f32[2304]{0:T(1024)}, f32[2304]{0:T(1024)}, f32[4,2304]{1,0:T(4,128)}), (f32[2048]{0:T(1024)}, f32[2048]{0:T(1024)}, f32[2304]{0:T(1024)}, f32[2304]{0:T(1024)}, ...) | async-done | bytes 71696 | tf_op jit(solution)/shard_map/psum | solution.py:323
  2030.4 678.9 %reduce-scatter.24.cloned.1.call-done = f32[288,4608]{1,0:T(8,128)} async-done(((f32[2304,4608]{1,0:T(8,128)}), f32[288,4608]{1,0:T(8,128)}) %reduce-scatter.24.cloned.1.call-update) | async-done | bytes 5308432 | tf_op jit(solution)/shard_map/reduce_scatter | solution.py:93
  (243 shorter events, 102.3 us)
Async XLA Ops:
  7.2 211.3 %copy-start = (bf16[2048,576]{0,1:T(8,128)(2,1)S(1)}, bf16[2048,576]{0,1:T(8,128)(2,1)}, u32[]{:S(2)}) copy-start(bf16[2048,576]{0,1:T(8,128)(2,1)} %param.22) | copy-start | bytes 7077892
  7.2 32.7 %all-gather.10.cloned.1.call-start = ((), (), s32[]{:S(2)}) async-start(), calls=%async_computation.17 | async-start | bytes 2949120 | tf_op jit(solution)/shard_map/all_gather | solution.py:69
  10.3 236.9 %copy-start.32 = (f32[2304]{0:T(1024)}, f32[2304]{0:T(1024)S(1)}, u32[]{:S(2)}) copy-start(f32[2304]{0:T(1024)S(1)} %get-tuple-element.95) | copy-start | bytes 27652
  13.0 3.4 copy-start.19
  46.9 7.5 copy-start.58
  49.8 30.2 %all-to-all-start = ((f32[4,128,1024]{1,2,0:T(8,128)}), f32[4,128,1024]{1,2,0:T(8,128)}, u32[]{:S(2)}, u32[]{:S(2)}) async-start(f32[4,128,1024]{1,2,0:T(8,128)} %copy.82), calls=%async_computation | async-start | bytes 4194304 | tf_op jit(solution)/shard_map/all_to_all | solution.py:73
  54.3 99.8 %all-gather.12.cloned.1.call-start = ((), (), s32[]{:S(2)}) async-start(), calls=%async_computation.18 | async-start | bytes 2359296 | tf_op jit(solution)/shard_map/all_gather | solution.py:226
  55.3 36.6 %copy-start.20 = (f32[128,128]{1,0:T(8,128)}, f32[128,128]{1,0:T(8,128)S(1)}, u32[]{:S(2)}) copy-start(f32[128,128]{1,0:T(8,128)S(1)} %get-tuple-element.154) | copy-start | bytes 196612
  90.1 101.7 %all-gather.14.cloned.1.call-start = ((), (), s32[]{:S(2)}) async-start(), calls=%async_computation.19 | async-start | bytes 2359296 | tf_op jit(solution)/shard_map/all_gather | solution.py:227
  91.9 126.6 %all-gather.16.cloned.1.call-start = ((), (), s32[]{:S(2)}) async-start(), calls=%async_computation.20 | async-start | bytes 2621440 | tf_op jit(solution)/shard_map/all_gather | solution.py:69
  151.6 40.2 %copy-start.28 = (pred[128,1024]{0,1:T(8,128)(4,1)}, pred[128,1024]{0,1:T(8,128)(4,1)S(1)}, u32[]{:S(2)}) copy-start(pred[128,1024]{0,1:T(8,128)(4,1)S(1)} %compare_or_fusion) | copy-start | bytes 393220
  153.9 3.0 copy-start.22
  154.1 2.8 copy-start.24
  156.9 1.9 copy-start.16
  156.9 40.4 %copy-start.48 = (f32[128,4,2]{0,2,1:T(2,128)}, f32[128,4,2]{0,2,1:T(2,128)S(1)}, u32[]{:S(2)}) copy-start(f32[128,4,2]{0,2,1:T(2,128)S(1)} %broadcast_maximum_fusion) | copy-start | bytes 12292
  160.0 37.3 %copy-start.56 = (f32[128,4,2]{0,2,1:T(2,128)}, f32[128,4,2]{0,2,1:T(2,128)S(1)}, u32[]{:S(2)}) copy-start(f32[128,4,2]{0,2,1:T(2,128)S(1)} %get-tuple-element.151) | copy-start | bytes 12292
  221.5 5.6 copy-start.30
  221.5 25.8 copy-start.5
  222.6 27.4 %copy-start.38 = (f32[2304]{0:T(1024)S(1)}, f32[2304]{0:T(1024)}, u32[]{:S(2)}) copy-start(f32[2304]{0:T(1024)} %get-tuple-element.97) | copy-start | bytes 27652
  222.6 20.3 all-to-all-start.1
  227.0 48.2 %all-gather.18.cloned.1.call-start = ((), (), s32[]{:S(2)}) async-start(), calls=%async_computation.21 | async-start | bytes 2949120 | tf_op jit(solution)/shard_map/all_gather | solution.py:69
  244.6 49.1 %copy-start.50 = (f32[128]{0:T(128)}, f32[128]{0:T(128)S(1)}, u32[]{:S(2)}) copy-start(f32[128]{0:T(128)S(1)} %add_rsqrt_fusion.2) | copy-start | bytes 1540
  251.0 233.2 %all-gather.20.cloned.1.call-start = ((), (), s32[]{:S(2)}) async-start(), calls=%async_computation.22 | async-start | bytes 11796480 | tf_op jit(solution)/shard_map/all_gather | solution.py:69
  402.2 6.7 copy-start.1
  402.2 6.7 copy-start.34
  413.5 3.6 copy-start.2
  495.4 6.5 copy-start.39
  496.5 19.4 all-to-all-start.3
  500.0 190.1 %reduce-scatter.10.cloned.1.call-start = ((), (), s32[]{:S(2)}) async-start(), calls=%async_computation.23 | async-start | bytes 23592960 | tf_op jit(solution)/shard_map/reduce_scatter | solution.py:87
  515.9 19.8 copy-start.3
  517.0 33.5 %copy-start.52 = (f32[128]{0:T(128)}, f32[128]{0:T(128)S(1)}, u32[]{:S(2)}) copy-start(f32[128]{0:T(128)S(1)} %add_rsqrt_fusion) | copy-start | bytes 1540
  550.5 286.7 %reduce-scatter.12.cloned.1.call-start = ((), (), s32[]{:S(2)}) async-start(), calls=%async_computation.24 | async-start | bytes 5898240 | tf_op jit(solution)/shard_map/reduce_scatter | solution.py:87
  771.1 2.1 copy-start.14
  789.2 50.6 %copy-start.7 = (f32[128,2304]{1,0:T(8,128)S(1)}, f32[128,2304]{1,0:T(8,128)}, u32[]{:S(2)}) copy-start(f32[128,2304]{1,0:T(8,128)} %copy.92) | copy-start | bytes 3538948
  789.2 50.6 %copy-start.31 = (f32[2304]{0:T(1024)S(1)}, f32[2304]{0:T(1024)}, u32[]{:S(2)}) copy-start(f32[2304]{0:T(1024)} %param.27) | copy-start | bytes 27652
  789.2 50.6 %copy-start.51 = (f32[128]{0:T(128)S(1)}, f32[128]{0:T(128)}, u32[]{:S(2)}) copy-start(f32[128]{0:T(128)} %copy-done.50) | copy-start | bytes 1540
  789.2 116.8 %reduce-scatter.14.cloned.1.call-start = ((), (), s32[]{:S(2)}) async-start(), calls=%async_computation.25 | async-start | bytes 5242880 | tf_op jit(solution)/shard_map/reduce_scatter | solution.py:87
  837.2 5.1 copy-start.33
  842.2 2.0 copy-start.10
  861.3 49.5 %copy-start.49 = (f32[128,4,2]{0,2,1:T(2,128)S(1)}, f32[128,4,2]{0,2,1:T(2,128)}, u32[]{:S(2)}) copy-start(f32[128,4,2]{0,2,1:T(2,128)} %copy-done.48) | copy-start | bytes 12292
  861.3 49.5 %copy-start.57 = (f32[128,4,2]{0,2,1:T(2,128)S(1)}, f32[128,4,2]{0,2,1:T(2,128)}, u32[]{:S(2)}) copy-start(f32[128,4,2]{0,2,1:T(2,128)} %copy-done.56) | copy-start | bytes 12292
  861.3 212.3 %reduce-scatter.16.cloned.1.call-start = ((), (), s32[]{:S(2)}) async-start(), calls=%async_computation.26 | async-start | bytes 9437184 | tf_op jit(solution)/shard_map/reduce_scatter | solution.py:298
  910.8 4.1 copy-start.17
  910.8 4.1 copy-start.29
  910.8 4.2 copy-start.59
  915.0 4.1 copy-start.23
  915.0 4.1 copy-start.25
  924.0 1.9 copy-start.26
  924.1 5.1 copy-start.27
  924.1 233.4 %reduce-scatter.18.cloned.1.call-start = ((), (), s32[]{:S(2)}) async-start(), calls=%async_computation.27 | async-start | bytes 5898240 | tf_op jit(solution)/shard_map/reduce_scatter | solution.py:87
  929.2 148.5 %copy-start.21 = (f32[128,128]{1,0:T(8,128)S(1)}, f32[128,128]{1,0:T(8,128)}, u32[]{:S(2)}) copy-start(f32[128,128]{1,0:T(8,128)} %copy-done.20) | copy-start | bytes 196612
  1111.4 213.4 %reduce-scatter.20.cloned.1.call-start = ((), (), s32[]{:S(2)}) async-start(), calls=%async_computation.28 | async-start | bytes 10616832 | tf_op jit(solution)/shard_map/reduce_scatter | solution.py:93
  1121.0 327.9 %all-reduce.4.cloned.1.call-start = ((), (), s32[]{:S(2)}) async-start(), calls=%async_computation.32 | async-start | bytes 147456 | tf_op jit(solution)/shard_map/psum | solution.py:323
  1122.7 680.1 %reduce-scatter.26.cloned.1.call-start = ((), (), s32[]{:S(2)}) async-start(), calls=%async_computation.31 | async-start | bytes 23887872 | tf_op jit(solution)/shard_map/reduce_scatter | solution.py:318
  1136.5 765.3 %reduce-scatter.22.cloned.1.call-start = ((), (), s32[]{:S(2)}) async-start(), calls=%async_computation.29 | async-start | bytes 5308416 | tf_op jit(solution)/shard_map/reduce_scatter | solution.py:93
  1141.9 2.0 copy-start.45
  1141.9 15.6 copy-start.6
  1141.9 15.6 copy-start.37
  1141.9 15.6 copy-start.55
  1142.0 888.4 %all-reduce.6.cloned.1.call-start = ((), (), s32[]{:S(2)}) async-start(), calls=%async_computation.33 | async-start | bytes 155648 | tf_op jit(solution)/shard_map/psum | solution.py:323
  1160.4 1548.9 %reduce-scatter.24.cloned.1.call-start = ((), (), s32[]{:S(2)}) async-start(), calls=%async_computation.30 | async-start | bytes 47775744 | tf_op jit(solution)/shard_map/reduce_scatter | solution.py:93
  1182.6 2.8 copy-start.4
  1186.8 4.0 copy-start.11
  1186.8 4.0 copy-start.15
  (16 other events, 17.8 us)
Sparse Core Ops, SparseCore 0:
  13.1 26.7 all-gather.9
  90.2 49.3 all-gather.11
  142.2 49.5 all-gather.13
  197.4 21.0 all-gather.15
  251.1 24.0 all-gather.17
  419.9 64.2 all-gather.19
  550.6 139.4 reduce-scatter.9
  789.3 47.7 reduce-scatter.11
  861.5 44.5 reduce-scatter.13
  924.2 149.3 reduce-scatter.15
  1111.5 45.9 reduce-scatter.17
  1161.4 163.4 reduce-scatter.19
  1331.4 117.4 all-reduce.3
  1453.7 349.0 reduce-scatter.25
  1806.9 94.9 reduce-scatter.21
  1909.3 121.0 all-reduce.5
  2034.7 674.5 reduce-scatter.23
where the time goes:
time: 2740 us; the launch traced here: 2720 us
  waiting for transfers between devices  2120 us (77%)
  blocking collectives  263 us (10%)
  matrix products  150 us (5%)
  local copies, waits for them, and re-layouts  85.6 us (3%)
  other arithmetic  80.3 us (3%)
    reduce_scatter x3, waiting for transfers between devices, weight_sum(): lax.psum_scatter(contract_first(gathered, grad_cols), 'seq', scatter_dime...  910 us
    reduce_scatter x1, waiting for transfers between devices, per_device(): lax.psum_scatter(contract_first(hidden_rows, down_cols), 'seq', scatter_d...  354 us
    psum x2, waiting for transfers between devices, per_device(): lax.psum((jnp.stack([gain_one, gain_two, gain_three, gain_four]), scale_q...  250 us
    reduce_scatter x4, waiting for transfers between devices, input_sum(): lax.psum_scatter(contract_last(grad_cols, weight), 'fsdp', scatter_dimens...  244 us
    reduce_scatter x1, waiting for transfers between devices, per_device(): lax.psum_scatter(grad_pairs, 'seq', scatter_dimension=0, tiled=True)  143 us
    all_gather x4, waiting for transfers between devices, group_rows(): return lax.all_gather(value, 'fsdp', axis=0, tiled=True)  132 us
    all_to_all x1, blocking collectives, column_product(): lax.all_to_all(jnp.dot(gathered, weight, preferred_element_type=jnp.float...  109 us
    all_to_all x4, blocking collectives, to_columns(): return lax.all_to_all(grad, 'fsdp', split_axis=1, concat_axis=0, tiled=True)  99.2 us
  transfers between devices with their start and end apart: 20, of which 19 were waited for; matrix products, arithmetic and copies ran while one was open for 4% of the time, Pallas kernels for 0%

commit v1 on v0

v1 whole, which is shorter than its diff:
```python
import functools
import math

import jax
import jax.numpy as jnp
from jax import lax
from jax.experimental import pallas as pl
from jax.experimental.pallas import tpu as pltpu
from jax.sharding import PartitionSpec as P

HQ = 8
HK = 4
DH = 256
FF = 9216
GROUP = 4
EPSILON = 1e-06
CAP = 50.0
BASE = 10000.0
VMEM_LIMIT = 56 * 1024 * 1024
MESH = pl.DeviceIdType.MESH
ANY = pl.BlockSpec(memory_space=pl.ANY)
VMEM = pl.BlockSpec(memory_space=pltpu.VMEM)
DMA = pltpu.SemaphoreType.DMA
F32 = jnp.float32
BF16 = jnp.bfloat16


def dot(left, right):
    return jnp.dot(left, right, preferred_element_type=F32)


def contract_last(left, right):
    return lax.dot_general(left, right, (((1,), (1,)), ((), ())), preferred_element_type=F32)


def contract_first(left, right):
    return lax.dot_general(left, right, (((0,), (0,)), ((), ())), preferred_element_type=F32)


def place_now():
    seq = lax.axis_index("seq")
    fsdp = lax.axis_index("fsdp")
    return seq, fsdp, fsdp // 2, fsdp % 2


def greet(peers):
    barrier = pltpu.get_barrier_semaphore()
    for peer in peers:
        pl.semaphore_signal(barrier, inc=1, device_id=peer, device_id_type=MESH)
    pl.semaphore_wait(barrier, len(peers))


def remote(src, dst, send, recv, peer):
    return pltpu.make_async_remote_copy(
        src_ref=src, dst_ref=dst, send_sem=send, recv_sem=recv, device_id=peer, device_id_type=MESH
    )


def comm_call(kernel, cid, out_shape, scratch, in_specs, out_specs):
    return pl.pallas_call(
        kernel,
        out_shape=out_shape,
        in_specs=in_specs,
        out_specs=out_specs,
        scratch_shapes=scratch,
        compiler_params=pltpu.CompilerParams(
            collective_id=cid, has_side_effects=True, vmem_limit_bytes=VMEM_LIMIT
        ),
    )


def group_gather_kernel(count, columns, parts, *refs):
    ins = refs[:count]
    outs = refs[count : 2 * count]
    local, xs, xr, cs, cr, fs, fr = refs[2 * count :]
    seq, me, x, c = place_now()
    across = (seq, (1 - x) * 2 + c)
    beside = (seq, x * 2 + 1 - c)
    greet([across, beside])
    waits = []
    forwards = []
    for i in range(count):
        src, out = ins[i], outs[i]
        rows = src.shape[0]
        step = rows // parts[i]

        def spot(owner, start, size, out=out, i=i):
            if columns[i]:
                width = out.shape[1] // GROUP
                return out.at[pl.ds(start, size), pl.ds(owner * width, width)]
            return out.at[owner, pl.ds(start, size)]

        own = pltpu.make_async_copy(src, spot(me, 0, rows), local.at[i])
        for k in range(parts[i]):
            part = src.at[pl.ds(k * step, step)]
            there = spot(me, k * step, step)
            copy = remote(part, there, xs.at[i, k], xr.at[i, k], across)
            copy.start()
            waits.append(copy.wait_send)
            got = spot((1 - x) * 2 + c, k * step, step)
            forwards.append((copy, remote(got, got, fs.at[i, k], fr.at[i, k], beside)))
        copy = remote(src, spot(me, 0, rows), cs.at[i], cr.at[i], beside)
        copy.start()
        own.start()
        waits += [copy.wait, own.wait]
    for copy, forward in forwards:
        copy.wait_recv()
        forward.start()
        waits.append(forward.wait)
    for wait in waits:
        wait()


def group_gather(cid, values, columns=None, parts=None):
    count = len(values)
    columns = columns or [False] * count
    parts = parts or [4] * count
    most = max(parts)
    shapes = [
        jax.ShapeDtypeStruct(
            (v.shape[0], v.shape[1] * GROUP) if col else (GROUP,) + v.shape, v.dtype
        )
        for v, col in zip(values, columns)
    ]
    return comm_call(
        functools.partial(group_gather_kernel, count, tuple(columns), tuple(parts)),
        cid,
        shapes,
        [DMA((count,)), DMA((count, most)), DMA((count, most)), DMA((count,)), DMA((count,)),
         DMA((count, most)), DMA((count, most))],
        [ANY] * count,
        [ANY] * count,
    )(*values)


def group_reduce_kernel(parts, src, out, from_core, to_x, from_x, cs, cr, xs, xr):
    seq, me, x, c = place_now()
    across = (seq, (1 - x) * 2 + c)
    beside = (seq, x * 2 + 1 - c)
    greet([across, beside])
    rows = src.shape[1]
    step = rows // parts
    order = [1 - x, x]
    cores = []
    for i in range(2):
        for k in range(parts):
            span = pl.ds(k * step, step)
            copy = remote(
                src.at[order[i] * 2 + 1 - c, span], from_core.at[i, span], cs.at[i, k], cr.at[i, k], beside
            )
            copy.start()
            cores.append(copy)
    sends = []
    for k in range(parts):
        span = pl.ds(k * step, step)
        cores[k].wait_recv()
        to_x[span, :] = (
            src[order[0] * 2 + c, span, :].astype(F32) + from_core[0, span, :].astype(F32)
        ).astype(BF16)
        copy = remote(to_x.at[span], from_x.at[span], xs.at[k], xr.at[k], across)
        copy.start()
        sends.append(copy)
    for k in range(parts):
        span = pl.ds(k * step, step)
        cores[parts + k].wait_recv()
        sends[k].wait_recv()
        out[span, :] = (
            src[order[1] * 2 + c, span, :].astype(F32)
            + from_core[1, span, :].astype(F32)
            + from_x[span, :].astype(F32)
        ).astype(out.dtype)
    for copy in cores + sends:
        copy.wait_send()


def group_reduce(cid, value, dtype, parts=4):
    rows, width = value.shape[1:]
    return comm_call(
        functools.partial(group_reduce_kernel, parts),
        cid,
        jax.ShapeDtypeStruct((rows, width), dtype),
        [pltpu.VMEM((2, rows, width), BF16), pltpu.VMEM((rows, width), BF16), pltpu.VMEM((rows, width), BF16),
         DMA((2, parts)), DMA((2, parts)), DMA((parts,)), DMA((parts,))],
        [VMEM],
        VMEM,
    )(value)


def group_exchange_kernel(src, out, local, ss, rs):
    seq, me, x, c = place_now()
    peers = [(seq, lax.rem(me + d, GROUP)) for d in range(1, GROUP)]
    greet(peers)
    copies = []
    for d in (2, 1, 3):
        peer = peers[d - 1]
        copy = remote(src.at[peer[1]], out.at[me], ss.at[d - 1], rs.at[d - 1], peer)
        copy.start()
        copies.append(copy)
    own = pltpu.make_async_copy(src.at[me], out.at[me], local)
    own.start()
    for copy in copies:
        copy.wait()
    own.wait()


def group_exchange(cid, value):
    return comm_call(
        group_exchange_kernel,
        cid,
        jax.ShapeDtypeStruct(value.shape, value.dtype),
        [DMA, DMA((GROUP - 1,)), DMA((GROUP - 1,))],
        [ANY],
        ANY,
    )(value)


def keys_gather_kernel(n, heads, meta, cot, out, metas, cots, own_sem, hs, hr, ms, mr, rs, rr, ls, lr, ys, yr,
                       local, xs, xr, cs, cr, fs, fr):
    seq, me, x, c = place_now()
    y = seq % 2
    z = seq // 2
    nz = n // 2
    across = (seq, (1 - x) * 2 + c)
    beside = (seq, x * 2 + 1 - c)
    peers = [(seq, lax.rem(me + d, GROUP)) for d in range(1, GROUP)]
    peers += [(lax.rem(seq + d, n), me) for d in range(1, n)]
    greet(peers)
    for j in range(2):
        target = c * 2 + j

        @pl.when(target == me)
        def _():
            pltpu.make_async_copy(heads.at[j], out.at[seq, x], own_sem.at[0]).start()

        @pl.when(target != me)
        def _():
            remote(heads.at[j], out.at[seq, x], hs.at[j], hr.at[x], (seq, target)).start()

    small = []
    for d in range(1, n):
        copy = remote(meta, metas.at[seq], ms.at[d - 1], mr.at[d - 1], (lax.rem(seq + d, n), me))
        copy.start()
        small.append(copy)
    own_meta = pltpu.make_async_copy(meta, metas.at[seq], own_sem.at[1])
    own_meta.start()
    for t in range(2):
        source = t * 2 + x

        @pl.when(source == me)
        def _():
            pltpu.make_async_copy(heads.at[0], out.at[seq, t], own_sem.at[0]).wait()

        @pl.when(source != me)
        def _():
            remote(heads.at[0], out.at[seq, t], hs.at[0], hr.at[t], (seq, source)).wait_recv()

    def block(owner_z, owner_y):
        return out.at[owner_z * 2 + owner_y]

    right = (seq + 2, me)
    left = (seq - 2, me)
    beyond = (z * 2 + 1 - y, me)

    def to_y(owner_z):
        remote(block(owner_z, y), block(owner_z, y), ys.at[owner_z], yr.at[owner_z], beyond).start()

    rows = cot.shape[0]
    parts = 2
    step = rows // parts

    for t in range(1, nz + 1):
        go_right = z - t + 1
        go_left = z + t - 1
        if t > 1:

            @pl.when(go_right >= 0)
            def _():
                remote(block(go_right, y), block(go_right, y), rs.at[t - 1], rr.at[t - 1], left).wait_recv()

            @pl.when(go_left < nz)
            def _():
                remote(block(go_left, y), block(go_left, y), ls.at[t - 1], lr.at[t - 1], right).wait_recv()

        if t < nz:

            @pl.when((go_right >= 0) & (z < nz - 1))
            def _():
                remote(block(go_right, y), block(go_right, y), rs.at[t], rr.at[t], right).start()

            @pl.when((go_left < nz) & (z > 0))
            def _():
                remote(block(go_left, y), block(go_left, y), ls.at[t], lr.at[t], left).start()

        @pl.when(go_right >= 0)
        def _():
            to_y(go_right)

        if t > 1:

            @pl.when(go_left < nz)
            def _():
                to_y(go_left)

        if t == 1:
            xcopies = []
            for k in range(parts):
                part = pl.ds(k * step, step)
                copy = remote(cot.at[part], cots.at[me, part], xs.at[k], xr.at[k], across)
                copy.start()
                xcopies.append(copy)
            ccopy = remote(cot, cots.at[me], cs, cr, beside)
            ccopy.start()
            own_cot = pltpu.make_async_copy(cot, cots.at[me], local)
            own_cot.start()
    forwards = []
    for k in range(parts):
        part = pl.ds(k * step, step)
        xcopies[k].wait()
        got = cots.at[(1 - x) * 2 + c, part]
        forward = remote(got, got, fs.at[k], fr.at[k], beside)
        forward.start()
        forwards.append(forward)
    for k in range(nz):
        remote(block(k, 1 - y), block(k, 1 - y), ys.at[k], yr.at[k], beyond).wait()
    for t in range(1, nz):

        @pl.when((z - t + 1 >= 0) & (z < nz - 1))
        def _():
            remote(block(z, y), block(z, y), rs.at[t], rr.at[t], right).wait_send()

        @pl.when((z + t - 1 < nz) & (z > 0))
        def _():
            remote(block(z, y), block(z, y), ls.at[t], lr.at[t], left).wait_send()

    for j in range(2):

        @pl.when(c * 2 + j != me)
        def _():
            remote(heads.at[j], out.at[seq, x], hs.at[j], hr.at[x], (seq, c * 2 + j)).wait_send()

    for copy in small + forwards + [ccopy]:
        copy.wait()
    own_meta.wait()
    own_cot.wait()


def keys_gather(cid, n, heads, meta, cot):
    nz = n // 2
    return comm_call(
        functools.partial(keys_gather_kernel, n),
        cid,
        [
            jax.ShapeDtypeStruct((n,) + heads.shape, BF16),
            jax.ShapeDtypeStruct((n,) + meta.shape, F32),
            jax.ShapeDtypeStruct((GROUP,) + cot.shape, BF16),
        ],
        [DMA((2,)), DMA((2,)), DMA((2,)), DMA((n - 1,)), DMA((n - 1,)), DMA((nz,)), DMA((nz,)), DMA((nz,)),
         DMA((nz,)), DMA((nz,)), DMA((nz,)), DMA, DMA((2,)), DMA((2,)), DMA, DMA, DMA((2,)), DMA((2,))],
        [ANY] * 3,
        [ANY] * 3,
    )(heads, meta, cot)


def keys_reduce_kernel(n, src, out, y_got, r_got, l_got, r_out, l_out, moved, ys, yr, rs, rr, ls, lr, hs, hr, local):
    seq, me, x, c = place_now()
    y = seq % 2
    z = seq // 2
    nz = n // 2
    right = (seq + 2, me)
    left = (seq - 2, me)
    beyond = (z * 2 + 1 - y, me)
    barrier = pltpu.get_barrier_semaphore()
    for d in range(1, GROUP):
        pl.semaphore_signal(barrier, inc=1, device_id=(seq, lax.rem(me + d, GROUP)), device_id_type=MESH)
    pl.semaphore_signal(barrier, inc=1, device_id=beyond, device_id_type=MESH)

    @pl.when(z > 0)
    def _():
        pl.semaphore_signal(barrier, inc=1, device_id=left, device_id_type=MESH)

    @pl.when(z < nz - 1)
    def _():
        pl.semaphore_signal(barrier, inc=1, device_id=right, device_id_type=MESH)

    chain = jnp.where(z > 0, 1, 0) + jnp.where(z < nz - 1, 1, 0)
    pl.semaphore_wait(barrier, GROUP + chain)

    def swap(k):
        return remote(src.at[k * 2 + 1 - y], y_got.at[k], ys.at[k], yr.at[k], beyond)

    for t in range(1, nz):
        go_right = z + nz - t
        go_left = z - nz + t

        @pl.when(go_right < nz)
        def _():
            swap(go_right).start()

        @pl.when(go_left >= 0)
        def _():
            swap(go_left).start()

    swap(z).start()

    def pair_sum(k, more, to):
        def body(i, carry):
            half = i // 2
            span = pl.ds(pl.multiple_of((i % 2) * 256, 256), 256)
            total = src[k * 2 + y, half, span, :].astype(F32) + y_got[k, half, span, :].astype(F32)
            for ref in more:
                total = total + ref[half, span, :].astype(F32)
            to[half, span, :] = total.astype(BF16)
            return carry

        lax.fori_loop(0, 4, body, 0)

    for t in range(1, nz):
        go_right = z + nz - t
        go_left = z - nz + t

        @pl.when(go_right < nz)
        def _():
            swap(go_right).wait_recv()
            if t == 1:
                pair_sum(go_right, [], r_out.at[t - 1])
            else:

                @pl.when(z > 0)
                def _():
                    remote(r_out.at[t - 1], r_got.at[t - 2], rs.at[t - 2], rr.at[t - 2], left).wait_recv()
                    pair_sum(go_right, [r_got.at[t - 2]], r_out.at[t - 1])

                @pl.when(z == 0)
                def _():
                    pair_sum(go_right, [], r_out.at[t - 1])

            remote(r_out.at[t - 1], r_got.at[t - 1], rs.at[t - 1], rr.at[t - 1], right).start()

        @pl.when(go_left >= 0)
        def _():
            swap(go_left).wait_recv()
            if t == 1:
                pair_sum(go_left, [], l_out.at[t - 1])
            else:

                @pl.when(z < nz - 1)
                def _():
                    remote(l_out.at[t - 1], l_got.at[t - 2], ls.at[t - 2], lr.at[t - 2], right).wait_recv()
                    pair_sum(go_left, [l_got.at[t - 2]], l_out.at[t - 1])

                @pl.when(z == nz - 1)
                def _():
                    pair_sum(go_left, [], l_out.at[t - 1])

            remote(l_out.at[t - 1], l_got.at[t - 1], ls.at[t - 1], lr.at[t - 1], left).start()

    swap(z).wait_recv()
    last = nz - 2

    def got_left():
        remote(r_out.at[last], r_got.at[last], rs.at[last], rr.at[last], left).wait_recv()

    def got_right():
        remote(l_out.at[last], l_got.at[last], ls.at[last], lr.at[last], right).wait_recv()

    @pl.when(z == 0)
    def _():
        got_right()
        pair_sum(z, [l_got.at[last]], moved)

    @pl.when(z == nz - 1)
    def _():
        got_left()
        pair_sum(z, [r_got.at[last]], moved)

    @pl.when((z > 0) & (z < nz - 1))
    def _():
        got_left()
        got_right()
        pair_sum(z, [r_got.at[last], l_got.at[last]], moved)

    for t in range(2):
        target = t * 2 + x

        @pl.when(target == me)
        def _():
            pltpu.make_async_copy(moved.at[t], out.at[c], local).start()

        @pl.when(target != me)
        def _():
            remote(moved.at[t], out.at[c], hs.at[t], hr.at[c], (seq, target)).start()

    for j in range(2):
        source = c * 2 + j

        @pl.when(source == me)
        def _():
            pltpu.make_async_copy(moved.at[0], out.at[j], local).wait()

        @pl.when(source != me)
        def _():
            remote(moved.at[0], out.at[j], hs.at[0], hr.at[j], (seq, source)).wait_recv()

    for t in range(2):

        @pl.when(t * 2 + x != me)
        def _():
            remote(moved.at[t], out.at[c], hs.at[t], hr.at[c], (seq, t * 2 + x)).wait_send()

    for k in range(nz):
        swap(k).wait_send()
    for t in range(1, nz):

        @pl.when(z + nz - t < nz)
        def _():
            remote(r_out.at[t - 1], r_got.at[t - 1], rs.at[t - 1], rr.at[t - 1], right).wait_send()

        @pl.when(z - nz + t >= 0)
        def _():
            remote(l_out.at[t - 1], l_got.at[t - 1], ls.at[t - 1], lr.at[t - 1], left).wait_send()


def keys_reduce(cid, n, value):
    nz = n // 2
    shape = value.shape[1:]
    chain = pltpu.VMEM((nz - 1,) + shape, BF16)
    return comm_call(
        functools.partial(keys_reduce_kernel, n),
        cid,
        jax.ShapeDtypeStruct(shape, BF16),
        [pltpu.VMEM((nz,) + shape, BF16), chain, chain, chain, chain, pltpu.VMEM(shape, BF16),
         DMA((nz,)), DMA((nz,)), DMA((nz - 1,)), DMA((nz - 1,)), DMA((nz - 1,)), DMA((nz - 1,)),
         DMA((2,)), DMA((2,)), DMA],
        [VMEM],
        VMEM,
    )(value)


def total_kernel(rounds, whole, part, whole_out, part_out, bufs, gots, mine, theirs, ss, rs):
    seq, me, x, c = place_now()
    across = (seq, (1 - x) * 2 + c)
    beside = (seq, x * 2 + 1 - c)
    partners = []
    for r in range(rounds):
        bit = 1 << r
        partners.append((seq + bit - 2 * bit * ((seq // bit) % 2), me))
    greet(partners + [across, beside])
    rows = whole.shape[0]
    bufs[0, :rows, :] = whole[...]
    bufs[0, rows:, :] = part[...]
    for r in range(rounds + 1):
        partner = partners[r] if r < rounds else across
        copy = remote(bufs.at[r], gots.at[r], ss.at[r], rs.at[r], partner)
        copy.start()
        copy.wait()
        if r < rounds:
            bufs[r + 1] = bufs[r] + gots[r]
    mine[0, :rows, :] = bufs[rounds, :rows, :] + gots[rounds, :rows, :]
    mine[0, rows:, :] = bufs[rounds, rows:, :]
    mine[1, rows:, :] = gots[rounds, rows:, :]
    mine[1, :rows, :] = jnp.zeros_like(whole)
    copy = remote(mine, theirs, ss.at[rounds + 1], rs.at[rounds + 1], beside)
    copy.start()
    copy.wait()
    whole_out[...] = mine[0, :rows, :] + theirs[0, :rows, :]
    part_out[x * 2 + c] = mine[0, rows:, :]
    part_out[(1 - x) * 2 + c] = mine[1, rows:, :]
    part_out[x * 2 + 1 - c] = theirs[0, rows:, :]
    part_out[(1 - x) * 2 + 1 - c] = theirs[1, rows:, :]


def totals(cid, n, whole, part):
    rounds = int(math.log2(n))
    rows = whole.shape[0] + part.shape[0]
    return comm_call(
        functools.partial(total_kernel, rounds),
        cid,
        [jax.ShapeDtypeStruct(whole.shape, F32), jax.ShapeDtypeStruct((GROUP,) + part.shape, F32)],
        [pltpu.VMEM((rounds + 1, rows, 128), F32), pltpu.VMEM((rounds + 1, rows, 128), F32),
         pltpu.VMEM((2, rows, 128), F32), pltpu.VMEM((2, rows, 128), F32),
         DMA((rounds + 2,)), DMA((rounds + 2,))],
        [VMEM, VMEM],
        [VMEM, VMEM],
    )(whole, part)


def masks(n, own_ref, meta_ref):
    def column(row):
        return jnp.broadcast_to(own_ref[0, row : row + 1, :], (128, 128)).T

    row_document = column(0)
    row_place = column(1)
    out = []
    for j in range(n):
        key_place = meta_ref[j, 0, 1:2, :]
        key_document = meta_ref[j, 0, 2:3, :]
        allowed = (row_document == key_document) & (key_place <= row_place) | (key_place == row_place)
        out.append(allowed)
    return out


def attend_kernel(n, q_ref, kv_ref, own_ref, meta_ref, low_ref, mixed_ref, total_ref):
    keys = kv_ref[:, 0].reshape(n * 128, DH)
    values = kv_ref[:, 1].reshape(n * 128, DH)
    allowed = masks(n, own_ref, meta_ref)
    for h in range(2):
        cols = slice(h * DH, (h + 1) * DH)
        raw = contract_last(q_ref[:, cols], keys)
        pieces = []
        total = jnp.zeros((128, 128), F32)
        for j in range(n):
            squash = jnp.tanh(raw[:, j * 128 : (j + 1) * 128] * (DH ** (-0.5) / CAP))
            mass = jnp.where(allowed[j], jnp.exp(CAP * squash), 0.0)
            total = total + mass
            pieces.append(mass.astype(BF16))
        row = jnp.sum(total, axis=1, keepdims=True)
        mixed = dot(jnp.concatenate(pieces, axis=1), values) / row
        mixed_ref[:, cols] = mixed
        low_ref[:, cols] = mixed.astype(BF16)
        total_ref[:, h * 128 : (h + 1) * 128] = jnp.broadcast_to(row, (128, 128))


def attend(n, query, pairs, own_meta, metas):
    return pl.pallas_call(
        functools.partial(attend_kernel, n),
        grid=(GROUP,),
        out_shape=[
            jax.ShapeDtypeStruct(query.shape, BF16),
            jax.ShapeDtypeStruct(query.shape, F32),
            jax.ShapeDtypeStruct((query.shape[0], 256), F32),
        ],
        in_specs=[
            pl.BlockSpec((128, 2 * DH), lambda p: (p, 0)),
            pl.BlockSpec((n, 2, 128, DH), lambda p: (0, 0, p, 0)),
            pl.BlockSpec((1, 8, 128), lambda p: (p, 0, 0)),
            pl.BlockSpec((n, 1, 8, 128), lambda p: (0, p, 0, 0)),
        ],
        out_specs=[
            pl.BlockSpec((128, 2 * DH), lambda p: (p, 0)),
            pl.BlockSpec((128, 2 * DH), lambda p: (p, 0)),
            pl.BlockSpec((128, 256), lambda p: (p, 0)),
        ],
        compiler_params=pltpu.CompilerParams(vmem_limit_bytes=VMEM_LIMIT),
    )(query, pairs, own_meta, metas)


def attend_back_kernel(n, q_ref, kv_ref, own_ref, meta_ref, mixed_ref, total_ref, grad_ref, dq_ref, dkv_ref):
    keys = kv_ref[:, 0].reshape(n * 128, DH)
    values = kv_ref[:, 1].reshape(n * 128, DH)
    allowed = masks(n, own_ref, meta_ref)
    grad_keys = None
    for h in range(2):
        cols = slice(h * DH, (h + 1) * DH)
        query = q_ref[:, cols]
        grad = grad_ref[:, cols]
        delta = jnp.sum(grad.astype(F32) * mixed_ref[:, cols], axis=1, keepdims=True)
        inverse = 1.0 / total_ref[:, h * 128 : (h + 1) * 128]
        raw = contract_last(query, keys)
        grad_share = contract_last(grad, values)
        shares = []
        grads = []
        for j in range(n):
            span = slice(j * 128, (j + 1) * 128)
            squash = jnp.tanh(raw[:, span] * (DH ** (-0.5) / CAP))
            share = jnp.where(allowed[j], jnp.exp(CAP * squash), 0.0) * inverse
            shares.append(share.astype(BF16))
            grads.append(
                (share * (grad_share[:, span] - delta) * ((1.0 - squash * squash) * DH ** (-0.5))).astype(BF16)
            )
        share = jnp.concatenate(shares, axis=1)
        grad_raw = jnp.concatenate(grads, axis=1)
        dq_ref[:, cols] = dot(grad_raw, keys)
        new_keys = contract_first(grad_raw, query)
        new_values = contract_first(share, grad)
        if grad_keys is None:
            grad_keys, grad_values = new_keys, new_values
        else:
            grad_keys, grad_values = grad_keys + new_keys, grad_values + new_values
    dkv_ref[:, 0] = grad_keys.astype(BF16).reshape(n, 128, DH)
    dkv_ref[:, 1] = grad_values.astype(BF16).reshape(n, 128, DH)


def attend_back(n, query, pairs, own_meta, metas, mixed, total, grad):
    rows = pl.BlockSpec((128, 2 * DH), lambda p: (p, 0))
    heads = pl.BlockSpec((n, 2, 128, DH), lambda p: (0, 0, p, 0))
    return pl.pallas_call(
        functools.partial(attend_back_kernel, n),
        grid=(GROUP,),
        out_shape=[
            jax.ShapeDtypeStruct(query.shape, F32),
            jax.ShapeDtypeStruct(pairs.shape, BF16),
        ],
        in_specs=[
            rows,
            heads,
            pl.BlockSpec((1, 8, 128), lambda p: (p, 0, 0)),
            pl.BlockSpec((n, 1, 8, 128), lambda p: (0, p, 0, 0)),
            rows,
            pl.BlockSpec((128, 256), lambda p: (p, 0)),
            rows,
        ],
        out_specs=[rows, heads],
        compiler_params=pltpu.CompilerParams(vmem_limit_bytes=VMEM_LIMIT),
    )(query, pairs, own_meta, metas, mixed, total, grad)


def rms_inverse(value):
    return lax.rsqrt(jnp.mean(value * value, axis=-1, keepdims=True) + EPSILON)


def norm_back(inverse, normed, upstream):
    return inverse * (upstream - normed * jnp.mean(upstream * normed, axis=-1, keepdims=True))


def rotate(value, cosine, sine):
    half = DH // 2
    first = value[..., :half]
    second = value[..., half:]
    return jnp.concatenate([first * cosine - second * sine, second * cosine + first * sine], axis=-1)


def code_levels(code, step):
    levels = code.astype(F32)
    return (jnp.floor(levels / step) * step + step / 2.0).astype(BF16)


def gelu_parts(gate):
    root = math.sqrt(2.0 / math.pi)
    square = gate * gate
    bend = jnp.tanh(root * gate * (1.0 + 0.044715 * square))
    value = 0.5 * gate * (1.0 + bend)
    slope = 0.5 * (1.0 + bend) + 0.5 * gate * (1.0 - bend * bend) * root * (1.0 + 3 * 0.044715 * square)
    return value, slope


def seq_swap(value, n):
    return lax.ppermute(value, "seq", [(s, s ^ 1) for s in range(n)])


def x_swap(value):
    return lax.ppermute(value, "fsdp", [(f, f ^ 2) for f in range(GROUP)])


def core_swap(value):
    return lax.ppermute(value, "fsdp", [(f, f ^ 1) for f in range(GROUP)])


def pair_rows(value, n, y):
    rows, width = value.shape
    split = value.reshape(rows, n // 2, 2, width // n)
    here = lax.dynamic_index_in_dim(split, y, 2, keepdims=False).reshape(rows, width // 2)
    there = lax.dynamic_index_in_dim(split, 1 - y, 2, keepdims=False).reshape(rows, width // 2)
    return here, seq_swap(there, n)


def chain_sum(block, n, z):
    nz = n // 2
    pick = lambda k: lax.dynamic_index_in_dim(block, jnp.clip(k, 0, nz - 1), 0, keepdims=False)
    from_left = from_right = None
    for t in range(1, nz):
        right = pick(z + nz - t)
        left = pick(z - nz + t)
        if t > 1:
            right = (right.astype(F32) + from_left.astype(F32)).astype(BF16)
            left = (left.astype(F32) + from_right.astype(F32)).astype(BF16)
        go_right = [(s, s + 2) for s in range(2 * t)]
        go_left = [(n - 1 - s, n - 3 - s) for s in range(2 * t)]
        from_left = lax.ppermute(right, "seq", go_right)
        from_right = lax.ppermute(left, "seq", go_left)
    return pick(z).astype(F32) + from_left.astype(F32) + from_right.astype(F32)


def pair_product(lefts, rights):
    return contract_first(lefts[0], rights[0]) + contract_first(lefts[1], rights[1])


def lanes(value, rows):
    flat = value.reshape(-1)
    return jnp.pad(flat, (0, rows * 128 - flat.shape[0])).reshape(rows, 128)


def per_device(
    n,
    tokens,
    doc_ids,
    padding,
    token_order,
    query_code,
    key_value_code,
    output_code,
    gate_up_code,
    down_code,
    query_scale,
    key_value_scale,
    output_scale,
    gate_up_scale,
    down_scale,
    norm_gains,
    cotangent,
):
    seq = lax.axis_index("seq")
    me = lax.axis_index("fsdp")
    is_gate = me < 2
    c = me % 2
    y = seq % 2
    z = seq // 2
    width = tokens.shape[2]
    part = width // GROUP
    rows = GROUP * tokens.shape[1]
    own = tokens.shape[1]

    def mine(vector):
        size = vector.shape[-1] // GROUP
        return lax.dynamic_slice_in_dim(vector, me * size, size, vector.ndim - 1)

    def blocks_to_rows(blocks):
        return jnp.concatenate([blocks[i] for i in range(GROUP)], axis=1)

    def own_rows(value):
        return lax.dynamic_slice_in_dim(value, me * own, own, 0)

    gain = 1.0 + norm_gains
    place = token_order[0].astype(F32)
    document = doc_ids[0].astype(F32)
    meta = jnp.stack([document, place, jnp.where(padding[0] == 1, document, -1.0)] + [document] * 5)

    token_blocks, own_meta = group_gather(1, [tokens[0], meta], parts=[4, 1])
    inputs = token_blocks.reshape(rows, width).astype(F32)
    turn = own_meta[:, 1, :].reshape(rows, 1) * (
        BASE ** (-2.0 * jnp.arange(DH // 2).astype(F32) / DH)
    )[None, :]
    cosine = jnp.cos(turn)
    sine = jnp.sin(turn)
    first_inverse = rms_inverse(inputs)
    first_input = (inputs * first_inverse * gain[0]).astype(BF16)
    query_raw = dot(first_input, query_code)
    pair_raw = dot(first_input, key_value_code)
    my_query_scale = mine(query_scale)
    my_pair_scale = mine(key_value_scale)
    pair_cosine = jnp.where(is_gate, cosine, 1.0)
    pair_sine = jnp.where(is_gate, sine, 0.0)
    query = rotate(
        (query_raw * my_query_scale).reshape(rows, 2, DH), cosine[:, None], sine[:, None]
    ).astype(BF16).reshape(rows, 2 * DH)
    pair_plain = pair_raw * my_pair_scale
    heads = jnp.stack(
        [rotate(pair_plain[:, j * DH : (j + 1) * DH], pair_cosine, pair_sine) for j in range(2)]
    ).astype(BF16)
    first_pair = pair_rows(first_input, n, y)
    pairs, metas, cot_blocks = keys_gather(2, n, heads, own_meta, cotangent[0])

    mixed_low, mixed, mass = attend(n, query, pairs, own_meta, metas)
    (mixed_rows,) = group_gather(3, [mixed_low], columns=[True])
    mixed_pair = pair_rows(mixed_rows, n, y)
    branch_own = dot(mixed_rows, output_code).astype(BF16)
    (branch_blocks,) = group_gather(4, [branch_own])
    branch_raw = blocks_to_rows(branch_blocks).astype(F32)
    branch = branch_raw * output_scale
    second_inverse = rms_inverse(branch)
    middle = inputs + branch * second_inverse * gain[1]
    third_inverse = rms_inverse(middle)
    second_input = (middle * third_inverse * gain[2]).astype(BF16)
    second_pair = pair_rows(second_input, n, y)

    gate_levels = code_levels(gate_up_code, 16.0)
    down_levels = code_levels(down_code, 64.0)
    my_gate_scale = mine(gate_up_scale)
    columns = gate_levels.shape[1]
    chunks = 4
    size = columns // chunks
    down_split = down_levels.reshape(2, columns, part)
    down_here = lax.dynamic_index_in_dim(down_split, c, 0, keepdims=False)
    down_there = lax.dynamic_index_in_dim(down_split, 1 - c, 0, keepdims=False)
    owns, others, hiddens, hiddens_core = [], [], [], []
    for k in range(chunks):
        span = slice(k * size, (k + 1) * size)
        owns.append((dot(second_input, gate_levels[:, span]) * my_gate_scale[span]).astype(BF16))
        others.append(x_swap(owns[k]))
    down_sum = 0.0
    for k in range(chunks):
        span = slice(k * size, (k + 1) * size)
        gate = jnp.where(is_gate, owns[k], others[k]).astype(F32)
        up = jnp.where(is_gate, others[k], owns[k]).astype(F32)
        hiddens.append((gelu_parts(gate)[0] * up).astype(BF16))
        hiddens_core.append(core_swap(hiddens[k]))
        down_sum = down_sum + dot(hiddens[k], down_here[span]) + dot(hiddens_core[k], down_there[span])
    down_own = down_sum.astype(BF16)
    (down_blocks,) = group_gather(5, [down_own])
    down_raw = blocks_to_rows(down_blocks).astype(F32)
    down = down_raw * down_scale
    fourth_inverse = rms_inverse(down)
    fourth = down * fourth_inverse
    result = own_rows(middle + fourth * gain[3]).astype(BF16)

    grad_result = cot_blocks.reshape(rows, width).astype(F32)
    gain_four = jnp.sum(own_rows(grad_result * fourth), axis=0)
    grad_down_full = norm_back(fourth_inverse, fourth, grad_result * gain[3])
    grad_down_own = lax.dynamic_slice_in_dim(grad_down_full, me * part, part, 1)
    scale_down = jnp.sum(down_own.astype(F32) * grad_down_own, axis=0)
    grad_down = (grad_down_own * mine(down_scale)).astype(BF16)
    grad_down_pair = (grad_down, seq_swap(grad_down, n))

    here = jnp.concatenate(hiddens, axis=1)
    there = jnp.concatenate(hiddens_core, axis=1)
    hidden_rows = jnp.concatenate([jnp.where(c == 0, here, there), jnp.where(c == 0, there, here)], axis=1)
    hidden_pair = pair_rows(hidden_rows, n, y)
    down_block = pair_product(hidden_pair, grad_down_pair).astype(BF16)
    down_grad = chain_sum(down_block.reshape(n // 2, -1, part), n, z)

    grads, gate_sums = [], []
    grad_second_sum = 0.0
    core_gots = []
    for k in range(chunks):
        span = slice(k * size, (k + 1) * size)
        core_gots.append(core_swap(contract_last(grad_down, down_there[span]).astype(BF16)))
    sums, x_gots = [], []
    for k in range(chunks):
        span = slice(k * size, (k + 1) * size)
        sums.append((contract_last(grad_down, down_here[span]) + core_gots[k].astype(F32)).astype(BF16))
        x_gots.append(x_swap(sums[k]))
    for k in range(chunks):
        span = slice(k * size, (k + 1) * size)
        grad_hidden = sums[k].astype(F32) + x_gots[k].astype(F32)
        gate = jnp.where(is_gate, owns[k], others[k]).astype(F32)
        up = jnp.where(is_gate, others[k], owns[k]).astype(F32)
        value, slope = gelu_parts(gate)
        grad_full = grad_hidden * jnp.where(is_gate, up * slope, value)
        gate_sums.append(jnp.sum(owns[k].astype(F32) * grad_full, axis=0) / my_gate_scale[span])
        grads.append((grad_full * my_gate_scale[span]).astype(BF16))
        grad_second_sum = grad_second_sum + contract_last(grads[k], gate_levels[:, span])
    scale_gate = jnp.concatenate(gate_sums)
    grad_gate_up = jnp.concatenate(grads, axis=1)
    grad_gate_pair = (grad_gate_up, seq_swap(grad_gate_up, n))

    grad_second_input = group_reduce(6, grad_second_sum.astype(BF16).reshape(GROUP, own, width), F32)
    gate_block = pair_product(second_pair, grad_gate_pair).astype(BF16)
    gate_grad = chain_sum(gate_block.reshape(n // 2, -1, columns), n, z)

    my_middle = own_rows(middle)
    third_inverse = own_rows(third_inverse)
    second_inverse = own_rows(second_inverse)
    my_branch_raw = own_rows(branch_raw)
    third = my_middle * third_inverse
    second = my_branch_raw * output_scale * second_inverse
    my_cot = cotangent[0].astype(F32)
    gain_three = jnp.sum(grad_second_input * third, axis=0)
    grad_middle = my_cot + norm_back(third_inverse, third, grad_second_input * gain[2])
    gain_two = jnp.sum(grad_middle * second, axis=0)
    grad_branch_full = norm_back(second_inverse, second, grad_middle * gain[1])
    scale_output = jnp.sum(my_branch_raw * grad_branch_full, axis=0)
    grad_branch_own = (grad_branch_full * output_scale).astype(BF16)
    grad_branch = group_exchange(
        7, grad_branch_own.reshape(own, GROUP, part).transpose(1, 0, 2)
    ).reshape(rows, part)
    grad_branch_pair = (grad_branch, seq_swap(grad_branch, n))
    output_block = pair_product(mixed_pair, grad_branch_pair).astype(BF16)
    output_grad = chain_sum(output_block.reshape(n // 2, -1, part), n, z)
    grad_mixed_sum = jnp.stack(
        [contract_last(grad_branch, output_code[i * 2 * DH : (i + 1) * 2 * DH]) for i in range(GROUP)]
    ).astype(BF16)
    grad_mixed = group_reduce(8, grad_mixed_sum, BF16)

    grad_query, grad_pairs = attend_back(n, query, pairs, own_meta, metas, mixed, mass, grad_mixed)
    grad_heads = keys_reduce(9, n, grad_pairs).astype(F32)
    grad_query_full = rotate(
        grad_query.reshape(rows, 2, DH), cosine[:, None], -sine[:, None]
    ).reshape(rows, 2 * DH)
    scale_query = jnp.sum(query_raw * grad_query_full, axis=0)
    grad_query_low = (grad_query_full * my_query_scale).astype(BF16)
    grad_pair_full = jnp.concatenate(
        [rotate(grad_heads[j], pair_cosine, -pair_sine) for j in range(2)], axis=1
    )
    scale_pair = jnp.sum(pair_raw * grad_pair_full, axis=0)
    grad_pair_low = (grad_pair_full * my_pair_scale).astype(BF16)
    joined = jnp.concatenate([grad_query_low, grad_pair_low], axis=1)
    joined_pair = (joined, seq_swap(joined, n))
    grad_first_sum = contract_last(grad_query_low, query_code) + contract_last(grad_pair_low, key_value_code)
    grad_first_input = group_reduce(10, grad_first_sum.astype(BF16).reshape(GROUP, own, width), F32)
    attention_block = pair_product(first_pair, joined_pair).astype(BF16)
    attention_grad = chain_sum(attention_block.reshape(n // 2, -1, joined.shape[1]), n, z)
    my_inputs = tokens[0].astype(F32)
    my_inverse = rms_inverse(my_inputs)
    first = my_inputs * my_inverse
    gain_one = jnp.sum(grad_first_input * first, axis=0)
    grad_inputs = grad_middle + norm_back(my_inverse, first, grad_first_input * gain[0])

    wholes = jnp.concatenate([gain_one, gain_two, gain_three, gain_four, scale_output])
    parts = [scale_query, scale_pair, scale_gate, scale_down]
    whole_total, part_total = totals(
        11, n, lanes(wholes, 96), lanes(jnp.concatenate(parts), 56)
    )
    whole_total = whole_total.reshape(-1)
    part_total = part_total.reshape(GROUP, -1)
    pieces = []
    start = 0
    for vector in parts:
        pieces.append(part_total[:, start : start + vector.shape[0]].reshape(-1))
        start += vector.shape[0]
    q_width = query_code.shape[1]
    return (
        result[None],
        grad_inputs[None],
        attention_grad[:, :q_width],
        attention_grad[:, q_width:],
        output_grad,
        gate_grad,
        down_grad,
        pieces[0],
        pieces[1],
        whole_total[4 * width : 5 * width],
        pieces[2],
        pieces[3],
        whole_total[: 4 * width].reshape(4, width),
    )


def solution(mesh):
    return jax.shard_map(
        functools.partial(per_device, mesh.shape["seq"]),
        mesh=mesh,
        in_specs=(
            P("fsdp", "seq", None),
            P("fsdp", "seq"),
            P("fsdp", "seq"),
            P("fsdp", "seq"),
            P(None, "fsdp"),
            P(None, "fsdp"),
            P(None, "fsdp"),
            P(None, "fsdp"),
            P(None, "fsdp"),
            P(),
            P(),
            P(),
            P(),
            P(),
            P(),
            P("fsdp", "seq", None),
        ),
        out_specs=(
            P("fsdp", "seq", None),
            P("fsdp", "seq", None),
            P("seq", "fsdp"),
            P("seq", "fsdp"),
            P("seq", "fsdp"),
            P("seq", "fsdp"),
            P("seq", "fsdp"),
            P(),
            P(),
            P(),
            P(),
            P(),
            P(),
        ),
        check_vma=False,
    )
```

time: 2740 us -> 1460 us (0.53)
  waiting for transfers between devices: 2120 us -> 323 us
  Pallas kernels: 0 us -> 368 us
  blocking collectives: 263 us -> 0 us
  local copies, waits for them, and re-layouts: 85.6 us -> 272 us
  starting transfers between devices: 14.5 us -> 146 us
  other arithmetic: 80.3 us -> 185 us
    reduce_scatter x9 -> x0, waiting for transfers between devices: 1650 us -> none  [the longest x3 910 us: weight_sum(): lax.psum_scatter(contract_first(gathered, grad_cols), 'seq', scatter_dime...]
    pallas_call x0 -> x13, Pallas kernels: none -> 368 us  [the longest x4 84.2 us: group_gather(): comm_call(functools.partial(group_gather_kernel, count, tuple(columns), t...]
    ppermute x0 -> x48, waiting for transfers between devices: none -> 323 us  [the longest x8 102 us: seq_swap(): return lax.ppermute(value, 'seq', [(s, s ^ 1) for s in range(n)])]
    psum x2 -> x0, waiting for transfers between devices: 250 us -> none  [per_device(): lax.psum((jnp.stack([gain_one, gain_two, gain_three, gain_four]), scale_q...]
    all_to_all x5 -> x0, blocking collectives: 208 us -> none  [the longest x1 109 us: column_product(): lax.all_to_all(jnp.dot(gathered, weight, preferred_element_type=jnp.float...]
    all_gather x6 -> x0, waiting for transfers between devices: 163 us -> none  [the longest x4 132 us: group_rows(): return lax.all_gather(value, 'fsdp', axis=0, tiled=True)]
    ppermute x0 -> x48, starting transfers between devices: none -> 146 us  [the longest x12 111 us: chain_sum(): from_left = lax.ppermute(right, 'seq', go_right)]
    convert_element_type x6 -> x32, other arithmetic: 11.1 us -> 89.9 us  [the longest x2 24.7 us: code_levels(): return (jnp.floor(levels / step) * step + step / 2.0).astype(BF16)]
  transfers between devices with their start and end apart: 20 -> 48, of which waited for: 19 -> 11; matrix products, arithmetic and copies ran while one was open for 4% -> 36% of each run, Pallas kernels for 0% -> 16%
where the time goes in v1:
time: 1460 us; the launch traced here: 1450 us
  Pallas kernels  368 us (25%)
  waiting for transfers between devices  323 us (22%)
  local copies, waits for them, and re-layouts  272 us (19%)
  other arithmetic  185 us (13%)
  matrix products  158 us (11%)
  starting transfers between devices  146 us (10%)
    ppermute x12, starting transfers between devices, chain_sum(): from_left = lax.ppermute(right, 'seq', go_right)  111 us
    ppermute x8, waiting for transfers between devices, seq_swap(): return lax.ppermute(value, 'seq', [(s, s ^ 1) for s in range(n)])  102 us
    pallas_call x4, Pallas kernels, group_gather(): comm_call(functools.partial(group_gather_kernel, count, tuple(columns), t...  84.2 us
    ppermute x12, waiting for transfers between devices, chain_sum(): from_left = lax.ppermute(right, 'seq', go_right)  78.4 us
    ppermute x12, waiting for transfers between devices, chain_sum(): from_right = lax.ppermute(left, 'seq', go_left)  76.9 us
    pallas_call x3, Pallas kernels, group_reduce(): comm_call(functools.partial(group_reduce_kernel, parts), cid, jax.ShapeDt...  67.2 us
    ppermute x8, waiting for transfers between devices, x_swap(): return lax.ppermute(value, 'fsdp', [(f, f ^ 2) for f in range(GROUP)])  66.3 us
    pallas_call x1, Pallas kernels, keys_reduce(): comm_call(functools.partial(keys_reduce_kernel, n), cid, jax.ShapeDtypeSt...  66.1 us
  transfers between devices with their start and end apart: 48, of which 11 were waited for; matrix products, arithmetic and copies ran while one was open for 36% of the time, Pallas kernels for 16%

profile of v1, /device:TPU:0, one launch (start us, length us, event | category | flops | bytes accessed | tf_op | source)
XLA Modules:
  0.0 1455.0 jit_solution(18022111226070847545)
XLA Ops:
  3.5 22.4 %shard_map.255 = (bf16[4,128,2304]{2,1,0:T(8,128)(2,1)}, f32[4,8,128]{2,1,0:T(8,128)}) custom-call(bf16[128,2304]{1,0:T(8,128)(2,1)} %bitcast.344, f32[8,128]{1,0:T(8,128)} %stack.43.refs_1_), custom_call_target="tpu_custom_call" | custom-call | tf_op jit(solution)/shard_map/pallas_call | solution.py:125
  47.2 61.3 %shard_map.256 = (bf16[8,2,512,256]{3,2,1,0:T(8,128)(2,1)}, f32[8,4,8,128]{3,2,1,0:T(8,128)}, bf16[4,128,2304]{2,1,0:T(8,128)(2,1)}) custom-call(bf16[2,512,256]{2,1,0:T(8,128)(2,1)} %pad_maximum_fusion.7.heads, f32[4,8,128]{2,1,0:T(8,128)} %get-tuple-element.26.meta.own_ref, bf16[128,2304]{1,0:T(8,128)(2,1)} %bitcast.366), custom_call_target="tpu_custom_call" | custom-call | tf_op jit(solution)/shard_map/pallas_call | solution.py:349
  108.5 6.2 shard_map.257
  114.7 17.2 %shard_map.258 = bf16[512,2048]{1,0:T(8,128)(2,1)} custom-call(bf16[512,512]{1,0:T(8,128)(2,1)} %get-tuple-element.29.refs_0_), custom_call_target="tpu_custom_call" | custom-call | tf_op jit(solution)/shard_map/pallas_call | solution.py:125
  136.1 23.1 %shard_map.259 = bf16[4,512,576]{2,1,0:T(8,128)(2,1)} custom-call(bf16[512,576]{1,0:T(8,128)(2,1)} %copy.172.refs_0_), custom_call_target="tpu_custom_call" | custom-call | tf_op jit(solution)/shard_map/pallas_call | solution.py:125
  163.1 5.2 concatenate.82
  170.7 5.1 concatenate.87
  180.2 14.0 add_convert_fusion
  230.1 5.1 copy.182
  235.9 6.7 reshape.531
  242.6 5.5 multiply_convert_fusion
  249.8 10.7 add_convert_fusion.1
  260.6 17.0 %reshape.501 = bf16[2,4608,576]{1,0,2:T(2,128)(2,1)} reshape(bf16[9216,576]{0,1:T(8,128)(2,1)} %add_convert_fusion.1) | data formatting | bytes 21233664 | tf_op jit(solution)/shard_map/reshape | solution.py:871
  277.5 37.2 %constant_dynamic-slice_fusion.27 = (bf16[1,1152,576]{1,0,2:T(2,128)(2,1)}, bf16[1,1152,576]{1,0,2:T(2,128)(2,1)}, bf16[1,1152,576]{1,0,2:T(2,128)(2,1)}, bf16[1...) fusion(bf16[2,4608,576]{1,0,2:T(2,128)(2,1)} %reshape.501, ...), kind=kLoop, calls=%fused_computation.379 | loop fusion | bytes 21233684 | tf_op jit(solution)/shard_map/slice | solution.py:886
  331.6 8.5 constant_dynamic-slice_fusion.21
  340.0 5.8 copy.225
  345.8 6.3 copy.226
  400.9 21.5 %shard_map.260 = bf16[4,512,576]{2,1,0:T(8,128)(2,1)} custom-call(bf16[512,576]{1,0:T(8,128)(2,1)} %add_convert_fusion.8.refs_0_), custom_call_target="tpu_custom_call" | custom-call | tf_op jit(solution)/shard_map/pallas_call | solution.py:125
  426.3 5.2 concatenate.88
  433.9 5.1 concatenate.93
  461.1 6.5 broadcast_select_fusion
  467.5 7.2 select_n.225
  474.7 12.4 copy.197
  487.1 7.2 select_n.227
  494.3 12.3 copy.198
  506.6 7.2 fusion.6
  518.9 5.7 fusion.219
  536.7 9.6 collective-permute-done.15
  553.0 18.5 %collective-permute-done.13 = bf16[512,1152]{1,0:T(8,128)(2,1)S(1)} collective-permute-done((bf16[512,1152]{1,0:T(8,128)(2,1)S(1)}, bf16[512,1152]{1,0:T(8,128)(2,1)S(1)}, u32[]{:S(2)}, u32[]{:S(2)}) %collective-permute-start.13) | collective-permute-done | bytes 1179680 | tf_op jit(solution)/shard_map/ppermute | solution.py:741
  577.8 19.0 %collective-permute-done.11 = bf16[512,1152]{1,0:T(8,128)(2,1)S(1)} collective-permute-done((bf16[512,1152]{1,0:T(8,128)(2,1)S(1)}, bf16[512,1152]{1,0:T(8,128)(2,1)S(1)}, u32[]{:S(2)}, u32[]{:S(2)}) %collective-permute-start.11) | collective-permute-done | bytes 1179680 | tf_op jit(solution)/shard_map/ppermute | solution.py:741
  602.1 19.1 %collective-permute-done.9 = bf16[512,1152]{1,0:T(8,128)(2,1)S(1)} collective-permute-done((bf16[512,1152]{1,0:T(8,128)(2,1)S(1)}, bf16[512,1152]{1,0:T(8,128)(2,1)S(1)}, u32[]{:S(2)}, u32[]{:S(2)}) %collective-permute-start.9) | collective-permute-done | bytes 1179680 | tf_op jit(solution)/shard_map/ppermute | solution.py:741
  621.3 5.0 multiply_reduce_fusion.6
  627.5 5.0 fusion.23
  632.4 6.7 convolution_add_fusion.4
  639.1 6.7 convolution_add_fusion.3
  645.8 6.2 fusion.27
  652.0 20.0 %shard_map.261 = f32[128,2304]{1,0:T(8,128)} custom-call(bf16[4,128,2304]{2,1,0:T(8,128)(2,1)} %bitcast.371), custom_call_target="tpu_custom_call" | custom-call | tf_op jit(solution)/shard_map/pallas_call | solution.py:178
  686.8 13.8 shard_map.262
  716.2 23.4 %shard_map.263.grad_ref = bf16[512,512]{1,0:T(8,128)(2,1)} custom-call(bf16[4,512,512]{2,1,0:T(8,128)(2,1)} %pad_maximum_fusion.2.src), custom_call_target="tpu_custom_call" | custom-call | tf_op jit(solution)/shard_map/pallas_call | solution.py:178
  739.7 9.4 shard_map.264
  749.0 66.1 %shard_map.265 = bf16[2,512,256]{2,1,0:T(8,128)(2,1)} custom-call(bf16[8,2,512,256]{3,2,1,0:T(8,128)(2,1)} %get-tuple-element.34.src), custom_call_target="tpu_custom_call" | custom-call | tf_op jit(solution)/shard_map/pallas_call | solution.py:527
  830.8 23.7 %shard_map.266 = f32[128,2304]{1,0:T(8,128)} custom-call(bf16[4,128,2304]{2,1,0:T(8,128)(2,1)} %bitcast.342), custom_call_target="tpu_custom_call" | custom-call | tf_op jit(solution)/shard_map/pallas_call | solution.py:178
  863.5 10.3 fusion.209
  880.0 92.1 %collective-permute-done.25 = bf16[512,576]{0,1:T(8,128)(2,1)S(1)} collective-permute-done((bf16[512,576]{0,1:T(8,128)(2,1)}, bf16[512,576]{0,1:T(8,128)(2,1)S(1)}, u32[]{:S(2)}, u32[]{:S(2)}) %collective-permute-start.25) | collective-permute-done | bytes 589856 | tf_op jit(solution)/shard_map/ppermute | solution.py:737
  979.8 14.1 fusion
  993.9 5.3 dynamic-slice_bitcast_fusion.1
  999.2 5.6 collective-permute-start.34
  1004.8 5.1 constant_dynamic-slice_fusion.20
  1014.2 5.0 collective-permute-done.17
  1027.4 59.8 %shard_map.267 = (f32[96,128]{1,0:T(8,128)}, f32[4,56,128]{2,1,0:T(8,128)}) custom-call(f32[96,128]{1,0:T(8,128)} %pad_bitcast_fusion.whole, f32[56,128]{1,0:T(8,128)} %pad_bitcast_fusion.1.part), custom_call_target="tpu_custom_call" | custom-call | tf_op jit(solution)/shard_map/pallas_call | solution.py:575
  1105.8 8.9 add_convert_fusion.2
  1114.7 8.1 reshape.520
  1130.1 6.1 collective-permute-start.35
  1136.2 20.5 %constant_dynamic-slice_fusion.11 = (bf16[1,1152,576]{1,0,2:T(2,128)(2,1)}, bf16[1,1152,576]{1,0,2:T(2,128)(2,1)}, bf16[1,1152,576]{1,0,2:T(2,128)(2,1)S(1)}, bf...) fusion(bf16[4,1152,576]{1,0,2:T(4,128)(2,1)S(1)} %copy-done.1, ...), kind=kLoop, calls=%fused_computation.363 | loop fusion | bytes 18579484 | tf_op jit(solution)/shard_map/jit(dynamic_index_in_dim)/dynamic_slice | solution.py:758
  1161.3 31.7 %collective-permute-done.35 = bf16[288,4608]{1,0:T(8,128)(2,1)} collective-permute-done((bf16[288,4608]{1,0:T(8,128)(2,1)}, bf16[288,4608]{1,0:T(8,128)(2,1)}, u32[]{:S(2)}, u32[]{:S(2)}) %collective-permute-start.35) | collective-permute-done | bytes 2654240 | tf_op jit(solution)/shard_map/ppermute | solution.py:768
  1193.0 5.6 collective-permute-start.42
  1198.7 6.2 fusion.4
  1205.6 27.1 %collective-permute-done.42 = bf16[1152,576]{0,1:T(8,128)(2,1)} collective-permute-done((bf16[1152,576]{0,1:T(8,128)(2,1)}, bf16[1152,576]{0,1:T(8,128)(2,1)}, u32[]{:S(2)}, u32[]{:S(2)}) %collective-permute-start.42) | collective-permute-done | bytes 1327136 | tf_op jit(solution)/shard_map/ppermute | solution.py:768
  1236.1 5.1 collective-permute-start.43
  1251.0 19.6 %collective-permute-done.43 = bf16[1152,576]{0,1:T(8,128)(2,1)S(1)} collective-permute-done((bf16[1152,576]{0,1:T(8,128)(2,1)S(1)}, bf16[1152,576]{0,1:T(8,128)(2,1)S(1)}, u32[]{:S(2)}, u32[]{:S(2)}) %collective-permute-start.43) | collective-permute-done | bytes 1327136 | tf_op jit(solution)/shard_map/ppermute | solution.py:768
  1272.7 27.0 %collective-permute-start.20 = (bf16[288,1024]{1,0:T(8,128)(2,1)S(1)}, bf16[288,1024]{1,0:T(8,128)(2,1)S(1)}, u32[]{:S(2)}, u32[]{:S(2)}) collective-permute-start(bf16[288,1024]{1,0:T(8,128)(2,1)S(1)} %get-tuple-element.109), channel_id=1, source_target_pairs={{0,8},{4,12},{8,16},{12,20},{16,24},{20,28},{1,9},{5,13},{9,17},{1... | collective-permute-start | bytes 1769480 | tf_op jit(solution)/shard_map/ppermute | solution.py:768
  1307.9 41.3 %collective-permute-start.44 = (bf16[1152,576]{0,1:T(8,128)(2,1)}, bf16[1152,576]{0,1:T(8,128)(2,1)}, u32[]{:S(2)}, u32[]{:S(2)}) collective-permute-start(bf16[1152,576]{0,1:T(8,128)(2,1)} %fusion.75), channel_id=1, source_target_pairs={{0,8},{4,12},{8,16},{12,20},{16,24},{20,28},{1,9},{5,13},{9,17},{1... | collective-permute-start | bytes 3981320 | tf_op jit(solution)/shard_map/ppermute | solution.py:768
  1365.0 76.8 %collective-permute-done.23 = bf16[288,1024]{1,0:T(8,128)(2,1)} collective-permute-done((bf16[288,1024]{1,0:T(8,128)(2,1)}, bf16[288,1024]{1,0:T(8,128)(2,1)}, u32[]{:S(2)}, u32[]{:S(2)}) %collective-permute-start.23) | collective-permute-done | bytes 589856 | tf_op jit(solution)/shard_map/ppermute | solution.py:769
  1448.1 6.7 fusion.5
  (532 shorter events, 364.5 us)
Async XLA Ops:
  28.7 199.3 %copy-start.71 = (f32[2304]{0:T(1024)}, f32[2304]{0:T(1024)S(1)}, u32[]{:S(2)}) copy-start(f32[2304]{0:T(1024)S(1)} %get-tuple-element.45) | copy-start | bytes 27652
  28.7 200.0 %copy-start.76 = (f32[2304]{0:T(1024)}, f32[2304]{0:T(1024)S(1)}, u32[]{:S(2)}) copy-start(f32[2304]{0:T(1024)S(1)} %get-tuple-element.46) | copy-start | bytes 27652
  28.7 200.7 %copy-start.74 = (f32[2304]{0:T(1024)}, f32[2304]{0:T(1024)S(1)}, u32[]{:S(2)}) copy-start(f32[2304]{0:T(1024)S(1)} %get-tuple-element.44) | copy-start | bytes 27652
  203.7 156.5 %collective-permute-start.2 = (bf16[512,1152]{1,0:T(8,128)(2,1)}, bf16[512,1152]{1,0:T(8,128)(2,1)}, u32[]{:S(2)}, u32[]{:S(2)}) collective-permute-start(bf16[512,1152]{1,0:T(8,128)(2,1)} %fusion.50), channel_id=1, source_target_pairs={{0,2},{1,3},{2,0},{3,1},{4,6},{5,7},{6,4},{7,5},{8,10},{9,11},{10,... | collective-permute-start | bytes 3538952 | tf_op jit(solution)/shard_map/ppermute | solution.py:741
  207.9 149.4 %collective-permute-start = (bf16[512,1152]{1,0:T(8,128)(2,1)}, bf16[512,1152]{1,0:T(8,128)(2,1)}, u32[]{:S(2)}, u32[]{:S(2)}) collective-permute-start(bf16[512,1152]{1,0:T(8,128)(2,1)} %fusion.53), channel_id=1, source_target_pairs={{0,2},{1,3},{2,0},{3,1},{4,6},{5,7},{6,4},{7,5},{8,10},{9,11},{10,... | collective-permute-start | bytes 3538952 | tf_op jit(solution)/shard_map/ppermute | solution.py:741
  214.2 150.3 %collective-permute-start.4 = (bf16[512,1152]{1,0:T(8,128)(2,1)}, bf16[512,1152]{1,0:T(8,128)(2,1)}, u32[]{:S(2)}, u32[]{:S(2)}) collective-permute-start(bf16[512,1152]{1,0:T(8,128)(2,1)} %fusion.47), channel_id=1, source_target_pairs={{0,2},{1,3},{2,0},{3,1},{4,6},{5,7},{6,4},{7,5},{8,10},{9,11},{10,... | collective-permute-start | bytes 3538952 | tf_op jit(solution)/shard_map/ppermute | solution.py:741
  218.4 150.2 %collective-permute-start.6 = (bf16[512,1152]{1,0:T(8,128)(2,1)}, bf16[512,1152]{1,0:T(8,128)(2,1)}, u32[]{:S(2)}, u32[]{:S(2)}) collective-permute-start(bf16[512,1152]{1,0:T(8,128)(2,1)} %fusion.44), channel_id=1, source_target_pairs={{0,2},{1,3},{2,0},{3,1},{4,6},{5,7},{6,4},{7,5},{8,10},{9,11},{10,... | collective-permute-start | bytes 3538952 | tf_op jit(solution)/shard_map/ppermute | solution.py:741
  249.8 730.0 %collective-permute-start.32 = (bf16[512,1152]{0,1:T(8,128)(2,1)}, bf16[512,1152]{0,1:T(8,128)(2,1)}, u32[]{:S(2)}, u32[]{:S(2)}) collective-permute-start(bf16[512,1152]{0,1:T(8,128)(2,1)} %bitcast.67), channel_id=1, source_target_pairs={{0,4},{4,0},{8,12},{12,8},{16,20},{20,16},{24,28},{28,24},{1,5},{5... | collective-permute-start | bytes 3538952 | tf_op jit(solution)/shard_map/ppermute | solution.py:737
  360.1 23.7 %collective-permute-start.1 = (bf16[512,1152]{1,0:T(8,128)(2,1)S(1)}, bf16[512,1152]{1,0:T(8,128)(2,1)S(1)}, u32[]{:S(2)}, u32[]{:S(2)}) collective-permute-start(bf16[512,1152]{1,0:T(8,128)(2,1)S(1)} %fusion.105), channel_id=1, source_target_pairs={{0,1},{1,0},{2,3},{3,2},{4,5},{5,4},{6,7},{7,6},{8,9},{9,8},{10,11... | collective-permute-start | bytes 3538952 | tf_op jit(solution)/shard_map/ppermute | solution.py:745
  364.3 26.4 %collective-permute-start.3 = (bf16[512,1152]{1,0:T(8,128)(2,1)}, bf16[512,1152]{1,0:T(8,128)(2,1)}, u32[]{:S(2)}, u32[]{:S(2)}) collective-permute-start(bf16[512,1152]{1,0:T(8,128)(2,1)} %fusion.108), channel_id=1, source_target_pairs={{0,1},{1,0},{2,3},{3,2},{4,5},{5,4},{6,7},{7,6},{8,9},{9,8},{10,11... | collective-permute-start | bytes 3538952 | tf_op jit(solution)/shard_map/ppermute | solution.py:745
  368.2 26.0 %collective-permute-start.5 = (bf16[512,1152]{1,0:T(8,128)(2,1)}, bf16[512,1152]{1,0:T(8,128)(2,1)}, u32[]{:S(2)}, u32[]{:S(2)}) collective-permute-start(bf16[512,1152]{1,0:T(8,128)(2,1)} %fusion.111), channel_id=1, source_target_pairs={{0,1},{1,0},{2,3},{3,2},{4,5},{5,4},{6,7},{7,6},{8,9},{9,8},{10,11... | collective-permute-start | bytes 3538952 | tf_op jit(solution)/shard_map/ppermute | solution.py:745
  372.5 24.3 %collective-permute-start.7 = (bf16[512,1152]{1,0:T(8,128)(2,1)}, bf16[512,1152]{1,0:T(8,128)(2,1)S(1)}, u32[]{:S(2)}, u32[]{:S(2)}) collective-permute-start(bf16[512,1152]{1,0:T(8,128)(2,1)} %fusion.114), channel_id=1, source_target_pairs={{0,1},{1,0},{2,3},{3,2},{4,5},{5,4},{6,7},{7,6},{8,9},{9,8},{10,11... | collective-permute-start | bytes 3538952 | tf_op jit(solution)/shard_map/ppermute | solution.py:745
  456.7 57.1 %collective-permute-start.14 = (bf16[512,1152]{1,0:T(8,128)(2,1)}, bf16[512,1152]{1,0:T(8,128)(2,1)}, u32[]{:S(2)}, u32[]{:S(2)}) collective-permute-start(bf16[512,1152]{1,0:T(8,128)(2,1)} %convolution_convert_fusion), channel_id=1, source_target_pairs={{0,1},{1,0},{2,3},{3,2},{4,5},{5,4},{6,7},{7,6},{8,9},{9,8},{10,11... | collective-permute-start | bytes 3538952 | tf_op jit(solution)/shard_map/ppermute | solution.py:745
  456.8 68.8 %collective-permute-start.12 = (bf16[512,1152]{1,0:T(8,128)(2,1)}, bf16[512,1152]{1,0:T(8,128)(2,1)}, u32[]{:S(2)}, u32[]{:S(2)}) collective-permute-start(bf16[512,1152]{1,0:T(8,128)(2,1)} %convolution_convert_fusion.1), channel_id=1, source_target_pairs={{0,1},{1,0},{2,3},{3,2},{4,5},{5,4},{6,7},{7,6},{8,9},{9,8},{10,11... | collective-permute-start | bytes 3538952 | tf_op jit(solution)/shard_map/ppermute | solution.py:745
  457.2 73.7 %collective-permute-start.10 = (bf16[512,1152]{1,0:T(8,128)(2,1)}, bf16[512,1152]{1,0:T(8,128)(2,1)}, u32[]{:S(2)}, u32[]{:S(2)}) collective-permute-start(bf16[512,1152]{1,0:T(8,128)(2,1)} %convolution_convert_fusion.2), channel_id=1, source_target_pairs={{0,1},{1,0},{2,3},{3,2},{4,5},{5,4},{6,7},{7,6},{8,9},{9,8},{10,11... | collective-permute-start | bytes 3538952 | tf_op jit(solution)/shard_map/ppermute | solution.py:745
  457.3 76.4 %collective-permute-start.8 = (bf16[512,1152]{1,0:T(8,128)(2,1)}, bf16[512,1152]{1,0:T(8,128)(2,1)}, u32[]{:S(2)}, u32[]{:S(2)}) collective-permute-start(bf16[512,1152]{1,0:T(8,128)(2,1)} %convolution_convert_fusion.3), channel_id=1, source_target_pairs={{0,1},{1,0},{2,3},{3,2},{4,5},{5,4},{6,7},{7,6},{8,9},{9,8},{10,11... | collective-permute-start | bytes 3538952 | tf_op jit(solution)/shard_map/ppermute | solution.py:745
  517.2 29.1 %collective-permute-start.15 = (bf16[512,1152]{1,0:T(8,128)(2,1)}, bf16[512,1152]{1,0:T(8,128)(2,1)}, u32[]{:S(2)}, u32[]{:S(2)}) collective-permute-start(bf16[512,1152]{1,0:T(8,128)(2,1)} %add_convert_fusion.4), channel_id=1, source_target_pairs={{0,2},{1,3},{2,0},{3,1},{4,6},{5,7},{6,4},{7,5},{8,10},{9,11},{10,... | collective-permute-start | bytes 3538952 | tf_op jit(solution)/shard_map/ppermute | solution.py:741
  525.6 352.5 %collective-permute-start.24 = (bf16[512,1024]{0,1:T(8,128)(2,1)}, bf16[512,1024]{0,1:T(8,128)(2,1)}, u32[]{:S(2)}, u32[]{:S(2)}) collective-permute-start(bf16[512,1024]{0,1:T(8,128)(2,1)} %bitcast.376), channel_id=1, source_target_pairs={{0,4},{4,0},{8,12},{12,8},{16,20},{20,16},{24,28},{28,24},{1,5},{5... | collective-permute-start | bytes 3145736 | tf_op jit(solution)/shard_map/ppermute | solution.py:737
  530.9 574.9 %collective-permute-start.40 = (bf16[512,4608]{0,1:T(8,128)(2,1)}, bf16[512,4608]{0,1:T(8,128)(2,1)}, u32[]{:S(2)}, u32[]{:S(2)}) collective-permute-start(bf16[512,4608]{0,1:T(8,128)(2,1)} %bitcast.77), channel_id=1, source_target_pairs={{0,4},{4,0},{8,12},{12,8},{16,20},{20,16},{24,28},{28,24},{1,5},{5... | collective-permute-start | bytes 14155784 | tf_op jit(solution)/shard_map/ppermute | solution.py:737
  533.7 37.8 %collective-permute-start.13 = (bf16[512,1152]{1,0:T(8,128)(2,1)S(1)}, bf16[512,1152]{1,0:T(8,128)(2,1)S(1)}, u32[]{:S(2)}, u32[]{:S(2)}) collective-permute-start(bf16[512,1152]{1,0:T(8,128)(2,1)S(1)} %add_convert_fusion.5), channel_id=1, source_target_pairs={{0,2},{1,3},{2,0},{3,1},{4,6},{5,7},{6,4},{7,5},{8,10},{9,11},{10,... | collective-permute-start | bytes 3538952 | tf_op jit(solution)/shard_map/ppermute | solution.py:741
  534.1 93.3 %slice-start.3 = ((s8[21233664]{0:T(1024)(128)(4,1)}), s8[4194304]{0:T(1024)(128)(4,1)S(1)}, s32[]{:S(2)}) async-start(s8[21233664]{0:T(1024)(128)(4,1)} %bitcast.333), calls=%async_computation.3 | async-start | bytes 8388608
  536.7 90.7 %slice-start.4 = ((s8[21233664]{0:T(1024)(128)(4,1)}), s8[4194304]{0:T(1024)(128)(4,1)S(1)}, s32[]{:S(2)}) async-start(s8[21233664]{0:T(1024)(128)(4,1)} %bitcast.333), calls=%async_computation.4 | async-start | bytes 8388608
  546.4 50.5 %collective-permute-start.11 = (bf16[512,1152]{1,0:T(8,128)(2,1)S(1)}, bf16[512,1152]{1,0:T(8,128)(2,1)S(1)}, u32[]{:S(2)}, u32[]{:S(2)}) collective-permute-start(bf16[512,1152]{1,0:T(8,128)(2,1)S(1)} %add_convert_fusion.6), channel_id=1, source_target_pairs={{0,2},{1,3},{2,0},{3,1},{4,6},{5,7},{6,4},{7,5},{8,10},{9,11},{10,... | collective-permute-start | bytes 3538952 | tf_op jit(solution)/shard_map/ppermute | solution.py:741
  552.9 74.6 %slice-start.5 = ((s8[21233664]{0:T(1024)(128)(4,1)}), s8[4194304]{0:T(1024)(128)(4,1)S(1)}, s32[]{:S(2)}) async-start(s8[21233664]{0:T(1024)(128)(4,1)} %bitcast.333), calls=%async_computation.5 | async-start | bytes 8388608
  553.0 92.8 %copy-start.22 = (bf16[512,1152]{1,0:T(8,128)(2,1)}, bf16[512,1152]{1,0:T(8,128)(2,1)S(1)}, u32[]{:S(2)}) copy-start(bf16[512,1152]{1,0:T(8,128)(2,1)S(1)} %multiply_convert_fusion.3) | copy-start | bytes 3538948
  571.5 49.7 %collective-permute-start.9 = (bf16[512,1152]{1,0:T(8,128)(2,1)S(1)}, bf16[512,1152]{1,0:T(8,128)(2,1)S(1)}, u32[]{:S(2)}, u32[]{:S(2)}) collective-permute-start(bf16[512,1152]{1,0:T(8,128)(2,1)S(1)} %add_convert_fusion.7), channel_id=1, source_target_pairs={{0,2},{1,3},{2,0},{3,1},{4,6},{5,7},{6,4},{7,5},{8,10},{9,11},{10,... | collective-permute-start | bytes 3538952 | tf_op jit(solution)/shard_map/ppermute | solution.py:741
  577.8 49.6 %slice-start.6 = ((s8[21233664]{0:T(1024)(128)(4,1)}), s8[4194304]{0:T(1024)(128)(4,1)S(1)}, s32[]{:S(2)}) async-start(s8[21233664]{0:T(1024)(128)(4,1)} %bitcast.333), calls=%async_computation.6 | async-start | bytes 8388608
  854.6 125.2 %collective-permute-start.33 = (bf16[512,4608]{1,0:T(8,128)(2,1)}, bf16[512,4608]{1,0:T(8,128)(2,1)}, u32[]{:S(2)}, u32[]{:S(2)}) collective-permute-start(bf16[512,4608]{1,0:T(8,128)(2,1)} %pad_maximum_fusion), channel_id=1, source_target_pairs={{0,4},{4,0},{8,12},{12,8},{16,20},{20,16},{24,28},{28,24},{1,5},{5... | collective-permute-start | bytes 14155784 | tf_op jit(solution)/shard_map/ppermute | solution.py:737
  856.5 115.6 %collective-permute-start.25 = (bf16[512,576]{0,1:T(8,128)(2,1)}, bf16[512,576]{0,1:T(8,128)(2,1)S(1)}, u32[]{:S(2)}, u32[]{:S(2)}) collective-permute-start(bf16[512,576]{0,1:T(8,128)(2,1)} %copy.185), channel_id=1, source_target_pairs={{0,4},{4,0},{8,12},{12,8},{16,20},{20,16},{24,28},{28,24},{1,5},{5... | collective-permute-start | bytes 1769480 | tf_op jit(solution)/shard_map/ppermute | solution.py:737
  878.1 95.9 %copy-start.106 = (f32[6208]{0:T(1024)}, f32[6208]{0:T(1024)S(1)}, u32[]{:S(2)}) copy-start(f32[6208]{0:T(1024)S(1)} %constant_dynamic-update-slice_fusion.10) | copy-start | bytes 74500
  878.1 134.7 %collective-permute-start.16 = (bf16[512,1152]{0,1:T(8,128)(2,1)}, bf16[512,1152]{0,1:T(8,128)(2,1)}, u32[]{:S(2)}, u32[]{:S(2)}) collective-permute-start(bf16[512,1152]{0,1:T(8,128)(2,1)} %bitcast.44), channel_id=1, source_target_pairs={{0,4},{4,0},{8,12},{12,8},{16,20},{20,16},{24,28},{28,24},{1,5},{5... | collective-permute-start | bytes 3538952 | tf_op jit(solution)/shard_map/ppermute | solution.py:737
  972.1 47.0 %collective-permute-start.17 = (bf16[512,1024]{1,0:T(8,128)(2,1)}, bf16[512,1024]{1,0:T(8,128)(2,1)}, u32[]{:S(2)}, u32[]{:S(2)}) collective-permute-start(bf16[512,1024]{1,0:T(8,128)(2,1)} %pad_maximum_fusion.5), channel_id=1, source_target_pairs={{0,4},{4,0},{8,12},{12,8},{16,20},{20,16},{24,28},{28,24},{1,5},{5... | collective-permute-start | bytes 3145736 | tf_op jit(solution)/shard_map/ppermute | solution.py:737
  999.2 126.0 %collective-permute-start.34 = (bf16[288,4608]{1,0:T(8,128)(2,1)}, bf16[288,4608]{1,0:T(8,128)(2,1)}, u32[]{:S(2)}, u32[]{:S(2)}) collective-permute-start(bf16[288,4608]{1,0:T(8,128)(2,1)} %get-tuple-element.61), channel_id=1, source_target_pairs={{0,8},{4,12},{1,9},{5,13},{2,10},{6,14},{3,11},{7,15}} | collective-permute-start | bytes 7962632 | tf_op jit(solution)/shard_map/ppermute | solution.py:768
  1010.7 78.1 %collective-permute-start.26 = (bf16[256,576]{0,1:T(8,128)(2,1)}, bf16[256,576]{0,1:T(8,128)(2,1)}, u32[]{:S(2)}, u32[]{:S(2)}) collective-permute-start(bf16[256,576]{0,1:T(8,128)(2,1)} %bitcast.323), channel_id=1, source_target_pairs={{0,8},{4,12},{1,9},{5,13},{2,10},{6,14},{3,11},{7,15}} | collective-permute-start | bytes 884744 | tf_op jit(solution)/shard_map/ppermute | solution.py:768
  1012.8 78.3 %collective-permute-start.29 = (bf16[256,576]{0,1:T(8,128)(2,1)S(1)}, bf16[256,576]{0,1:T(8,128)(2,1)}, u32[]{:S(2)}, u32[]{:S(2)}) collective-permute-start(bf16[256,576]{0,1:T(8,128)(2,1)S(1)} %bitcast.380), channel_id=1, source_target_pairs={{28,20},{24,16},{29,21},{25,17},{30,22},{26,18},{31,23},{27,19}} | collective-permute-start | bytes 884744 | tf_op jit(solution)/shard_map/ppermute | solution.py:769
  1022.2 76.4 %copy-start.6 = (bf16[1152,1024]{1,0:T(8,128)(2,1)}, bf16[1152,1024]{1,0:T(8,128)(2,1)S(1)}, u32[]{:S(2)}) copy-start(bf16[1152,1024]{1,0:T(8,128)(2,1)S(1)} %fusion.31) | copy-start | bytes 7077892
  1022.2 66.6 %copy-start.69 = (bf16[512,576]{0,1:T(8,128)(2,1)S(1)}, bf16[512,576]{0,1:T(8,128)(2,1)}, u32[]{:S(2)}) copy-start(bf16[512,576]{0,1:T(8,128)(2,1)} %copy.199) | copy-start | bytes 1769476
  1023.1 74.1 %collective-permute-start.18 = (bf16[288,1024]{1,0:T(8,128)(2,1)}, bf16[288,1024]{1,0:T(8,128)(2,1)S(1)}, u32[]{:S(2)}, u32[]{:S(2)}) collective-permute-start(bf16[288,1024]{1,0:T(8,128)(2,1)} %get-tuple-element.111), channel_id=1, source_target_pairs={{0,8},{4,12},{1,9},{5,13},{2,10},{6,14},{3,11},{7,15}} | collective-permute-start | bytes 1769480 | tf_op jit(solution)/shard_map/ppermute | solution.py:768
  1088.8 15.6 %collective-permute-start.41 = (bf16[512,576]{0,1:T(8,128)(2,1)S(1)}, bf16[512,576]{0,1:T(8,128)(2,1)S(1)}, u32[]{:S(2)}, u32[]{:S(2)}) collective-permute-start(bf16[512,576]{0,1:T(8,128)(2,1)S(1)} %copy-done.69), channel_id=1, source_target_pairs={{0,4},{4,0},{8,12},{12,8},{16,20},{20,16},{24,28},{28,24},{1,5},{5... | collective-permute-start | bytes 1769480 | tf_op jit(solution)/shard_map/ppermute | solution.py:737
  1091.1 113.8 %collective-permute-start.27 = (bf16[256,576]{0,1:T(8,128)(2,1)}, bf16[256,576]{0,1:T(8,128)(2,1)S(1)}, u32[]{:S(2)}, u32[]{:S(2)}) collective-permute-start(bf16[256,576]{0,1:T(8,128)(2,1)} %fusion.177), channel_id=1, source_target_pairs={{0,8},{4,12},{8,16},{12,20},{1,9},{5,13},{9,17},{13,21},{2,10},{6,... | collective-permute-start | bytes 884744 | tf_op jit(solution)/shard_map/ppermute | solution.py:768
  1097.2 138.9 %collective-permute-start.30 = (bf16[256,576]{0,1:T(8,128)(2,1)}, bf16[256,576]{0,1:T(8,128)(2,1)}, u32[]{:S(2)}, u32[]{:S(2)}) collective-permute-start(bf16[256,576]{0,1:T(8,128)(2,1)} %fusion.175), channel_id=1, source_target_pairs={{28,20},{24,16},{20,12},{16,8},{29,21},{25,17},{21,13},{17,9},{30,... | collective-permute-start | bytes 884744 | tf_op jit(solution)/shard_map/ppermute | solution.py:769
  1104.4 138.1 %collective-permute-start.21 = (bf16[288,1024]{1,0:T(8,128)(2,1)S(1)}, bf16[288,1024]{1,0:T(8,128)(2,1)}, u32[]{:S(2)}, u32[]{:S(2)}) collective-permute-start(bf16[288,1024]{1,0:T(8,128)(2,1)S(1)} %get-tuple-element.112), channel_id=1, source_target_pairs={{28,20},{24,16},{29,21},{25,17},{30,22},{26,18},{31,23},{27,19}} | collective-permute-start | bytes 1769480 | tf_op jit(solution)/shard_map/ppermute | solution.py:769
  1122.8 36.4 %collective-permute-start.37 = (bf16[288,4608]{1,0:T(8,128)(2,1)}, bf16[288,4608]{1,0:T(8,128)(2,1)}, u32[]{:S(2)}, u32[]{:S(2)}) collective-permute-start(bf16[288,4608]{1,0:T(8,128)(2,1)} %get-tuple-element.62), channel_id=1, source_target_pairs={{28,20},{24,16},{29,21},{25,17},{30,22},{26,18},{31,23},{27,19}} | collective-permute-start | bytes 7962632 | tf_op jit(solution)/shard_map/ppermute | solution.py:769
  1125.2 73.4 %slice-start = ((s8[10616832]{0:T(1024)(128)(4,1)}), s8[4194304]{0:T(1024)(128)(4,1)S(1)}, s32[]{:S(2)}) async-start(s8[10616832]{0:T(1024)(128)(4,1)} %bitcast.328), calls=%async_computation | async-start | bytes 8388608
  1130.1 68.6 %slice-start.1 = ((s8[10616832]{0:T(1024)(128)(4,1)}), s8[4194304]{0:T(1024)(128)(4,1)S(1)}, s32[]{:S(2)}) async-start(s8[10616832]{0:T(1024)(128)(4,1)} %bitcast.328), calls=%async_computation.1 | async-start | bytes 8388608
  1130.1 68.6 %slice-start.2 = ((s8[10616832]{0:T(1024)(128)(4,1)}), s8[2228224]{0:T(1024)(128)(4,1)S(1)}, s32[]{:S(2)}) async-start(s8[10616832]{0:T(1024)(128)(4,1)} %bitcast.328), calls=%async_computation.2 | async-start | bytes 4456448
  1130.1 62.9 %collective-permute-start.35 = (bf16[288,4608]{1,0:T(8,128)(2,1)}, bf16[288,4608]{1,0:T(8,128)(2,1)}, u32[]{:S(2)}, u32[]{:S(2)}) collective-permute-start(bf16[288,4608]{1,0:T(8,128)(2,1)} %fusion.3), channel_id=1, source_target_pairs={{0,8},{4,12},{8,16},{12,20},{1,9},{5,13},{9,17},{13,21},{2,10},{6,... | collective-permute-start | bytes 7962632 | tf_op jit(solution)/shard_map/ppermute | solution.py:768
  1159.2 87.7 %collective-permute-start.19 = (bf16[288,1024]{1,0:T(8,128)(2,1)}, bf16[288,1024]{1,0:T(8,128)(2,1)}, u32[]{:S(2)}, u32[]{:S(2)}) collective-permute-start(bf16[288,1024]{1,0:T(8,128)(2,1)} %fusion.171), channel_id=1, source_target_pairs={{0,8},{4,12},{8,16},{12,20},{1,9},{5,13},{9,17},{13,21},{2,10},{6,... | collective-permute-start | bytes 1769480 | tf_op jit(solution)/shard_map/ppermute | solution.py:768
  1193.0 39.7 %collective-permute-start.42 = (bf16[1152,576]{0,1:T(8,128)(2,1)}, bf16[1152,576]{0,1:T(8,128)(2,1)}, u32[]{:S(2)}, u32[]{:S(2)}) collective-permute-start(bf16[1152,576]{0,1:T(8,128)(2,1)} %bitcast.321), channel_id=1, source_target_pairs={{0,8},{4,12},{1,9},{5,13},{2,10},{6,14},{3,11},{7,15}} | collective-permute-start | bytes 3981320 | tf_op jit(solution)/shard_map/ppermute | solution.py:768
  1204.9 45.1 %collective-permute-start.45 = (bf16[1152,576]{0,1:T(8,128)(2,1)}, bf16[1152,576]{0,1:T(8,128)(2,1)S(1)}, u32[]{:S(2)}, u32[]{:S(2)}) collective-permute-start(bf16[1152,576]{0,1:T(8,128)(2,1)} %bitcast.374), channel_id=1, source_target_pairs={{28,20},{24,16},{29,21},{25,17},{30,22},{26,18},{31,23},{27,19}} | collective-permute-start | bytes 3981320 | tf_op jit(solution)/shard_map/ppermute | solution.py:769
  1232.7 40.0 %collective-permute-start.38 = (bf16[288,4608]{1,0:T(8,128)(2,1)}, bf16[288,4608]{1,0:T(8,128)(2,1)S(1)}, u32[]{:S(2)}, u32[]{:S(2)}) collective-permute-start(bf16[288,4608]{1,0:T(8,128)(2,1)} %get-tuple-element.60), channel_id=1, source_target_pairs={{28,20},{24,16},{20,12},{16,8},{29,21},{25,17},{21,13},{17,9},{30,... | collective-permute-start | bytes 7962632 | tf_op jit(solution)/shard_map/ppermute | solution.py:769
  1236.1 34.6 %collective-permute-start.43 = (bf16[1152,576]{0,1:T(8,128)(2,1)S(1)}, bf16[1152,576]{0,1:T(8,128)(2,1)S(1)}, u32[]{:S(2)}, u32[]{:S(2)}) collective-permute-start(bf16[1152,576]{0,1:T(8,128)(2,1)S(1)} %fusion.74), channel_id=1, source_target_pairs={{0,8},{4,12},{8,16},{12,20},{1,9},{5,13},{9,17},{13,21},{2,10},{6,... | collective-permute-start | bytes 3981320 | tf_op jit(solution)/shard_map/ppermute | solution.py:768
  1242.5 59.4 %collective-permute-start.28 = (bf16[256,576]{0,1:T(8,128)(2,1)S(1)}, bf16[256,576]{0,1:T(8,128)(2,1)S(1)}, u32[]{:S(2)}, u32[]{:S(2)}) collective-permute-start(bf16[256,576]{0,1:T(8,128)(2,1)S(1)} %fusion.178), channel_id=1, source_target_pairs={{0,8},{4,12},{8,16},{12,20},{16,24},{20,28},{1,9},{5,13},{9,17},{1... | collective-permute-start | bytes 884744 | tf_op jit(solution)/shard_map/ppermute | solution.py:768
  1247.0 61.0 %collective-permute-start.31 = (bf16[256,576]{0,1:T(8,128)(2,1)S(1)}, bf16[256,576]{0,1:T(8,128)(2,1)S(1)}, u32[]{:S(2)}, u32[]{:S(2)}) collective-permute-start(bf16[256,576]{0,1:T(8,128)(2,1)S(1)} %fusion.176), channel_id=1, source_target_pairs={{28,20},{24,16},{20,12},{16,8},{12,4},{8,0},{29,21},{25,17},{21,13... | collective-permute-start | bytes 884744 | tf_op jit(solution)/shard_map/ppermute | solution.py:769
  1250.0 99.3 %collective-permute-start.22 = (bf16[288,1024]{1,0:T(8,128)(2,1)S(1)}, bf16[288,1024]{1,0:T(8,128)(2,1)S(1)}, u32[]{:S(2)}, u32[]{:S(2)}) collective-permute-start(bf16[288,1024]{1,0:T(8,128)(2,1)S(1)} %get-tuple-element.110), channel_id=1, source_target_pairs={{28,20},{24,16},{20,12},{16,8},{29,21},{25,17},{21,13},{17,9},{30,... | collective-permute-start | bytes 1769480 | tf_op jit(solution)/shard_map/ppermute | solution.py:769
  1270.6 34.7 %collective-permute-start.46 = (bf16[1152,576]{0,1:T(8,128)(2,1)S(1)}, bf16[1152,576]{0,1:T(8,128)(2,1)S(1)}, u32[]{:S(2)}, u32[]{:S(2)}) collective-permute-start(bf16[1152,576]{0,1:T(8,128)(2,1)S(1)} %fusion.72), channel_id=1, source_target_pairs={{28,20},{24,16},{20,12},{16,8},{29,21},{25,17},{21,13},{17,9},{30,... | collective-permute-start | bytes 3981320 | tf_op jit(solution)/shard_map/ppermute | solution.py:769
  1272.7 78.9 %collective-permute-start.20 = (bf16[288,1024]{1,0:T(8,128)(2,1)S(1)}, bf16[288,1024]{1,0:T(8,128)(2,1)S(1)}, u32[]{:S(2)}, u32[]{:S(2)}) collective-permute-start(bf16[288,1024]{1,0:T(8,128)(2,1)S(1)} %get-tuple-element.109), channel_id=1, source_target_pairs={{0,8},{4,12},{8,16},{12,20},{16,24},{20,28},{1,9},{5,13},{9,17},{1... | collective-permute-start | bytes 1769480 | tf_op jit(solution)/shard_map/ppermute | solution.py:768
  1301.9 146.2 %collective-permute-start.36 = (bf16[288,4608]{1,0:T(8,128)(2,1)}, bf16[288,4608]{1,0:T(8,128)(2,1)}, u32[]{:S(2)}, u32[]{:S(2)}) collective-permute-start(bf16[288,4608]{1,0:T(8,128)(2,1)} %get-tuple-element.59), channel_id=1, source_target_pairs={{0,8},{4,12},{8,16},{12,20},{16,24},{20,28},{1,9},{5,13},{9,17},{1... | collective-permute-start | bytes 7962632 | tf_op jit(solution)/shard_map/ppermute | solution.py:768
  1305.3 142.8 %collective-permute-start.39 = (bf16[288,4608]{1,0:T(8,128)(2,1)}, bf16[288,4608]{1,0:T(8,128)(2,1)}, u32[]{:S(2)}, u32[]{:S(2)}) collective-permute-start(bf16[288,4608]{1,0:T(8,128)(2,1)} %fusion.2), channel_id=1, source_target_pairs={{28,20},{24,16},{20,12},{16,8},{12,4},{8,0},{29,21},{25,17},{21,13... | collective-permute-start | bytes 7962632 | tf_op jit(solution)/shard_map/ppermute | solution.py:769
  1307.9 55.2 %copy-start.52 = (bf16[1,256,576]{1,0,2:T(2,128)(2,1)S(1)}, bf16[1,256,576]{1,0,2:T(2,128)(2,1)}, u32[]{:S(2)}) copy-start(bf16[1,256,576]{1,0,2:T(2,128)(2,1)} %get-tuple-element.121) | copy-start | bytes 884740
  1307.9 136.6 %collective-permute-start.44 = (bf16[1152,576]{0,1:T(8,128)(2,1)}, bf16[1152,576]{0,1:T(8,128)(2,1)}, u32[]{:S(2)}, u32[]{:S(2)}) collective-permute-start(bf16[1152,576]{0,1:T(8,128)(2,1)} %fusion.75), channel_id=1, source_target_pairs={{0,8},{4,12},{8,16},{12,20},{16,24},{20,28},{1,9},{5,13},{9,17},{1... | collective-permute-start | bytes 3981320 | tf_op jit(solution)/shard_map/ppermute | solution.py:768
  1349.3 95.2 %collective-permute-start.47 = (bf16[1152,576]{0,1:T(8,128)(2,1)}, bf16[1152,576]{0,1:T(8,128)(2,1)}, u32[]{:S(2)}, u32[]{:S(2)}) collective-permute-start(bf16[1152,576]{0,1:T(8,128)(2,1)} %fusion.73), channel_id=1, source_target_pairs={{28,20},{24,16},{20,12},{16,8},{12,4},{8,0},{29,21},{25,17},{21,13... | collective-permute-start | bytes 3981320 | tf_op jit(solution)/shard_map/ppermute | solution.py:769
  1351.6 90.2 %collective-permute-start.23 = (bf16[288,1024]{1,0:T(8,128)(2,1)}, bf16[288,1024]{1,0:T(8,128)(2,1)}, u32[]{:S(2)}, u32[]{:S(2)}) collective-permute-start(bf16[288,1024]{1,0:T(8,128)(2,1)} %fusion.170), channel_id=1, source_target_pairs={{28,20},{24,16},{20,12},{16,8},{12,4},{8,0},{29,21},{25,17},{21,13... | collective-permute-start | bytes 1769480 | tf_op jit(solution)/shard_map/ppermute | solution.py:769
  1365.0 79.5 %copy-start.11 = (bf16[1,1152,576]{1,0,2:T(2,128)(2,1)S(1)}, bf16[1,1152,576]{1,0,2:T(2,128)(2,1)}, u32[]{:S(2)}) copy-start(bf16[1,1152,576]{1,0,2:T(2,128)(2,1)} %get-tuple-element.78) | copy-start | bytes 3981316
  (120 other events, 1304.5 us)

commit v2 on v1

--- a/solution.py
+++ b/solution.py
@@ -13,10 +13,11 @@
 DH = 256
 FF = 9216
 GROUP = 4
+TILE = 384
 EPSILON = 1e-06
 CAP = 50.0
 BASE = 10000.0
-VMEM_LIMIT = 56 * 1024 * 1024
+VMEM_LIMIT = 60 * 1024 * 1024
 MESH = pl.DeviceIdType.MESH
 ANY = pl.BlockSpec(memory_space=pl.ANY)
 VMEM = pl.BlockSpec(memory_space=pltpu.VMEM)
@@ -704,24 +705,8 @@
     )(query, pairs, own_meta, metas, mixed, total, grad)
 
 
-def rms_inverse(value):
-    return lax.rsqrt(jnp.mean(value * value, axis=-1, keepdims=True) + EPSILON)
-
-
-def norm_back(inverse, normed, upstream):
-    return inverse * (upstream - normed * jnp.mean(upstream * normed, axis=-1, keepdims=True))
-
-
-def rotate(value, cosine, sine):
-    half = DH // 2
-    first = value[..., :half]
-    second = value[..., half:]
-    return jnp.concatenate([first * cosine - second * sine, second * cosine + first * sine], axis=-1)
-
-
-def code_levels(code, step):
-    levels = code.astype(F32)
-    return (jnp.floor(levels / step) * step + step / 2.0).astype(BF16)
+def levels(code, step):
+    return (jnp.floor(code.astype(F32) * (1.0 / step)) * step + step / 2.0).astype(BF16)
 
 
 def gelu_parts(gate):
@@ -733,45 +718,713 @@
     return value, slope
 
 
+def strips(count, size, body):
+    def step(i, carry):
+        body(pl.ds(pl.multiple_of(i * size, size), size))
+        return carry
+
+    lax.fori_loop(0, count, step, 0)
+
+
+def ffn_forward_kernel(tiles, riders, *refs):
+    b, wgu, gs, wd, cots, g3, ds = refs[:7]
+    refs = refs[7:]
+    rider_in, refs = refs[:riders], refs[riders:]
+    gu_o, hid_o, hidy_o, down_o, gf_o, sums_o = refs[:6]
+    refs = refs[6:]
+    rider_out, refs = refs[:riders], refs[riders:]
+    (gu, hid, hidy, wbuf, wlev, dbuf, dlev, acc, downs, wsem, dsem, xs, xr, hs, hr, ys, yr, fs, fr,
+     gxs, gxr, gcs, gcr, gfs, gfr, rs, rr, ks, outs) = refs
+    seq, me, x, c = place_now()
+    y = seq % 2
+    across = (seq, (1 - x) * 2 + c)
+    beside = (seq, x * 2 + 1 - c)
+    beyond = (seq + 1 - 2 * y, me)
+    rows, tw = gu.shape[2:]
+    deep = b.shape[1]
+    per = tiles // 4
+
+    def load_up(t):
+        return pltpu.make_async_copy(wgu.at[:, pl.ds(pl.multiple_of(t * tw, 128), tw)], wbuf.at[t % 2], wsem.at[t % 2])
+
+    def load_down(t, half):
+        start = ((c + half) % 2 * tiles + t) * tw
+        return pltpu.make_async_copy(
+            wd.at[pl.ds(pl.multiple_of(start, 128), tw)], dbuf.at[t % 2, half], dsem.at[t % 2, half]
+        )
+
+    load_up(0).start()
+    load_up(1).start()
+    for t in range(2):
+        for half in range(2):
+            load_down(t, half).start()
+    greet([across, beside, beyond])
+    travellers = []
+    for i in range(riders):
+        copy = remote(rider_in[i], rider_out[i], rs.at[i], rr.at[i], beyond)
+        copy.start()
+        travellers.append(copy)
+    acc[...] = jnp.zeros_like(acc)
+
+    def to_x(t):
+        return remote(gu.at[x, t], gu.at[x, t], xs.at[t], xr.at[t], across)
+
+    def to_core(t):
+        return remote(hid.at[c * tiles + t], hid.at[c * tiles + t], hs.at[t], hr.at[t], beside)
+
+    def slot(t, core):
+        return (2 * core + t // (2 * per)) * per + t % per
+
+    def to_y(t):
+        return remote(hid.at[c * tiles + t], hidy.at[slot(t, c)], ys.at[t], yr.at[t], beyond)
+
+    def keep(t, i, core):
+        return pltpu.make_async_copy(hid.at[core * tiles + t], hid_o.at[slot(t, core)], ks.at[i, t])
+
+    def wide(t):
+        load_up(t).wait()
+
+        def level(span):
+            wlev[span, :] = levels(wbuf[t % 2, span, :], 16.0)
+
+        strips(deep // 128, 128, level)
+
+        @pl.when(t + 2 < tiles)
+        def _():
+            load_up(t + 2).start()
+
+        scale = gs[t]
+
+        def product(span):
+            gu[x, t, span, :] = (dot(b[span, :], wlev[...]) * scale).astype(BF16)
+
+        strips(rows // 256, 256, product)
+        to_x(t).start()
+
+    def middle(t):
+        to_x(t).wait_recv()
+
+        def body(span):
+            gate = gu[0, t, span, :].astype(F32)
+            up = gu[1, t, span, :].astype(F32)
+            hid[c * tiles + t, span, :] = (gelu_parts(gate)[0] * up).astype(BF16)
+
+        strips(rows // 64, 64, body)
+        to_core(t).start()
+
+        @pl.when((t // per) % 2 != y)
+        def _():
+            to_y(t).start()
+
+        @pl.when((t // per) % 2 == y)
+        def _():
+            keep(t, 0, c).start()
+
+    def narrow(t):
+        for half in range(2):
+            load_down(t, half).wait()
+
+            def level(span):
+                dlev[half, span, :] = levels(dbuf[t % 2, half, span, :], 64.0)
+
+            strips(tw // 128, 128, level)
+
+        @pl.when(t + 2 < tiles)
+        def _():
+            for half in range(2):
+                load_down(t + 2, half).start()
+
+        to_core(t).wait_recv()
+
+        def product(span):
+            acc[span, :] += dot(hid[c * tiles + t, span, :], dlev[0]) + dot(
+                hid[(1 - c) * tiles + t, span, :], dlev[1]
+            )
+
+        strips(rows // 256, 256, product)
+
+        @pl.when((t // per) % 2 == y)
+        def _():
+            keep(t, 1, 1 - c).start()
+
+    def step(i, carry):
+        @pl.when(i < tiles)
+        def _():
+            wide(i)
+
+        @pl.when((i >= 1) & (i < tiles + 1))
+        def _():
+            middle(i - 1)
+
+        @pl.when(i >= 2)
+        def _():
+            narrow(i - 2)
+
+        return carry
+
+    lax.fori_loop(0, tiles + 2, step, 0)
+    gu_out = pltpu.make_async_copy(gu, gu_o, outs.at[0])
+    gu_out.start()
+
+    parts = 4
+    size = rows // parts
+    sends = []
+    own_sends = []
+    for k in range(parts):
+        span = pl.ds(k * size, size)
+        downs[me, span, :] = acc[span, :].astype(BF16)
+        part = downs.at[me, span]
+        copy = remote(part, part, gxs.at[k], gxr.at[k], across)
+        copy.start()
+        sends.append(copy)
+        copy = remote(part, part, gcs.at[k], gcr.at[k], beside)
+        copy.start()
+        own_sends.append(copy)
+
+    def pass_on(t, carry):
+        @pl.when((t // per) % 2 == y)
+        def _():
+            remote(hid.at[0], hidy.at[slot(t, c)], ys.at[t], yr.at[t], beyond).wait_recv()
+            got = hidy.at[slot(t, c)]
+            remote(got, got, fs.at[t], fr.at[t], beside).start()
+
+        return carry
+
+    lax.fori_loop(0, tiles, pass_on, 0)
+    forwards = []
+    for k in range(parts):
+        sends[k].wait_recv()
+        got = downs.at[(1 - x) * 2 + c, pl.ds(k * size, size)]
+        copy = remote(got, got, gfs.at[k], gfr.at[k], beside)
+        copy.start()
+        forwards.append(copy)
+    for copy in own_sends + forwards:
+        copy.wait_recv()
+    down_out = pltpu.make_async_copy(downs, down_o, outs.at[3])
+    down_out.start()
+    sums_o[...] = jnp.zeros_like(sums_o)
+    width = GROUP * acc.shape[1]
+
+    def last_norm(i, carry):
+        pack = i // 2
+        span = pl.ds(pl.multiple_of(i * 64, 64), 64)
+        inner = (i % 2) * 64
+
+        def cot_of(j):
+            return cots[pack, pl.ds(pl.multiple_of(j * 128 + inner, 64), 64), :].astype(F32)
+
+        square = jnp.zeros((64, 1), F32)
+        cross = jnp.zeros((64, 1), F32)
+        for j in range(GROUP):
+            value = downs[j, span, :].astype(F32) * ds[j]
+            square = square + jnp.sum(value * value, axis=1, keepdims=True)
+            cross = cross + jnp.sum(value * (cot_of(j) * g3[j]), axis=1, keepdims=True)
+        inverse = lax.rsqrt(square * (1.0 / width) + EPSILON)
+        raw = downs[me, span, :].astype(F32)
+        normed = raw * ds[me] * inverse
+        cot = cot_of(me)
+        grad = inverse * (cot * g3[me] - normed * (cross * inverse * (1.0 / width)))
+        gf_o[span, :] = (grad * ds[me]).astype(BF16)
+        sums_o[0:1, :] += jnp.sum(raw * grad, axis=0, keepdims=True)
+        sums_o[1:2, :] += jnp.sum(cot * normed, axis=0, keepdims=True)
+        return carry
+
+    lax.fori_loop(0, rows // 64, last_norm, 0)
+
+    def drain(t, carry):
+        to_x(t).wait_send()
+        to_core(t).wait_send()
+
+        @pl.when((t // per) % 2 != y)
+        def _():
+            to_y(t).wait_send()
+
+        @pl.when((t // per) % 2 == y)
+        def _():
+            keep(t, 0, c).wait()
+            keep(t, 1, 1 - c).wait()
+            got = hidy.at[slot(t, c)]
+            remote(got, got, fs.at[t], fr.at[t], beside).wait_send()
+            got = hidy.at[slot(t, 1 - c)]
+            remote(got, got, fs.at[t], fr.at[t], beside).wait_recv()
+
+        return carry
+
+    lax.fori_loop(0, tiles, drain, 0)
+    hidy_out = pltpu.make_async_copy(hidy, hidy_o, outs.at[4])
+    hidy_out.start()
+    for copy in sends + own_sends + forwards:
+        copy.wait_send()
+    for copy in travellers:
+        copy.wait()
+    gu_out.wait()
+    down_out.wait()
+    hidy_out.wait()
+
+
+def ffn_forward(cid, b, wgu, gs, wd, cots, g3, ds, riders):
+    rows, deep = b.shape
+    tiles, _, tw = gs.shape
+    part = wd.shape[1]
+    count = len(riders)
+    lone = max(count, 1)
+    return comm_call(
+        functools.partial(ffn_forward_kernel, tiles, count),
+        cid,
+        [
+            jax.ShapeDtypeStruct((2, tiles, rows, tw), BF16),
+            jax.ShapeDtypeStruct((tiles, rows, tw), BF16),
+            jax.ShapeDtypeStruct((tiles, rows, tw), BF16),
+            jax.ShapeDtypeStruct((GROUP, rows, part), BF16),
+            jax.ShapeDtypeStruct((rows, part), BF16),
+            jax.ShapeDtypeStruct((8, part), F32),
+        ]
+        + [jax.ShapeDtypeStruct(r.shape, r.dtype) for r in riders],
+        [
+            pltpu.VMEM((2, tiles, rows, tw), BF16),
+            pltpu.VMEM((2 * tiles, rows, tw), BF16),
+            pltpu.VMEM((tiles, rows, tw), BF16),
+            pltpu.VMEM((2, deep, tw), BF16),
+            pltpu.VMEM((deep, tw), BF16),
+            pltpu.VMEM((2, 2, tw, part), BF16),
+            pltpu.VMEM((2, tw, part), BF16),
+            pltpu.VMEM((rows, part), F32),
+            pltpu.VMEM((GROUP, rows, part), BF16),
+            DMA((2,)), DMA((2, 2)), DMA((tiles,)), DMA((tiles,)), DMA((tiles,)), DMA((tiles,)), DMA((tiles,)),
+            DMA((tiles,)), DMA((tiles,)), DMA((tiles,)), DMA((4,)), DMA((4,)), DMA((4,)), DMA((4,)), DMA((4,)),
+            DMA((4,)), DMA((lone,)), DMA((lone,)), DMA((2, tiles)), DMA((5,)),
+        ],
+        [VMEM, ANY, VMEM, ANY, VMEM, VMEM, VMEM] + [ANY] * count,
+        [ANY, ANY, ANY, ANY, VMEM, VMEM] + [ANY] * count,
+    )(b, wgu, gs, wd, cots, g3, ds, *riders)
+
+
+def ffn_backward_kernel(tiles, nz, chained, *refs):
+    gf, wd, wgu, gs, gu, hid, hidy = refs[:7]
+    dg_o, dgy_o, gsum_o, out, ddown_o = refs[7:12]
+    (hh, hy, gfy, wbuf, wlev, dbuf, dlev, pair, co, cgot, near, sx, xgot, dg, acc, low, from_core, to_xb, from_x,
+     r_out, l_out, r_got, l_got,
+     hsem, wsem, dsem, psem, cs, cr, xs, xr, ys, yr, os, gys, gyr, ccs, ccr, cxs, cxr, rs, rr, ls, lr) = refs[12:]
+    seq, me, x, c = place_now()
+    y = seq % 2
+    z = seq // 2
+    across = (seq, (1 - x) * 2 + c)
+    beside = (seq, x * 2 + 1 - c)
+    beyond = (seq + 1 - 2 * y, me)
+    right = (seq + 2, me)
+    left = (seq - 2, me)
+    rows, tw = dg.shape[1:]
+    deep = acc.shape[1]
+    per = hid.shape[0] // 4 if chained else 0
+    ring = dg.shape[0]
+
+    def load_up(t):
+        return pltpu.make_async_copy(wgu.at[:, pl.ds(pl.multiple_of(t * tw, 128), tw)], wbuf.at[t % 2], wsem.at[t % 2])
+
+    def load_down(t, half):
+        start = ((c + half) % 2 * tiles + t) * tw
+        return pltpu.make_async_copy(
+            wd.at[pl.ds(pl.multiple_of(start, 128), tw)], dbuf.at[t % 2, half], dsem.at[t % 2, half]
+        )
+
+    def load_pair(t):
+        return pltpu.make_async_copy(gu.at[:, t], pair.at[t % 2], psem.at[t % 2])
+
+    for t in range(2):
+        for half in range(2):
+            load_down(t, half).start()
+        load_pair(t).start()
+        load_up(t).start()
+    if chained:
+        load_hid = pltpu.make_async_copy(hid, hh, hsem.at[0])
+        load_hidy = pltpu.make_async_copy(hidy, hy, hsem.at[1])
+        load_hid.start()
+        load_hidy.start()
+    barrier = pltpu.get_barrier_semaphore()
+    for peer in (across, beside, beyond):
+        pl.semaphore_signal(barrier, inc=1, device_id=peer, device_id_type=MESH)
+    if chained:
+
+        @pl.when(z > 0)
+        def _():
+            pl.semaphore_signal(barrier, inc=1, device_id=left, device_id_type=MESH)
+
+        @pl.when(z < nz - 1)
+        def _():
+            pl.semaphore_signal(barrier, inc=1, device_id=right, device_id_type=MESH)
+
+        pl.semaphore_wait(barrier, 3 + jnp.where(z > 0, 1, 0) + jnp.where(z < nz - 1, 1, 0))
+        gf_swap = remote(gf, gfy, gys, gyr, beyond)
+        gf_swap.start()
+    else:
+        pl.semaphore_wait(barrier, 3)
+    acc[...] = jnp.zeros_like(acc)
+
+    def to_core(t):
+        return remote(co.at[t % 2], cgot.at[t], cs.at[t], cr.at[t], beside)
+
+    def to_x(t):
+        return remote(sx.at[t % 4], xgot.at[t], xs.at[t], xr.at[t], across)
+
+    def columns(ref, t):
+        return ref.at[:, pl.ds(pl.multiple_of(t * tw, 128), tw)]
+
+    def to_y(t):
+        return remote(dg.at[t % ring], columns(dgy_o, t), ys.at[t], yr.at[t], beyond)
+
+    def keep(t):
+        return pltpu.make_async_copy(dg.at[t % ring], columns(dg_o, t), os.at[t])
+
+    def hidden(t):
+        for half in range(2):
+            load_down(t, half).wait()
+
+            def level(span):
+                dlev[half, span, :] = levels(dbuf[t % 2, half, span, :], 64.0)
+
+            strips(tw // 128, 128, level)
+
+        @pl.when(t + 2 < tiles)
+        def _():
+            for half in range(2):
+                load_down(t + 2, half).start()
+
+        @pl.when(t >= 2)
+        def _():
+            to_core(t - 2).wait_send()
+
+        def product(span):
+            co[t % 2, span, :] = contract_last(gf[span, :], dlev[1]).astype(BF16)
+
+        strips(rows // 256, 256, product)
+        to_core(t).start()
+
+        def product_near(span):
+            near[t % 2, span, :] = contract_last(gf[span, :], dlev[0])
+
+        strips(rows // 256, 256, product_near)
+
+    def chip(t):
+        @pl.when(t >= 4)
+        def _():
+            to_x(t - 4).wait_send()
+
+        to_core(t).wait_recv()
+
+        def body(span):
+            sx[t % 4, span, :] = (near[t % 2, span, :] + cgot[t, span, :].astype(F32)).astype(BF16)
+
+        strips(rows // 64, 64, body)
+        to_x(t).start()
+
+    is_gate = jnp.where(x == 0, 1.0, 0.0).astype(F32)
+
+    def own(t):
+        load_pair(t).wait()
+
+        @pl.when(t >= ring)
+        def _():
+            to_y(t - ring).wait_send()
+            keep(t - ring).wait()
+
+        to_x(t).wait_recv()
+        scale = gs[t]
+        gsum_o[t] = jnp.zeros((8, tw), F32)
+
+        def body(span):
+            grad = sx[t % 4, span, :].astype(F32) + xgot[t, span, :].astype(F32)
+            gate = pair[t % 2, 0, span, :].astype(F32)
+            up = pair[t % 2, 1, span, :].astype(F32)
+            value, slope = gelu_parts(gate)
+            full = grad * (is_gate * (up * slope) + (1.0 - is_gate) * value)
+            gsum_o[t, 0:1, :] += jnp.sum(pair[t % 2, x, span, :].astype(F32) * full, axis=0, keepdims=True)
+            dg[t % ring, span, :] = (full * scale).astype(BF16)
+
+        strips(rows // 64, 64, body)
+
+        @pl.when(t + 2 < tiles)
+        def _():
+            load_pair(t + 2).start()
+
+        to_y(t).start()
+        keep(t).start()
+
+    def back(t):
+        load_up(t).wait()
+
+        def level(span):
+            wlev[span, :] = levels(wbuf[t % 2, span, :], 16.0)
+
+        strips(deep // 128, 128, level)
+
+        @pl.when(t + 2 < tiles)
+        def _():
+            load_up(t + 2).start()
+
+        def product(span):
+            acc[span, :] += contract_last(dg[t % ring, span, :], wlev[...])
+
+        strips(rows // 128, 128, product)
+
+    def partial(k, j):
+        return contract_first(hh[k * per + j], gf[...]) + contract_first(hy[k * per + j], gfy[...])
+
+    def chain(j, s):
+        go_right = z + nz - s
+        go_left = z - nz + s
+
+        def one(go, got, out_buf, ss, sr, to, source, first):
+            @pl.when(j > 0)
+            def _():
+                remote(out_buf.at[s - 1], got.at[j - 1, s - 1], ss.at[j - 1, s - 1], sr.at[j - 1, s - 1], to).wait_send()
+
+            total = partial(go, j)
+            more = (s > 1) & jnp.logical_not(first)
+
+            @pl.when(more)
+            def _():
+                remote(out_buf.at[0], got.at[j, s - 2], ss.at[j, s - 2], sr.at[j, s - 2], source).wait_recv()
+                out_buf[s - 1] = (total + got[j, s - 2].astype(F32)).astype(BF16)
+
+            @pl.when(jnp.logical_not(more))
+            def _():
+                out_buf[s - 1] = total.astype(BF16)
+
+            remote(out_buf.at[s - 1], got.at[j, s - 1], ss.at[j, s - 1], sr.at[j, s - 1], to).start()
+
+        @pl.when(go_right < nz)
+        def _():
+            one(go_right, r_got, r_out, rs, rr, right, left, z == 0)
+
+        @pl.when(go_left >= 0)
+        def _():
+            one(go_left, l_got, l_out, ls, lr, left, right, z == nz - 1)
+
+    def chain_end(j):
+        ddown_o[j] = partial(z, j)
+
+        @pl.when(z > 0)
+        def _():
+            remote(r_out.at[0], r_got.at[j, nz - 2], rs.at[j, nz - 2], rr.at[j, nz - 2], left).wait_recv()
+            ddown_o[j] += r_got[j, nz - 2].astype(F32)
+
+        @pl.when(z < nz - 1)
+        def _():
+            remote(l_out.at[0], l_got.at[j, nz - 2], ls.at[j, nz - 2], lr.at[j, nz - 2], right).wait_recv()
+            ddown_o[j] += l_got[j, nz - 2].astype(F32)
+
+    hops = nz - 1
+
+    def step(i, carry):
+        @pl.when(i < tiles)
+        def _():
+            hidden(i)
+
+        @pl.when((i >= 1) & (i < tiles + 1))
+        def _():
+            chip(i - 1)
+
+        if chained:
+
+            @pl.when(i == 1)
+            def _():
+                gf_swap.wait_recv()
+                load_hid.wait()
+                load_hidy.wait()
+
+            @pl.when((i >= 1) & (i < 1 + per * hops))
+            def _():
+                chain((i - 1) // hops, (i - 1) % hops + 1)
+
+        @pl.when(i >= 2)
+        def _():
+            own(i - 2)
+            back(i - 2)
+
+        return carry
+
+    lax.fori_loop(0, tiles + 2, step, 0)
+
+    parts = 4
+    block = rows // GROUP
+    size = block // parts
+    order = [1 - x, x]
+    cores = []
+    for i in range(2):
+        for k in range(parts):
+            owner = order[i] * 2 + 1 - c
+            span = pl.ds(k * size, size)
+            low[i, span, :] = acc[pl.ds(pl.multiple_of(owner * block + k * size, 16), size), :].astype(BF16)
+            copy = remote(low.at[i, span], from_core.at[i, span], ccs.at[i, k], ccr.at[i, k], beside)
+            copy.start()
+            cores.append(copy)
+    sends = []
+    for k in range(parts):
+        span = pl.ds(k * size, size)
+        here = pl.ds(pl.multiple_of((order[0] * 2 + c) * block + k * size, 16), size)
+        cores[k].wait_recv()
+        to_xb[span, :] = (acc[here, :] + from_core[0, span, :].astype(F32)).astype(BF16)
+        copy = remote(to_xb.at[span], from_x.at[span], cxs.at[k], cxr.at[k], across)
+        copy.start()
+        sends.append(copy)
+    if chained:
+        for j in range(per):
+            chain_end(j)
+    for k in range(parts):
+        span = pl.ds(k * size, size)
+        here = pl.ds(pl.multiple_of((order[1] * 2 + c) * block + k * size, 16), size)
+        cores[parts + k].wait_recv()
+        sends[k].wait_recv()
+        out[span, :] = acc[here, :] + from_core[1, span, :].astype(F32) + from_x[span, :].astype(F32)
+
+    for copy in cores + sends:
+        copy.wait_send()
+    for t in range(tiles - 2, tiles):
+        to_core(t).wait_send()
+    for t in range(tiles - 4, tiles):
+        to_x(t).wait_send()
+    for t in range(tiles - ring, tiles):
+        to_y(t).wait_send()
+        keep(t).wait()
+
+    def drain(t, carry):
+        to_y(t).wait_recv()
+        return carry
+
+    lax.fori_loop(0, tiles, drain, 0)
+    if chained:
+        gf_swap.wait_send()
+        j = per - 1
+        for s in range(1, nz):
+
+            @pl.when(z + nz - s < nz)
+            def _():
+                remote(r_out.at[s - 1], r_got.at[j, s - 1], rs.at[j, s - 1], rr.at[j, s - 1], right).wait_send()
+
+            @pl.when(z - nz + s >= 0)
+            def _():
+                remote(l_out.at[s - 1], l_got.at[j, s - 1], ls.at[j, s - 1], lr.at[j, s - 1], left).wait_send()
+
+
+def ffn_backward(cid, n, gf, wd, wgu, gs, gu, hid, hidy):
+    rows, part = gf.shape
+    deep = wgu.shape[0]
+    tiles, _, tw = gs.shape
+    nz = n // 2
+    chained = nz == 4
+    per = tiles // nz if chained else 1
+    hops = nz - 1 if chained else 1
+    block = rows // GROUP
+    half = (tiles, rows, tw) if chained else (1, 16, 128)
+    message = (tw, part) if chained else (16, 128)
+    ring = 4
+    return comm_call(
+        functools.partial(ffn_backward_kernel, tiles, nz, chained),
+        cid,
+        [
+            jax.ShapeDtypeStruct((rows, tiles * tw), BF16),
+            jax.ShapeDtypeStruct((rows, tiles * tw), BF16),
+            jax.ShapeDtypeStruct((tiles, 8, tw), F32),
+            jax.ShapeDtypeStruct((block, deep), F32),
+            jax.ShapeDtypeStruct((per,) + message, F32),
+        ],
+        [
+            pltpu.VMEM(half, BF16),
+            pltpu.VMEM(half, BF16),
+            pltpu.VMEM((rows, part), BF16),
+            pltpu.VMEM((2, deep, tw), BF16),
+            pltpu.VMEM((deep, tw), BF16),
+            pltpu.VMEM((2, 2, tw, part), BF16),
+            pltpu.VMEM((2, tw, part), BF16),
+            pltpu.VMEM((2, 2, rows, tw), BF16),
+            pltpu.VMEM((2, rows, tw), BF16),
+            pltpu.VMEM((tiles, rows, tw), BF16),
+            pltpu.VMEM((2, rows, tw), F32),
+            pltpu.VMEM((4, rows, tw), BF16),
+            pltpu.VMEM((tiles, rows, tw), BF16),
+            pltpu.VMEM((ring, rows, tw), BF16),
+            pltpu.VMEM((rows, deep), F32),
+            pltpu.VMEM((2, block, deep), BF16),
+            pltpu.VMEM((2, block, deep), BF16),
+            pltpu.VMEM((block, deep), BF16),
+            pltpu.VMEM((block, deep), BF16),
+            pltpu.VMEM((hops,) + message, BF16),
+            pltpu.VMEM((hops,) + message, BF16),
+            pltpu.VMEM((per, hops) + message, BF16),
+            pltpu.VMEM((per, hops) + message, BF16),
+            DMA((2,)), DMA((2,)), DMA((2, 2)), DMA((2,)), DMA((tiles,)), DMA((tiles,)), DMA((tiles,)), DMA((tiles,)),
+            DMA((tiles,)), DMA((tiles,)), DMA((tiles,)), DMA, DMA, DMA((2, 4)), DMA((2, 4)), DMA((4,)), DMA((4,)),
+            DMA((per, hops)), DMA((per, hops)), DMA((per, hops)), DMA((per, hops)),
+        ],
+        [VMEM, ANY, ANY, VMEM, ANY, ANY, ANY],
+        [ANY, ANY, VMEM, VMEM, VMEM],
+    )(gf, wd, wgu, gs, gu, hid, hidy)
+
+
+def rms_inverse(value):
+    return lax.rsqrt(jnp.mean(value * value, axis=-1, keepdims=True) + EPSILON)
+
+
+def norm_back(inverse, normed, upstream):
+    return inverse * (upstream - normed * jnp.mean(upstream * normed, axis=-1, keepdims=True))
+
+
+def rotate(value, cosine, sine):
+    half = DH // 2
+    first = value[..., :half]
+    second = value[..., half:]
+    return jnp.concatenate([first * cosine - second * sine, second * cosine + first * sine], axis=-1)
+
+
 def seq_swap(value, n):
     return lax.ppermute(value, "seq", [(s, s ^ 1) for s in range(n)])
 
 
-def x_swap(value):
-    return lax.ppermute(value, "fsdp", [(f, f ^ 2) for f in range(GROUP)])
-
-
 def core_swap(value):
     return lax.ppermute(value, "fsdp", [(f, f ^ 1) for f in range(GROUP)])
 
 
-def pair_rows(value, n, y):
+def slice_halves(value, n, y):
     rows, width = value.shape
-    split = value.reshape(rows, n // 2, 2, width // n)
-    here = lax.dynamic_index_in_dim(split, y, 2, keepdims=False).reshape(rows, width // 2)
-    there = lax.dynamic_index_in_dim(split, 1 - y, 2, keepdims=False).reshape(rows, width // 2)
-    return here, seq_swap(there, n)
-
-
-def chain_sum(block, n, z):
-    nz = n // 2
-    pick = lambda k: lax.dynamic_index_in_dim(block, jnp.clip(k, 0, nz - 1), 0, keepdims=False)
-    from_left = from_right = None
-    for t in range(1, nz):
-        right = pick(z + nz - t)
-        left = pick(z - nz + t)
+    turned = value.T.reshape(n // 2, 2, width // n, rows)
+    here = lax.dynamic_index_in_dim(turned, y, 1, keepdims=False).reshape(width // 2, rows)
+    there = lax.dynamic_index_in_dim(turned, 1 - y, 1, keepdims=False).reshape(width // 2, rows)
+    return here, there
+
+
+class ChainSum:
+    def __init__(self, block, n, z):
+        self.block, self.n, self.z, self.t = block, n, z, 1
+        self.got = None
+
+    def pick(self, k):
+        return lax.dynamic_index_in_dim(self.block, jnp.clip(k, 0, self.n // 2 - 1), 0, keepdims=False)
+
+    def hop(self):
+        n, z, t = self.n, self.z, self.t
+        right = self.pick(z + n // 2 - t)
+        left = self.pick(z - n // 2 + t)
         if t > 1:
-            right = (right.astype(F32) + from_left.astype(F32)).astype(BF16)
-            left = (left.astype(F32) + from_right.astype(F32)).astype(BF16)
-        go_right = [(s, s + 2) for s in range(2 * t)]
-        go_left = [(n - 1 - s, n - 3 - s) for s in range(2 * t)]
-        from_left = lax.ppermute(right, "seq", go_right)
-        from_right = lax.ppermute(left, "seq", go_left)
-    return pick(z).astype(F32) + from_left.astype(F32) + from_right.astype(F32)
+            right = (right.astype(F32) + self.got[0].astype(F32)).astype(BF16)
+            left = (left.astype(F32) + self.got[1].astype(F32)).astype(BF16)
+        self.got = (
+            lax.ppermute(right, "seq", [(s, s + 2) for s in range(2 * t)]),
+            lax.ppermute(left, "seq", [(n - 1 - s, n - 3 - s) for s in range(2 * t)]),
+        )
+        self.t += 1
+
+    def after(self, value):
+        self.got, value = lax.optimization_barrier((self.got, value))
+        return value
+
+    def end(self):
+        while self.t < self.n // 2:
+            self.hop()
+        return self.pick(self.z).astype(F32) + self.got[0].astype(F32) + self.got[1].astype(F32)
 
 
 def pair_product(lefts, rights):
-    return contract_first(lefts[0], rights[0]) + contract_first(lefts[1], rights[1])
+    return dot(lefts[0], rights[0]) + dot(lefts[1], rights[1])
 
 
 def lanes(value, rows):
@@ -846,12 +1499,11 @@
     heads = jnp.stack(
         [rotate(pair_plain[:, j * DH : (j + 1) * DH], pair_cosine, pair_sine) for j in range(2)]
     ).astype(BF16)
-    first_pair = pair_rows(first_input, n, y)
-    pairs, metas, cot_blocks = keys_gather(2, n, heads, own_meta, cotangent[0])
+    cot_columns = cotangent[0].reshape(own, GROUP, part).transpose(1, 0, 2).reshape(rows, part)
+    pairs, metas, cot_blocks = keys_gather(2, n, heads, own_meta, cot_columns)
 
     mixed_low, mixed, mass = attend(n, query, pairs, own_meta, metas)
     (mixed_rows,) = group_gather(3, [mixed_low], columns=[True])
-    mixed_pair = pair_rows(mixed_rows, n, y)
     branch_own = dot(mixed_rows, output_code).astype(BF16)
     (branch_blocks,) = group_gather(4, [branch_own])
     branch_raw = blocks_to_rows(branch_blocks).astype(F32)
@@ -860,83 +1512,54 @@
     middle = inputs + branch * second_inverse * gain[1]
     third_inverse = rms_inverse(middle)
     second_input = (middle * third_inverse * gain[2]).astype(BF16)
-    second_pair = pair_rows(second_input, n, y)
-
-    gate_levels = code_levels(gate_up_code, 16.0)
-    down_levels = code_levels(down_code, 64.0)
+
+    halves = [slice_halves(v, n, y) for v in (first_input, mixed_rows, second_input)]
     my_gate_scale = mine(gate_up_scale)
-    columns = gate_levels.shape[1]
-    chunks = 4
-    size = columns // chunks
-    down_split = down_levels.reshape(2, columns, part)
-    down_here = lax.dynamic_index_in_dim(down_split, c, 0, keepdims=False)
-    down_there = lax.dynamic_index_in_dim(down_split, 1 - c, 0, keepdims=False)
-    owns, others, hiddens, hiddens_core = [], [], [], []
-    for k in range(chunks):
-        span = slice(k * size, (k + 1) * size)
-        owns.append((dot(second_input, gate_levels[:, span]) * my_gate_scale[span]).astype(BF16))
-        others.append(x_swap(owns[k]))
-    down_sum = 0.0
-    for k in range(chunks):
-        span = slice(k * size, (k + 1) * size)
-        gate = jnp.where(is_gate, owns[k], others[k]).astype(F32)
-        up = jnp.where(is_gate, others[k], owns[k]).astype(F32)
-        hiddens.append((gelu_parts(gate)[0] * up).astype(BF16))
-        hiddens_core.append(core_swap(hiddens[k]))
-        down_sum = down_sum + dot(hiddens[k], down_here[span]) + dot(hiddens_core[k], down_there[span])
-    down_own = down_sum.astype(BF16)
-    (down_blocks,) = group_gather(5, [down_own])
-    down_raw = blocks_to_rows(down_blocks).astype(F32)
-    down = down_raw * down_scale
-    fourth_inverse = rms_inverse(down)
-    fourth = down * fourth_inverse
-    result = own_rows(middle + fourth * gain[3]).astype(BF16)
-
-    grad_result = cot_blocks.reshape(rows, width).astype(F32)
-    gain_four = jnp.sum(own_rows(grad_result * fourth), axis=0)
-    grad_down_full = norm_back(fourth_inverse, fourth, grad_result * gain[3])
-    grad_down_own = lax.dynamic_slice_in_dim(grad_down_full, me * part, part, 1)
-    scale_down = jnp.sum(down_own.astype(F32) * grad_down_own, axis=0)
-    grad_down = (grad_down_own * mine(down_scale)).astype(BF16)
-    grad_down_pair = (grad_down, seq_swap(grad_down, n))
-
-    here = jnp.concatenate(hiddens, axis=1)
-    there = jnp.concatenate(hiddens_core, axis=1)
-    hidden_rows = jnp.concatenate([jnp.where(c == 0, here, there), jnp.where(c == 0, there, here)], axis=1)
-    hidden_pair = pair_rows(hidden_rows, n, y)
-    down_block = pair_product(hidden_pair, grad_down_pair).astype(BF16)
-    down_grad = chain_sum(down_block.reshape(n // 2, -1, part), n, z)
-
-    grads, gate_sums = [], []
-    grad_second_sum = 0.0
-    core_gots = []
-    for k in range(chunks):
-        span = slice(k * size, (k + 1) * size)
-        core_gots.append(core_swap(contract_last(grad_down, down_there[span]).astype(BF16)))
-    sums, x_gots = [], []
-    for k in range(chunks):
-        span = slice(k * size, (k + 1) * size)
-        sums.append((contract_last(grad_down, down_here[span]) + core_gots[k].astype(F32)).astype(BF16))
-        x_gots.append(x_swap(sums[k]))
-    for k in range(chunks):
-        span = slice(k * size, (k + 1) * size)
-        grad_hidden = sums[k].astype(F32) + x_gots[k].astype(F32)
-        gate = jnp.where(is_gate, owns[k], others[k]).astype(F32)
-        up = jnp.where(is_gate, others[k], owns[k]).astype(F32)
-        value, slope = gelu_parts(gate)
-        grad_full = grad_hidden * jnp.where(is_gate, up * slope, value)
-        gate_sums.append(jnp.sum(owns[k].astype(F32) * grad_full, axis=0) / my_gate_scale[span])
-        grads.append((grad_full * my_gate_scale[span]).astype(BF16))
-        grad_second_sum = grad_second_sum + contract_last(grads[k], gate_levels[:, span])
-    scale_gate = jnp.concatenate(gate_sums)
-    grad_gate_up = jnp.concatenate(grads, axis=1)
-    grad_gate_pair = (grad_gate_up, seq_swap(grad_gate_up, n))
-
-    grad_second_input = group_reduce(6, grad_second_sum.astype(BF16).reshape(GROUP, own, width), F32)
-    gate_block = pair_product(second_pair, grad_gate_pair).astype(BF16)
-    gate_grad = chain_sum(gate_block.reshape(n // 2, -1, columns), n, z)
-
+    columns = gate_up_code.shape[1]
+    tiles = columns // TILE
+    gate_scales = my_gate_scale.reshape(tiles, 1, TILE)
+    gate_up, hidden, hidden_y, down_blocks, grad_down, down_sums, *riders = ffn_forward(
+        5,
+        second_input,
+        gate_up_code,
+        gate_scales,
+        down_code,
+        cot_blocks,
+        gain[3].reshape(GROUP, 1, part),
+        down_scale.reshape(GROUP, 1, part),
+        [half[1] for half in halves],
+    )
+    first_pair, mixed_pair, second_pair = [(half[0], rider) for half, rider in zip(halves, riders)]
     my_middle = own_rows(middle)
+    my_down = blocks_to_rows(lax.dynamic_slice_in_dim(down_blocks, me * own, own, 1)).astype(F32) * down_scale
+    result = (my_middle + my_down * rms_inverse(my_down) * gain[3]).astype(BF16)
+    grad_gate_up, grad_gate_up_y, gate_sums, grad_second_input, down_grad = ffn_backward(
+        6, n, grad_down, down_code, gate_up_code, gate_scales, gate_up, hidden, hidden_y
+    )
+    if n == 8:
+        down_grad = down_grad.reshape(-1, part)
+    else:
+        hidden_own = jnp.concatenate(
+            [
+                (jax.nn.gelu(gate_up[0, t].astype(F32)) * gate_up[1, t].astype(F32)).astype(BF16)
+                for t in range(tiles)
+            ],
+            axis=1,
+        )
+        hidden_core = core_swap(hidden_own)
+        hidden_rows = jnp.concatenate(
+            [jnp.where(c == 0, hidden_own, hidden_core), jnp.where(c == 0, hidden_core, hidden_own)], axis=1
+        )
+        down_grad = lax.psum_scatter(
+            contract_first(hidden_rows, grad_down), "seq", scatter_dimension=0, tiled=True
+        )
+    scale_down = down_sums[0]
+    gain_four = down_sums[1]
+    scale_gate = gate_sums[:, 0, :].reshape(columns) / my_gate_scale
+    gate_block = pair_product(second_pair, (grad_gate_up, grad_gate_up_y)).astype(BF16)
+    gate_chain = ChainSum(gate_block.reshape(n // 2, -1, columns), n, z)
+    gate_chain.hop()
+
     third_inverse = own_rows(third_inverse)
     second_inverse = own_rows(second_inverse)
     my_branch_raw = own_rows(branch_raw)
@@ -954,13 +1577,15 @@
     ).reshape(rows, part)
     grad_branch_pair = (grad_branch, seq_swap(grad_branch, n))
     output_block = pair_product(mixed_pair, grad_branch_pair).astype(BF16)
-    output_grad = chain_sum(output_block.reshape(n // 2, -1, part), n, z)
+    output_chain = ChainSum(output_block.reshape(n // 2, -1, part), n, z)
     grad_mixed_sum = jnp.stack(
         [contract_last(grad_branch, output_code[i * 2 * DH : (i + 1) * 2 * DH]) for i in range(GROUP)]
     ).astype(BF16)
     grad_mixed = group_reduce(8, grad_mixed_sum, BF16)
 
     grad_query, grad_pairs = attend_back(n, query, pairs, own_meta, metas, mixed, mass, grad_mixed)
+    grad_pairs = gate_chain.after(grad_pairs)
+    gate_chain.hop()
     grad_heads = keys_reduce(9, n, grad_pairs).astype(F32)
     grad_query_full = rotate(
         grad_query.reshape(rows, 2, DH), cosine[:, None], -sine[:, None]
@@ -977,17 +1602,19 @@
     grad_first_sum = contract_last(grad_query_low, query_code) + contract_last(grad_pair_low, key_value_code)
     grad_first_input = group_reduce(10, grad_first_sum.astype(BF16).reshape(GROUP, own, width), F32)
     attention_block = pair_product(first_pair, joined_pair).astype(BF16)
-    attention_grad = chain_sum(attention_block.reshape(n // 2, -1, joined.shape[1]), n, z)
+    attention_chain = ChainSum(attention_block.reshape(n // 2, -1, joined.shape[1]), n, z)
+    grad_first_input = gate_chain.after(grad_first_input)
+    gate_chain.hop()
     my_inputs = tokens[0].astype(F32)
     my_inverse = rms_inverse(my_inputs)
     first = my_inputs * my_inverse
     gain_one = jnp.sum(grad_first_input * first, axis=0)
     grad_inputs = grad_middle + norm_back(my_inverse, first, grad_first_input * gain[0])
 
-    wholes = jnp.concatenate([gain_one, gain_two, gain_three, gain_four, scale_output])
-    parts = [scale_query, scale_pair, scale_gate, scale_down]
+    wholes = jnp.concatenate([gain_one, gain_two, gain_three, scale_output])
+    parts = [scale_query, scale_pair, scale_gate, scale_down, gain_four]
     whole_total, part_total = totals(
-        11, n, lanes(wholes, 96), lanes(jnp.concatenate(parts), 56)
+        11, n, lanes(wholes, 72), lanes(jnp.concatenate(parts), 56)
     )
     whole_total = whole_total.reshape(-1)
     part_total = part_total.reshape(GROUP, -1)
@@ -997,20 +1624,21 @@
         pieces.append(part_total[:, start : start + vector.shape[0]].reshape(-1))
         start += vector.shape[0]
     q_width = query_code.shape[1]
+    attention_grad = attention_chain.end()
     return (
         result[None],
         grad_inputs[None],
         attention_grad[:, :q_width],
         attention_grad[:, q_width:],
-        output_grad,
-        gate_grad,
+        output_chain.end(),
+        gate_chain.end(),
         down_grad,
         pieces[0],
         pieces[1],
-        whole_total[4 * width : 5 * width],
+        whole_total[3 * width :],
         pieces[2],
         pieces[3],
-        whole_total[: 4 * width].reshape(4, width),
+        jnp.concatenate([whole_total[: 3 * width], pieces[4]]).reshape(4, width),
     )
 
 

time: 1460 us -> 1020 us (0.70)
  waiting for transfers between devices: 323 us -> 117 us
  Pallas kernels: 368 us -> 544 us
  local copies, waits for them, and re-layouts: 272 us -> 130 us
  matrix products: 158 us -> 57.7 us
  other arithmetic: 185 us -> 87.9 us
  starting transfers between devices: 146 us -> 72.3 us
    pallas_call x0 -> x2, Pallas kernels: none -> 275 us  [the longest x1 141 us: ffn_backward(): comm_call(functools.partial(ffn_backward_kernel, tiles, nz, chained), cid...]
    ppermute x40 -> x18, waiting for transfers between devices: 222 us -> 109 us  [the longest x9 58.8 us: hop(): lax.ppermute(left, 'seq', [(n - 1 - s, n - 3 - s) for s in range(2 * t)])]
    ppermute x8 -> x2, waiting for transfers between devices: 102 us -> 7.76 us  [seq_swap(): return lax.ppermute(value, 'seq', [(s, s ^ 1) for s in range(n)])]
    ppermute x40 -> x18, starting transfers between devices: 137 us -> 68.4 us  [the longest x9 55.2 us: hop(): lax.ppermute(right, 'seq', [(s, s + 2) for s in range(2 * t)])]
    dot_general x8 -> x0, matrix products: 49.4 us -> none  [contract_first(): lax.dot_general(left, right, (((0,), (0,)), ((), ())), preferred_element_...]
    slice x10 -> x5, local copies, waits for them, and re-layouts: 53.1 us -> 4.36 us  [the longest x1 1.42 us: per_device(): gain_four = down_sums[1]]
    convert_element_type x25 -> x9, other arithmetic: 71.3 us -> 26.7 us  [the longest x5 14.7 us: hop(): right = (right.astype(F32) + self.got[0].astype(F32)).astype(BF16)]
    dot_general x18 -> x6, matrix products: 57.4 us -> 13.8 us  [contract_last(): lax.dot_general(left, right, (((1,), (1,)), ((), ())), preferred_element_...]
  transfers between devices with their start and end apart: 48 -> 20, of which waited for: 11 -> 4; matrix products, arithmetic and copies ran while one was open for 36% -> 12% of each run, Pallas kernels for 16% -> 14%
where the time goes in v2:
time: 1020 us; the launch traced here: 1010 us
  Pallas kernels  544 us (53%)
  local copies, waits for them, and re-layouts  130 us (13%)
  waiting for transfers between devices  117 us (11%)
  other arithmetic  87.9 us (9%)
  starting transfers between devices  72.3 us (7%)
  matrix products  57.7 us (6%)
    pallas_call x1, Pallas kernels, ffn_backward(): comm_call(functools.partial(ffn_backward_kernel, tiles, nz, chained), cid...  141 us
    pallas_call x1, Pallas kernels, ffn_forward(): comm_call(functools.partial(ffn_forward_kernel, tiles, count), cid, [jax....  135 us
    pallas_call x3, Pallas kernels, group_gather(): comm_call(functools.partial(group_gather_kernel, count, tuple(columns), t...  62.7 us
    pallas_call x1, Pallas kernels, keys_gather(): comm_call(functools.partial(keys_gather_kernel, n), cid, [jax.ShapeDtypeS...  61.3 us
    pallas_call x1, Pallas kernels, keys_reduce(): comm_call(functools.partial(keys_reduce_kernel, n), cid, jax.ShapeDtypeSt...  60.8 us
    ppermute x9, waiting for transfers between devices, hop(): lax.ppermute(left, 'seq', [(n - 1 - s, n - 3 - s) for s in range(2 * t)])  58.8 us
    ppermute x9, starting transfers between devices, hop(): lax.ppermute(right, 'seq', [(s, s + 2) for s in range(2 * t)])  55.2 us
    ppermute x9, waiting for transfers between devices, hop(): lax.ppermute(right, 'seq', [(s, s + 2) for s in range(2 * t)])  50.1 us
  transfers between devices with their start and end apart: 20, of which 4 were waited for; matrix products, arithmetic and copies ran while one was open for 12% of the time, Pallas kernels for 14%

profile of v2, /device:TPU:0, one launch (start us, length us, event | category | flops | bytes accessed | tf_op | source)
XLA Modules:
  0.0 1010.0 jit_solution(2004598230797694755)
XLA Ops:
  5.3 22.4 %shard_map.255 = (bf16[4,128,2304]{2,1,0:T(8,128)(2,1)}, f32[4,8,128]{2,1,0:T(8,128)}) custom-call(bf16[128,2304]{1,0:T(8,128)(2,1)} %bitcast.225, f32[8,128]{1,0:T(8,128)} %stack.43.refs_1_), custom_call_target="tpu_custom_call" | custom-call | tf_op jit(solution)/shard_map/pallas_call | solution.py:126
  27.7 2.2 fusion.6
  34.2 2.3 fusion.10
  36.5 2.7 broadcast_multiply_fusion.1
  41.1 4.7 broadcast_multiply_fusion
  50.2 61.3 %shard_map.256 = (bf16[8,2,512,256]{3,2,1,0:T(8,128)(2,1)}, f32[8,4,8,128]{3,2,1,0:T(8,128)}, bf16[4,512,576]{2,1,0:T(8,128)(2,1)}) custom-call(bf16[2,512,256]{2,1,0:T(8,128)(2,1)} %pad_maximum_fusion.5.heads, f32[4,8,128]{2,1,0:T(8,128)} %get-tuple-element.46.meta.own_ref, bf16[512,576]{1,0:T(8,128)(2,1)} %bitcast.243), custom_call_target="tpu_custom_call" | custom-call | tf_op jit(solution)/shard_map/pallas_call | solution.py:350
  111.5 6.2 shard_map.257
  117.7 17.2 %shard_map.258 = bf16[512,2048]{1,0:T(8,128)(2,1)} custom-call(bf16[512,512]{1,0:T(8,128)(2,1)} %get-tuple-element.49.refs_0_), custom_call_target="tpu_custom_call" | custom-call | tf_op jit(solution)/shard_map/pallas_call | solution.py:126
  134.9 3.7 convolution_convert_fusion
  139.7 23.1 %shard_map.259 = bf16[4,512,576]{2,1,0:T(8,128)(2,1)} custom-call(bf16[512,576]{1,0:T(8,128)(2,1)} %copy.98.refs_0_), custom_call_target="tpu_custom_call" | custom-call | tf_op jit(solution)/shard_map/pallas_call | solution.py:126
  162.9 3.9 slice_bitcast_fusion.6
  166.8 5.2 concatenate.59
  172.0 2.4 multiply_reduce_fusion
  174.4 5.1 concatenate.64
  179.5 3.9 fusion.8
  184.0 4.5 multiply_convert_fusion
  188.5 4.3 copy.101
  192.8 4.7 reshape.390
  197.5 3.0 constant_dynamic-slice_fusion.9
  200.6 6.3 constant_dynamic-slice_fusion.7
  206.9 5.8 copy.120
  212.7 4.3 copy.99
  217.0 3.2 constant_dynamic-slice_fusion.8
  224.3 15.6 %copy.102.refs_3_.refs_1_ = bf16[9216,576]{1,0:T(8,128)(2,1)} copy(bf16[9216,576]{0,1:T(8,128)(2,1)} %param.24) | data formatting | bytes 21233664 | tf_op args[8]
  241.3 134.8 %shard_map.260 = (bf16[2,12,512,384]{3,2,1,0:T(8,128)(2,1)}, bf16[12,512,384]{2,1,0:T(8,128)(2,1)}, bf16[12,512,384]{2,1,0:T(8,128)(2,1)}, bf16[4,512,576]{2,1,0...) custom-call(bf16[512,2304]{1,0:T(8,128)(2,1)} %get-tuple-element.143, ...), custom_call_target="tpu_custom_call" | custom-call | tf_op jit(solution)/shard_map/pallas_call | solution.py:971
  376.1 140.6 %shard_map.261 = (bf16[512,4608]{1,0:T(8,128)(2,1)}, bf16[512,4608]{1,0:T(8,128)(2,1)}, f32[12,8,384]{2,1,0:T(8,128)}, f32[128,2304]{1,0:T(8,128)}, f32[3,384,576]{2,1,0:T(8,128)}) custom-call(bf16[512,576]{1,0:T(8,128)(2,1)} %get-tuple-element.52.refs_0_, bf16[9216,576]{1,0:T(8,128)(2,1)} %copy.102.refs_3_.refs_1_, bf16[2304,4608]{1,0:T(8,128)(2,1)} %refs_2_.1, ...), custom_call_target="tpu_custom_call" | custom-call | tf_op jit(solution)/shard_map/pallas_call | solution.py:1321
  516.8 12.4 %fusion.50 = f32[1152,4608]{1,0:T(8,128)} fusion(bf16[1152,512]{1,0:T(8,128)(2,1)S(1)} %bitcast.252, bf16[512,4608]{1,0:T(8,128)(2,1)} %get-tuple-element.57), kind=kOutput, calls=%fused_computation.184 | convolution fusion | flops 5435817984 | bytes 27131904 | tf_op jit(solution)/shard_map/dot_general | solution.py:30
  529.2 13.7 %fusion = bf16[1152,4608]{1,0:T(8,128)(2,1)} fusion(f32[1152,4608]{1,0:T(8,128)} %fusion.50, bf16[1152,512]{1,0:T(8,128)(2,1)S(1)} %copy-done.54, bf16[512,4608]{1,0:T(8,128)(2,1)} %get-tuple-element.59), kind=kOutput, calls=%fused_computation.1 | convolution fusion | flops 5446434816 | bytes 37748736 | tf_op jit(solution)/shard_map/dot_general | solution.py:30
  542.9 5.2 dynamic-slice_bitcast_fusion
  548.1 27.2 %collective-permute-start = (bf16[288,4608]{1,0:T(8,128)(2,1)}, bf16[288,4608]{1,0:T(8,128)(2,1)}, u32[]{:S(2)}, u32[]{:S(2)}) collective-permute-start(bf16[288,4608]{1,0:T(8,128)(2,1)} %get-tuple-element.150), channel_id=1, source_target_pairs={{0,8},{4,12},{1,9},{5,13},{2,10},{6,14},{3,11},{7,15}} | collective-permute-start | bytes 7962632 | tf_op jit(solution)/shard_map/ppermute | solution.py:1411
  577.5 4.2 convert_element_type.278
  588.3 2.6 multiply_reduce_fusion.2
  590.9 3.4 multiply_reduce_fusion.4
  595.3 2.4 multiply_reduce_fusion.3
  599.1 10.9 %shard_map.262 = bf16[4,128,576]{2,1,0:T(8,128)(2,1)} custom-call(bf16[4,128,576]{2,1,0:T(8,128)(2,1)} %bitcast.244), custom_call_target="tpu_custom_call" | custom-call | tf_op jit(solution)/shard_map/pallas_call | solution.py:208
  613.5 2.6 fusion.16
  619.3 2.7 fusion.17
  622.0 5.8 copy.121
  627.8 2.5 fusion.18
  631.6 2.9 add_convert_fusion
  634.5 2.7 reshape.404
  637.2 5.1 constant_dynamic-slice_fusion.6
  647.8 2.7 collective-permute-done.12
  651.3 5.1 collective-permute-start.13
  660.0 16.9 %shard_map.263.grad_ref = bf16[512,512]{1,0:T(8,128)(2,1)} custom-call(bf16[4,512,512]{2,1,0:T(8,128)(2,1)} %pad_maximum_fusion.src), custom_call_target="tpu_custom_call" | custom-call | tf_op jit(solution)/shard_map/pallas_call | solution.py:179
  676.9 9.6 shard_map.264
  688.4 3.4 copy.117
  698.3 60.8 %shard_map.265 = bf16[2,512,256]{2,1,0:T(8,128)(2,1)} custom-call(bf16[8,2,512,256]{3,2,1,0:T(8,128)(2,1)} %get-tuple-element.66.src), custom_call_target="tpu_custom_call" | custom-call | tf_op jit(solution)/shard_map/pallas_call | solution.py:528
  765.3 2.5 collective-permute-start.4
  767.8 7.8 fusion.4
  775.6 4.5 collective-permute-start.2
  783.7 7.8 collective-permute-done.4
  793.8 2.7 collective-permute-start.5
  801.4 47.4 %collective-permute-done.5 = bf16[288,1024]{1,0:T(8,128)(2,1)S(1)} collective-permute-done((bf16[288,1024]{1,0:T(8,128)(2,1)S(1)}, bf16[288,1024]{1,0:T(8,128)(2,1)S(1)}, u32[]{:S(2)}, u32[]{:S(2)}) %collective-permute-start.5) | collective-permute-done | bytes 589856 | tf_op jit(solution)/shard_map/ppermute | solution.py:1411
  849.9 5.4 collective-permute-start.6
  855.3 2.9 fusion.11
  858.3 18.6 %shard_map.266 = f32[128,2304]{1,0:T(8,128)} custom-call(bf16[4,128,2304]{2,1,0:T(8,128)(2,1)} %bitcast.221), custom_call_target="tpu_custom_call" | custom-call | tf_op jit(solution)/shard_map/pallas_call | solution.py:179
  879.8 3.1 fusion.30
  888.2 21.2 %shard_map.267 = (f32[72,128]{1,0:T(8,128)}, f32[4,56,128]{2,1,0:T(8,128)}) custom-call(f32[72,128]{1,0:T(8,128)} %pad_maximum_fusion.6.whole, f32[56,128]{1,0:T(8,128)} %pad_bitcast_fusion.part), custom_call_target="tpu_custom_call" | custom-call | tf_op jit(solution)/shard_map/pallas_call | solution.py:576
  913.1 7.8 fusion.2
  920.9 5.3 collective-permute-start.18
  939.3 2.5 fusion.24
  941.8 58.7 %collective-permute-done.10 = bf16[288,1024]{1,0:T(8,128)(2,1)S(1)} collective-permute-done((bf16[288,1024]{1,0:T(8,128)(2,1)S(1)}, bf16[288,1024]{1,0:T(8,128)(2,1)S(1)}, u32[]{:S(2)}, u32[]{:S(2)}) %collective-permute-start.10) | collective-permute-done | bytes 589856 | tf_op jit(solution)/shard_map/ppermute | solution.py:1412
  1003.1 6.6 fusion.3
  (229 shorter events, 104.8 us)
Async XLA Ops:
  0.6 35.8 %copy-start = (bf16[2304,512]{1,0:T(8,128)(2,1)S(1)}, bf16[2304,512]{1,0:T(8,128)(2,1)}, u32[]{:S(2)}) copy-start(bf16[2304,512]{1,0:T(8,128)(2,1)} %param.20) | copy-start | bytes 7077892
  0.7 30.6 %copy-start.17 = (bf16[1,128,2304]{2,1,0:T(8,128)(2,1)S(1)}, bf16[1,128,2304]{2,1,0:T(8,128)(2,1)}, u32[]{:S(2)}) copy-start(bf16[1,128,2304]{2,1,0:T(8,128)(2,1)} %param.31) | copy-start | bytes 1769476
  2.7 31.4 %copy-start.33 = (f32[2304]{0:T(1024)}, f32[2304]{0:T(1024)S(1)}, u32[]{:S(2)}) copy-start(f32[2304]{0:T(1024)S(1)} %get-tuple-element.138) | copy-start | bytes 27652
  33.4 7.7 copy-start.46
  36.4 2.7 copy-start.8
  41.1 4.7 copy-start.50
  166.8 5.3 copy-start.30
  174.4 9.6 copy-start.45
  174.4 5.1 copy-start.31
  179.5 4.5 copy-start.1
  179.5 4.5 copy-start.2
  179.5 4.5 copy-start.35
  197.5 3.0 copy-start.3
  516.8 12.5 %copy-start.54 = (bf16[1152,512]{1,0:T(8,128)(2,1)S(1)}, bf16[1152,512]{1,0:T(8,128)(2,1)}, u32[]{:S(2)}) copy-start(bf16[1152,512]{1,0:T(8,128)(2,1)} %get-tuple-element.58) | copy-start | bytes 3538948
  548.1 150.1 %collective-permute-start = (bf16[288,4608]{1,0:T(8,128)(2,1)}, bf16[288,4608]{1,0:T(8,128)(2,1)}, u32[]{:S(2)}, u32[]{:S(2)}) collective-permute-start(bf16[288,4608]{1,0:T(8,128)(2,1)} %get-tuple-element.150), channel_id=1, source_target_pairs={{0,8},{4,12},{1,9},{5,13},{2,10},{6,14},{3,11},{7,15}} | collective-permute-start | bytes 7962632 | tf_op jit(solution)/shard_map/ppermute | solution.py:1411
  575.4 122.9 %collective-permute-start.1 = (bf16[288,4608]{1,0:T(8,128)(2,1)}, bf16[288,4608]{1,0:T(8,128)(2,1)}, u32[]{:S(2)}, u32[]{:S(2)}) collective-permute-start(bf16[288,4608]{1,0:T(8,128)(2,1)} %get-tuple-element.149), channel_id=1, source_target_pairs={{28,20},{24,16},{29,21},{25,17},{30,22},{26,18},{31,23},{27,19}} | collective-permute-start | bytes 7962632 | tf_op jit(solution)/shard_map/ppermute | solution.py:1412
  584.9 5.9 copy-start.18
  586.5 4.4 copy-start.14
  586.5 4.3 copy-start.32
  586.5 4.3 copy-start.36
  586.5 4.3 copy-start.37
  586.6 4.3 copy-start.38
  590.9 4.4 copy-start.52
  599.1 17.1 %copy-start.9 = (bf16[1,128,2304]{2,1,0:T(8,128)(2,1)S(1)}, bf16[1,128,2304]{2,1,0:T(8,128)(2,1)}, u32[]{:S(2)}) copy-start(bf16[1,128,2304]{2,1,0:T(8,128)(2,1)} %param.16) | copy-start | bytes 1769476
  612.1 19.1 %collective-permute-start.11 = (bf16[512,576]{0,1:T(8,128)(2,1)}, bf16[512,576]{0,1:T(8,128)(2,1)}, u32[]{:S(2)}, u32[]{:S(2)}) collective-permute-start(bf16[512,576]{0,1:T(8,128)(2,1)} %copy.107), channel_id=1, source_target_pairs={{0,4},{4,0},{8,12},{12,8},{16,20},{20,16},{24,28},{28,24},{1,5},{5... | collective-permute-start | bytes 1769480 | tf_op jit(solution)/shard_map/ppermute | solution.py:1380
  619.3 8.5 copy-start.11
  627.8 2.5 copy-start.15
  637.2 6.6 copy-start.12
  642.3 3.9 copy-start.26
  642.3 3.9 copy-start.27
  642.3 3.9 copy-start.28
  642.4 8.1 collective-permute-start.12
  645.5 10.9 %collective-permute-start.15 = (bf16[256,576]{0,1:T(8,128)(2,1)S(1)}, bf16[256,576]{0,1:T(8,128)(2,1)S(1)}, u32[]{:S(2)}, u32[]{:S(2)}) collective-permute-start(bf16[256,576]{0,1:T(8,128)(2,1)S(1)} %bitcast.256), channel_id=1, source_target_pairs={{28,20},{24,16},{29,21},{25,17},{30,22},{26,18},{31,23},{27,19}} | collective-permute-start | bytes 884744 | tf_op jit(solution)/shard_map/ppermute | solution.py:1412
  651.3 40.5 %collective-permute-start.13 = (bf16[256,576]{0,1:T(8,128)(2,1)}, bf16[256,576]{0,1:T(8,128)(2,1)}, u32[]{:S(2)}, u32[]{:S(2)}) collective-permute-start(bf16[256,576]{0,1:T(8,128)(2,1)} %fusion.35), channel_id=1, source_target_pairs={{0,8},{4,12},{8,16},{12,20},{1,9},{5,13},{9,17},{13,21},{2,10},{6,... | collective-permute-start | bytes 884744 | tf_op jit(solution)/shard_map/ppermute | solution.py:1411
  657.2 37.8 %collective-permute-start.16 = (bf16[256,576]{0,1:T(8,128)(2,1)}, bf16[256,576]{0,1:T(8,128)(2,1)}, u32[]{:S(2)}, u32[]{:S(2)}) collective-permute-start(bf16[256,576]{0,1:T(8,128)(2,1)} %fusion.33), channel_id=1, source_target_pairs={{28,20},{24,16},{20,12},{16,8},{29,21},{25,17},{21,13},{17,9},{30,... | collective-permute-start | bytes 884744 | tf_op jit(solution)/shard_map/ppermute | solution.py:1412
  693.7 102.8 %collective-permute-start.14 = (bf16[256,576]{0,1:T(8,128)(2,1)}, bf16[256,576]{0,1:T(8,128)(2,1)S(1)}, u32[]{:S(2)}, u32[]{:S(2)}) collective-permute-start(bf16[256,576]{0,1:T(8,128)(2,1)} %fusion.36), channel_id=1, source_target_pairs={{0,8},{4,12},{8,16},{12,20},{16,24},{20,28},{1,9},{5,13},{9,17},{1... | collective-permute-start | bytes 884744 | tf_op jit(solution)/shard_map/ppermute | solution.py:1411
  697.0 99.6 %collective-permute-start.17 = (bf16[256,576]{0,1:T(8,128)(2,1)}, bf16[256,576]{0,1:T(8,128)(2,1)}, u32[]{:S(2)}, u32[]{:S(2)}) collective-permute-start(bf16[256,576]{0,1:T(8,128)(2,1)} %fusion.34), channel_id=1, source_target_pairs={{28,20},{24,16},{20,12},{16,8},{12,4},{8,0},{29,21},{25,17},{21,13... | collective-permute-start | bytes 884744 | tf_op jit(solution)/shard_map/ppermute | solution.py:1412
  765.3 17.0 %copy-start.13 = (bf16[4,1,288,512]{3,2,1,0:T(8,128)(2,1)S(1)}, bf16[4,1,288,512]{3,2,1,0:T(8,128)(2,1)}, u32[]{:S(2)}) copy-start(bf16[4,1,288,512]{3,2,1,0:T(8,128)(2,1)} %get-tuple-element.169) | copy-start | bytes 3538948
  765.3 26.1 %collective-permute-start.4 = (bf16[512,1024]{1,0:T(8,128)(2,1)S(1)}, bf16[512,1024]{1,0:T(8,128)(2,1)S(1)}, u32[]{:S(2)}, u32[]{:S(2)}) collective-permute-start(bf16[512,1024]{1,0:T(8,128)(2,1)S(1)} %pad_maximum_fusion.3), channel_id=1, source_target_pairs={{0,4},{4,0},{8,12},{12,8},{16,20},{20,16},{24,28},{28,24},{1,5},{5... | collective-permute-start | bytes 3145736 | tf_op jit(solution)/shard_map/ppermute | solution.py:1380
  775.6 110.9 %collective-permute-start.2 = (bf16[288,4608]{1,0:T(8,128)(2,1)}, bf16[288,4608]{1,0:T(8,128)(2,1)}, u32[]{:S(2)}, u32[]{:S(2)}) collective-permute-start(bf16[288,4608]{1,0:T(8,128)(2,1)} %get-tuple-element.148), channel_id=1, source_target_pairs={{0,8},{4,12},{8,16},{12,20},{1,9},{5,13},{9,17},{13,21},{2,10},{6,... | collective-permute-start | bytes 7962632 | tf_op jit(solution)/shard_map/ppermute | solution.py:1411
  780.1 106.4 %collective-permute-start.3 = (bf16[288,4608]{1,0:T(8,128)(2,1)}, bf16[288,4608]{1,0:T(8,128)(2,1)}, u32[]{:S(2)}, u32[]{:S(2)}) collective-permute-start(bf16[288,4608]{1,0:T(8,128)(2,1)} %get-tuple-element.147), channel_id=1, source_target_pairs={{28,20},{24,16},{20,12},{16,8},{29,21},{25,17},{21,13},{17,9},{30,... | collective-permute-start | bytes 7962632 | tf_op jit(solution)/shard_map/ppermute | solution.py:1412
  782.3 9.2 copy-start.22
  792.9 55.9 %copy-start.4 = (bf16[1152,1024]{1,0:T(8,128)(2,1)}, bf16[1152,1024]{1,0:T(8,128)(2,1)S(1)}, u32[]{:S(2)}) copy-start(bf16[1152,1024]{1,0:T(8,128)(2,1)S(1)} %fusion.12) | copy-start | bytes 7077892
  792.9 3.7 copy-start.16
  793.8 55.0 %collective-permute-start.5 = (bf16[288,1024]{1,0:T(8,128)(2,1)S(1)}, bf16[288,1024]{1,0:T(8,128)(2,1)S(1)}, u32[]{:S(2)}, u32[]{:S(2)}) collective-permute-start(bf16[288,1024]{1,0:T(8,128)(2,1)S(1)} %get-tuple-element.167), channel_id=1, source_target_pairs={{0,8},{4,12},{1,9},{5,13},{2,10},{6,14},{3,11},{7,15}} | collective-permute-start | bytes 1769480 | tf_op jit(solution)/shard_map/ppermute | solution.py:1411
  798.5 56.9 %copy-start.19 = (bf16[2304,512]{1,0:T(8,128)(2,1)S(1)}, bf16[2304,512]{1,0:T(8,128)(2,1)}, u32[]{:S(2)}) copy-start(bf16[2304,512]{1,0:T(8,128)(2,1)} %param.21) | copy-start | bytes 7077892
  799.9 79.9 %collective-permute-start.8 = (bf16[288,1024]{1,0:T(8,128)(2,1)}, bf16[288,1024]{1,0:T(8,128)(2,1)}, u32[]{:S(2)}, u32[]{:S(2)}) collective-permute-start(bf16[288,1024]{1,0:T(8,128)(2,1)} %get-tuple-element.168), channel_id=1, source_target_pairs={{28,20},{24,16},{29,21},{25,17},{30,22},{26,18},{31,23},{27,19}} | collective-permute-start | bytes 1769480 | tf_op jit(solution)/shard_map/ppermute | solution.py:1412
  849.9 29.9 %collective-permute-start.6 = (bf16[288,1024]{1,0:T(8,128)(2,1)}, bf16[288,1024]{1,0:T(8,128)(2,1)}, u32[]{:S(2)}, u32[]{:S(2)}) collective-permute-start(bf16[288,1024]{1,0:T(8,128)(2,1)} %fusion.29), channel_id=1, source_target_pairs={{0,8},{4,12},{8,16},{12,20},{1,9},{5,13},{9,17},{13,21},{2,10},{6,... | collective-permute-start | bytes 1769480 | tf_op jit(solution)/shard_map/ppermute | solution.py:1411
  858.3 18.6 %copy-start.44 = (f32[576]{0:T(1024)S(1)}, f32[576]{0:T(1024)}, u32[]{:S(2)}) copy-start(f32[576]{0:T(1024)} %get-tuple-element.139) | copy-start | bytes 6916
  876.8 9.7 copy-start.5
  876.9 9.7 copy-start.34
  878.4 8.2 copy-start.10
  878.4 8.2 copy-start.53
  879.8 7.7 copy-start.39
  879.8 7.7 copy-start.40
  879.8 7.7 copy-start.41
  882.9 53.6 %collective-permute-start.9 = (bf16[288,1024]{1,0:T(8,128)(2,1)}, bf16[288,1024]{1,0:T(8,128)(2,1)}, u32[]{:S(2)}, u32[]{:S(2)}) collective-permute-start(bf16[288,1024]{1,0:T(8,128)(2,1)} %get-tuple-element.166), channel_id=1, source_target_pairs={{28,20},{24,16},{20,12},{16,8},{29,21},{25,17},{21,13},{17,9},{30,... | collective-permute-start | bytes 1769480 | tf_op jit(solution)/shard_map/ppermute | solution.py:1412
  884.4 57.3 %collective-permute-start.7 = (bf16[288,1024]{1,0:T(8,128)(2,1)}, bf16[288,1024]{1,0:T(8,128)(2,1)}, u32[]{:S(2)}, u32[]{:S(2)}) collective-permute-start(bf16[288,1024]{1,0:T(8,128)(2,1)} %get-tuple-element.165), channel_id=1, source_target_pairs={{0,8},{4,12},{8,16},{12,20},{16,24},{20,28},{1,9},{5,13},{9,17},{1... | collective-permute-start | bytes 1769480 | tf_op jit(solution)/shard_map/ppermute | solution.py:1411
  913.1 14.5 %copy-start.43 = (f32[72,128]{1,0:T(8,128)S(1)}, f32[72,128]{1,0:T(8,128)}, u32[]{:S(2)}) copy-start(f32[72,128]{1,0:T(8,128)} %get-tuple-element.76) | copy-start | bytes 110596
  913.1 14.5 %copy-start.42 = (f32[2304]{0:T(1024)S(1)}, f32[2304]{0:T(1024)}, u32[]{:S(2)}) copy-start(f32[2304]{0:T(1024)} %reshape.412) | copy-start | bytes 27652
  920.9 82.2 %collective-permute-start.18 = (bf16[288,4608]{1,0:T(8,128)(2,1)}, bf16[288,4608]{1,0:T(8,128)(2,1)}, u32[]{:S(2)}, u32[]{:S(2)}) collective-permute-start(bf16[288,4608]{1,0:T(8,128)(2,1)} %get-tuple-element.145), channel_id=1, source_target_pairs={{0,8},{4,12},{8,16},{12,20},{16,24},{20,28},{1,9},{5,13},{9,17},{1... | collective-permute-start | bytes 7962632 | tf_op jit(solution)/shard_map/ppermute | solution.py:1411
  926.2 76.9 %collective-permute-start.19 = (bf16[288,4608]{1,0:T(8,128)(2,1)}, bf16[288,4608]{1,0:T(8,128)(2,1)}, u32[]{:S(2)}, u32[]{:S(2)}) collective-permute-start(bf16[288,4608]{1,0:T(8,128)(2,1)} %get-tuple-element.146), channel_id=1, source_target_pairs={{28,20},{24,16},{20,12},{16,8},{12,4},{8,0},{29,21},{25,17},{21,13... | collective-permute-start | bytes 7962632 | tf_op jit(solution)/shard_map/ppermute | solution.py:1412
  932.5 6.8 copy-start.7
  937.9 62.5 %collective-permute-start.10 = (bf16[288,1024]{1,0:T(8,128)(2,1)S(1)}, bf16[288,1024]{1,0:T(8,128)(2,1)S(1)}, u32[]{:S(2)}, u32[]{:S(2)}) collective-permute-start(bf16[288,1024]{1,0:T(8,128)(2,1)S(1)} %fusion.28), channel_id=1, source_target_pairs={{28,20},{24,16},{20,12},{16,8},{12,4},{8,0},{29,21},{25,17},{21,13... | collective-permute-start | bytes 1769480 | tf_op jit(solution)/shard_map/ppermute | solution.py:1412
  (11 other events, 15.6 us)

commit v3 on v2

--- a/solution.py
+++ b/solution.py
@@ -187,34 +187,6 @@
     )(value)
 
 
-def group_exchange_kernel(src, out, local, ss, rs):
-    seq, me, x, c = place_now()
-    peers = [(seq, lax.rem(me + d, GROUP)) for d in range(1, GROUP)]
-    greet(peers)
-    copies = []
-    for d in (2, 1, 3):
-        peer = peers[d - 1]
-        copy = remote(src.at[peer[1]], out.at[me], ss.at[d - 1], rs.at[d - 1], peer)
-        copy.start()
-        copies.append(copy)
-    own = pltpu.make_async_copy(src.at[me], out.at[me], local)
-    own.start()
-    for copy in copies:
-        copy.wait()
-    own.wait()
-
-
-def group_exchange(cid, value):
-    return comm_call(
-        group_exchange_kernel,
-        cid,
-        jax.ShapeDtypeStruct(value.shape, value.dtype),
-        [DMA, DMA((GROUP - 1,)), DMA((GROUP - 1,))],
-        [ANY],
-        ANY,
-    )(value)
-
-
 def keys_gather_kernel(n, heads, meta, cot, out, metas, cots, own_sem, hs, hr, ms, mr, rs, rr, ls, lr, ys, yr,
                        local, xs, xr, cs, cr, fs, fr):
     seq, me, x, c = place_now()
@@ -645,10 +617,7 @@
     )(query, pairs, own_meta, metas)
 
 
-def attend_back_kernel(n, q_ref, kv_ref, own_ref, meta_ref, mixed_ref, total_ref, grad_ref, dq_ref, dkv_ref):
-    keys = kv_ref[:, 0].reshape(n * 128, DH)
-    values = kv_ref[:, 1].reshape(n * 128, DH)
-    allowed = masks(n, own_ref, meta_ref)
+def back_pack(n, keys, values, allowed, q_ref, grad_ref, mixed_ref, total_ref, dq_ref, dkv_ref):
     grad_keys = None
     for h in range(2):
         cols = slice(h * DH, (h + 1) * DH)
@@ -681,28 +650,141 @@
     dkv_ref[:, 1] = grad_values.astype(BF16).reshape(n, 128, DH)
 
 
-def attend_back(n, query, pairs, own_meta, metas, mixed, total, grad):
-    rows = pl.BlockSpec((128, 2 * DH), lambda p: (p, 0))
-    heads = pl.BlockSpec((n, 2, 128, DH), lambda p: (0, 0, p, 0))
-    return pl.pallas_call(
-        functools.partial(attend_back_kernel, n),
-        grid=(GROUP,),
-        out_shape=[
-            jax.ShapeDtypeStruct(query.shape, F32),
-            jax.ShapeDtypeStruct(pairs.shape, BF16),
-        ],
-        in_specs=[
-            rows,
-            heads,
-            pl.BlockSpec((1, 8, 128), lambda p: (p, 0, 0)),
-            pl.BlockSpec((n, 1, 8, 128), lambda p: (0, p, 0, 0)),
-            rows,
-            pl.BlockSpec((128, 256), lambda p: (p, 0)),
-            rows,
-        ],
-        out_specs=[rows, heads],
-        compiler_params=pltpu.CompilerParams(vmem_limit_bytes=VMEM_LIMIT),
-    )(query, pairs, own_meta, metas, mixed, total, grad)
+class Chain:
+    def __init__(self, nz, count, seq, me, partial, keep, scratch):
+        self.nz, self.count, self.partial, self.keep = nz, count, partial, keep
+        self.z = seq // 2
+        self.right, self.left = (seq + 2, me), (seq - 2, me)
+        (self.out_r, self.out_l, self.got_r, self.got_l, self.stage, self.ss_r, self.sr_r, self.ss_l, self.sr_l,
+         self.keep_sem) = scratch
+
+    @staticmethod
+    def scratch(nz, count, rows, width):
+        hops = nz - 1
+        message = (rows, width)
+        sems = DMA((count, hops))
+        return [
+            pltpu.VMEM((hops,) + message, BF16), pltpu.VMEM((hops,) + message, BF16),
+            pltpu.VMEM((count, hops) + message, BF16), pltpu.VMEM((count, hops) + message, BF16),
+            pltpu.VMEM((2,) + message, F32), sems, sems, sems, sems, DMA((2,)),
+        ]
+
+    def copy_right(self, j, s, peer):
+        return remote(
+            self.out_r.at[s - 1], self.got_r.at[j, s - 1], self.ss_r.at[j, s - 1], self.sr_r.at[j, s - 1], peer
+        )
+
+    def copy_left(self, j, s, peer):
+        return remote(
+            self.out_l.at[s - 1], self.got_l.at[j, s - 1], self.ss_l.at[j, s - 1], self.sr_l.at[j, s - 1], peer
+        )
+
+    def step(self, j, s):
+        z, nz = self.z, self.nz
+
+        def one(go, copy, out, got, to, source, first):
+            @pl.when(j > 0)
+            def _():
+                copy(j - 1, s, to).wait_send()
+
+            total = self.partial(go, j)
+            more = (s > 1) & jnp.logical_not(first)
+
+            @pl.when(more)
+            def _():
+                copy(j, s - 1, source).wait_recv()
+                out[s - 1] = (total + got[j, s - 2].astype(F32)).astype(BF16)
+
+            @pl.when(jnp.logical_not(more))
+            def _():
+                out[s - 1] = total.astype(BF16)
+
+            copy(j, s, to).start()
+
+        go_right = z + nz - s
+        go_left = z - nz + s
+
+        @pl.when(go_right < nz)
+        def _():
+            one(go_right, self.copy_right, self.out_r, self.got_r, self.right, self.left, z == 0)
+
+        @pl.when(go_left >= 0)
+        def _():
+            one(go_left, self.copy_left, self.out_l, self.got_l, self.left, self.right, z == nz - 1)
+
+    def end(self, j):
+        z, nz = self.z, self.nz
+        k = j % 2
+
+        @pl.when(j >= 2)
+        def _():
+            self.keep(j - 2, self.stage.at[k], self.keep_sem.at[k]).wait()
+
+        self.stage[k] = self.partial(z, j)
+
+        @pl.when(z > 0)
+        def _():
+            self.copy_right(j, nz - 1, self.left).wait_recv()
+            self.stage[k] += self.got_r[j, nz - 2].astype(F32)
+
+        @pl.when(z < nz - 1)
+        def _():
+            self.copy_left(j, nz - 1, self.right).wait_recv()
+            self.stage[k] += self.got_l[j, nz - 2].astype(F32)
+
+        self.keep(j, self.stage.at[k], self.keep_sem.at[k]).start()
+
+    def run(self, first, last):
+        hops = self.nz - 1
+
+        def unit(u, carry):
+            j = u // hops
+            s = u % hops + 1
+            self.step(j, s)
+
+            @pl.when((s == hops) & (j > 0))
+            def _():
+                self.end(j - 1)
+
+            return carry
+
+        lax.fori_loop(first, last, unit, 0)
+
+    def units(self):
+        return self.count * (self.nz - 1)
+
+    def finish(self):
+        z, nz = self.z, self.nz
+        last = self.count - 1
+        self.end(jnp.int32(last))
+        for j in range(max(0, last - 1), last + 1):
+            self.keep(j, self.stage.at[j % 2], self.keep_sem.at[j % 2]).wait()
+        for s in range(1, nz):
+
+            @pl.when(z + nz - s < nz)
+            def _():
+                self.copy_right(last, s, self.right).wait_send()
+
+            @pl.when(z - nz + s >= 0)
+            def _():
+                self.copy_left(last, s, self.left).wait_send()
+
+
+def greet_all(seq, me, nz, others):
+    z = seq // 2
+    barrier = pltpu.get_barrier_semaphore()
+    for peer in others + [(seq + 1 - 2 * (seq % 2), me)]:
+        pl.semaphore_signal(barrier, inc=1, device_id=peer, device_id_type=MESH)
+
+    @pl.when(z > 0)
+    def _():
+        pl.semaphore_signal(barrier, inc=1, device_id=(seq - 2, me), device_id_type=MESH)
+
+    @pl.when(z < nz - 1)
+    def _():
+        pl.semaphore_signal(barrier, inc=1, device_id=(seq + 2, me), device_id_type=MESH)
+
+    pl.semaphore_wait(barrier, len(others) + 1 + jnp.where(z > 0, 1, 0) + jnp.where(z < nz - 1, 1, 0))
 
 
 def levels(code, step):
@@ -750,7 +832,7 @@
     def load_down(t, half):
         start = ((c + half) % 2 * tiles + t) * tw
         return pltpu.make_async_copy(
-            wd.at[pl.ds(pl.multiple_of(start, 128), tw)], dbuf.at[t % 2, half], dsem.at[t % 2, half]
+            wd.at[:, pl.ds(pl.multiple_of(start, 128), tw)], dbuf.at[t % 2, half], dsem.at[t % 2, half]
         )
 
     load_up(0).start()
@@ -827,7 +909,7 @@
             def level(span):
                 dlev[half, span, :] = levels(dbuf[t % 2, half, span, :], 64.0)
 
-            strips(tw // 128, 128, level)
+            strips(dlev.shape[1] // 64, 64, level)
 
         @pl.when(t + 2 < tiles)
         def _():
@@ -837,7 +919,7 @@
         to_core(t).wait_recv()
 
         def product(span):
-            acc[span, :] += dot(hid[c * tiles + t, span, :], dlev[0]) + dot(
+            acc[span, :] += contract_last(hid[c * tiles + t, span, :], dlev[0]) + contract_last(
                 hid[(1 - c) * tiles + t, span, :], dlev[1]
             )
 
@@ -965,7 +1047,7 @@
 def ffn_forward(cid, b, wgu, gs, wd, cots, g3, ds, riders):
     rows, deep = b.shape
     tiles, _, tw = gs.shape
-    part = wd.shape[1]
+    part = wd.shape[0]
     count = len(riders)
     lone = max(count, 1)
     return comm_call(
@@ -986,8 +1068,8 @@
             pltpu.VMEM((tiles, rows, tw), BF16),
             pltpu.VMEM((2, deep, tw), BF16),
             pltpu.VMEM((deep, tw), BF16),
-            pltpu.VMEM((2, 2, tw, part), BF16),
-            pltpu.VMEM((2, tw, part), BF16),
+            pltpu.VMEM((2, 2, part, tw), BF16),
+            pltpu.VMEM((2, part, tw), BF16),
             pltpu.VMEM((rows, part), F32),
             pltpu.VMEM((GROUP, rows, part), BF16),
             DMA((2,)), DMA((2, 2)), DMA((tiles,)), DMA((tiles,)), DMA((tiles,)), DMA((tiles,)), DMA((tiles,)),
@@ -1003,18 +1085,17 @@
     gf, wd, wgu, gs, gu, hid, hidy = refs[:7]
     dg_o, dgy_o, gsum_o, out, ddown_o = refs[7:12]
     (hh, hy, gfy, wbuf, wlev, dbuf, dlev, pair, co, cgot, near, sx, xgot, dg, acc, low, from_core, to_xb, from_x,
-     r_out, l_out, r_got, l_got,
-     hsem, wsem, dsem, psem, cs, cr, xs, xr, ys, yr, os, gys, gyr, ccs, ccr, cxs, cxr, rs, rr, ls, lr) = refs[12:]
+     hsem, wsem, dsem, psem, cs, cr, xs, xr, ys, yr, os, gys, gyr, ccs, ccr, cxs, cxr) = refs[12:48]
+    chain_refs = refs[48:]
     seq, me, x, c = place_now()
     y = seq % 2
     z = seq // 2
     across = (seq, (1 - x) * 2 + c)
     beside = (seq, x * 2 + 1 - c)
     beyond = (seq + 1 - 2 * y, me)
-    right = (seq + 2, me)
-    left = (seq - 2, me)
     rows, tw = dg.shape[1:]
-    deep = acc.shape[1]
+    part = acc.shape[2]
+    deep = GROUP * part
     per = hid.shape[0] // 4 if chained else 0
     ring = dg.shape[0]
 
@@ -1024,7 +1105,7 @@
     def load_down(t, half):
         start = ((c + half) % 2 * tiles + t) * tw
         return pltpu.make_async_copy(
-            wd.at[pl.ds(pl.multiple_of(start, 128), tw)], dbuf.at[t % 2, half], dsem.at[t % 2, half]
+            wd.at[:, pl.ds(pl.multiple_of(start, 128), tw)], dbuf.at[t % 2, half], dsem.at[t % 2, half]
         )
 
     def load_pair(t):
@@ -1040,24 +1121,12 @@
         load_hidy = pltpu.make_async_copy(hidy, hy, hsem.at[1])
         load_hid.start()
         load_hidy.start()
-    barrier = pltpu.get_barrier_semaphore()
-    for peer in (across, beside, beyond):
-        pl.semaphore_signal(barrier, inc=1, device_id=peer, device_id_type=MESH)
     if chained:
-
-        @pl.when(z > 0)
-        def _():
-            pl.semaphore_signal(barrier, inc=1, device_id=left, device_id_type=MESH)
-
-        @pl.when(z < nz - 1)
-        def _():
-            pl.semaphore_signal(barrier, inc=1, device_id=right, device_id_type=MESH)
-
-        pl.semaphore_wait(barrier, 3 + jnp.where(z > 0, 1, 0) + jnp.where(z < nz - 1, 1, 0))
+        greet_all(seq, me, nz, [across, beside])
         gf_swap = remote(gf, gfy, gys, gyr, beyond)
         gf_swap.start()
     else:
-        pl.semaphore_wait(barrier, 3)
+        greet([across, beside, beyond])
     acc[...] = jnp.zeros_like(acc)
 
     def to_core(t):
@@ -1082,7 +1151,7 @@
             def level(span):
                 dlev[half, span, :] = levels(dbuf[t % 2, half, span, :], 64.0)
 
-            strips(tw // 128, 128, level)
+            strips(dlev.shape[1] // 64, 64, level)
 
         @pl.when(t + 2 < tiles)
         def _():
@@ -1094,13 +1163,13 @@
             to_core(t - 2).wait_send()
 
         def product(span):
-            co[t % 2, span, :] = contract_last(gf[span, :], dlev[1]).astype(BF16)
+            co[t % 2, span, :] = dot(gf[span, :], dlev[1]).astype(BF16)
 
         strips(rows // 256, 256, product)
         to_core(t).start()
 
         def product_near(span):
-            near[t % 2, span, :] = contract_last(gf[span, :], dlev[0])
+            near[t % 2, span, :] = dot(gf[span, :], dlev[0])
 
         strips(rows // 256, 256, product_near)
 
@@ -1162,57 +1231,19 @@
             load_up(t + 2).start()
 
         def product(span):
-            acc[span, :] += contract_last(dg[t % ring, span, :], wlev[...])
+            for j in range(GROUP):
+                acc[j, span, :] += contract_last(dg[t % ring, span, :], wlev[j * part : (j + 1) * part, :])
 
         strips(rows // 128, 128, product)
 
-    def partial(k, j):
-        return contract_first(hh[k * per + j], gf[...]) + contract_first(hy[k * per + j], gfy[...])
-
-    def chain(j, s):
-        go_right = z + nz - s
-        go_left = z - nz + s
-
-        def one(go, got, out_buf, ss, sr, to, source, first):
-            @pl.when(j > 0)
-            def _():
-                remote(out_buf.at[s - 1], got.at[j - 1, s - 1], ss.at[j - 1, s - 1], sr.at[j - 1, s - 1], to).wait_send()
-
-            total = partial(go, j)
-            more = (s > 1) & jnp.logical_not(first)
-
-            @pl.when(more)
-            def _():
-                remote(out_buf.at[0], got.at[j, s - 2], ss.at[j, s - 2], sr.at[j, s - 2], source).wait_recv()
-                out_buf[s - 1] = (total + got[j, s - 2].astype(F32)).astype(BF16)
-
-            @pl.when(jnp.logical_not(more))
-            def _():
-                out_buf[s - 1] = total.astype(BF16)
-
-            remote(out_buf.at[s - 1], got.at[j, s - 1], ss.at[j, s - 1], sr.at[j, s - 1], to).start()
-
-        @pl.when(go_right < nz)
-        def _():
-            one(go_right, r_got, r_out, rs, rr, right, left, z == 0)
-
-        @pl.when(go_left >= 0)
-        def _():
-            one(go_left, l_got, l_out, ls, lr, left, right, z == nz - 1)
-
-    def chain_end(j):
-        ddown_o[j] = partial(z, j)
-
-        @pl.when(z > 0)
-        def _():
-            remote(r_out.at[0], r_got.at[j, nz - 2], rs.at[j, nz - 2], rr.at[j, nz - 2], left).wait_recv()
-            ddown_o[j] += r_got[j, nz - 2].astype(F32)
-
-        @pl.when(z < nz - 1)
-        def _():
-            remote(l_out.at[0], l_got.at[j, nz - 2], ls.at[j, nz - 2], lr.at[j, nz - 2], right).wait_recv()
-            ddown_o[j] += l_got[j, nz - 2].astype(F32)
-
+    if chained:
+
+        def partial(k, j):
+            return contract_first(hh[k * per + j], gf[...]) + contract_first(hy[k * per + j], gfy[...])
+
+        downs = Chain(
+            nz, per, seq, me, partial, lambda j, stage, sem: pltpu.make_async_copy(stage, ddown_o.at[j], sem), chain_refs
+        )
     hops = nz - 1
 
     def step(i, carry):
@@ -1234,7 +1265,7 @@
 
             @pl.when((i >= 1) & (i < 1 + per * hops))
             def _():
-                chain((i - 1) // hops, (i - 1) % hops + 1)
+                downs.run(i - 1, i)
 
         @pl.when(i >= 2)
         def _():
@@ -1244,6 +1275,531 @@
         return carry
 
     lax.fori_loop(0, tiles + 2, step, 0)
+
+    parts = 4
+    block = rows // GROUP
+    size = block // parts
+    order = [1 - x, x]
+    js = range(GROUP)
+    cores = []
+    for i in range(2):
+        for k in range(parts):
+            owner = order[i] * 2 + 1 - c
+            span = pl.ds(k * size, size)
+            for j in js:
+                low[i, j, span, :] = acc[j, pl.ds(pl.multiple_of(owner * block + k * size, 16), size), :].astype(BF16)
+            copy = remote(low.at[i, :, span], from_core.at[i, :, span], ccs.at[i, k], ccr.at[i, k], beside)
+            copy.start()
+            cores.append(copy)
+    sends = []
+    for k in range(parts):
+        span = pl.ds(k * size, size)
+        here = pl.ds(pl.multiple_of((order[0] * 2 + c) * block + k * size, 16), size)
+        cores[k].wait_recv()
+        for j in js:
+            to_xb[j, span, :] = (acc[j, here, :] + from_core[0, j, span, :].astype(F32)).astype(BF16)
+        copy = remote(to_xb.at[:, span], from_x.at[:, span], cxs.at[k], cxr.at[k], across)
+        copy.start()
+        sends.append(copy)
+    if chained:
+        downs.finish()
+    for k in range(parts):
+        span = pl.ds(k * size, size)
+        here = pl.ds(pl.multiple_of((order[1] * 2 + c) * block + k * size, 16), size)
+        cores[parts + k].wait_recv()
+        sends[k].wait_recv()
+        for j in js:
+            out[j, span, :] = acc[j, here, :] + from_core[1, j, span, :].astype(F32) + from_x[j, span, :].astype(F32)
+
+    for copy in cores + sends:
+        copy.wait_send()
+    for t in range(tiles - 2, tiles):
+        to_core(t).wait_send()
+    for t in range(tiles - 4, tiles):
+        to_x(t).wait_send()
+    for t in range(tiles - ring, tiles):
+        to_y(t).wait_send()
+        keep(t).wait()
+
+    def drain(t, carry):
+        to_y(t).wait_recv()
+        return carry
+
+    lax.fori_loop(0, tiles, drain, 0)
+    if chained:
+        gf_swap.wait_send()
+
+
+def ffn_backward(cid, n, gf, wd, wgu, gs, gu, hid, hidy):
+    rows, part = gf.shape
+    deep = wgu.shape[0]
+    tiles, _, tw = gs.shape
+    nz = n // 2
+    chained = nz == 4
+    per = tiles // nz if chained else 1
+    hops = nz - 1 if chained else 1
+    block = rows // GROUP
+    half = (tiles, rows, tw) if chained else (1, 16, 128)
+    message = (tw, part) if chained else (16, 128)
+    ring = 4
+    return comm_call(
+        functools.partial(ffn_backward_kernel, tiles, nz, chained),
+        cid,
+        [
+            jax.ShapeDtypeStruct((rows, tiles * tw), BF16),
+            jax.ShapeDtypeStruct((rows, tiles * tw), BF16),
+            jax.ShapeDtypeStruct((tiles, 8, tw), F32),
+            jax.ShapeDtypeStruct((GROUP, block, part), F32),
+            jax.ShapeDtypeStruct((per,) + message, F32),
+        ],
+        [
+            pltpu.VMEM(half, BF16),
+            pltpu.VMEM(half, BF16),
+            pltpu.VMEM((rows, part), BF16),
+            pltpu.VMEM((2, deep, tw), BF16),
+            pltpu.VMEM((deep, tw), BF16),
+            pltpu.VMEM((2, 2, part, tw), BF16),
+            pltpu.VMEM((2, part, tw), BF16),
+            pltpu.VMEM((2, 2, rows, tw), BF16),
+            pltpu.VMEM((2, rows, tw), BF16),
+            pltpu.VMEM((tiles, rows, tw), BF16),
+            pltpu.VMEM((2, rows, tw), F32),
+            pltpu.VMEM((4, rows, tw), BF16),
+            pltpu.VMEM((tiles, rows, tw), BF16),
+            pltpu.VMEM((ring, rows, tw), BF16),
+            pltpu.VMEM((GROUP, rows, part), F32),
+            pltpu.VMEM((2, GROUP, block, part), BF16),
+            pltpu.VMEM((2, GROUP, block, part), BF16),
+            pltpu.VMEM((GROUP, block, part), BF16),
+            pltpu.VMEM((GROUP, block, part), BF16),
+            DMA((2,)), DMA((2,)), DMA((2, 2)), DMA((2,)), DMA((tiles,)), DMA((tiles,)), DMA((tiles,)), DMA((tiles,)),
+            DMA((tiles,)), DMA((tiles,)), DMA((tiles,)), DMA, DMA, DMA((2, 4)), DMA((2, 4)), DMA((4,)), DMA((4,)),
+        ]
+        + (Chain.scratch(nz, per, *message) if chained else []),
+        [VMEM, ANY, ANY, VMEM, ANY, ANY, ANY],
+        [ANY, ANY, VMEM, VMEM, ANY],
+    )(gf, wd, wgu, gs, gu, hid, hidy)
+
+
+def gate_chain(nz, first, count, seq, me, bt, bty, dg, dgy, out, slabs, slab_sem, scratch):
+    size = bt.shape[0] // nz
+    loads = []
+    for i, ref in enumerate((dg, dgy)):
+        copy = pltpu.make_async_copy(ref.at[:, pl.ds(first * TILE, count * TILE)], slabs.at[i], slab_sem.at[i])
+        copy.start()
+        loads.append(copy)
+
+    def partial(k, j):
+        rows = pl.ds(pl.multiple_of(k * size, 16), size)
+        cols = pl.ds(pl.multiple_of(j * TILE, 128), TILE)
+        return dot(bt[rows, :], slabs[0, :, cols]) + dot(bty[rows, :], slabs[1, :, cols])
+
+    def keep(j, stage, sem):
+        return pltpu.make_async_copy(stage, out.at[:, pl.ds(pl.multiple_of(j * TILE, 128), TILE)], sem)
+
+    return Chain(nz, count, seq, me, partial, keep, scratch), loads
+
+
+def gate_scratch(nz, count, bt):
+    rows = bt.shape[1]
+    return [pltpu.VMEM((2, rows, count * TILE), BF16), DMA((2,))] + Chain.scratch(
+        nz, count, bt.shape[0] // nz, TILE
+    )
+
+
+def branch_back_kernel(n, tiles, *refs):
+    (gsi, mid, raw, cot, g2, g3, scale, wo, q, mixed, mass, own_meta, metas, kv, bt, bty, dg, dgy) = refs[:18]
+    dmid, sums, gy, gyy, dq, dkv, gate_o = refs[18:25]
+    (low, gys, gy_all, part, from_core, to_x, from_x, grad, kvs, dkvs, es, er, el, cs, cr, xs, xr, ks, ds, yss, ysr,
+     ows) = refs[25:47]
+    rest = refs[47:]
+    seq, me, x, c = place_now()
+    nz = n // 2
+    across = (seq, (1 - x) * 2 + c)
+    beside = (seq, x * 2 + 1 - c)
+    beyond = (seq + 1 - 2 * (seq % 2), me)
+    peers = [(seq, lax.rem(me + d, GROUP)) for d in range(1, GROUP)]
+    chain = None
+    if tiles:
+        chain, loads = gate_chain(nz, 0, tiles, seq, me, bt, bty, dg, dgy, gate_o, rest[0], rest[1], rest[2:])
+        greet_all(seq, me, nz, peers)
+    else:
+        greet(peers + [beyond])
+    width = GROUP * raw.shape[2]
+    mean = 1.0 / width
+    sums[...] = jnp.zeros_like(sums)
+    js = range(GROUP)
+
+    def rowsum(values):
+        total = values[0]
+        for value in values[1:]:
+            total = total + value
+        return jnp.sum(total, axis=1, keepdims=True) * mean
+
+    def norms(span):
+        middle = [mid[j, span, :] for j in js]
+        up = [gsi[j, span, :] for j in js]
+        inverse = lax.rsqrt(rowsum([v * v for v in middle]) + EPSILON)
+        third = [v * inverse for v in middle]
+        scaled = [up[j] * g3[j] for j in js]
+        cross = rowsum([scaled[j] * third[j] for j in js])
+        grad_middle = [
+            cot[j, span, :].astype(F32) + inverse * (scaled[j] - third[j] * cross) for j in js
+        ]
+        plain = [raw[j, span, :].astype(F32) for j in js]
+        branch = [plain[j] * scale[j] for j in js]
+        inverse = lax.rsqrt(rowsum([v * v for v in branch]) + EPSILON)
+        second = [v * inverse for v in branch]
+        scaled = [grad_middle[j] * g2[j] for j in js]
+        cross = rowsum([scaled[j] * second[j] for j in js])
+        for j in js:
+            full = inverse * (scaled[j] - second[j] * cross)
+            gys[j, span, :] = (full * scale[j]).astype(BF16)
+            dmid[j, span, :] = grad_middle[j]
+            sums[j, 0:1, :] += jnp.sum(grad_middle[j] * second[j], axis=0, keepdims=True)
+            sums[j, 1:2, :] += jnp.sum(up[j] * third[j], axis=0, keepdims=True)
+            sums[j, 2:3, :] += jnp.sum(plain[j] * full, axis=0, keepdims=True)
+
+    strips(raw.shape[1] // 16, 16, norms)
+
+    copies = []
+    for d in (2, 1, 3):
+        peer = peers[d - 1]
+        copy = remote(gys.at[peer[1]], gy_all.at[me], es.at[d - 1], er.at[d - 1], peer)
+        copy.start()
+        copies.append(copy)
+    own = pltpu.make_async_copy(gys.at[me], gy_all.at[me], el)
+    own.start()
+    for p in range(2):
+        pltpu.make_async_copy(kv.at[:, :, pl.ds(p * 128, 128)], kvs.at[p], ks.at[p]).start()
+    units = chain.units() if chain else 0
+    at = [0]
+
+    def beside_work(count):
+        if chain:
+            last = min(units, at[0] + count)
+            chain.run(at[0], last)
+            at[0] = last
+
+    if chain:
+        for load in loads:
+            load.wait()
+    beside_work(3)
+    for copy in copies:
+        copy.wait_recv()
+    own.wait()
+    gy_out = pltpu.make_async_copy(gy_all, gy, ows)
+    gy_out.start()
+    swap = remote(gy_all, gyy, yss, ysr, beyond)
+    swap.start()
+
+    heads = part.shape[3]
+    rows = part.shape[2]
+    order = [1 - x, x]
+
+    def product(i, k, to):
+        grad_branch = gy_all[...].reshape(rows, raw.shape[2])
+        start = (order[i] * 2 + k) * heads
+        to[...] = dot(grad_branch, wo[:, pl.ds(pl.multiple_of(start, 128), heads)]).astype(BF16)
+
+    cores = []
+    for i in range(2):
+        product(i, 1 - c, part.at[i, 0])
+        copy = remote(part.at[i, 0], from_core.at[i], cs.at[i], cr.at[i], beside)
+        copy.start()
+        cores.append(copy)
+    for i in range(2):
+        product(i, c, part.at[i, 1])
+    cores[0].wait_recv()
+
+    def add_core(span):
+        to_x[span, :] = (part[0, 1, span, :].astype(F32) + from_core[0, span, :].astype(F32)).astype(BF16)
+
+    strips(rows // 64, 64, add_core)
+    over = remote(to_x, from_x, xs, xr, across)
+    over.start()
+    beside_work(4)
+    cores[1].wait_recv()
+    over.wait_recv()
+
+    def add_all(span):
+        grad[span, :] = (
+            part[1, 1, span, :].astype(F32) + from_core[1, span, :].astype(F32) + from_x[span, :].astype(F32)
+        ).astype(BF16)
+
+    strips(rows // 64, 64, add_all)
+
+    def load_pack(p):
+        return pltpu.make_async_copy(
+            kv.at[:, :, pl.ds(pl.multiple_of(p * 128, 128), 128)], kvs.at[p % 2], ks.at[p % 2]
+        )
+
+    def store_pack(p):
+        return pltpu.make_async_copy(
+            dkvs.at[p % 2], dkv.at[:, :, pl.ds(pl.multiple_of(p * 128, 128), 128)], ds.at[p % 2]
+        )
+
+    base = at[0]
+    each = max(0, units - base) // GROUP
+
+    def one_pack(p, carry):
+        load_pack(p).wait()
+
+        @pl.when(p >= 2)
+        def _():
+            store_pack(p - 2).wait()
+
+        span = pl.ds(pl.multiple_of(p * 128, 128), 128)
+        keys = kvs[p % 2, :, 0].reshape(n * 128, DH)
+        values = kvs[p % 2, :, 1].reshape(n * 128, DH)
+        allowed = masks(n, own_meta.at[pl.ds(p, 1)], metas.at[:, pl.ds(p, 1)])
+        back_pack(
+            n, keys, values, allowed, q.at[span], grad.at[span], mixed.at[span], mass.at[span], dq.at[span],
+            dkvs.at[p % 2],
+        )
+        store_pack(p).start()
+
+        @pl.when(p + 2 < GROUP)
+        def _():
+            load_pack(p + 2).start()
+
+        if each:
+            chain.run(base + p * each, base + (p + 1) * each)
+        return carry
+
+    lax.fori_loop(0, GROUP, one_pack, 0)
+    at[0] = base + GROUP * each
+    beside_work(units)
+    if chain:
+        chain.finish()
+    for copy in copies + cores + [over]:
+        copy.wait_send()
+    store_pack(2).wait()
+    store_pack(3).wait()
+    swap.wait()
+    gy_out.wait()
+
+
+def branch_back(cid, n, tiles, gsi, mid, raw, cot, g2, g3, scale, wo, q, mixed, mass, own_meta, metas, kv, pairs):
+    bt, bty, dg, dgy = pairs
+    own, part = raw.shape[1:]
+    rows = q.shape[0]
+    heads = q.shape[1]
+    block = lambda kind: jax.ShapeDtypeStruct((GROUP, own, part), kind)
+    gate_rows = bt.shape[0] // (n // 2)
+    pack = (2, n, 2, own, DH)
+    return comm_call(
+        functools.partial(branch_back_kernel, n, tiles),
+        cid,
+        [
+            block(F32),
+            jax.ShapeDtypeStruct((GROUP, 8, part), F32),
+            block(BF16),
+            block(BF16),
+            jax.ShapeDtypeStruct(q.shape, F32),
+            jax.ShapeDtypeStruct(kv.shape, BF16),
+            jax.ShapeDtypeStruct((gate_rows, max(tiles, 1) * TILE), F32),
+        ],
+        [
+            pltpu.VMEM((8, 128), BF16),
+            pltpu.VMEM((GROUP, own, part), BF16),
+            pltpu.VMEM((GROUP, own, part), BF16),
+            pltpu.VMEM((2, 2, rows, heads), BF16),
+            pltpu.VMEM((2, rows, heads), BF16),
+            pltpu.VMEM((rows, heads), BF16),
+            pltpu.VMEM((rows, heads), BF16),
+            pltpu.VMEM((rows, heads), BF16),
+            pltpu.VMEM(pack, BF16),
+            pltpu.VMEM(pack, BF16),
+            DMA((3,)), DMA((3,)), DMA, DMA((2,)), DMA((2,)), DMA, DMA, DMA((2,)), DMA((2,)), DMA, DMA, DMA,
+        ]
+        + (gate_scratch(n // 2, tiles, bt) if tiles else []),
+        [VMEM] * 13 + [ANY] + [VMEM] * 2 + [ANY] * 2,
+        [VMEM, VMEM, ANY, ANY, VMEM, ANY, ANY],
+    )(gsi, mid, raw, cot, g2, g3, scale, wo, q, mixed, mass, own_meta, metas, kv, bt, bty, dg, dgy)
+
+
+def keys_back_kernel(n, first, tiles, *refs):
+    (src, dq, q_raw, p_raw, cosine, sine, q_scale, p_scale, wq, wkv, bt, bty, dg, dgy) = refs[:14]
+    joined, joined_y, out, sums, gate_o = refs[14:19]
+    (y_got, r_got, l_got, r_out, l_out, moved, back, acc, low, from_core, to_xb, from_x,
+     ys, yr, rs, rr, ls, lr, hs, hr, local, jys, jyr, ccs, ccr, cxs, cxr) = refs[19:46]
+    slabs, slab_sem, *rest = refs[46:]
+    seq, me, x, c = place_now()
+    y = seq % 2
+    z = seq // 2
+    nz = n // 2
+    right = (seq + 2, me)
+    left = (seq - 2, me)
+    beyond = (z * 2 + 1 - y, me)
+    across = (seq, (1 - x) * 2 + c)
+    beside = (seq, x * 2 + 1 - c)
+    chain, loads = gate_chain(nz, first, tiles, seq, me, bt, bty, dg, dgy, gate_o, slabs, slab_sem, rest)
+    greet_all(seq, me, nz, [(seq, lax.rem(me + d, GROUP)) for d in range(1, GROUP)])
+    rows, width = dq.shape
+    deep = acc.shape[1]
+    half = DH // 2
+
+    def swap(k):
+        return remote(src.at[k * 2 + 1 - y], y_got.at[k], ys.at[k], yr.at[k], beyond)
+
+    for t in range(1, nz):
+        go_right = z + nz - t
+        go_left = z - nz + t
+
+        @pl.when(go_right < nz)
+        def _():
+            swap(go_right).start()
+
+        @pl.when(go_left >= 0)
+        def _():
+            swap(go_left).start()
+
+    swap(z).start()
+    sums[...] = jnp.zeros_like(sums)
+
+    def turn_queries(span):
+        cos = cosine[span, :]
+        sin = sine[span, :]
+        for h in range(2):
+            a = slice(h * DH, h * DH + half)
+            b = slice(h * DH + half, (h + 1) * DH)
+            one = dq[span, a]
+            two = dq[span, b]
+            for cols, full in ((a, one * cos + two * sin), (b, two * cos - one * sin)):
+                sums[0:1, cols] += jnp.sum(q_raw[span, cols] * full, axis=0, keepdims=True)
+                joined[span, cols] = (full * q_scale[:, cols]).astype(BF16)
+
+    strips(rows // 64, 64, turn_queries)
+
+    def query_part(span):
+        acc[span, :] = contract_last(joined[span, :width], wq[...])
+
+    strips(rows // 128, 128, query_part)
+
+    def pair_sum(k, more, to):
+        def body(i, carry):
+            part = i // 4
+            span = pl.ds(pl.multiple_of((i % 4) * 128, 128), 128)
+            total = src[k * 2 + y, part, span, :].astype(F32) + y_got[k, part, span, :].astype(F32)
+            for ref in more:
+                total = total + ref[part, span, :].astype(F32)
+            to[part, span, :] = total.astype(BF16)
+            return carry
+
+        lax.fori_loop(0, 8, body, 0)
+
+    for load in loads:
+        load.wait()
+    units = chain.units()
+    at = [0]
+
+    def beside_work(count):
+        last = min(units, at[0] + count)
+        chain.run(at[0], last)
+        at[0] = last
+
+    for t in range(1, nz):
+        go_right = z + nz - t
+        go_left = z - nz + t
+
+        def hop(go, at_end, got, send, ss, sr, to, source):
+            swap(go).wait_recv()
+            if t == 1:
+                pair_sum(go, [], send.at[t - 1])
+            else:
+
+                @pl.when(jnp.logical_not(at_end))
+                def _():
+                    remote(send.at[t - 1], got.at[t - 2], ss.at[t - 2], sr.at[t - 2], source).wait_recv()
+                    pair_sum(go, [got.at[t - 2]], send.at[t - 1])
+
+                @pl.when(at_end)
+                def _():
+                    pair_sum(go, [], send.at[t - 1])
+
+            remote(send.at[t - 1], got.at[t - 1], ss.at[t - 1], sr.at[t - 1], to).start()
+
+        @pl.when(go_right < nz)
+        def _():
+            hop(go_right, z == 0, r_got, r_out, rs, rr, right, left)
+
+        @pl.when(go_left >= 0)
+        def _():
+            hop(go_left, z == nz - 1, l_got, l_out, ls, lr, left, right)
+
+        beside_work(1)
+
+    swap(z).wait_recv()
+    last = nz - 2
+
+    def got_left():
+        remote(r_out.at[last], r_got.at[last], rs.at[last], rr.at[last], left).wait_recv()
+
+    def got_right():
+        remote(l_out.at[last], l_got.at[last], ls.at[last], lr.at[last], right).wait_recv()
+
+    @pl.when(z == 0)
+    def _():
+        got_right()
+        pair_sum(z, [l_got.at[last]], moved)
+
+    @pl.when(z == nz - 1)
+    def _():
+        got_left()
+        pair_sum(z, [r_got.at[last]], moved)
+
+    @pl.when((z > 0) & (z < nz - 1))
+    def _():
+        got_left()
+        got_right()
+        pair_sum(z, [r_got.at[last], l_got.at[last]], moved)
+
+    for t in range(2):
+        target = t * 2 + x
+
+        @pl.when(target == me)
+        def _():
+            pltpu.make_async_copy(moved.at[t], back.at[c], local).start()
+
+        @pl.when(target != me)
+        def _():
+            remote(moved.at[t], back.at[c], hs.at[t], hr.at[c], (seq, target)).start()
+
+    beside_work(1)
+    for j in range(2):
+        source = c * 2 + j
+
+        @pl.when(source == me)
+        def _():
+            pltpu.make_async_copy(moved.at[0], back.at[j], local).wait()
+
+        @pl.when(source != me)
+        def _():
+            remote(moved.at[0], back.at[j], hs.at[0], hr.at[j], (seq, source)).wait_recv()
+
+    is_key = jnp.where(x == 0, 1.0, 0.0).astype(F32)
+
+    def turn_pairs(span):
+        cos = is_key * cosine[span, :] + (1.0 - is_key)
+        sin = is_key * sine[span, :]
+        for h in range(2):
+            a = slice(h * DH, h * DH + half)
+            b = slice(h * DH + half, (h + 1) * DH)
+            one = back[h, span, :half].astype(F32)
+            two = back[h, span, half:].astype(F32)
+            for cols, full in ((a, one * cos + two * sin), (b, two * cos - one * sin)):
+                sums[1:2, cols] += jnp.sum(p_raw[span, cols] * full, axis=0, keepdims=True)
+                joined[span, width + cols.start : width + cols.stop] = (full * p_scale[:, cols]).astype(BF16)
+
+    strips(rows // 64, 64, turn_pairs)
+    joined_swap = remote(joined, joined_y, jys, jyr, beyond)
+    joined_swap.start()
+
+    def pair_part(span):
+        acc[span, :] += contract_last(joined[span, width:], wkv[...])
+
+    strips(rows // 128, 128, pair_part)
 
     parts = 4
     block = rows // GROUP
@@ -1267,9 +1823,8 @@
         copy = remote(to_xb.at[span], from_x.at[span], cxs.at[k], cxr.at[k], across)
         copy.start()
         sends.append(copy)
-    if chained:
-        for j in range(per):
-            chain_end(j)
+    beside_work(units)
+    chain.finish()
     for k in range(parts):
         span = pl.ds(k * size, size)
         here = pl.ds(pl.multiple_of((order[1] * 2 + c) * block + k * size, 16), size)
@@ -1277,88 +1832,186 @@
         sends[k].wait_recv()
         out[span, :] = acc[here, :] + from_core[1, span, :].astype(F32) + from_x[span, :].astype(F32)
 
+    for t in range(2):
+
+        @pl.when(t * 2 + x != me)
+        def _():
+            remote(moved.at[t], back.at[c], hs.at[t], hr.at[c], (seq, t * 2 + x)).wait_send()
+
+    for k in range(nz):
+        swap(k).wait_send()
+    for t in range(1, nz):
+
+        @pl.when(z + nz - t < nz)
+        def _():
+            remote(r_out.at[t - 1], r_got.at[t - 1], rs.at[t - 1], rr.at[t - 1], right).wait_send()
+
+        @pl.when(z - nz + t >= 0)
+        def _():
+            remote(l_out.at[t - 1], l_got.at[t - 1], ls.at[t - 1], lr.at[t - 1], left).wait_send()
+
     for copy in cores + sends:
         copy.wait_send()
-    for t in range(tiles - 2, tiles):
-        to_core(t).wait_send()
-    for t in range(tiles - 4, tiles):
-        to_x(t).wait_send()
-    for t in range(tiles - ring, tiles):
-        to_y(t).wait_send()
-        keep(t).wait()
-
-    def drain(t, carry):
-        to_y(t).wait_recv()
-        return carry
-
-    lax.fori_loop(0, tiles, drain, 0)
-    if chained:
-        gf_swap.wait_send()
-        j = per - 1
-        for s in range(1, nz):
-
-            @pl.when(z + nz - s < nz)
-            def _():
-                remote(r_out.at[s - 1], r_got.at[j, s - 1], rs.at[j, s - 1], rr.at[j, s - 1], right).wait_send()
-
-            @pl.when(z - nz + s >= 0)
-            def _():
-                remote(l_out.at[s - 1], l_got.at[j, s - 1], ls.at[j, s - 1], lr.at[j, s - 1], left).wait_send()
-
-
-def ffn_backward(cid, n, gf, wd, wgu, gs, gu, hid, hidy):
-    rows, part = gf.shape
-    deep = wgu.shape[0]
-    tiles, _, tw = gs.shape
+    joined_swap.wait()
+
+
+def keys_back(cid, n, first, tiles, src, dq, q_raw, p_raw, cosine, sine, q_scale, p_scale, wq, wkv, pairs):
+    bt, bty, dg, dgy = pairs
     nz = n // 2
-    chained = nz == 4
-    per = tiles // nz if chained else 1
-    hops = nz - 1 if chained else 1
+    rows, width = dq.shape
+    deep = wq.shape[0]
     block = rows // GROUP
-    half = (tiles, rows, tw) if chained else (1, 16, 128)
-    message = (tw, part) if chained else (16, 128)
-    ring = 4
+    shape = src.shape[1:]
+    chain = pltpu.VMEM((nz - 1,) + shape, BF16)
+    joined = jax.ShapeDtypeStruct((rows, 2 * width), BF16)
     return comm_call(
-        functools.partial(ffn_backward_kernel, tiles, nz, chained),
+        functools.partial(keys_back_kernel, n, first, tiles),
         cid,
         [
-            jax.ShapeDtypeStruct((rows, tiles * tw), BF16),
-            jax.ShapeDtypeStruct((rows, tiles * tw), BF16),
-            jax.ShapeDtypeStruct((tiles, 8, tw), F32),
+            joined,
+            joined,
             jax.ShapeDtypeStruct((block, deep), F32),
-            jax.ShapeDtypeStruct((per,) + message, F32),
+            jax.ShapeDtypeStruct((8, width), F32),
+            jax.ShapeDtypeStruct((bt.shape[0] // nz, tiles * TILE), F32),
         ],
         [
-            pltpu.VMEM(half, BF16),
-            pltpu.VMEM(half, BF16),
-            pltpu.VMEM((rows, part), BF16),
-            pltpu.VMEM((2, deep, tw), BF16),
-            pltpu.VMEM((deep, tw), BF16),
-            pltpu.VMEM((2, 2, tw, part), BF16),
-            pltpu.VMEM((2, tw, part), BF16),
-            pltpu.VMEM((2, 2, rows, tw), BF16),
-            pltpu.VMEM((2, rows, tw), BF16),
-            pltpu.VMEM((tiles, rows, tw), BF16),
-            pltpu.VMEM((2, rows, tw), F32),
-            pltpu.VMEM((4, rows, tw), BF16),
-            pltpu.VMEM((tiles, rows, tw), BF16),
-            pltpu.VMEM((ring, rows, tw), BF16),
+            pltpu.VMEM((nz,) + shape, BF16), chain, chain, chain, chain, pltpu.VMEM(shape, BF16), pltpu.VMEM(shape, BF16),
             pltpu.VMEM((rows, deep), F32),
             pltpu.VMEM((2, block, deep), BF16),
             pltpu.VMEM((2, block, deep), BF16),
             pltpu.VMEM((block, deep), BF16),
             pltpu.VMEM((block, deep), BF16),
-            pltpu.VMEM((hops,) + message, BF16),
-            pltpu.VMEM((hops,) + message, BF16),
-            pltpu.VMEM((per, hops) + message, BF16),
-            pltpu.VMEM((per, hops) + message, BF16),
-            DMA((2,)), DMA((2,)), DMA((2, 2)), DMA((2,)), DMA((tiles,)), DMA((tiles,)), DMA((tiles,)), DMA((tiles,)),
-            DMA((tiles,)), DMA((tiles,)), DMA((tiles,)), DMA, DMA, DMA((2, 4)), DMA((2, 4)), DMA((4,)), DMA((4,)),
-            DMA((per, hops)), DMA((per, hops)), DMA((per, hops)), DMA((per, hops)),
+            DMA((nz,)), DMA((nz,)), DMA((nz - 1,)), DMA((nz - 1,)), DMA((nz - 1,)), DMA((nz - 1,)),
+            DMA((2,)), DMA((2,)), DMA, DMA, DMA, DMA((2, 4)), DMA((2, 4)), DMA((4,)), DMA((4,)),
+        ]
+        + gate_scratch(nz, tiles, bt),
+        [VMEM] * 12 + [ANY] * 2,
+        [VMEM, ANY, VMEM, VMEM, ANY],
+    )(src, dq, q_raw, p_raw, cosine, sine, q_scale, p_scale, wq, wkv, bt, bty, dg, dgy)
+
+
+def finish_kernel(n, rounds, first, tiles, *refs):
+    (whole, part, bt, bty, dg, dgy, ot, oty, gy, gyy, at, aty, joined, joined_y) = refs[:14]
+    whole_out, part_out, gate_o, output_o, attention_o = refs[14:19]
+    bufs, gots, mine, theirs, ss, rs = refs[19:25]
+    slabs, slab_sem = refs[25:27]
+    gate_refs, output_refs, attention_refs = refs[27:37], refs[37:47], refs[47:57]
+    seq, me, x, c = place_now()
+    nz = n // 2
+    across = (seq, (1 - x) * 2 + c)
+    beside = (seq, x * 2 + 1 - c)
+    gates, loads = gate_chain(nz, first, tiles, seq, me, bt, bty, dg, dgy, gate_o, slabs, slab_sem, gate_refs)
+    output_rows = ot.shape[0] // nz
+    attention_rows = at.shape[0] // nz
+    wide = joined.shape[1] // 2
+
+    def output_partial(k, j):
+        rows = pl.ds(pl.multiple_of(k * output_rows, 16), output_rows)
+        return dot(ot[rows, :], gy[...]) + dot(oty[rows, :], gyy[...])
+
+    def attention_partial(k, j):
+        rows = pl.ds(pl.multiple_of(k * attention_rows, 16), attention_rows)
+        cols = pl.ds(pl.multiple_of(j * wide, 128), wide)
+        return dot(at[rows, :], joined[:, cols]) + dot(aty[rows, :], joined_y[:, cols])
+
+    outputs = Chain(
+        nz, 1, seq, me, output_partial, lambda j, stage, sem: pltpu.make_async_copy(stage, output_o, sem), output_refs
+    )
+    attentions = Chain(
+        nz,
+        2,
+        seq,
+        me,
+        attention_partial,
+        lambda j, stage, sem: pltpu.make_async_copy(
+            stage, attention_o.at[:, pl.ds(pl.multiple_of(j * wide, 128), wide)], sem
+        ),
+        attention_refs,
+    )
+    partners = []
+    for r in range(rounds):
+        bit = 1 << r
+        partners.append((seq + bit - 2 * bit * ((seq // bit) % 2), me))
+    greet([(lax.rem(seq + d, n), me) for d in range(1, n)] + [across, beside])
+    for load in loads:
+        load.wait()
+    rows = whole.shape[0]
+    bufs[0, :rows, :] = whole[...]
+    bufs[0, rows:, :] = part[...]
+    work = [(gates, u) for u in range(0, gates.units(), 3)]
+    work += [(outputs, 0), (attentions, 0), (attentions, 3)]
+    at_work = [0]
+
+    def beside_work(count):
+        todo = work[at_work[0] : at_work[0] + count]
+        at_work[0] += count
+        start = None
+        for i, (chain, u) in enumerate(todo):
+            if start is None:
+                start = u
+            if i + 1 == len(todo) or todo[i + 1][0] is not chain:
+                chain.run(start, u + 3)
+                start = None
+
+    for r in range(rounds + 1):
+        partner = partners[r] if r < rounds else across
+        copy = remote(bufs.at[r], gots.at[r], ss.at[r], rs.at[r], partner)
+        copy.start()
+        beside_work(1)
+        copy.wait()
+        if r < rounds:
+            bufs[r + 1] = bufs[r] + gots[r]
+    mine[0, :rows, :] = bufs[rounds, :rows, :] + gots[rounds, :rows, :]
+    mine[0, rows:, :] = bufs[rounds, rows:, :]
+    mine[1, rows:, :] = gots[rounds, rows:, :]
+    mine[1, :rows, :] = jnp.zeros((rows, 128), F32)
+    copy = remote(mine, theirs, ss.at[rounds + 1], rs.at[rounds + 1], beside)
+    copy.start()
+    beside_work(len(work))
+    copy.wait()
+    whole_out[...] = mine[0, :rows, :] + theirs[0, :rows, :]
+    part_out[x * 2 + c] = mine[0, rows:, :]
+    part_out[(1 - x) * 2 + c] = mine[1, rows:, :]
+    part_out[x * 2 + 1 - c] = theirs[0, rows:, :]
+    part_out[(1 - x) * 2 + 1 - c] = theirs[1, rows:, :]
+    gates.finish()
+    outputs.finish()
+    attentions.finish()
+
+
+def finish(cid, n, first, tiles, whole, part, pairs, output_pairs, attention_pairs):
+    bt, bty, dg, dgy = pairs
+    ot, oty, gy, gyy = output_pairs
+    at, aty, joined, joined_y = attention_pairs
+    nz = n // 2
+    rounds = int(math.log2(n))
+    rows = whole.shape[0] + part.shape[0]
+    output_rows = ot.shape[0] // nz
+    attention_rows = at.shape[0] // nz
+    return comm_call(
+        functools.partial(finish_kernel, n, rounds, first, tiles),
+        cid,
+        [
+            jax.ShapeDtypeStruct(whole.shape, F32),
+            jax.ShapeDtypeStruct((GROUP,) + part.shape, F32),
+            jax.ShapeDtypeStruct((bt.shape[0] // nz, tiles * TILE), F32),
+            jax.ShapeDtypeStruct((output_rows, gy.shape[1]), F32),
+            jax.ShapeDtypeStruct((attention_rows, joined.shape[1]), F32),
         ],
-        [VMEM, ANY, ANY, VMEM, ANY, ANY, ANY],
-        [ANY, ANY, VMEM, VMEM, VMEM],
-    )(gf, wd, wgu, gs, gu, hid, hidy)
+        [
+            pltpu.VMEM((rounds + 1, rows, 128), F32),
+            pltpu.VMEM((rounds + 1, rows, 128), F32),
+            pltpu.VMEM((2, rows, 128), F32),
+            pltpu.VMEM((2, rows, 128), F32),
+            DMA((rounds + 2,)),
+            DMA((rounds + 2,)),
+        ]
+        + gate_scratch(nz, tiles, bt)
+        + Chain.scratch(nz, 1, output_rows, gy.shape[1])
+        + Chain.scratch(nz, 2, attention_rows, joined.shape[1] // 2),
+        [VMEM] * 4 + [ANY] * 2 + [VMEM] * 8,
+        [VMEM, VMEM, ANY, ANY, ANY],
+    )(whole, part, bt, bty, dg, dgy, ot, oty, gy, gyy, at, aty, joined, joined_y)
 
 
 def rms_inverse(value):
@@ -1374,10 +2027,6 @@
     first = value[..., :half]
     second = value[..., half:]
     return jnp.concatenate([first * cosine - second * sine, second * cosine + first * sine], axis=-1)
-
-
-def seq_swap(value, n):
-    return lax.ppermute(value, "seq", [(s, s ^ 1) for s in range(n)])
 
 
 def core_swap(value):
@@ -1390,41 +2039,6 @@
     here = lax.dynamic_index_in_dim(turned, y, 1, keepdims=False).reshape(width // 2, rows)
     there = lax.dynamic_index_in_dim(turned, 1 - y, 1, keepdims=False).reshape(width // 2, rows)
     return here, there
-
-
-class ChainSum:
-    def __init__(self, block, n, z):
-        self.block, self.n, self.z, self.t = block, n, z, 1
-        self.got = None
-
-    def pick(self, k):
-        return lax.dynamic_index_in_dim(self.block, jnp.clip(k, 0, self.n // 2 - 1), 0, keepdims=False)
-
-    def hop(self):
-        n, z, t = self.n, self.z, self.t
-        right = self.pick(z + n // 2 - t)
-        left = self.pick(z - n // 2 + t)
-        if t > 1:
-            right = (right.astype(F32) + self.got[0].astype(F32)).astype(BF16)
-            left = (left.astype(F32) + self.got[1].astype(F32)).astype(BF16)
-        self.got = (
-            lax.ppermute(right, "seq", [(s, s + 2) for s in range(2 * t)]),
-            lax.ppermute(left, "seq", [(n - 1 - s, n - 3 - s) for s in range(2 * t)]),
-        )
-        self.t += 1
-
-    def after(self, value):
-        self.got, value = lax.optimization_barrier((self.got, value))
-        return value
-
-    def end(self):
-        while self.t < self.n // 2:
-            self.hop()
-        return self.pick(self.z).astype(F32) + self.got[0].astype(F32) + self.got[1].astype(F32)
-
-
-def pair_product(lefts, rights):
-    return dot(lefts[0], rights[0]) + dot(lefts[1], rights[1])
 
 
 def lanes(value, rows):
@@ -1456,7 +2070,6 @@
     is_gate = me < 2
     c = me % 2
     y = seq % 2
-    z = seq // 2
     width = tokens.shape[2]
     part = width // GROUP
     rows = GROUP * tokens.shape[1]
@@ -1513,7 +2126,7 @@
     third_inverse = rms_inverse(middle)
     second_input = (middle * third_inverse * gain[2]).astype(BF16)
 
-    halves = [slice_halves(v, n, y) for v in (first_input, mixed_rows, second_input)]
+    halves = [slice_halves(v, n, y) for v in (second_input, mixed_rows, first_input)]
     my_gate_scale = mine(gate_up_scale)
     columns = gate_up_code.shape[1]
     tiles = columns // TILE
@@ -1523,18 +2136,18 @@
         second_input,
         gate_up_code,
         gate_scales,
-        down_code,
+        down_code.T,
         cot_blocks,
         gain[3].reshape(GROUP, 1, part),
         down_scale.reshape(GROUP, 1, part),
         [half[1] for half in halves],
     )
-    first_pair, mixed_pair, second_pair = [(half[0], rider) for half, rider in zip(halves, riders)]
+    second_pair, mixed_pair, first_pair = [(half[0], rider) for half, rider in zip(halves, riders)]
     my_middle = own_rows(middle)
     my_down = blocks_to_rows(lax.dynamic_slice_in_dim(down_blocks, me * own, own, 1)).astype(F32) * down_scale
     result = (my_middle + my_down * rms_inverse(my_down) * gain[3]).astype(BF16)
     grad_gate_up, grad_gate_up_y, gate_sums, grad_second_input, down_grad = ffn_backward(
-        6, n, grad_down, down_code, gate_up_code, gate_scales, gate_up, hidden, hidden_y
+        6, n, grad_down, down_code.T, gate_up_code, gate_scales, gate_up, hidden, hidden_y
     )
     if n == 8:
         down_grad = down_grad.reshape(-1, part)
@@ -1556,66 +2169,106 @@
     scale_down = down_sums[0]
     gain_four = down_sums[1]
     scale_gate = gate_sums[:, 0, :].reshape(columns) / my_gate_scale
-    gate_block = pair_product(second_pair, (grad_gate_up, grad_gate_up_y)).astype(BF16)
-    gate_chain = ChainSum(gate_block.reshape(n // 2, -1, columns), n, z)
-    gate_chain.hop()
-
-    third_inverse = own_rows(third_inverse)
-    second_inverse = own_rows(second_inverse)
-    my_branch_raw = own_rows(branch_raw)
-    third = my_middle * third_inverse
-    second = my_branch_raw * output_scale * second_inverse
-    my_cot = cotangent[0].astype(F32)
-    gain_three = jnp.sum(grad_second_input * third, axis=0)
-    grad_middle = my_cot + norm_back(third_inverse, third, grad_second_input * gain[2])
-    gain_two = jnp.sum(grad_middle * second, axis=0)
-    grad_branch_full = norm_back(second_inverse, second, grad_middle * gain[1])
-    scale_output = jnp.sum(my_branch_raw * grad_branch_full, axis=0)
-    grad_branch_own = (grad_branch_full * output_scale).astype(BF16)
-    grad_branch = group_exchange(
-        7, grad_branch_own.reshape(own, GROUP, part).transpose(1, 0, 2)
-    ).reshape(rows, part)
-    grad_branch_pair = (grad_branch, seq_swap(grad_branch, n))
-    output_block = pair_product(mixed_pair, grad_branch_pair).astype(BF16)
-    output_chain = ChainSum(output_block.reshape(n // 2, -1, part), n, z)
-    grad_mixed_sum = jnp.stack(
-        [contract_last(grad_branch, output_code[i * 2 * DH : (i + 1) * 2 * DH]) for i in range(GROUP)]
-    ).astype(BF16)
-    grad_mixed = group_reduce(8, grad_mixed_sum, BF16)
-
-    grad_query, grad_pairs = attend_back(n, query, pairs, own_meta, metas, mixed, mass, grad_mixed)
-    grad_pairs = gate_chain.after(grad_pairs)
-    gate_chain.hop()
-    grad_heads = keys_reduce(9, n, grad_pairs).astype(F32)
-    grad_query_full = rotate(
-        grad_query.reshape(rows, 2, DH), cosine[:, None], -sine[:, None]
-    ).reshape(rows, 2 * DH)
-    scale_query = jnp.sum(query_raw * grad_query_full, axis=0)
-    grad_query_low = (grad_query_full * my_query_scale).astype(BF16)
-    grad_pair_full = jnp.concatenate(
-        [rotate(grad_heads[j], pair_cosine, -pair_sine) for j in range(2)], axis=1
+    gate_pairs = second_pair + (grad_gate_up, grad_gate_up_y)
+    tiles_one, tiles_two = (4, 3) if n == 8 else (0, 0)
+    tiles_three = tiles - tiles_one - tiles_two
+
+    def to_blocks(value):
+        return value.reshape(own, GROUP, part).transpose(1, 0, 2)
+
+    grad_middle, branch_sums, grad_branch, grad_branch_y, grad_query, grad_pairs, gate_one = branch_back(
+        7,
+        n,
+        tiles_one,
+        grad_second_input,
+        to_blocks(my_middle),
+        lax.dynamic_slice_in_dim(branch_blocks, me * own, own, 1),
+        to_blocks(cotangent[0]),
+        gain[1].reshape(GROUP, 1, part),
+        gain[2].reshape(GROUP, 1, part),
+        output_scale.reshape(GROUP, 1, part),
+        output_code.T,
+        query,
+        mixed,
+        mass,
+        own_meta,
+        metas,
+        pairs,
+        gate_pairs,
     )
-    scale_pair = jnp.sum(pair_raw * grad_pair_full, axis=0)
-    grad_pair_low = (grad_pair_full * my_pair_scale).astype(BF16)
-    joined = jnp.concatenate([grad_query_low, grad_pair_low], axis=1)
-    joined_pair = (joined, seq_swap(joined, n))
-    grad_first_sum = contract_last(grad_query_low, query_code) + contract_last(grad_pair_low, key_value_code)
-    grad_first_input = group_reduce(10, grad_first_sum.astype(BF16).reshape(GROUP, own, width), F32)
-    attention_block = pair_product(first_pair, joined_pair).astype(BF16)
-    attention_chain = ChainSum(attention_block.reshape(n // 2, -1, joined.shape[1]), n, z)
-    grad_first_input = gate_chain.after(grad_first_input)
-    gate_chain.hop()
+    grad_middle = blocks_to_rows(grad_middle)
+    gain_two = branch_sums[:, 0].reshape(width)
+    gain_three = branch_sums[:, 1].reshape(width)
+    scale_output = branch_sums[:, 2].reshape(width)
+    grad_branch = grad_branch.reshape(rows, part)
+    grad_branch_y = grad_branch_y.reshape(rows, part)
+
+    if n == 8:
+        joined, joined_y, grad_first_input, key_sums, gate_two = keys_back(
+            9,
+            n,
+            tiles_one,
+            tiles_two,
+            grad_pairs,
+            grad_query,
+            query_raw,
+            pair_raw,
+            cosine,
+            sine,
+            my_query_scale[None],
+            my_pair_scale[None],
+            query_code,
+            key_value_code,
+            gate_pairs,
+        )
+        scale_query = key_sums[0]
+        scale_pair = key_sums[1]
+    else:
+        grad_heads = keys_reduce(9, n, grad_pairs).astype(F32)
+        grad_query_full = rotate(
+            grad_query.reshape(rows, 2, DH), cosine[:, None], -sine[:, None]
+        ).reshape(rows, 2 * DH)
+        scale_query = jnp.sum(query_raw * grad_query_full, axis=0)
+        grad_query_low = (grad_query_full * my_query_scale).astype(BF16)
+        grad_pair_full = jnp.concatenate(
+            [rotate(grad_heads[j], pair_cosine, -pair_sine) for j in range(2)], axis=1
+        )
+        scale_pair = jnp.sum(pair_raw * grad_pair_full, axis=0)
+        grad_pair_low = (grad_pair_full * my_pair_scale).astype(BF16)
+        joined = jnp.concatenate([grad_query_low, grad_pair_low], axis=1)
+        grad_first_sum = contract_last(grad_query_low, query_code) + contract_last(grad_pair_low, key_value_code)
+        grad_first_input = group_reduce(10, grad_first_sum.astype(BF16).reshape(GROUP, own, width), F32)
     my_inputs = tokens[0].astype(F32)
     my_inverse = rms_inverse(my_inputs)
     first = my_inputs * my_inverse
     gain_one = jnp.sum(grad_first_input * first, axis=0)
     grad_inputs = grad_middle + norm_back(my_inverse, first, grad_first_input * gain[0])
 
-    wholes = jnp.concatenate([gain_one, gain_two, gain_three, scale_output])
+    wholes = lanes(jnp.concatenate([gain_one, gain_two, gain_three, scale_output]), 72)
     parts = [scale_query, scale_pair, scale_gate, scale_down, gain_four]
-    whole_total, part_total = totals(
-        11, n, lanes(wholes, 72), lanes(jnp.concatenate(parts), 56)
-    )
+    part_rows = lanes(jnp.concatenate(parts), 56)
+    if n == 8:
+        whole_total, part_total, gate_three, output_grad, attention_grad = finish(
+            11,
+            n,
+            tiles_one + tiles_two,
+            tiles_three,
+            wholes,
+            part_rows,
+            gate_pairs,
+            mixed_pair + (grad_branch, grad_branch_y),
+            first_pair + (joined, joined_y),
+        )
+        gate_grad = jnp.concatenate([gate_one, gate_two, gate_three], axis=1)
+    else:
+        whole_total, part_total = totals(11, n, wholes, part_rows)
+
+        def weight_sum(left, right):
+            return lax.psum_scatter(contract_first(left, right), "seq", scatter_dimension=0, tiled=True)
+
+        gate_grad = weight_sum(second_input, grad_gate_up)
+        output_grad = weight_sum(mixed_rows, grad_branch)
+        attention_grad = weight_sum(first_input, joined)
     whole_total = whole_total.reshape(-1)
     part_total = part_total.reshape(GROUP, -1)
     pieces = []
@@ -1624,14 +2277,13 @@
         pieces.append(part_total[:, start : start + vector.shape[0]].reshape(-1))
         start += vector.shape[0]
     q_width = query_code.shape[1]
-    attention_grad = attention_chain.end()
     return (
         result[None],
         grad_inputs[None],
         attention_grad[:, :q_width],
         attention_grad[:, q_width:],
-        output_chain.end(),
-        gate_chain.end(),
+        output_grad,
+        gate_grad,
         down_grad,
         pieces[0],
         pieces[1],

time: 1020 us -> 906 us (0.89)
  Pallas kernels: 544 us -> 759 us
  waiting for transfers between devices: 117 us -> 0 us
  starting transfers between devices: 72.3 us -> 0 us
  other arithmetic: 87.9 us -> 34.6 us
  matrix products: 57.7 us -> 8.47 us
  local copies, waits for them, and re-layouts: 130 us -> 93.4 us
    pallas_call x6 -> x3, Pallas kernels: 138 us -> 350 us  [the longest x1 148 us: finish(): comm_call(functools.partial(finish_kernel, n, rounds, first, tiles), cid,...]
    ppermute x20 -> x0, waiting for transfers between devices: 117 us -> none  [the longest x9 58.8 us: hop(): lax.ppermute(left, 'seq', [(n - 1 - s, n - 3 - s) for s in range(2 * t)])]
    ppermute x20 -> x0, starting transfers between devices: 72.3 us -> none  [the longest x9 55.2 us: hop(): lax.ppermute(right, 'seq', [(s, s + 2) for s in range(2 * t)])]
    dot_general x9 -> x3, matrix products: 43.8 us -> 8.47 us  [dot(): return jnp.dot(left, right, preferred_element_type=F32)]
    convert_element_type x11 -> x0, other arithmetic: 32 us -> none  [the longest x5 14.7 us: hop(): right = (right.astype(F32) + self.got[0].astype(F32)).astype(BF16)]
    unnamed x123 -> x62, local copies, waits for them, and re-layouts: 37.2 us -> 23.1 us
    dot_general x6 -> x0, matrix products: 13.8 us -> none  [contract_last(): lax.dot_general(left, right, (((1,), (1,)), ((), ())), preferred_element_...]
  transfers between devices with their start and end apart: 20 -> 0, of which waited for: 4 -> 0; matrix products, arithmetic and copies ran while one was open for 12% -> 0% of each run, Pallas kernels for 14% -> 0%
where the time goes in v3:
time: 906 us; the launch traced here: 897 us
  Pallas kernels  759 us (84%)
  local copies, waits for them, and re-layouts  93.4 us (10%)
  other arithmetic  34.6 us (4%)
    pallas_call x1, Pallas kernels, finish(): comm_call(functools.partial(finish_kernel, n, rounds, first, tiles), cid,...  148 us
    pallas_call x1, Pallas kernels, ffn_backward(): comm_call(functools.partial(ffn_backward_kernel, tiles, nz, chained), cid...  144 us
    pallas_call x1, Pallas kernels, ffn_forward(): comm_call(functools.partial(ffn_forward_kernel, tiles, count), cid, [jax....  135 us
    pallas_call x1, Pallas kernels, keys_back(): comm_call(functools.partial(keys_back_kernel, n, first, tiles), cid, [joi...  107 us
    pallas_call x1, Pallas kernels, branch_back(): comm_call(functools.partial(branch_back_kernel, n, tiles), cid, [block(F3...  95.4 us
    pallas_call x3, Pallas kernels, group_gather(): comm_call(functools.partial(group_gather_kernel, count, tuple(columns), t...  62.7 us
    pallas_call x1, Pallas kernels, keys_gather(): comm_call(functools.partial(keys_gather_kernel, n), cid, [jax.ShapeDtypeS...  61.3 us
    unnamed x62, local copies, waits for them, and re-layouts  23.1 us

profile of v3, /device:TPU:0, one launch (start us, length us, event | category | flops | bytes accessed | tf_op | source)
XLA Modules:
  0.0 896.5 jit_solution(6617172045610554040)
XLA Ops:
  2.7 1.3 fusion.14
  4.5 0.8 dynamic_slice.38
  5.3 0.8 dynamic_slice.39
  6.7 1.4 reshape.282.refs_6_
  8.0 1.4 reshape.290.refs_6_
  9.4 0.8 dynamic_slice.41
  10.9 0.8 broadcast_add_fusion
  13.8 1.4 copy.62
  15.2 1.1 copy.63
  16.3 22.4 %shard_map.255 = (bf16[4,128,2304]{2,1,0:T(8,128)(2,1)}, f32[4,8,128]{2,1,0:T(8,128)}) custom-call(bf16[128,2304]{1,0:T(8,128)(2,1)} %bitcast.119, f32[8,128]{1,0:T(8,128)} %stack.11.refs_1_), custom_call_target="tpu_custom_call" | custom-call | tf_op jit(solution)/shard_map/pallas_call | solution.py:126
  38.7 2.4 fusion
  41.0 0.7 slice.138
  42.4 1.2 copy-done.9
  43.6 2.4 broadcast_multiply_fusion
  46.0 1.3 subtract_convert_fusion.2
  47.4 0.9 pad_maximum_fusion.2.heads
  48.2 2.4 broadcast_multiply_fusion.1
  50.6 1.0 fusion.18
  51.7 1.3 copy.77
  52.9 2.0 copy.76
  55.0 1.6 subtract_convert_fusion
  57.1 0.9 copy.80
  58.0 1.4 copy.70.refs_2_
  59.4 4.3 copy.67
  63.7 3.2 constant_dynamic-slice_fusion
  66.9 61.3 %shard_map.256 = (bf16[8,2,512,256]{3,2,1,0:T(8,128)(2,1)}, f32[8,4,8,128]{3,2,1,0:T(8,128)}, bf16[4,512,576]{2,1,0:T(8,128)(2,1)}) custom-call(bf16[2,512,256]{2,1,0:T(8,128)(2,1)} %pad_maximum_fusion.2.heads, f32[4,8,128]{2,1,0:T(8,128)} %get-tuple-element.53.meta.own_ref.refs_11_, bf16[512,576]{1,0:T(8,128)(2,1)} %bitcast.121), custom_call_target="tpu_custom_call" | custom-call | tf_op jit(solution)/shard_map/pallas_call | solution.py:322
  128.2 6.2 shard_map.257
  134.4 17.2 %shard_map.258 = bf16[512,2048]{1,0:T(8,128)(2,1)} custom-call(bf16[512,512]{1,0:T(8,128)(2,1)} %get-tuple-element.56.refs_0_), custom_call_target="tpu_custom_call" | custom-call | tf_op jit(solution)/shard_map/pallas_call | solution.py:126
  151.6 3.7 convolution_convert_fusion
  155.3 1.1 copy.64.refs_0_
  156.4 23.1 %shard_map.259 = bf16[4,512,576]{2,1,0:T(8,128)(2,1)} custom-call(bf16[512,576]{1,0:T(8,128)(2,1)} %copy.64.refs_0_), custom_call_target="tpu_custom_call" | custom-call | tf_op jit(solution)/shard_map/pallas_call | solution.py:126
  179.5 2.0 constant_dynamic-slice_fusion.3.refs_2_
  181.5 4.7 reshape.285
  186.2 8.6 constant_dynamic-slice_fusion.1
  194.8 5.8 copy.79
  200.6 5.8 copy.78
  206.4 3.9 slice_bitcast_fusion.8
  210.3 5.2 concatenate.56
  215.5 2.4 multiply_reduce_fusion
  217.9 5.1 concatenate.61
  223.0 3.2 fusion.2
  226.2 4.5 multiply_convert_fusion
  230.7 2.8 copy.65
  233.5 1.7 constant_dynamic-slice_fusion.2
  235.2 134.9 %shard_map.260 = (bf16[2,12,512,384]{3,2,1,0:T(8,128)(2,1)}, bf16[12,512,384]{2,1,0:T(8,128)(2,1)}, bf16[12,512,384]{2,1,0:T(8,128)(2,1)}, bf16[4,512,576]{2,1,0...) custom-call(bf16[512,2304]{1,0:T(8,128)(2,1)} %get-tuple-element.143, ...), custom_call_target="tpu_custom_call" | custom-call | tf_op jit(solution)/shard_map/pallas_call | solution.py:1053
  370.1 1.2 dynamic-slice_bitcast_fusion
  372.0 2.4 fusion.15
  374.4 0.8 slice_reduce_fusion.8
  375.6 1.5 copy.69
  377.0 143.7 %shard_map.261 = (bf16[512,4608]{1,0:T(8,128)(2,1)}, bf16[512,4608]{1,0:T(8,128)(2,1)}, f32[12,8,384]{2,1,0:T(8,128)}, f32[4,128,576]{2,1,0:T(8,128)}, f32[3,384,576]{2,1,0:T(8,128)}) custom-call(bf16[512,576]{1,0:T(8,128)(2,1)} %get-tuple-element.59.refs_0_, bf16[576,9216]{1,0:T(8,128)(2,1)} %bitcast.111, bf16[2304,4608]{1,0:T(8,128)(2,1)} %refs_2_.1, ...), custom_call_target="tpu_custom_call" | custom-call | tf_op jit(solution)/shard_map/pallas_call | solution.py:1345
  520.8 95.4 %shard_map.262 = (f32[4,128,576]{2,1,0:T(8,128)}, f32[4,8,576]{2,1,0:T(8,128)}, bf16[4,128,576]{2,1,0:T(8,128)(2,1)}, bf16[4,128,576]{2,1,0:T(8,128)(2,1)}, f32[...) custom-call(f32[4,128,576]{2,1,0:T(8,128)} %get-tuple-element.63.refs_0_, ...), custom_call_target="tpu_custom_call" | custom-call | tf_op jit(solution)/shard_map/pallas_call | solution.py:1591
  616.2 1.4 slice_bitcast_fusion
  618.1 1.0 slice_reduce_fusion
  619.1 0.8 dynamic-slice_divide_fusion
  619.9 1.1 slice_reduce_fusion.3
  621.3 106.5 %shard_map.263 = (bf16[512,1024]{1,0:T(8,128)(2,1)}, bf16[512,1024]{1,0:T(8,128)(2,1)}, f32[128,2304]{1,0:T(8,128)}, f32[8,512]{1,0:T(8,128)}, f32[288,1152]{1,0:T(8,128)}) custom-call(bf16[8,2,512,256]{3,2,1,0:T(8,128)(2,1)} %get-tuple-element.70.refs_0_, f32[512,512]{1,0:T(8,128)} %get-tuple-element.71.refs_1_, f32[512,512]{1,0:T(8,128)} %copy.70.refs_2_, ...), custom_call_target="tpu_custom_call" | custom-call | tf_op jit(solution)/shard_map/pallas_call | solution.py:1867
  727.8 0.8 fusion.20
  729.3 1.7 fusion.13
  731.6 147.8 %shard_map.264 = (f32[72,128]{1,0:T(8,128)}, f32[4,56,128]{2,1,0:T(8,128)}, f32[288,1920]{1,0:T(8,128)}, f32[256,576]{1,0:T(8,128)}, f32[288,1024]{1,0:T(8,128)}) custom-call(f32[72,128]{1,0:T(8,128)} %pad_maximum_fusion.3.refs_0_, f32[56,128]{1,0:T(8,128)} %pad_bitcast_fusion.refs_1_, bf16[1152,512]{1,0:T(8,128)(2,1)} %bitcast.115, ...), custom_call_target="tpu_custom_call" | custom-call | tf_op jit(solution)/shard_map/pallas_call | solution.py:1991
  879.4 2.4 fusion.17
  881.9 1.4 fusion.12
  887.3 1.0 copy.73
  888.3 5.5 pad_maximum_fusion
  893.8 2.3 copy.74
  (92 shorter events, 14.4 us)
Async XLA Ops:
  5.3 42.9 %copy-start.22 = (f32[512]{0:T(512)}, f32[512]{0:T(512)S(1)}, u32[]{:S(2)}) copy-start(f32[512]{0:T(512)S(1)} %dynamic_slice.38) | copy-start | bytes 6148
  6.0 36.3 %copy-start.23 = (f32[512]{0:T(512)}, f32[512]{0:T(512)S(1)}, u32[]{:S(2)}) copy-start(f32[512]{0:T(512)S(1)} %dynamic_slice.39) | copy-start | bytes 6148
  11.7 1.4 copy-start.13
  11.7 1.4 copy-start.16
  11.8 1.4 copy-start.18
  38.6 3.1 copy-start
  41.7 1.9 copy-start.9
  42.4 5.9 copy-start.2
  46.0 2.2 copy-start.8
  47.2 7.7 copy-start.6
  47.3 7.7 copy-start.7
  56.6 1.5 copy-start.10
  210.3 5.2 copy-start.12
  217.9 5.1 copy-start.14
  223.0 3.2 copy-start.1
  223.0 3.2 copy-start.17
  370.1 1.7 copy-start.20
  370.1 1.9 copy-start.19
  621.3 108.0 %copy-start.3 = (bf16[1,128,2304]{2,1,0:T(8,128)(2,1)S(1)}, bf16[1,128,2304]{2,1,0:T(8,128)(2,1)}, u32[]{:S(2)}) copy-start(bf16[1,128,2304]{2,1,0:T(8,128)(2,1)} %param.16) | copy-start | bytes 1769476
  621.3 108.0 %copy-start.24 = (f32[128]{0:T(128)S(1)}, f32[128]{0:T(128)}, u32[]{:S(2)}) copy-start(f32[128]{0:T(128)} %add_rsqrt_fusion.1) | copy-start | bytes 1540
  879.4 2.5 copy-start.4
  881.8 1.5 copy-start.21
  881.8 2.1 copy-start.15
  881.8 5.5 copy-start.11
  888.3 5.5 copy-start.5

commit v4 on v3

--- a/solution.py
+++ b/solution.py
@@ -68,70 +68,6 @@
             collective_id=cid, has_side_effects=True, vmem_limit_bytes=VMEM_LIMIT
         ),
     )
-
-
-def group_gather_kernel(count, columns, parts, *refs):
-    ins = refs[:count]
-    outs = refs[count : 2 * count]
-    local, xs, xr, cs, cr, fs, fr = refs[2 * count :]
-    seq, me, x, c = place_now()
-    across = (seq, (1 - x) * 2 + c)
-    beside = (seq, x * 2 + 1 - c)
-    greet([across, beside])
-    waits = []
-    forwards = []
-    for i in range(count):
-        src, out = ins[i], outs[i]
-        rows = src.shape[0]
-        step = rows // parts[i]
-
-        def spot(owner, start, size, out=out, i=i):
-            if columns[i]:
-                width = out.shape[1] // GROUP
-                return out.at[pl.ds(start, size), pl.ds(owner * width, width)]
-            return out.at[owner, pl.ds(start, size)]
-
-        own = pltpu.make_async_copy(src, spot(me, 0, rows), local.at[i])
-        for k in range(parts[i]):
-            part = src.at[pl.ds(k * step, step)]
-            there = spot(me, k * step, step)
-            copy = remote(part, there, xs.at[i, k], xr.at[i, k], across)
-            copy.start()
-            waits.append(copy.wait_send)
-            got = spot((1 - x) * 2 + c, k * step, step)
-            forwards.append((copy, remote(got, got, fs.at[i, k], fr.at[i, k], beside)))
-        copy = remote(src, spot(me, 0, rows), cs.at[i], cr.at[i], beside)
-        copy.start()
-        own.start()
-        waits += [copy.wait, own.wait]
-    for copy, forward in forwards:
-        copy.wait_recv()
-        forward.start()
-        waits.append(forward.wait)
-    for wait in waits:
-        wait()
-
-
-def group_gather(cid, values, columns=None, parts=None):
-    count = len(values)
-    columns = columns or [False] * count
-    parts = parts or [4] * count
-    most = max(parts)
-    shapes = [
-        jax.ShapeDtypeStruct(
-            (v.shape[0], v.shape[1] * GROUP) if col else (GROUP,) + v.shape, v.dtype
-        )
-        for v, col in zip(values, columns)
-    ]
-    return comm_call(
-        functools.partial(group_gather_kernel, count, tuple(columns), tuple(parts)),
-        cid,
-        shapes,
-        [DMA((count,)), DMA((count, most)), DMA((count, most)), DMA((count,)), DMA((count,)),
-         DMA((count, most)), DMA((count, most))],
-        [ANY] * count,
-        [ANY] * count,
-    )(*values)
 
 
 def group_reduce_kernel(parts, src, out, from_core, to_x, from_x, cs, cr, xs, xr):
@@ -187,153 +123,6 @@
     )(value)
 
 
-def keys_gather_kernel(n, heads, meta, cot, out, metas, cots, own_sem, hs, hr, ms, mr, rs, rr, ls, lr, ys, yr,
-                       local, xs, xr, cs, cr, fs, fr):
-    seq, me, x, c = place_now()
-    y = seq % 2
-    z = seq // 2
-    nz = n // 2
-    across = (seq, (1 - x) * 2 + c)
-    beside = (seq, x * 2 + 1 - c)
-    peers = [(seq, lax.rem(me + d, GROUP)) for d in range(1, GROUP)]
-    peers += [(lax.rem(seq + d, n), me) for d in range(1, n)]
-    greet(peers)
-    for j in range(2):
-        target = c * 2 + j
-
-        @pl.when(target == me)
-        def _():
-            pltpu.make_async_copy(heads.at[j], out.at[seq, x], own_sem.at[0]).start()
-
-        @pl.when(target != me)
-        def _():
-            remote(heads.at[j], out.at[seq, x], hs.at[j], hr.at[x], (seq, target)).start()
-
-    small = []
-    for d in range(1, n):
-        copy = remote(meta, metas.at[seq], ms.at[d - 1], mr.at[d - 1], (lax.rem(seq + d, n), me))
-        copy.start()
-        small.append(copy)
-    own_meta = pltpu.make_async_copy(meta, metas.at[seq], own_sem.at[1])
-    own_meta.start()
-    for t in range(2):
-        source = t * 2 + x
-
-        @pl.when(source == me)
-        def _():
-            pltpu.make_async_copy(heads.at[0], out.at[seq, t], own_sem.at[0]).wait()
-
-        @pl.when(source != me)
-        def _():
-            remote(heads.at[0], out.at[seq, t], hs.at[0], hr.at[t], (seq, source)).wait_recv()
-
-    def block(owner_z, owner_y):
-        return out.at[owner_z * 2 + owner_y]
-
-    right = (seq + 2, me)
-    left = (seq - 2, me)
-    beyond = (z * 2 + 1 - y, me)
-
-    def to_y(owner_z):
-        remote(block(owner_z, y), block(owner_z, y), ys.at[owner_z], yr.at[owner_z], beyond).start()
-
-    rows = cot.shape[0]
-    parts = 2
-    step = rows // parts
-
-    for t in range(1, nz + 1):
-        go_right = z - t + 1
-        go_left = z + t - 1
-        if t > 1:
-
-            @pl.when(go_right >= 0)
-            def _():
-                remote(block(go_right, y), block(go_right, y), rs.at[t - 1], rr.at[t - 1], left).wait_recv()
-
-            @pl.when(go_left < nz)
-            def _():
-                remote(block(go_left, y), block(go_left, y), ls.at[t - 1], lr.at[t - 1], right).wait_recv()
-
-        if t < nz:
-
-            @pl.when((go_right >= 0) & (z < nz - 1))
-            def _():
-                remote(block(go_right, y), block(go_right, y), rs.at[t], rr.at[t], right).start()
-
-            @pl.when((go_left < nz) & (z > 0))
-            def _():
-                remote(block(go_left, y), block(go_left, y), ls.at[t], lr.at[t], left).start()
-
-        @pl.when(go_right >= 0)
-        def _():
-            to_y(go_right)
-
-        if t > 1:
-
-            @pl.when(go_left < nz)
-            def _():
-                to_y(go_left)
-
-        if t == 1:
-            xcopies = []
-            for k in range(parts):
-                part = pl.ds(k * step, step)
-                copy = remote(cot.at[part], cots.at[me, part], xs.at[k], xr.at[k], across)
-                copy.start()
-                xcopies.append(copy)
-            ccopy = remote(cot, cots.at[me], cs, cr, beside)
-            ccopy.start()
-            own_cot = pltpu.make_async_copy(cot, cots.at[me], local)
-            own_cot.start()
-    forwards = []
-    for k in range(parts):
-        part = pl.ds(k * step, step)
-        xcopies[k].wait()
-        got = cots.at[(1 - x) * 2 + c, part]
-        forward = remote(got, got, fs.at[k], fr.at[k], beside)
-        forward.start()
-        forwards.append(forward)
-    for k in range(nz):
-        remote(block(k, 1 - y), block(k, 1 - y), ys.at[k], yr.at[k], beyond).wait()
-    for t in range(1, nz):
-
-        @pl.when((z - t + 1 >= 0) & (z < nz - 1))
-        def _():
-            remote(block(z, y), block(z, y), rs.at[t], rr.at[t], right).wait_send()
-
-        @pl.when((z + t - 1 < nz) & (z > 0))
-        def _():
-            remote(block(z, y), block(z, y), ls.at[t], lr.at[t], left).wait_send()
-
-    for j in range(2):
-
-        @pl.when(c * 2 + j != me)
-        def _():
-            remote(heads.at[j], out.at[seq, x], hs.at[j], hr.at[x], (seq, c * 2 + j)).wait_send()
-
-    for copy in small + forwards + [ccopy]:
-        copy.wait()
-    own_meta.wait()
-    own_cot.wait()
-
-
-def keys_gather(cid, n, heads, meta, cot):
-    nz = n // 2
-    return comm_call(
-        functools.partial(keys_gather_kernel, n),
-        cid,
-        [
-            jax.ShapeDtypeStruct((n,) + heads.shape, BF16),
-            jax.ShapeDtypeStruct((n,) + meta.shape, F32),
-            jax.ShapeDtypeStruct((GROUP,) + cot.shape, BF16),
-        ],
-        [DMA((2,)), DMA((2,)), DMA((2,)), DMA((n - 1,)), DMA((n - 1,)), DMA((nz,)), DMA((nz,)), DMA((nz,)),
-         DMA((nz,)), DMA((nz,)), DMA((nz,)), DMA, DMA((2,)), DMA((2,)), DMA, DMA, DMA((2,)), DMA((2,))],
-        [ANY] * 3,
-        [ANY] * 3,
-    )(heads, meta, cot)
-
-
 def keys_reduce_kernel(n, src, out, y_got, r_got, l_got, r_out, l_out, moved, ys, yr, rs, rr, ls, lr, hs, hr, local):
     seq, me, x, c = place_now()
     y = seq % 2
@@ -557,6 +346,454 @@
     )(whole, part)
 
 
+def turned(block, unit, to):
+    half = to.shape[1]
+    flat = contract_first(block, unit[...])
+    to[0] = flat[:half].astype(BF16)
+    to[1] = flat[half:].astype(BF16)
+
+
+def fill_unit(unit):
+    shape = unit.shape
+    unit[...] = jnp.where(
+        lax.broadcasted_iota(jnp.int32, shape, 0) == lax.broadcasted_iota(jnp.int32, shape, 1), 1.0, 0.0
+    ).astype(BF16)
+
+
+def front_kernel(n, *refs):
+    tok, cot, meta, g1, rates, q_scale, p_scale, wq, wkv = refs[:9]
+    toks, cots, own_meta, metas, out, q, q_raw, p_raw, cosine, sine, turned_o = refs[9:20]
+    (tb, ab, wqs, wkvs, heads, om, unit, at,
+     ws, txs, txr, tcs, tcr, tfs, tfr, gms, gmr, own_sem, hs, hr, ms, mr, rs, rr, ls, lr, ys, yr,
+     xs, xr, cs, cr, fs, fr, os) = refs[20:]
+    seq, me, x, c = place_now()
+    y = seq % 2
+    z = seq // 2
+    nz = n // 2
+    across = (seq, (1 - x) * 2 + c)
+    beside = (seq, x * 2 + 1 - c)
+    group = [(seq, lax.rem(me + d, GROUP)) for d in range(1, GROUP)]
+    load_q = pltpu.make_async_copy(wq, wqs, ws.at[0])
+    load_kv = pltpu.make_async_copy(wkv, wkvs, ws.at[1])
+    load_q.start()
+    load_kv.start()
+    greet(group + [(lax.rem(seq + d, n), me) for d in range(1, n)])
+    blk = tok.shape[0] // GROUP
+    part = tok.shape[1]
+    own = blk
+
+    sends = []
+    for k in range(GROUP):
+        rows = pl.ds(k * blk, blk)
+        copy = remote(tok.at[rows], tb.at[me, rows], txs.at[k], txr.at[k], across)
+        copy.start()
+        sends.append(copy)
+    to_core = remote(tok, tb.at[me], tcs, tcr, beside)
+    to_core.start()
+    group_meta = []
+    for d in range(1, GROUP):
+        copy = remote(meta, om.at[me], gms.at[d - 1], gmr.at[d - 1], group[d - 1])
+        copy.start()
+        group_meta.append(copy)
+    own_tok = pltpu.make_async_copy(tok, tb.at[me], own_sem.at[0])
+    own_tok.start()
+    own_row = pltpu.make_async_copy(meta, om.at[me], own_sem.at[1])
+    own_row.start()
+    fill_unit(unit)
+    for copy in group_meta:
+        copy.wait()
+    own_row.wait()
+    width = GROUP * part
+    half = DH // 2
+    js = range(GROUP)
+    is_key = jnp.where(x == 0, 1.0, 0.0).astype(F32)
+
+    def process(p):
+        def norm(i, carry):
+            span = lambda j: pl.ds(pl.multiple_of(j * blk + i * 32, 32), 32)
+            values = [tb[p, span(j), :].astype(F32) for j in js]
+            total = values[0] * values[0]
+            for value in values[1:]:
+                total = total + value * value
+            inverse = lax.rsqrt(jnp.sum(total, axis=1, keepdims=True) * (1.0 / width) + EPSILON)
+            to = pl.ds(pl.multiple_of(p * own + i * 32, 32), 32)
+            for j in js:
+                ab[j, to, :] = (values[j] * inverse * g1[j]).astype(BF16)
+            return carry
+
+        lax.fori_loop(0, blk // 32, norm, 0)
+        rows = pl.ds(pl.multiple_of(p * own, 128), own)
+        turn = jnp.broadcast_to(om[p, 1:2, :], (128, 128)).T * rates[...]
+        cos = jnp.cos(turn)
+        sin = jnp.sin(turn)
+        cosine[rows, :] = cos
+        sine[rows, :] = sin
+
+        def product(weights):
+            total = dot(ab[0, rows, :], weights[0:part, :])
+            for j in range(1, GROUP):
+                total = total + dot(ab[j, rows, :], weights[j * part : (j + 1) * part, :])
+            return total
+
+        plain = product(wqs)
+        q_raw[rows, :] = plain
+        plain = plain * q_scale[...]
+        for h in range(2):
+            one = plain[:, h * DH : h * DH + half]
+            two = plain[:, h * DH + half : (h + 1) * DH]
+            q[rows, h * DH : h * DH + half] = (one * cos - two * sin).astype(BF16)
+            q[rows, h * DH + half : (h + 1) * DH] = (two * cos + one * sin).astype(BF16)
+        cos = is_key * cos + (1.0 - is_key)
+        sin = is_key * sin
+        plain = product(wkvs)
+        p_raw[rows, :] = plain
+        plain = plain * p_scale[...]
+        for h in range(2):
+            one = plain[:, h * DH : h * DH + half]
+            two = plain[:, h * DH + half : (h + 1) * DH]
+            heads[h, rows, :half] = (one * cos - two * sin).astype(BF16)
+            heads[h, rows, half:] = (two * cos + one * sin).astype(BF16)
+
+    own_tok.wait()
+    load_q.wait()
+    load_kv.wait()
+    process(me)
+    to_core.wait_recv()
+    process(x * 2 + 1 - c)
+    forwards = []
+    for k in range(GROUP):
+        sends[k].wait_recv()
+        got = tb.at[(1 - x) * 2 + c, pl.ds(k * blk, blk)]
+        forward = remote(got, got, tfs.at[k], tfr.at[k], beside)
+        forward.start()
+        forwards.append(forward)
+    process((1 - x) * 2 + c)
+    for forward in forwards:
+        forward.wait_recv()
+    process((1 - x) * 2 + 1 - c)
+
+    for j in range(2):
+        target = c * 2 + j
+
+        @pl.when(target == me)
+        def _():
+            pltpu.make_async_copy(heads.at[j], out.at[seq, x], own_sem.at[0]).start()
+
+        @pl.when(target != me)
+        def _():
+            remote(heads.at[j], out.at[seq, x], hs.at[j], hr.at[x], (seq, target)).start()
+
+    small = []
+    for d in range(1, n):
+        copy = remote(om, metas.at[seq], ms.at[d - 1], mr.at[d - 1], (lax.rem(seq + d, n), me))
+        copy.start()
+        small.append(copy)
+    outs = [
+        pltpu.make_async_copy(om, metas.at[seq], os.at[0]),
+        pltpu.make_async_copy(om, own_meta, os.at[1]),
+        pltpu.make_async_copy(tb, toks, os.at[2]),
+    ]
+    for copy in outs:
+        copy.start()
+    for t in range(2):
+        source = t * 2 + x
+
+        @pl.when(source == me)
+        def _():
+            pltpu.make_async_copy(heads.at[0], out.at[seq, t], own_sem.at[0]).wait()
+
+        @pl.when(source != me)
+        def _():
+            remote(heads.at[0], out.at[seq, t], hs.at[0], hr.at[t], (seq, source)).wait_recv()
+
+    def block(owner_z, owner_y):
+        return out.at[owner_z * 2 + owner_y]
+
+    right = (seq + 2, me)
+    left = (seq - 2, me)
+    beyond = (z * 2 + 1 - y, me)
+
+    def to_y(owner_z):
+        remote(block(owner_z, y), block(owner_z, y), ys.at[owner_z], yr.at[owner_z], beyond).start()
+
+    parts = 2
+    step = cot.shape[0] // parts
+    for t in range(1, nz + 1):
+        go_right = z - t + 1
+        go_left = z + t - 1
+        if t > 1:
+
+            @pl.when(go_right >= 0)
+            def _():
+                remote(block(go_right, y), block(go_right, y), rs.at[t - 1], rr.at[t - 1], left).wait_recv()
+
+            @pl.when(go_left < nz)
+            def _():
+                remote(block(go_left, y), block(go_left, y), ls.at[t - 1], lr.at[t - 1], right).wait_recv()
+
+        if t < nz:
+
+            @pl.when((go_right >= 0) & (z < nz - 1))
+            def _():
+                remote(block(go_right, y), block(go_right, y), rs.at[t], rr.at[t], right).start()
+
+            @pl.when((go_left < nz) & (z > 0))
+            def _():
+                remote(block(go_left, y), block(go_left, y), ls.at[t], lr.at[t], left).start()
+
+        @pl.when(go_right >= 0)
+        def _():
+            to_y(go_right)
+
+        if t > 1:
+
+            @pl.when(go_left < nz)
+            def _():
+                to_y(go_left)
+
+        if t == 1:
+            xcopies = []
+            for k in range(parts):
+                rows = pl.ds(k * step, step)
+                copy = remote(cot.at[rows], cots.at[me, rows], xs.at[k], xr.at[k], across)
+                copy.start()
+                xcopies.append(copy)
+            ccopy = remote(cot, cots.at[me], cs, cr, beside)
+            ccopy.start()
+            own_cot = pltpu.make_async_copy(cot, cots.at[me], os.at[3])
+            own_cot.start()
+            for j in js:
+                turned(ab[j], unit, at.at[j])
+            turned_out = pltpu.make_async_copy(at, turned_o, os.at[4])
+            turned_out.start()
+    later = []
+    for k in range(parts):
+        rows = pl.ds(k * step, step)
+        xcopies[k].wait()
+        got = cots.at[(1 - x) * 2 + c, rows]
+        forward = remote(got, got, fs.at[k], fr.at[k], beside)
+        forward.start()
+        later.append(forward)
+    for k in range(nz):
+        remote(block(k, 1 - y), block(k, 1 - y), ys.at[k], yr.at[k], beyond).wait()
+    for t in range(1, nz):
+
+        @pl.when((z - t + 1 >= 0) & (z < nz - 1))
+        def _():
+            remote(block(z, y), block(z, y), rs.at[t], rr.at[t], right).wait_send()
+
+        @pl.when((z + t - 1 < nz) & (z > 0))
+        def _():
+            remote(block(z, y), block(z, y), ls.at[t], lr.at[t], left).wait_send()
+
+    for j in range(2):
+
+        @pl.when(c * 2 + j != me)
+        def _():
+            remote(heads.at[j], out.at[seq, x], hs.at[j], hr.at[x], (seq, c * 2 + j)).wait_send()
+
+    for copy in small + later + [ccopy]:
+        copy.wait()
+    for copy in sends + forwards + [to_core]:
+        copy.wait_send()
+    for copy in outs + [own_cot, turned_out]:
+        copy.wait()
+
+
+def front(cid, n, tok, cot, meta, g1, rates, q_scale, p_scale, wq, wkv):
+    nz = n // 2
+    rows, part = tok.shape
+    own = rows // GROUP
+    deep, wide = wq.shape
+    blocks = jax.ShapeDtypeStruct((GROUP, rows, part), BF16)
+    table = jax.ShapeDtypeStruct((rows, DH // 2), F32)
+    raw = jax.ShapeDtypeStruct((rows, wide), F32)
+    turned_shape = (GROUP, 2, part // 2, rows)
+    return comm_call(
+        functools.partial(front_kernel, n),
+        cid,
+        [
+            blocks,
+            blocks,
+            jax.ShapeDtypeStruct((GROUP,) + meta.shape, F32),
+            jax.ShapeDtypeStruct((n, GROUP) + meta.shape, F32),
+            jax.ShapeDtypeStruct((n, 2, rows, DH), BF16),
+            jax.ShapeDtypeStruct((rows, wide), BF16),
+            raw,
+            raw,
+            table,
+            table,
+            jax.ShapeDtypeStruct(turned_shape, BF16),
+        ],
+        [
+            pltpu.VMEM((GROUP, rows, part), BF16),
+            pltpu.VMEM((GROUP, rows, part), BF16),
+            pltpu.VMEM((deep, wide), BF16),
+            pltpu.VMEM((deep, wide), BF16),
+            pltpu.VMEM((2, rows, DH), BF16),
+            pltpu.VMEM((GROUP,) + meta.shape, F32),
+            pltpu.VMEM((rows, rows), BF16),
+            pltpu.VMEM(turned_shape, BF16),
+            DMA((2,)), DMA((GROUP,)), DMA((GROUP,)), DMA, DMA, DMA((GROUP,)), DMA((GROUP,)), DMA((GROUP - 1,)),
+            DMA((GROUP - 1,)), DMA((2,)), DMA((2,)), DMA((2,)), DMA((n - 1,)), DMA((n - 1,)), DMA((nz,)), DMA((nz,)),
+            DMA((nz,)), DMA((nz,)), DMA((nz,)), DMA((nz,)), DMA((2,)), DMA((2,)), DMA, DMA, DMA((2,)), DMA((2,)),
+            DMA((5,)),
+        ],
+        [VMEM, ANY, VMEM, VMEM, VMEM, VMEM, VMEM, ANY, ANY],
+        [ANY, ANY, ANY, ANY, ANY, VMEM, VMEM, VMEM, VMEM, VMEM, ANY],
+    )(tok, cot, meta, g1, rates, q_scale, p_scale, wq, wkv)
+
+
+def branch_kernel(low, wo, toks, scale, g2, g3, b_o, raw_o, mid_o, ot_o, bt_o, ob, pb, bb, acc, unit, ot, bt,
+                  xs, xr, cs, cr, fs, fr, gxs, gxr, gcs, gcr, gfs, gfr, local, os):
+    seq, me, x, c = place_now()
+    across = (seq, (1 - x) * 2 + c)
+    beside = (seq, x * 2 + 1 - c)
+    greet([across, beside])
+    rows, heads = low.shape
+    part = pb.shape[2]
+    parts = 4
+    size = rows // parts
+    own = rows // GROUP
+    js = range(GROUP)
+
+    def spot(owner, k):
+        return ob.at[pl.ds(k * size, size), pl.ds(pl.multiple_of(owner * heads, 128), heads)]
+
+    sends = []
+    for k in range(parts):
+        copy = remote(low.at[pl.ds(k * size, size)], spot(me, k), xs.at[k], xr.at[k], across)
+        copy.start()
+        sends.append(copy)
+    mine = ob.at[:, pl.ds(pl.multiple_of(me * heads, 128), heads)]
+    to_core = remote(low, mine, cs, cr, beside)
+    to_core.start()
+    own_copy = pltpu.make_async_copy(low, mine, local)
+    own_copy.start()
+    fill_unit(unit)
+
+    def add(owner, start):
+        cols = pl.ds(pl.multiple_of(owner * heads, 128), heads)
+        more = contract_last(ob[:, cols], wo[:, cols])
+        acc[...] = more if start else acc[...] + more
+
+    own_copy.wait()
+    add(me, True)
+    to_core.wait_recv()
+    add(x * 2 + 1 - c, False)
+    forwards = []
+    for k in range(parts):
+        sends[k].wait_recv()
+        got = spot((1 - x) * 2 + c, k)
+        forward = remote(got, got, fs.at[k], fr.at[k], beside)
+        forward.start()
+        forwards.append(forward)
+    add((1 - x) * 2 + c, False)
+    for forward in forwards:
+        forward.wait_recv()
+    add((1 - x) * 2 + 1 - c, False)
+
+    over = []
+    core = []
+    for k in range(parts):
+        span = pl.ds(k * size, size)
+        pb[me, span, :] = acc[span, :].astype(BF16)
+        piece = pb.at[me, span]
+        copy = remote(piece, piece, gxs.at[k], gxr.at[k], across)
+        copy.start()
+        over.append(copy)
+        copy = remote(piece, piece, gcs.at[k], gcr.at[k], beside)
+        copy.start()
+        core.append(copy)
+    for j in js:
+        turned(ob[:, j * heads : (j + 1) * heads], unit, ot.at[j])
+    ot_out = pltpu.make_async_copy(ot, ot_o, os.at[0])
+    ot_out.start()
+    passed = []
+    for k in range(parts):
+        over[k].wait_recv()
+        got = pb.at[(1 - x) * 2 + c, pl.ds(k * size, size)]
+        forward = remote(got, got, gfs.at[k], gfr.at[k], beside)
+        forward.start()
+        passed.append(forward)
+    for copy in core + passed:
+        copy.wait_recv()
+    mean = 1.0 / (GROUP * part)
+
+    def rowsum(values):
+        total = values[0] * values[0]
+        for value in values[1:]:
+            total = total + value * value
+        return jnp.sum(total, axis=1, keepdims=True) * mean
+
+    def norms(i, carry):
+        pack = i // (own // 16)
+        inner = i % (own // 16) * 16
+        span = pl.ds(pl.multiple_of(i * 16, 16), 16)
+        branch = [pb[j, span, :].astype(F32) * scale[j] for j in js]
+        inverse = lax.rsqrt(rowsum(branch) + EPSILON)
+        middle = [
+            toks[pack, pl.ds(pl.multiple_of(j * own + inner, 16), 16), :].astype(F32) + branch[j] * inverse * g2[j]
+            for j in js
+        ]
+        inverse = lax.rsqrt(rowsum(middle) + EPSILON)
+        for j in js:
+            bb[j, span, :] = (middle[j] * inverse * g3[j]).astype(BF16)
+
+        @pl.when(pack == me)
+        def _():
+            for j in js:
+                mid_o[j, pl.ds(pl.multiple_of(inner, 16), 16), :] = middle[j]
+
+        return carry
+
+    lax.fori_loop(0, rows // 16, norms, 0)
+    b_out = pltpu.make_async_copy(bb, b_o, os.at[1])
+    b_out.start()
+    raw_out = pltpu.make_async_copy(pb.at[:, pl.ds(pl.multiple_of(me * own, 128), own)], raw_o, os.at[2])
+    raw_out.start()
+    for j in js:
+        turned(bb[j], unit, bt.at[j])
+    bt_out = pltpu.make_async_copy(bt, bt_o, os.at[3])
+    bt_out.start()
+    for copy in sends + forwards + over + core + passed + [to_core]:
+        copy.wait_send()
+    for copy in (ot_out, b_out, raw_out, bt_out):
+        copy.wait()
+
+
+def branch_forward(cid, low, wo, toks, scale, g2, g3):
+    rows, heads = low.shape
+    part = wo.shape[0]
+    own = rows // GROUP
+    turned_b = (GROUP, 2, part // 2, rows)
+    turned_o = (GROUP, 2, heads // 2, rows)
+    four = DMA((4,))
+    return comm_call(
+        branch_kernel,
+        cid,
+        [
+            jax.ShapeDtypeStruct((GROUP, rows, part), BF16),
+            jax.ShapeDtypeStruct((GROUP, own, part), BF16),
+            jax.ShapeDtypeStruct((GROUP, own, part), F32),
+            jax.ShapeDtypeStruct(turned_o, BF16),
+            jax.ShapeDtypeStruct(turned_b, BF16),
+        ],
+        [
+            pltpu.VMEM((rows, GROUP * heads), BF16),
+            pltpu.VMEM((GROUP, rows, part), BF16),
+            pltpu.VMEM((GROUP, rows, part), BF16),
+            pltpu.VMEM((rows, part), F32),
+            pltpu.VMEM((rows, rows), BF16),
+            pltpu.VMEM(turned_o, BF16),
+            pltpu.VMEM(turned_b, BF16),
+            four, four, DMA, DMA, four, four, four, four, four, four, four, four, DMA, four,
+        ],
+        [VMEM] * 6,
+        [ANY, ANY, VMEM, ANY, ANY],
+    )(low, wo, toks, scale, g2, g3)
+
+
 def masks(n, own_ref, meta_ref):
     def column(row):
         return jnp.broadcast_to(own_ref[0, row : row + 1, :], (128, 128)).T
@@ -823,7 +1060,8 @@
     beside = (seq, x * 2 + 1 - c)
     beyond = (seq + 1 - 2 * y, me)
     rows, tw = gu.shape[2:]
-    deep = b.shape[1]
+    part = b.shape[2]
+    deep = GROUP * part
     per = tiles // 4
 
     def load_up(t):
@@ -843,7 +1081,7 @@
     greet([across, beside, beyond])
     travellers = []
     for i in range(riders):
-        copy = remote(rider_in[i], rider_out[i], rs.at[i], rr.at[i], beyond)
+        copy = remote(rider_in[i].at[:, 1 - y], rider_out[i], rs.at[i], rr.at[i], beyond)
         copy.start()
         travellers.append(copy)
     acc[...] = jnp.zeros_like(acc)
@@ -878,7 +1116,10 @@
         scale = gs[t]
 
         def product(span):
-            gu[x, t, span, :] = (dot(b[span, :], wlev[...]) * scale).astype(BF16)
+            total = dot(b[0, span, :], wlev[0:part, :])
+            for j in range(1, GROUP):
+                total = total + dot(b[j, span, :], wlev[j * part : (j + 1) * part, :])
+            gu[x, t, span, :] = (total * scale).astype(BF16)
 
         strips(rows // 256, 256, product)
         to_x(t).start()
@@ -1045,9 +1286,9 @@
 
 
 def ffn_forward(cid, b, wgu, gs, wd, cots, g3, ds, riders):
-    rows, deep = b.shape
+    rows, part = b.shape[1:]
+    deep = GROUP * part
     tiles, _, tw = gs.shape
-    part = wd.shape[0]
     count = len(riders)
     lone = max(count, 1)
     return comm_call(
@@ -1061,7 +1302,7 @@
             jax.ShapeDtypeStruct((rows, part), BF16),
             jax.ShapeDtypeStruct((8, part), F32),
         ]
-        + [jax.ShapeDtypeStruct(r.shape, r.dtype) for r in riders],
+        + [jax.ShapeDtypeStruct(r.shape[:1] + r.shape[2:], r.dtype) for r in riders],
         [
             pltpu.VMEM((2, tiles, rows, tw), BF16),
             pltpu.VMEM((2 * tiles, rows, tw), BF16),
@@ -1381,18 +1622,19 @@
     )(gf, wd, wgu, gs, gu, hid, hidy)
 
 
-def gate_chain(nz, first, count, seq, me, bt, bty, dg, dgy, out, slabs, slab_sem, scratch):
-    size = bt.shape[0] // nz
-    loads = []
+def gate_chain(nz, first, count, seq, me, bt, bty, dg, dgy, out, slabs, halves, slab_sem, scratch):
+    loads = [pltpu.make_async_copy(bt.at[:, seq % 2], halves.at[0], slab_sem.at[2])]
+    loads.append(pltpu.make_async_copy(bty, halves.at[1], slab_sem.at[3]))
     for i, ref in enumerate((dg, dgy)):
-        copy = pltpu.make_async_copy(ref.at[:, pl.ds(first * TILE, count * TILE)], slabs.at[i], slab_sem.at[i])
+        loads.append(
+            pltpu.make_async_copy(ref.at[:, pl.ds(first * TILE, count * TILE)], slabs.at[i], slab_sem.at[i])
+        )
+    for copy in loads:
         copy.start()
-        loads.append(copy)
 
     def partial(k, j):
-        rows = pl.ds(pl.multiple_of(k * size, 16), size)
         cols = pl.ds(pl.multiple_of(j * TILE, 128), TILE)
-        return dot(bt[rows, :], slabs[0, :, cols]) + dot(bty[rows, :], slabs[1, :, cols])
+        return dot(halves[0, k], slabs[0, :, cols]) + dot(halves[1, k], slabs[1, :, cols])
 
     def keep(j, stage, sem):
         return pltpu.make_async_copy(stage, out.at[:, pl.ds(pl.multiple_of(j * TILE, 128), TILE)], sem)
@@ -1401,10 +1643,10 @@
 
 
 def gate_scratch(nz, count, bt):
-    rows = bt.shape[1]
-    return [pltpu.VMEM((2, rows, count * TILE), BF16), DMA((2,))] + Chain.scratch(
-        nz, count, bt.shape[0] // nz, TILE
-    )
+    rows = bt.shape[3]
+    return [
+        pltpu.VMEM((2, rows, count * TILE), BF16), pltpu.VMEM((2, nz) + bt.shape[2:], BF16), DMA((4,))
+    ] + Chain.scratch(nz, count, bt.shape[2], TILE)
 
 
 def branch_back_kernel(n, tiles, *refs):
@@ -1421,7 +1663,7 @@
     peers = [(seq, lax.rem(me + d, GROUP)) for d in range(1, GROUP)]
     chain = None
     if tiles:
-        chain, loads = gate_chain(nz, 0, tiles, seq, me, bt, bty, dg, dgy, gate_o, rest[0], rest[1], rest[2:])
+        chain, loads = gate_chain(nz, 0, tiles, seq, me, bt, bty, dg, dgy, gate_o, *rest[:3], rest[3:])
         greet_all(seq, me, nz, peers)
     else:
         greet(peers + [beyond])
@@ -1586,7 +1828,7 @@
     rows = q.shape[0]
     heads = q.shape[1]
     block = lambda kind: jax.ShapeDtypeStruct((GROUP, own, part), kind)
-    gate_rows = bt.shape[0] // (n // 2)
+    gate_rows = bt.shape[2]
     pack = (2, n, 2, own, DH)
     return comm_call(
         functools.partial(branch_back_kernel, n, tiles),
@@ -1614,7 +1856,7 @@
             DMA((3,)), DMA((3,)), DMA, DMA((2,)), DMA((2,)), DMA, DMA, DMA((2,)), DMA((2,)), DMA, DMA, DMA,
         ]
         + (gate_scratch(n // 2, tiles, bt) if tiles else []),
-        [VMEM] * 13 + [ANY] + [VMEM] * 2 + [ANY] * 2,
+        [VMEM] * 13 + [ANY] * 5,
         [VMEM, VMEM, ANY, ANY, VMEM, ANY, ANY],
     )(gsi, mid, raw, cot, g2, g3, scale, wo, q, mixed, mass, own_meta, metas, kv, bt, bty, dg, dgy)
 
@@ -1624,7 +1866,7 @@
     joined, joined_y, out, sums, gate_o = refs[14:19]
     (y_got, r_got, l_got, r_out, l_out, moved, back, acc, low, from_core, to_xb, from_x,
      ys, yr, rs, rr, ls, lr, hs, hr, local, jys, jyr, ccs, ccr, cxs, cxr) = refs[19:46]
-    slabs, slab_sem, *rest = refs[46:]
+    slabs, halves, slab_sem, *rest = refs[46:]
     seq, me, x, c = place_now()
     y = seq % 2
     z = seq // 2
@@ -1634,7 +1876,7 @@
     beyond = (z * 2 + 1 - y, me)
     across = (seq, (1 - x) * 2 + c)
     beside = (seq, x * 2 + 1 - c)
-    chain, loads = gate_chain(nz, first, tiles, seq, me, bt, bty, dg, dgy, gate_o, slabs, slab_sem, rest)
+    chain, loads = gate_chain(nz, first, tiles, seq, me, bt, bty, dg, dgy, gate_o, slabs, halves, slab_sem, rest)
     greet_all(seq, me, nz, [(seq, lax.rem(me + d, GROUP)) for d in range(1, GROUP)])
     rows, width = dq.shape
     deep = acc.shape[1]
@@ -1872,7 +2114,7 @@
             joined,
             jax.ShapeDtypeStruct((block, deep), F32),
             jax.ShapeDtypeStruct((8, width), F32),
-            jax.ShapeDtypeStruct((bt.shape[0] // nz, tiles * TILE), F32),
+            jax.ShapeDtypeStruct((bt.shape[2], tiles * TILE), F32),
         ],
         [
             pltpu.VMEM((nz,) + shape, BF16), chain, chain, chain, chain, pltpu.VMEM(shape, BF16), pltpu.VMEM(shape, BF16),
@@ -1885,7 +2127,7 @@
             DMA((2,)), DMA((2,)), DMA, DMA, DMA, DMA((2, 4)), DMA((2, 4)), DMA((4,)), DMA((4,)),
         ]
         + gate_scratch(nz, tiles, bt),
-        [VMEM] * 12 + [ANY] * 2,
+        [VMEM] * 10 + [ANY] * 4,
         [VMEM, ANY, VMEM, VMEM, ANY],
     )(src, dq, q_raw, p_raw, cosine, sine, q_scale, p_scale, wq, wkv, bt, bty, dg, dgy)
 
@@ -1894,25 +2136,29 @@
     (whole, part, bt, bty, dg, dgy, ot, oty, gy, gyy, at, aty, joined, joined_y) = refs[:14]
     whole_out, part_out, gate_o, output_o, attention_o = refs[14:19]
     bufs, gots, mine, theirs, ss, rs = refs[19:25]
-    slabs, slab_sem = refs[25:27]
-    gate_refs, output_refs, attention_refs = refs[27:37], refs[37:47], refs[47:57]
+    slabs, halves, slab_sem = refs[25:28]
+    gate_refs, output_refs, attention_refs = refs[28:38], refs[38:48], refs[48:58]
+    output_halves, attention_halves, half_sem = refs[58:]
     seq, me, x, c = place_now()
     nz = n // 2
     across = (seq, (1 - x) * 2 + c)
     beside = (seq, x * 2 + 1 - c)
-    gates, loads = gate_chain(nz, first, tiles, seq, me, bt, bty, dg, dgy, gate_o, slabs, slab_sem, gate_refs)
-    output_rows = ot.shape[0] // nz
-    attention_rows = at.shape[0] // nz
+    gates, loads = gate_chain(nz, first, tiles, seq, me, bt, bty, dg, dgy, gate_o, slabs, halves, slab_sem, gate_refs)
+    for i, (ref, to) in enumerate(
+        ((ot.at[:, seq % 2], output_halves.at[0]), (oty, output_halves.at[1]),
+         (at.at[:, seq % 2], attention_halves.at[0]), (aty, attention_halves.at[1]))
+    ):
+        load = pltpu.make_async_copy(ref, to, half_sem.at[i])
+        load.start()
+        loads.append(load)
     wide = joined.shape[1] // 2
 
     def output_partial(k, j):
-        rows = pl.ds(pl.multiple_of(k * output_rows, 16), output_rows)
-        return dot(ot[rows, :], gy[...]) + dot(oty[rows, :], gyy[...])
+        return dot(output_halves[0, k], gy[...]) + dot(output_halves[1, k], gyy[...])
 
     def attention_partial(k, j):
-        rows = pl.ds(pl.multiple_of(k * attention_rows, 16), attention_rows)
         cols = pl.ds(pl.multiple_of(j * wide, 128), wide)
-        return dot(at[rows, :], joined[:, cols]) + dot(aty[rows, :], joined_y[:, cols])
+        return dot(attention_halves[0, k], joined[:, cols]) + dot(attention_halves[1, k], joined_y[:, cols])
 
     outputs = Chain(
         nz, 1, seq, me, output_partial, lambda j, stage, sem: pltpu.make_async_copy(stage, output_o, sem), output_refs
@@ -1986,15 +2232,15 @@
     nz = n // 2
     rounds = int(math.log2(n))
     rows = whole.shape[0] + part.shape[0]
-    output_rows = ot.shape[0] // nz
-    attention_rows = at.shape[0] // nz
+    output_rows = ot.shape[2]
+    attention_rows = at.shape[2]
     return comm_call(
         functools.partial(finish_kernel, n, rounds, first, tiles),
         cid,
         [
             jax.ShapeDtypeStruct(whole.shape, F32),
             jax.ShapeDtypeStruct((GROUP,) + part.shape, F32),
-            jax.ShapeDtypeStruct((bt.shape[0] // nz, tiles * TILE), F32),
+            jax.ShapeDtypeStruct((bt.shape[2], tiles * TILE), F32),
             jax.ShapeDtypeStruct((output_rows, gy.shape[1]), F32),
             jax.ShapeDtypeStruct((attention_rows, joined.shape[1]), F32),
         ],
@@ -2008,8 +2254,13 @@
         ]
         + gate_scratch(nz, tiles, bt)
         + Chain.scratch(nz, 1, output_rows, gy.shape[1])
-        + Chain.scratch(nz, 2, attention_rows, joined.shape[1] // 2),
-        [VMEM] * 4 + [ANY] * 2 + [VMEM] * 8,
+        + Chain.scratch(nz, 2, attention_rows, joined.shape[1] // 2)
+        + [
+            pltpu.VMEM((2, nz) + ot.shape[2:], BF16),
+            pltpu.VMEM((2, nz) + at.shape[2:], BF16),
+            DMA((4,)),
+        ],
+        [VMEM] * 2 + [ANY] * 6 + [VMEM] * 2 + [ANY] * 2 + [VMEM] * 2,
         [VMEM, VMEM, ANY, ANY, ANY],
     )(whole, part, bt, bty, dg, dgy, ot, oty, gy, gyy, at, aty, joined, joined_y)
 
@@ -2031,14 +2282,6 @@
 
 def core_swap(value):
     return lax.ppermute(value, "fsdp", [(f, f ^ 1) for f in range(GROUP)])
-
-
-def slice_halves(value, n, y):
-    rows, width = value.shape
-    turned = value.T.reshape(n // 2, 2, width // n, rows)
-    here = lax.dynamic_index_in_dim(turned, y, 1, keepdims=False).reshape(width // 2, rows)
-    there = lax.dynamic_index_in_dim(turned, 1 - y, 1, keepdims=False).reshape(width // 2, rows)
-    return here, there
 
 
 def lanes(value, rows):
@@ -2065,11 +2308,8 @@
     norm_gains,
     cotangent,
 ):
-    seq = lax.axis_index("seq")
     me = lax.axis_index("fsdp")
-    is_gate = me < 2
     c = me % 2
-    y = seq % 2
     width = tokens.shape[2]
     part = width // GROUP
     rows = GROUP * tokens.shape[1]
@@ -2082,51 +2322,46 @@
     def blocks_to_rows(blocks):
         return jnp.concatenate([blocks[i] for i in range(GROUP)], axis=1)
 
-    def own_rows(value):
-        return lax.dynamic_slice_in_dim(value, me * own, own, 0)
-
     gain = 1.0 + norm_gains
     place = token_order[0].astype(F32)
     document = doc_ids[0].astype(F32)
     meta = jnp.stack([document, place, jnp.where(padding[0] == 1, document, -1.0)] + [document] * 5)
 
-    token_blocks, own_meta = group_gather(1, [tokens[0], meta], parts=[4, 1])
-    inputs = token_blocks.reshape(rows, width).astype(F32)
-    turn = own_meta[:, 1, :].reshape(rows, 1) * (
-        BASE ** (-2.0 * jnp.arange(DH // 2).astype(F32) / DH)
-    )[None, :]
-    cosine = jnp.cos(turn)
-    sine = jnp.sin(turn)
-    first_inverse = rms_inverse(inputs)
-    first_input = (inputs * first_inverse * gain[0]).astype(BF16)
-    query_raw = dot(first_input, query_code)
-    pair_raw = dot(first_input, key_value_code)
+    def to_blocks(value):
+        return value.reshape(own, GROUP, part).transpose(1, 0, 2)
+
     my_query_scale = mine(query_scale)
     my_pair_scale = mine(key_value_scale)
-    pair_cosine = jnp.where(is_gate, cosine, 1.0)
-    pair_sine = jnp.where(is_gate, sine, 0.0)
-    query = rotate(
-        (query_raw * my_query_scale).reshape(rows, 2, DH), cosine[:, None], sine[:, None]
-    ).astype(BF16).reshape(rows, 2 * DH)
-    pair_plain = pair_raw * my_pair_scale
-    heads = jnp.stack(
-        [rotate(pair_plain[:, j * DH : (j + 1) * DH], pair_cosine, pair_sine) for j in range(2)]
-    ).astype(BF16)
-    cot_columns = cotangent[0].reshape(own, GROUP, part).transpose(1, 0, 2).reshape(rows, part)
-    pairs, metas, cot_blocks = keys_gather(2, n, heads, own_meta, cot_columns)
+    token_cols = to_blocks(tokens[0])
+    cot_cols = to_blocks(cotangent[0])
+    rates = BASE ** (-2.0 * jnp.arange(DH // 2).astype(F32) / DH)
+    (
+        token_blocks, cot_blocks, own_meta, metas, pairs, query, query_raw, pair_raw, cosine, sine, first_turned
+    ) = front(
+        1,
+        n,
+        token_cols.reshape(rows, part),
+        cot_cols.reshape(rows, part),
+        meta,
+        gain[0].reshape(GROUP, 1, part),
+        rates[None],
+        my_query_scale[None],
+        my_pair_scale[None],
+        query_code,
+        key_value_code,
+    )
 
     mixed_low, mixed, mass = attend(n, query, pairs, own_meta, metas)
-    (mixed_rows,) = group_gather(3, [mixed_low], columns=[True])
-    branch_own = dot(mixed_rows, output_code).astype(BF16)
-    (branch_blocks,) = group_gather(4, [branch_own])
-    branch_raw = blocks_to_rows(branch_blocks).astype(F32)
-    branch = branch_raw * output_scale
-    second_inverse = rms_inverse(branch)
-    middle = inputs + branch * second_inverse * gain[1]
-    third_inverse = rms_inverse(middle)
-    second_input = (middle * third_inverse * gain[2]).astype(BF16)
-
-    halves = [slice_halves(v, n, y) for v in (second_input, mixed_rows, first_input)]
+    second_input, branch_own, my_middle, mixed_turned, second_turned = branch_forward(
+        3,
+        mixed_low,
+        output_code.T,
+        token_blocks,
+        output_scale.reshape(GROUP, 1, part),
+        gain[1].reshape(GROUP, 1, part),
+        gain[2].reshape(GROUP, 1, part),
+    )
+
     my_gate_scale = mine(gate_up_scale)
     columns = gate_up_code.shape[1]
     tiles = columns // TILE
@@ -2140,12 +2375,12 @@
         cot_blocks,
         gain[3].reshape(GROUP, 1, part),
         down_scale.reshape(GROUP, 1, part),
-        [half[1] for half in halves],
+        [second_turned, mixed_turned, first_turned],
     )
-    second_pair, mixed_pair, first_pair = [(half[0], rider) for half, rider in zip(halves, riders)]
-    my_middle = own_rows(middle)
-    my_down = blocks_to_rows(lax.dynamic_slice_in_dim(down_blocks, me * own, own, 1)).astype(F32) * down_scale
-    result = (my_middle + my_down * rms_inverse(my_down) * gain[3]).astype(BF16)
+    second_pair, mixed_pair, first_pair = zip((second_turned, mixed_turned, first_turned), riders)
+    my_down = lax.dynamic_slice_in_dim(down_blocks, me * own, own, 1).astype(F32) * down_scale.reshape(GROUP, 1, part)
+    down_inverse = lax.rsqrt(jnp.mean(my_down * my_down, axis=(0, 2), keepdims=True) + EPSILON)
+    result = blocks_to_rows((my_middle + my_down * down_inverse * gain[3].reshape(GROUP, 1, part)).astype(BF16))
     grad_gate_up, grad_gate_up_y, gate_sums, grad_second_input, down_grad = ffn_backward(
         6, n, grad_down, down_code.T, gate_up_code, gate_scales, gate_up, hidden, hidden_y
     )
@@ -2172,18 +2407,14 @@
     gate_pairs = second_pair + (grad_gate_up, grad_gate_up_y)
     tiles_one, tiles_two = (4, 3) if n == 8 else (0, 0)
     tiles_three = tiles - tiles_one - tiles_two
-
-    def to_blocks(value):
-        return value.reshape(own, GROUP, part).transpose(1, 0, 2)
-
     grad_middle, branch_sums, grad_branch, grad_branch_y, grad_query, grad_pairs, gate_one = branch_back(
         7,
         n,
         tiles_one,
         grad_second_input,
-        to_blocks(my_middle),
-        lax.dynamic_slice_in_dim(branch_blocks, me * own, own, 1),
-        to_blocks(cotangent[0]),
+        my_middle,
+        branch_own,
+        cot_cols,
         gain[1].reshape(GROUP, 1, part),
         gain[2].reshape(GROUP, 1, part),
         output_scale.reshape(GROUP, 1, part),
@@ -2224,6 +2455,9 @@
         scale_query = key_sums[0]
         scale_pair = key_sums[1]
     else:
+        is_key = me < 2
+        pair_cosine = jnp.where(is_key, cosine, 1.0)
+        pair_sine = jnp.where(is_key, sine, 0.0)
         grad_heads = keys_reduce(9, n, grad_pairs).astype(F32)
         grad_query_full = rotate(
             grad_query.reshape(rows, 2, DH), cosine[:, None], -sine[:, None]
@@ -2264,11 +2498,11 @@
         whole_total, part_total = totals(11, n, wholes, part_rows)
 
         def weight_sum(left, right):
-            return lax.psum_scatter(contract_first(left, right), "seq", scatter_dimension=0, tiled=True)
-
-        gate_grad = weight_sum(second_input, grad_gate_up)
-        output_grad = weight_sum(mixed_rows, grad_branch)
-        attention_grad = weight_sum(first_input, joined)
+            return lax.psum_scatter(dot(left.reshape(-1, rows), right), "seq", scatter_dimension=0, tiled=True)
+
+        gate_grad = weight_sum(second_turned, grad_gate_up)
+        output_grad = weight_sum(mixed_turned, grad_branch)
+        attention_grad = weight_sum(first_turned, joined)
     whole_total = whole_total.reshape(-1)
     part_total = part_total.reshape(GROUP, -1)
     pieces = []

time: 906 us -> 821 us (0.906)
  local copies, waits for them, and re-layouts: 93.4 us -> 29.7 us
  other arithmetic: 34.6 us -> 13 us
    unnamed x62 -> x38, local copies, waits for them, and re-layouts: 23.1 us -> 6.36 us
    dynamic_slice x5 -> x0, local copies, waits for them, and re-layouts: 15.8 us -> none  [the longest x3 13.4 us: slice_halves(): lax.dynamic_index_in_dim(turned, y, 1, keepdims=False)]
    pallas_call x4 -> x2, Pallas kernels: 124 us -> 135 us  [the longest x1 87.8 us: front(): comm_call(functools.partial(front_kernel, n), cid, [blocks, blocks, jax.S...]
    concatenate x4 -> x2, local copies, waits for them, and re-layouts: 11.3 us -> 1.66 us  [blocks_to_rows(): return jnp.concatenate([blocks[i] for i in range(GROUP)], axis=1)]
    reduce_sum x5 -> x1, other arithmetic: 9.38 us -> 0.2 us  [rms_inverse(): return lax.rsqrt(jnp.mean(value * value, axis=-1, keepdims=True) + EPSILON)]
where the time goes in v4:
time: 821 us; the launch traced here: 812 us
  Pallas kernels  768 us (94%)
  local copies, waits for them, and re-layouts  29.7 us (4%)
  other arithmetic  13 us (2%)
    pallas_call x1, Pallas kernels, finish(): comm_call(functools.partial(finish_kernel, n, rounds, first, tiles), cid,...  146 us
    pallas_call x1, Pallas kernels, ffn_backward(): comm_call(functools.partial(ffn_backward_kernel, tiles, nz, chained), cid...  143 us
    pallas_call x1, Pallas kernels, ffn_forward(): comm_call(functools.partial(ffn_forward_kernel, tiles, count), cid, [jax....  139 us
    pallas_call x1, Pallas kernels, keys_back(): comm_call(functools.partial(keys_back_kernel, n, first, tiles), cid, [joi...  105 us
    pallas_call x1, Pallas kernels, branch_back(): comm_call(functools.partial(branch_back_kernel, n, tiles), cid, [block(F3...  94.5 us
    pallas_call x1, Pallas kernels, front(): comm_call(functools.partial(front_kernel, n), cid, [blocks, blocks, jax.S...  87.8 us
    pallas_call x1, Pallas kernels, branch_forward(): comm_call(branch_kernel, cid, [jax.ShapeDtypeStruct((GROUP, rows, part),...  46.8 us

profile of v4, /device:TPU:0, one launch (start us, length us, event | category | flops | bytes accessed | tf_op | source)
XLA Modules:
  0.0 811.7 jit_solution(1456970039350572244)
XLA Ops:
  0.7 1.4 copy.32
  2.1 1.1 copy.33
  3.2 0.3 copy.34
  3.5 1.1 copy.35
  4.6 0.6 stack.2.refs_2_
  5.3 0.1 slice_reduce_fusion.4
  5.4 0.7 reshape_squeeze.29.refs_3_
  6.0 0.5 multiply_power_fusion.refs_4_
  6.6 1.3 dynamic_slice.12
  7.9 1.3 dynamic_slice.13
  9.2 87.8 %shard_map.255 = (bf16[4,512,576]{2,1,0:T(8,128)(2,1)}, bf16[4,512,576]{2,1,0:T(8,128)(2,1)}, f32[4,8,128]{2,1,0:T(8,128)}, f32[8,4,8,128]{3,2,1,0:T(8,128)}, bf...) custom-call(bf16[512,576]{1,0:T(8,128)(2,1)} %bitcast.66, ...), custom_call_target="tpu_custom_call" | custom-call | tf_op jit(solution)/shard_map/pallas_call | solution.py:612
  97.1 0.0 copy-start.11
  97.1 6.2 shard_map.256
  103.3 0.0 copy-done.11
  103.3 0.7 reshape.126.scale.refs_6_
  104.0 0.7 reshape_squeeze.30.g2.refs_4_
  104.7 0.7 reshape_squeeze.31.g3.refs_5_
  105.4 46.8 %shard_map.257 = (bf16[4,512,576]{2,1,0:T(8,128)(2,1)}, bf16[4,128,576]{2,1,0:T(8,128)(2,1)}, f32[4,128,576]{2,1,0:T(8,128)}, bf16[4,2,256,512]{3,2,1,0:T(8,128)(2,1)}, bf16[4,2,288,512]{3,2,1,0:T(8,128)(2,1)}) custom-call(bf16[512,512]{1,0:T(8,128)(2,1)} %get-tuple-element.67.low, bf16[576,2048]{1,0:T(8,128)(2,1)} %bitcast.61, ...), custom_call_target="tpu_custom_call" | custom-call | tf_op jit(solution)/shard_map/pallas_call | solution.py:772
  152.2 0.1 mul.94
  152.3 0.0 copy-done.7
  152.3 0.1 mul.88
  152.4 0.1 dynamic_slice.14
  152.4 0.6 reshape.127.refs_2_.refs_3_
  153.1 0.7 reshape_squeeze.32.refs_5_
  153.7 0.7 reshape.128.refs_6_
  154.4 138.5 %shard_map.258 = (bf16[2,12,512,384]{3,2,1,0:T(8,128)(2,1)}, bf16[12,512,384]{2,1,0:T(8,128)(2,1)}, bf16[12,512,384]{2,1,0:T(8,128)(2,1)}, bf16[4,512,576]{2,1,0...) custom-call(bf16[4,512,576]{2,1,0:T(8,128)(2,1)} %get-tuple-element., ...), custom_call_target="tpu_custom_call" | custom-call | tf_op jit(solution)/shard_map/pallas_call | solution.py:1294
  292.9 1.4 multiply_reduce_fusion
  294.3 0.0 copy-done.1
  294.3 1.4 add_convert_fusion
  295.7 0.1 slice_bitcast_fusion.4
  295.8 1.1 concatenate.27
  296.9 142.9 %shard_map.259 = (bf16[512,4608]{1,0:T(8,128)(2,1)}, bf16[512,4608]{1,0:T(8,128)(2,1)}, f32[12,8,384]{2,1,0:T(8,128)}, f32[4,128,576]{2,1,0:T(8,128)}, f32[3,384,576]{2,1,0:T(8,128)}) custom-call(bf16[512,576]{1,0:T(8,128)(2,1)} %get-tuple-element.76.refs_0_, bf16[576,9216]{1,0:T(8,128)(2,1)} %bitcast.60, bf16[2304,4608]{1,0:T(8,128)(2,1)} %refs_2_.1, ...), custom_call_target="tpu_custom_call" | custom-call | tf_op jit(solution)/shard_map/pallas_call | solution.py:1586
  439.9 94.5 %shard_map.260 = (f32[4,128,576]{2,1,0:T(8,128)}, f32[4,8,576]{2,1,0:T(8,128)}, bf16[4,128,576]{2,1,0:T(8,128)(2,1)}, bf16[4,128,576]{2,1,0:T(8,128)(2,1)}, f32[...) custom-call(f32[4,128,576]{2,1,0:T(8,128)} %get-tuple-element.80.refs_0_, ...), custom_call_target="tpu_custom_call" | custom-call | tf_op jit(solution)/shard_map/pallas_call | solution.py:1833
  534.4 1.4 slice_bitcast_fusion
  535.8 0.5 concatenate.28
  536.3 0.0 copy-start
  536.3 105.1 %shard_map.261 = (bf16[512,1024]{1,0:T(8,128)(2,1)}, bf16[512,1024]{1,0:T(8,128)(2,1)}, f32[128,2304]{1,0:T(8,128)}, f32[8,512]{1,0:T(8,128)}, f32[288,1152]{1,0:T(8,128)}) custom-call(bf16[8,2,512,256]{3,2,1,0:T(8,128)(2,1)} %get-tuple-element.88.refs_0_, f32[512,512]{1,0:T(8,128)} %get-tuple-element.89.refs_1_, f32[512,512]{1,0:T(8,128)} %get-tuple-element.90.refs_2_, ...), custom_call_target="tpu_custom_call" | custom-call | tf_op jit(solution)/shard_map/pallas_call | solution.py:2109
  641.5 0.2 fusion.9
  641.7 1.8 fusion.8
  643.5 1.4 fusion.7
  644.9 1.1 slice_reduce_fusion.3
  646.0 0.1 concatenate.32
  646.1 0.1 concatenate.31
  646.2 0.1 concatenate.30
  646.3 0.6 pad_maximum_fusion.1.refs_0_
  646.9 0.8 fusion.12
  647.7 1.0 slice_reduce_fusion
  648.7 0.1 dynamic-slice_divide_fusion
  648.8 0.8 slice_reduce_fusion.8
  649.6 0.1 concatenate.34
  649.7 0.6 pad_bitcast_fusion.refs_1_
  650.3 145.9 %shard_map.262 = (f32[72,128]{1,0:T(8,128)}, f32[4,56,128]{2,1,0:T(8,128)}, f32[288,1920]{1,0:T(8,128)}, f32[256,576]{1,0:T(8,128)}, f32[288,1024]{1,0:T(8,128)}) custom-call(f32[72,128]{1,0:T(8,128)} %pad_maximum_fusion.1.refs_0_, f32[56,128]{1,0:T(8,128)} %pad_bitcast_fusion.refs_1_, ...), custom_call_target="tpu_custom_call" | custom-call | tf_op jit(solution)/shard_map/pallas_call | solution.py:2237
  796.2 2.4 fusion.10
  798.6 1.0 copy.36
  799.7 5.5 pad_maximum_fusion
  805.2 2.3 copy.37
  807.5 0.6 copy.39
  808.1 0.6 copy.40
  808.7 0.6 slice_bitcast_fusion.9
  809.4 0.7 reshape.136
  810.0 0.1 fusion.11
  810.1 0.7 reshape.137
  810.8 0.1 reshape.138
  810.9 0.6 reshape.139
  (38 shorter events, 0.1 us)
Async XLA Ops:
  0.6 2.5 copy-start.5
  3.2 1.4 copy-start.13
  3.2 1.4 copy-start.12
  3.2 1.4 copy-start.14
  3.2 2.1 copy-start.9
  97.1 6.3 copy-start.11
  105.3 46.9 %copy-start.7 = (f32[2304]{0:T(1024)S(1)}, f32[2304]{0:T(1024)}, u32[]{:S(2)}) copy-start(f32[2304]{0:T(1024)} %param.29) | copy-start | bytes 27652
  105.3 47.0 %copy-start.10 = (f32[18432]{0:T(1024)S(1)}, f32[18432]{0:T(1024)}, u32[]{:S(2)}) copy-start(f32[18432]{0:T(1024)} %param.28) | copy-start | bytes 221188
  154.4 139.9 %copy-start.1 = (f32[4,128,576]{2,1,0:T(8,128)S(1)}, f32[4,128,576]{2,1,0:T(8,128)}, u32[]{:S(2)}) copy-start(f32[4,128,576]{2,1,0:T(8,128)} %get-tuple-element.69.refs_1_) | copy-start | bytes 3538948
  536.3 105.2 %copy-start = (bf16[1,128,2304]{2,1,0:T(8,128)(2,1)S(1)}, bf16[1,128,2304]{2,1,0:T(8,128)(2,1)}, u32[]{:S(2)}) copy-start(bf16[1,128,2304]{2,1,0:T(8,128)(2,1)} %param.16) | copy-start | bytes 1769476
  641.4 2.0 copy-start.2
  796.2 2.4 copy-start.4
  799.7 5.5 copy-start.3
  805.2 2.3 copy-start.6
  805.2 3.6 copy-start.8

commit v5 on v4

--- a/solution.py
+++ b/solution.py
@@ -348,7 +348,7 @@
 
 def turned(block, unit, to):
     half = to.shape[1]
-    flat = contract_first(block, unit[...])
+    flat = contract_last(unit[...], block)
     to[0] = flat[:half].astype(BF16)
     to[1] = flat[half:].astype(BF16)
 
@@ -632,7 +632,7 @@
             pltpu.VMEM((deep, wide), BF16),
             pltpu.VMEM((2, rows, DH), BF16),
             pltpu.VMEM((GROUP,) + meta.shape, F32),
-            pltpu.VMEM((rows, rows), BF16),
+            pltpu.VMEM((part, part), BF16),
             pltpu.VMEM(turned_shape, BF16),
             DMA((2,)), DMA((GROUP,)), DMA((GROUP,)), DMA, DMA, DMA((GROUP,)), DMA((GROUP,)), DMA((GROUP - 1,)),
             DMA((GROUP - 1,)), DMA((2,)), DMA((2,)), DMA((2,)), DMA((n - 1,)), DMA((n - 1,)), DMA((nz,)), DMA((nz,)),
@@ -644,8 +644,8 @@
     )(tok, cot, meta, g1, rates, q_scale, p_scale, wq, wkv)
 
 
-def branch_kernel(low, wo, toks, scale, g2, g3, b_o, raw_o, mid_o, ot_o, bt_o, ob, pb, bb, acc, unit, ot, bt,
-                  xs, xr, cs, cr, fs, fr, gxs, gxr, gcs, gcr, gfs, gfr, local, os):
+def branch_kernel(low, wo, toks, scale, g2, g3, b_o, raw_o, mid_o, ot_o, bt_o, ob, pb, bb, acc, unit, bt,
+                  xs, xr, cs, cr, fs, fr, gxs, gxr, gcs, gcr, gfs, gfr, local, os, hos):
     seq, me, x, c = place_now()
     across = (seq, (1 - x) * 2 + c)
     beside = (seq, x * 2 + 1 - c)
@@ -705,10 +705,13 @@
         copy = remote(piece, piece, gcs.at[k], gcr.at[k], beside)
         copy.start()
         core.append(copy)
+    head_outs = []
     for j in js:
-        turned(ob[:, j * heads : (j + 1) * heads], unit, ot.at[j])
-    ot_out = pltpu.make_async_copy(ot, ot_o, os.at[0])
-    ot_out.start()
+        for i in range(2):
+            cols = pl.ds(j * heads + i * (heads // 2), heads // 2)
+            copy = pltpu.make_async_copy(ob.at[:, cols], ot_o.at[j, i], hos.at[j, i])
+            copy.start()
+            head_outs.append(copy)
     passed = []
     for k in range(parts):
         over[k].wait_recv()
@@ -758,7 +761,7 @@
     bt_out.start()
     for copy in sends + forwards + over + core + passed + [to_core]:
         copy.wait_send()
-    for copy in (ot_out, b_out, raw_out, bt_out):
+    for copy in head_outs + [b_out, raw_out, bt_out]:
         copy.wait()
 
 
@@ -767,7 +770,7 @@
     part = wo.shape[0]
     own = rows // GROUP
     turned_b = (GROUP, 2, part // 2, rows)
-    turned_o = (GROUP, 2, heads // 2, rows)
+    slices = (GROUP, 2, rows, heads // 2)
     four = DMA((4,))
     return comm_call(
         branch_kernel,
@@ -776,7 +779,7 @@
             jax.ShapeDtypeStruct((GROUP, rows, part), BF16),
             jax.ShapeDtypeStruct((GROUP, own, part), BF16),
             jax.ShapeDtypeStruct((GROUP, own, part), F32),
-            jax.ShapeDtypeStruct(turned_o, BF16),
+            jax.ShapeDtypeStruct(slices, BF16),
             jax.ShapeDtypeStruct(turned_b, BF16),
         ],
         [
@@ -784,10 +787,9 @@
             pltpu.VMEM((GROUP, rows, part), BF16),
             pltpu.VMEM((GROUP, rows, part), BF16),
             pltpu.VMEM((rows, part), F32),
-            pltpu.VMEM((rows, rows), BF16),
-            pltpu.VMEM(turned_o, BF16),
+            pltpu.VMEM((part, part), BF16),
             pltpu.VMEM(turned_b, BF16),
-            four, four, DMA, DMA, four, four, four, four, four, four, four, four, DMA, four,
+            four, four, DMA, DMA, four, four, four, four, four, four, four, four, DMA, four, DMA((GROUP, 2)),
         ],
         [VMEM] * 6,
         [ANY, ANY, VMEM, ANY, ANY],
@@ -888,12 +890,17 @@
 
 
 class Chain:
-    def __init__(self, nz, count, seq, me, partial, keep, scratch):
+    def __init__(self, nz, count, seq, me, partial, keep, landing, scratch):
         self.nz, self.count, self.partial, self.keep = nz, count, partial, keep
         self.z = seq // 2
         self.right, self.left = (seq + 2, me), (seq - 2, me)
-        (self.out_r, self.out_l, self.got_r, self.got_l, self.stage, self.ss_r, self.sr_r, self.ss_l, self.sr_l,
-         self.keep_sem) = scratch
+        self.got_r, self.got_l = landing
+        (self.out_r, self.out_l, self.in_r, self.in_l, self.stage, self.ss_r, self.sr_r, self.ss_l, self.sr_l,
+         self.keep_sem, self.load_sem) = scratch
+
+    @staticmethod
+    def landing(nz, count, rows, width):
+        return [jax.ShapeDtypeStruct((count, nz - 1, rows, width), BF16)] * 2
 
     @staticmethod
     def scratch(nz, count, rows, width):
@@ -902,8 +909,8 @@
         sems = DMA((count, hops))
         return [
             pltpu.VMEM((hops,) + message, BF16), pltpu.VMEM((hops,) + message, BF16),
-            pltpu.VMEM((count, hops) + message, BF16), pltpu.VMEM((count, hops) + message, BF16),
-            pltpu.VMEM((2,) + message, F32), sems, sems, sems, sems, DMA((2,)),
+            pltpu.VMEM(message, BF16), pltpu.VMEM(message, BF16),
+            pltpu.VMEM((2,) + message, F32), sems, sems, sems, sems, DMA((2,)), DMA((2,)),
         ]
 
     def copy_right(self, j, s, peer):
@@ -916,21 +923,33 @@
             self.out_l.at[s - 1], self.got_l.at[j, s - 1], self.ss_l.at[j, s - 1], self.sr_l.at[j, s - 1], peer
         )
 
+    def load_right(self, j, s):
+        return pltpu.make_async_copy(self.got_r.at[j, s - 1], self.in_r, self.load_sem.at[0])
+
+    def load_left(self, j, s):
+        return pltpu.make_async_copy(self.got_l.at[j, s - 1], self.in_l, self.load_sem.at[1])
+
     def step(self, j, s):
         z, nz = self.z, self.nz
 
-        def one(go, copy, out, got, to, source, first):
+        def one(go, copy, load, out, into, to, source, first):
+            more = (s > 1) & jnp.logical_not(first)
+
+            @pl.when(more)
+            def _():
+                copy(j, s - 1, source).wait_recv()
+                load(j, s - 1).start()
+
             @pl.when(j > 0)
             def _():
                 copy(j - 1, s, to).wait_send()
 
             total = self.partial(go, j)
-            more = (s > 1) & jnp.logical_not(first)
 
             @pl.when(more)
             def _():
-                copy(j, s - 1, source).wait_recv()
-                out[s - 1] = (total + got[j, s - 2].astype(F32)).astype(BF16)
+                load(j, s - 1).wait()
+                out[s - 1] = (total + into[...].astype(F32)).astype(BF16)
 
             @pl.when(jnp.logical_not(more))
             def _():
@@ -943,11 +962,11 @@
 
         @pl.when(go_right < nz)
         def _():
-            one(go_right, self.copy_right, self.out_r, self.got_r, self.right, self.left, z == 0)
+            one(go_right, self.copy_right, self.load_right, self.out_r, self.in_r, self.right, self.left, z == 0)
 
         @pl.when(go_left >= 0)
         def _():
-            one(go_left, self.copy_left, self.out_l, self.got_l, self.left, self.right, z == nz - 1)
+            one(go_left, self.copy_left, self.load_left, self.out_l, self.in_l, self.left, self.right, z == nz - 1)
 
     def end(self, j):
         z, nz = self.z, self.nz
@@ -957,17 +976,27 @@
         def _():
             self.keep(j - 2, self.stage.at[k], self.keep_sem.at[k]).wait()
 
+        @pl.when(z > 0)
+        def _():
+            self.copy_right(j, nz - 1, self.left).wait_recv()
+            self.load_right(j, nz - 1).start()
+
+        @pl.when(z < nz - 1)
+        def _():
+            self.copy_left(j, nz - 1, self.right).wait_recv()
+            self.load_left(j, nz - 1).start()
+
         self.stage[k] = self.partial(z, j)
 
         @pl.when(z > 0)
         def _():
-            self.copy_right(j, nz - 1, self.left).wait_recv()
-            self.stage[k] += self.got_r[j, nz - 2].astype(F32)
+            self.load_right(j, nz - 1).wait()
+            self.stage[k] += self.in_r[...].astype(F32)
 
         @pl.when(z < nz - 1)
         def _():
-            self.copy_left(j, nz - 1, self.right).wait_recv()
-            self.stage[k] += self.got_l[j, nz - 2].astype(F32)
+            self.load_left(j, nz - 1).wait()
+            self.stage[k] += self.in_l[...].astype(F32)
 
         self.keep(j, self.stage.at[k], self.keep_sem.at[k]).start()
 
@@ -975,25 +1004,28 @@
         hops = self.nz - 1
 
         def unit(u, carry):
-            j = u // hops
+            slot = u // hops
             s = u % hops + 1
-            self.step(j, s)
-
-            @pl.when((s == hops) & (j > 0))
+            j = slot - (s - 1)
+
+            @pl.when((j >= 0) & (j < self.count))
             def _():
-                self.end(j - 1)
+                self.step(j, s)
+
+            @pl.when((s == hops) & (slot >= hops))
+            def _():
+                self.end(slot - hops)
 
             return carry
 
         lax.fori_loop(first, last, unit, 0)
 
     def units(self):
-        return self.count * (self.nz - 1)
+        return (self.count + self.nz - 1) * (self.nz - 1)
 
     def finish(self):
         z, nz = self.z, self.nz
         last = self.count - 1
-        self.end(jnp.int32(last))
         for j in range(max(0, last - 1), last + 1):
             self.keep(j, self.stage.at[j % 2], self.keep_sem.at[j % 2]).wait()
         for s in range(1, nz):
@@ -1022,6 +1054,35 @@
         pl.semaphore_signal(barrier, inc=1, device_id=(seq + 2, me), device_id_type=MESH)
 
     pl.semaphore_wait(barrier, len(others) + 1 + jnp.where(z > 0, 1, 0) + jnp.where(z < nz - 1, 1, 0))
+
+
+def gate_chain(nz, first, count, seq, me, bt, bty, dg, dgy, out, landing, slabs, halves, slab_sem, scratch):
+    loads = [pltpu.make_async_copy(bt.at[:, seq % 2], halves.at[0], slab_sem.at[2])]
+    loads.append(pltpu.make_async_copy(bty, halves.at[1], slab_sem.at[3]))
+    for i, ref in enumerate((dg, dgy)):
+        loads.append(
+            pltpu.make_async_copy(ref.at[:, pl.ds(first * TILE, count * TILE)], slabs.at[i], slab_sem.at[i])
+        )
+
+    def partial(k, j):
+        cols = pl.ds(pl.multiple_of(j * TILE, 128), TILE)
+        return dot(halves[0, k], slabs[0, :, cols]) + dot(halves[1, k], slabs[1, :, cols])
+
+    def keep(j, stage, sem):
+        return pltpu.make_async_copy(stage, out.at[:, pl.ds(pl.multiple_of(j * TILE, 128), TILE)], sem)
+
+    return Chain(nz, count, seq, me, partial, keep, landing, scratch), loads
+
+
+def gate_landing(nz, count, bt):
+    return Chain.landing(nz, count, bt.shape[2], TILE)
+
+
+def gate_scratch(nz, count, bt):
+    rows = bt.shape[3]
+    return [
+        pltpu.VMEM((2, rows, count * TILE), BF16), pltpu.VMEM((2, nz) + bt.shape[2:], BF16), DMA((4,))
+    ] + Chain.scratch(nz, count, bt.shape[2], TILE)
 
 
 def levels(code, step):
@@ -1049,17 +1110,17 @@
     b, wgu, gs, wd, cots, g3, ds = refs[:7]
     refs = refs[7:]
     rider_in, refs = refs[:riders], refs[riders:]
-    gu_o, hid_o, hidy_o, down_o, gf_o, sums_o = refs[:6]
-    refs = refs[6:]
+    gu_o, hid_o, hidy_o, down_o, gf_o, gft_o, sums_o, lev_o, levd_o = refs[:9]
+    refs = refs[9:]
     rider_out, refs = refs[:riders], refs[riders:]
-    (gu, hid, hidy, wbuf, wlev, dbuf, dlev, acc, downs, wsem, dsem, xs, xr, hs, hr, ys, yr, fs, fr,
-     gxs, gxr, gcs, gcr, gfs, gfr, rs, rr, ks, outs) = refs
+    (both, hid, unit, wbuf, wlev, dbuf, dlev, acc, downs, wsem, dsem, lsem, ldsem, osem, xs, xr, oks, hs, hr, ks,
+     ys, yr, fs, fr, gxs, gxr, gcs, gcr, gfs, gfr, rs, rr, outs) = refs
     seq, me, x, c = place_now()
     y = seq % 2
     across = (seq, (1 - x) * 2 + c)
     beside = (seq, x * 2 + 1 - c)
     beyond = (seq + 1 - 2 * y, me)
-    rows, tw = gu.shape[2:]
+    rows, tw = both.shape[2:]
     part = b.shape[2]
     deep = GROUP * part
     per = tiles // 4
@@ -1081,13 +1142,31 @@
     greet([across, beside, beyond])
     travellers = []
     for i in range(riders):
-        copy = remote(rider_in[i].at[:, 1 - y], rider_out[i], rs.at[i], rr.at[i], beyond)
+        share = pl.ds(2 * c, 2)
+        copy = remote(rider_in[i].at[share, 1 - y], rider_out[i].at[share], rs.at[i, 0], rr.at[i, 0], beyond)
         copy.start()
-        travellers.append(copy)
+        got = rider_out[i].at[share]
+        travellers.append((copy, remote(got, got, rs.at[i, 1], rr.at[i, 1], beside)))
     acc[...] = jnp.zeros_like(acc)
+    fill_unit(unit)
 
     def to_x(t):
-        return remote(gu.at[x, t], gu.at[x, t], xs.at[t], xr.at[t], across)
+        return remote(both.at[t % 3, x], gu_o.at[x, t], xs.at[t], xr.at[t], across)
+
+    def from_x(t):
+        return remote(both.at[t % 3, x], gu_o.at[1 - x, t], xs.at[t], xr.at[t], across)
+
+    def keep_own(t):
+        return pltpu.make_async_copy(both.at[t % 3, x], gu_o.at[x, t], oks.at[t])
+
+    def load_other(t):
+        return pltpu.make_async_copy(gu_o.at[1 - x, t], both.at[t % 3, 1 - x], osem.at[t % 2])
+
+    def keep_level(t):
+        return pltpu.make_async_copy(wlev.at[t % 2], lev_o.at[t], lsem.at[t % 2])
+
+    def keep_down(t, half):
+        return pltpu.make_async_copy(dlev.at[t % 2, half], levd_o.at[half, t], ldsem.at[t % 2, half])
 
     def to_core(t):
         return remote(hid.at[c * tiles + t], hid.at[c * tiles + t], hs.at[t], hr.at[t], beside)
@@ -1095,80 +1174,102 @@
     def slot(t, core):
         return (2 * core + t // (2 * per)) * per + t % per
 
+    def keep(t, core, i):
+        return pltpu.make_async_copy(hid.at[core * tiles + t], hid_o.at[slot(t, core)], ks.at[i, t])
+
     def to_y(t):
-        return remote(hid.at[c * tiles + t], hidy.at[slot(t, c)], ys.at[t], yr.at[t], beyond)
-
-    def keep(t, i, core):
-        return pltpu.make_async_copy(hid.at[core * tiles + t], hid_o.at[slot(t, core)], ks.at[i, t])
+        return remote(hid.at[c * tiles + t], hidy_o.at[slot(t, c)], ys.at[t], yr.at[t], beyond)
+
+    def for_mine(t):
+        return (t // per) % 2 == y
 
     def wide(t):
         load_up(t).wait()
 
+        @pl.when(t >= 2)
+        def _():
+            keep_level(t - 2).wait()
+
         def level(span):
-            wlev[span, :] = levels(wbuf[t % 2, span, :], 16.0)
+            wlev[t % 2, span, :] = levels(wbuf[t % 2, span, :], 16.0)
 
         strips(deep // 128, 128, level)
+        keep_level(t).start()
 
         @pl.when(t + 2 < tiles)
         def _():
             load_up(t + 2).start()
 
+        @pl.when(t >= 3)
+        def _():
+            to_x(t - 3).wait_send()
+            keep_own(t - 3).wait()
+
         scale = gs[t]
 
         def product(span):
-            total = dot(b[0, span, :], wlev[0:part, :])
+            total = dot(b[0, span, :], wlev[t % 2, 0:part, :])
             for j in range(1, GROUP):
-                total = total + dot(b[j, span, :], wlev[j * part : (j + 1) * part, :])
-            gu[x, t, span, :] = (total * scale).astype(BF16)
+                total = total + dot(b[j, span, :], wlev[t % 2, j * part : (j + 1) * part, :])
+            both[t % 3, x, span, :] = (total * scale).astype(BF16)
 
         strips(rows // 256, 256, product)
         to_x(t).start()
+        keep_own(t).start()
+
+    def arrive(t):
+        from_x(t).wait_recv()
+        load_other(t).start()
 
     def middle(t):
-        to_x(t).wait_recv()
+        load_other(t).wait()
 
         def body(span):
-            gate = gu[0, t, span, :].astype(F32)
-            up = gu[1, t, span, :].astype(F32)
+            gate = both[t % 3, 0, span, :].astype(F32)
+            up = both[t % 3, 1, span, :].astype(F32)
             hid[c * tiles + t, span, :] = (gelu_parts(gate)[0] * up).astype(BF16)
 
         strips(rows // 64, 64, body)
         to_core(t).start()
 
-        @pl.when((t // per) % 2 != y)
+        @pl.when(for_mine(t))
+        def _():
+            keep(t, c, 0).start()
+
+        @pl.when(jnp.logical_not(for_mine(t)))
         def _():
             to_y(t).start()
-
-        @pl.when((t // per) % 2 == y)
-        def _():
-            keep(t, 0, c).start()
 
     def narrow(t):
         for half in range(2):
             load_down(t, half).wait()
 
+            @pl.when(t >= 2)
+            def _():
+                keep_down(t - 2, half).wait()
+
             def level(span):
-                dlev[half, span, :] = levels(dbuf[t % 2, half, span, :], 64.0)
-
-            strips(dlev.shape[1] // 64, 64, level)
-
-        @pl.when(t + 2 < tiles)
-        def _():
-            for half in range(2):
+                dlev[t % 2, half, span, :] = levels(dbuf[t % 2, half, span, :], 64.0)
+
+            strips(part // 64, 64, level)
+            keep_down(t, half).start()
+
+            @pl.when(t + 2 < tiles)
+            def _():
                 load_down(t + 2, half).start()
 
         to_core(t).wait_recv()
 
         def product(span):
-            acc[span, :] += contract_last(hid[c * tiles + t, span, :], dlev[0]) + contract_last(
-                hid[(1 - c) * tiles + t, span, :], dlev[1]
+            acc[span, :] += contract_last(hid[c * tiles + t, span, :], dlev[t % 2, 0]) + contract_last(
+                hid[(1 - c) * tiles + t, span, :], dlev[t % 2, 1]
             )
 
         strips(rows // 256, 256, product)
 
-        @pl.when((t // per) % 2 == y)
-        def _():
-            keep(t, 1, 1 - c).start()
+        @pl.when(for_mine(t))
+        def _():
+            keep(t, 1 - c, 1).start()
 
     def step(i, carry):
         @pl.when(i < tiles)
@@ -1177,18 +1278,23 @@
 
         @pl.when((i >= 1) & (i < tiles + 1))
         def _():
+            arrive(i - 1)
+
+        @pl.when(i >= 2)
+        def _():
+            narrow(i - 2)
+
+        @pl.when((i >= 1) & (i < tiles + 1))
+        def _():
             middle(i - 1)
 
-        @pl.when(i >= 2)
-        def _():
-            narrow(i - 2)
-
         return carry
 
     lax.fori_loop(0, tiles + 2, step, 0)
-    gu_out = pltpu.make_async_copy(gu, gu_o, outs.at[0])
-    gu_out.start()
-
+
+    for copy, forward in travellers:
+        copy.wait_recv()
+        forward.start()
     parts = 4
     size = rows // parts
     sends = []
@@ -1196,19 +1302,19 @@
     for k in range(parts):
         span = pl.ds(k * size, size)
         downs[me, span, :] = acc[span, :].astype(BF16)
-        part = downs.at[me, span]
-        copy = remote(part, part, gxs.at[k], gxr.at[k], across)
+        piece = downs.at[me, span]
+        copy = remote(piece, piece, gxs.at[k], gxr.at[k], across)
         copy.start()
         sends.append(copy)
-        copy = remote(part, part, gcs.at[k], gcr.at[k], beside)
+        copy = remote(piece, piece, gcs.at[k], gcr.at[k], beside)
         copy.start()
         own_sends.append(copy)
 
     def pass_on(t, carry):
-        @pl.when((t // per) % 2 == y)
-        def _():
-            remote(hid.at[0], hidy.at[slot(t, c)], ys.at[t], yr.at[t], beyond).wait_recv()
-            got = hidy.at[slot(t, c)]
+        @pl.when(for_mine(t))
+        def _():
+            got = hidy_o.at[slot(t, c)]
+            remote(hid.at[0], got, ys.at[t], yr.at[t], beyond).wait_recv()
             remote(got, got, fs.at[t], fr.at[t], beside).start()
 
         return carry
@@ -1223,7 +1329,7 @@
         forwards.append(copy)
     for copy in own_sends + forwards:
         copy.wait_recv()
-    down_out = pltpu.make_async_copy(downs, down_o, outs.at[3])
+    down_out = pltpu.make_async_copy(downs, down_o, outs)
     down_out.start()
     sums_o[...] = jnp.zeros_like(sums_o)
     width = GROUP * acc.shape[1]
@@ -1253,36 +1359,41 @@
         return carry
 
     lax.fori_loop(0, rows // 64, last_norm, 0)
+    gft_o[...] = contract_last(unit[...], gf_o[...]).astype(BF16)
+
+    for t in range(tiles - 3, tiles):
+        to_x(t).wait_send()
+        keep_own(t).wait()
+    for t in range(tiles - 2, tiles):
+        keep_level(t).wait()
+        for half in range(2):
+            keep_down(t, half).wait()
 
     def drain(t, carry):
-        to_x(t).wait_send()
         to_core(t).wait_send()
 
-        @pl.when((t // per) % 2 != y)
+        @pl.when(for_mine(t))
+        def _():
+            keep(t, c, 0).wait()
+            keep(t, 1 - c, 1).wait()
+            got = hidy_o.at[slot(t, c)]
+            remote(got, got, fs.at[t], fr.at[t], beside).wait_send()
+            got = hidy_o.at[slot(t, 1 - c)]
+            remote(got, got, fs.at[t], fr.at[t], beside).wait_recv()
+
+        @pl.when(jnp.logical_not(for_mine(t)))
         def _():
             to_y(t).wait_send()
 
-        @pl.when((t // per) % 2 == y)
-        def _():
-            keep(t, 0, c).wait()
-            keep(t, 1, 1 - c).wait()
-            got = hidy.at[slot(t, c)]
-            remote(got, got, fs.at[t], fr.at[t], beside).wait_send()
-            got = hidy.at[slot(t, 1 - c)]
-            remote(got, got, fs.at[t], fr.at[t], beside).wait_recv()
-
         return carry
 
     lax.fori_loop(0, tiles, drain, 0)
-    hidy_out = pltpu.make_async_copy(hidy, hidy_o, outs.at[4])
-    hidy_out.start()
     for copy in sends + own_sends + forwards:
         copy.wait_send()
-    for copy in travellers:
-        copy.wait()
-    gu_out.wait()
+    for copy, forward in travellers:
+        copy.wait_send()
+        forward.wait()
     down_out.wait()
-    hidy_out.wait()
 
 
 def ffn_forward(cid, b, wgu, gs, wd, cots, g3, ds, riders):
@@ -1291,6 +1402,8 @@
     tiles, _, tw = gs.shape
     count = len(riders)
     lone = max(count, 1)
+    each = DMA((tiles,))
+    four = DMA((4,))
     return comm_call(
         functools.partial(ffn_forward_kernel, tiles, count),
         cid,
@@ -1300,54 +1413,53 @@
             jax.ShapeDtypeStruct((tiles, rows, tw), BF16),
             jax.ShapeDtypeStruct((GROUP, rows, part), BF16),
             jax.ShapeDtypeStruct((rows, part), BF16),
+            jax.ShapeDtypeStruct((part, rows), BF16),
             jax.ShapeDtypeStruct((8, part), F32),
+            jax.ShapeDtypeStruct((tiles, deep, tw), BF16),
+            jax.ShapeDtypeStruct((2, tiles, part, tw), BF16),
         ]
         + [jax.ShapeDtypeStruct(r.shape[:1] + r.shape[2:], r.dtype) for r in riders],
         [
-            pltpu.VMEM((2, tiles, rows, tw), BF16),
+            pltpu.VMEM((3, 2, rows, tw), BF16),
             pltpu.VMEM((2 * tiles, rows, tw), BF16),
-            pltpu.VMEM((tiles, rows, tw), BF16),
+            pltpu.VMEM((part, part), BF16),
             pltpu.VMEM((2, deep, tw), BF16),
-            pltpu.VMEM((deep, tw), BF16),
+            pltpu.VMEM((2, deep, tw), BF16),
             pltpu.VMEM((2, 2, part, tw), BF16),
-            pltpu.VMEM((2, part, tw), BF16),
+            pltpu.VMEM((2, 2, part, tw), BF16),
             pltpu.VMEM((rows, part), F32),
             pltpu.VMEM((GROUP, rows, part), BF16),
-            DMA((2,)), DMA((2, 2)), DMA((tiles,)), DMA((tiles,)), DMA((tiles,)), DMA((tiles,)), DMA((tiles,)),
-            DMA((tiles,)), DMA((tiles,)), DMA((tiles,)), DMA((4,)), DMA((4,)), DMA((4,)), DMA((4,)), DMA((4,)),
-            DMA((4,)), DMA((lone,)), DMA((lone,)), DMA((2, tiles)), DMA((5,)),
+            DMA((2,)), DMA((2, 2)), DMA((2,)), DMA((2, 2)), DMA((2,)), each, each, each, each, each, DMA((2, tiles)),
+            each, each, each, each, four, four, four, four, four, four, DMA((lone, 2)), DMA((lone, 2)), DMA,
         ],
         [VMEM, ANY, VMEM, ANY, VMEM, VMEM, VMEM] + [ANY] * count,
-        [ANY, ANY, ANY, ANY, VMEM, VMEM] + [ANY] * count,
+        [ANY, ANY, ANY, ANY, VMEM, VMEM, VMEM, ANY, ANY] + [ANY] * count,
     )(b, wgu, gs, wd, cots, g3, ds, *riders)
 
 
-def ffn_backward_kernel(tiles, nz, chained, *refs):
-    gf, wd, wgu, gs, gu, hid, hidy = refs[:7]
-    dg_o, dgy_o, gsum_o, out, ddown_o = refs[7:12]
-    (hh, hy, gfy, wbuf, wlev, dbuf, dlev, pair, co, cgot, near, sx, xgot, dg, acc, low, from_core, to_xb, from_x,
-     hsem, wsem, dsem, psem, cs, cr, xs, xr, ys, yr, os, gys, gyr, ccs, ccr, cxs, cxr) = refs[12:48]
-    chain_refs = refs[48:]
+def ffn_backward_kernel(tiles, nz, chained, gate_tiles, *refs):
+    gf, gft, levd, lev, gs, gu, hid, hidy, bt, bty = refs[:10]
+    dg_o, dgy_o, xg_o, gsum_o, out, ddown_o, gate_o = refs[10:17]
+    landing = refs[17:21] if chained else []
+    refs = refs[len(landing) + 1 :]
+    (hh, hy, gfy, wbuf, dbuf, pair, co, cgot, near, sx, xgot, dg, acc, low, from_core, to_xb, from_x,
+     hsem, wsem, dsem, psem, lsem, cs, cr, xs, xr, ys, yr, os, gys, gyr, ccs, ccr, cxs, cxr) = refs[16:51]
+    rest = refs[51:]
     seq, me, x, c = place_now()
     y = seq % 2
-    z = seq // 2
     across = (seq, (1 - x) * 2 + c)
     beside = (seq, x * 2 + 1 - c)
     beyond = (seq + 1 - 2 * y, me)
     rows, tw = dg.shape[1:]
     part = acc.shape[2]
-    deep = GROUP * part
     per = hid.shape[0] // 4 if chained else 0
     ring = dg.shape[0]
 
     def load_up(t):
-        return pltpu.make_async_copy(wgu.at[:, pl.ds(pl.multiple_of(t * tw, 128), tw)], wbuf.at[t % 2], wsem.at[t % 2])
+        return pltpu.make_async_copy(lev.at[t], wbuf.at[t % 2], wsem.at[t % 2])
 
     def load_down(t, half):
-        start = ((c + half) % 2 * tiles + t) * tw
-        return pltpu.make_async_copy(
-            wd.at[:, pl.ds(pl.multiple_of(start, 128), tw)], dbuf.at[t % 2, half], dsem.at[t % 2, half]
-        )
+        return pltpu.make_async_copy(levd.at[half, t], dbuf.at[t % 2, half], dsem.at[t % 2, half])
 
     def load_pair(t):
         return pltpu.make_async_copy(gu.at[:, t], pair.at[t % 2], psem.at[t % 2])
@@ -1362,19 +1474,34 @@
         load_hidy = pltpu.make_async_copy(hidy, hy, hsem.at[1])
         load_hid.start()
         load_hidy.start()
-    if chained:
+
+        def partial(k, j):
+            return dot(gft[...], hh[k * per + j]) + dot(gfy[...], hy[k * per + j])
+
+        def keep_sum(j, stage, sem):
+            return pltpu.make_async_copy(stage, ddown_o.at[:, pl.ds(pl.multiple_of(j * tw, 128), tw)], sem)
+
+        downs = Chain(nz, per, seq, me, partial, keep_sum, landing[:2], rest[:11])
+        gates, gate_loads = gate_chain(
+            nz, 0, gate_tiles, seq, me, bt, bty, dg_o, dgy_o, gate_o, landing[2:], *rest[11:14], rest[14:]
+        )
+        gate_loads[0].start()
+        gate_loads[1].start()
         greet_all(seq, me, nz, [across, beside])
-        gf_swap = remote(gf, gfy, gys, gyr, beyond)
+        gf_swap = remote(gft, gfy, gys, gyr, beyond)
         gf_swap.start()
     else:
         greet([across, beside, beyond])
     acc[...] = jnp.zeros_like(acc)
 
     def to_core(t):
-        return remote(co.at[t % 2], cgot.at[t], cs.at[t], cr.at[t], beside)
+        return remote(co.at[t % 2], cgot.at[t % 4], cs.at[t], cr.at[t], beside)
 
     def to_x(t):
-        return remote(sx.at[t % 4], xgot.at[t], xs.at[t], xr.at[t], across)
+        return remote(sx.at[t % 4], xg_o.at[t], xs.at[t], xr.at[t], across)
+
+    def load_got(t):
+        return pltpu.make_async_copy(xg_o.at[t], xgot.at[t % 2], lsem.at[t % 2])
 
     def columns(ref, t):
         return ref.at[:, pl.ds(pl.multiple_of(t * tw, 128), tw)]
@@ -1389,31 +1516,26 @@
         for half in range(2):
             load_down(t, half).wait()
 
-            def level(span):
-                dlev[half, span, :] = levels(dbuf[t % 2, half, span, :], 64.0)
-
-            strips(dlev.shape[1] // 64, 64, level)
+        @pl.when(t >= 2)
+        def _():
+            to_core(t - 2).wait_send()
+
+        def product(span):
+            co[t % 2, span, :] = dot(gf[span, :], dbuf[t % 2, 1]).astype(BF16)
+
+        strips(rows // 256, 256, product)
+        to_core(t).start()
+
+        def product_near(span):
+            near[t % 2, span, :] = dot(gf[span, :], dbuf[t % 2, 0])
+
+        strips(rows // 256, 256, product_near)
 
         @pl.when(t + 2 < tiles)
         def _():
             for half in range(2):
                 load_down(t + 2, half).start()
 
-        @pl.when(t >= 2)
-        def _():
-            to_core(t - 2).wait_send()
-
-        def product(span):
-            co[t % 2, span, :] = dot(gf[span, :], dlev[1]).astype(BF16)
-
-        strips(rows // 256, 256, product)
-        to_core(t).start()
-
-        def product_near(span):
-            near[t % 2, span, :] = dot(gf[span, :], dlev[0])
-
-        strips(rows // 256, 256, product_near)
-
     def chip(t):
         @pl.when(t >= 4)
         def _():
@@ -1422,13 +1544,17 @@
         to_core(t).wait_recv()
 
         def body(span):
-            sx[t % 4, span, :] = (near[t % 2, span, :] + cgot[t, span, :].astype(F32)).astype(BF16)
+            sx[t % 4, span, :] = (near[t % 2, span, :] + cgot[t % 4, span, :].astype(F32)).astype(BF16)
 
         strips(rows // 64, 64, body)
         to_x(t).start()
 
     is_gate = jnp.where(x == 0, 1.0, 0.0).astype(F32)
 
+    def arrive(t):
+        to_x(t).wait_recv()
+        load_got(t).start()
+
     def own(t):
         load_pair(t).wait()
 
@@ -1437,12 +1563,12 @@
             to_y(t - ring).wait_send()
             keep(t - ring).wait()
 
-        to_x(t).wait_recv()
+        load_got(t).wait()
         scale = gs[t]
         gsum_o[t] = jnp.zeros((8, tw), F32)
 
         def body(span):
-            grad = sx[t % 4, span, :].astype(F32) + xgot[t, span, :].astype(F32)
+            grad = sx[t % 4, span, :].astype(F32) + xgot[t % 2, span, :].astype(F32)
             gate = pair[t % 2, 0, span, :].astype(F32)
             up = pair[t % 2, 1, span, :].astype(F32)
             value, slope = gelu_parts(gate)
@@ -1462,30 +1588,26 @@
     def back(t):
         load_up(t).wait()
 
-        def level(span):
-            wlev[span, :] = levels(wbuf[t % 2, span, :], 16.0)
-
-        strips(deep // 128, 128, level)
-
-        @pl.when(t + 2 < tiles)
-        def _():
-            load_up(t + 2).start()
-
         def product(span):
             for j in range(GROUP):
-                acc[j, span, :] += contract_last(dg[t % ring, span, :], wlev[j * part : (j + 1) * part, :])
+                acc[j, span, :] += contract_last(dg[t % ring, span, :], wbuf[t % 2, j * part : (j + 1) * part, :])
 
         strips(rows // 128, 128, product)
 
-    if chained:
-
-        def partial(k, j):
-            return contract_first(hh[k * per + j], gf[...]) + contract_first(hy[k * per + j], gfy[...])
-
-        downs = Chain(
-            nz, per, seq, me, partial, lambda j, stage, sem: pltpu.make_async_copy(stage, ddown_o.at[j], sem), chain_refs
-        )
-    hops = nz - 1
+        @pl.when(t + 2 < tiles)
+        def _():
+            load_up(t + 2).start()
+
+    def units(chain, i, table):
+        unit = jnp.int32(0)
+        hit = i < 0
+        for when, u in table:
+            unit = unit + jnp.where(i == when, u, 0)
+            hit = hit | (i == when)
+
+        @pl.when(hit)
+        def _():
+            chain.run(unit, unit + 1)
 
     def step(i, carry):
         @pl.when(i < tiles)
@@ -1495,6 +1617,10 @@
         @pl.when((i >= 1) & (i < tiles + 1))
         def _():
             chip(i - 1)
+
+        @pl.when((i >= 2) & (i < tiles + 2))
+        def _():
+            arrive(i - 2)
 
         if chained:
 
@@ -1504,18 +1630,32 @@
                 load_hid.wait()
                 load_hidy.wait()
 
-            @pl.when((i >= 1) & (i < 1 + per * hops))
+            @pl.when(i == 9)
             def _():
-                downs.run(i - 1, i)
-
-        @pl.when(i >= 2)
+                for t in range(gate_tiles):
+                    to_y(t).wait_recv()
+                gate_loads[2].start()
+                gate_loads[3].start()
+
+            @pl.when(i == 10)
+            def _():
+                for load in gate_loads:
+                    load.wait()
+
+            units(downs, i, ((1, 0), (2, 3), (3, 4), (4, 6), (5, 7), (6, 8), (7, 10), (8, 11), (10, 14), (12, 17)))
+            units(gates, i, ((10, 0), (11, 3), (12, 4), (13, 7), (14, 8)))
+
+        @pl.when(i >= 3)
+        def _():
+            back(i - 3)
+
+        @pl.when((i >= 2) & (i < tiles + 2))
         def _():
             own(i - 2)
-            back(i - 2)
 
         return carry
 
-    lax.fori_loop(0, tiles + 2, step, 0)
+    lax.fori_loop(0, tiles + 3, step, 0)
 
     parts = 4
     block = rows // GROUP
@@ -1543,7 +1683,9 @@
         copy.start()
         sends.append(copy)
     if chained:
+        gates.run(9, gates.units())
         downs.finish()
+        gates.finish()
     for k in range(parts):
         span = pl.ds(k * size, size)
         here = pl.ds(pl.multiple_of((order[1] * 2 + c) * block + k * size, 16), size)
@@ -1566,95 +1708,72 @@
         to_y(t).wait_recv()
         return carry
 
-    lax.fori_loop(0, tiles, drain, 0)
+    lax.fori_loop(gate_tiles if chained else 0, tiles, drain, 0)
     if chained:
         gf_swap.wait_send()
 
 
-def ffn_backward(cid, n, gf, wd, wgu, gs, gu, hid, hidy):
+def ffn_backward(cid, n, gate_tiles, gf, gft, levd, lev, gs, gu, hid, hidy, bt, bty):
     rows, part = gf.shape
-    deep = wgu.shape[0]
+    deep = lev.shape[1]
     tiles, _, tw = gs.shape
     nz = n // 2
     chained = nz == 4
     per = tiles // nz if chained else 1
-    hops = nz - 1 if chained else 1
     block = rows // GROUP
     half = (tiles, rows, tw) if chained else (1, 16, 128)
-    message = (tw, part) if chained else (16, 128)
+    message = (part, tw)
     ring = 4
+    each = DMA((tiles,))
+    wide = jax.ShapeDtypeStruct((rows, tiles * tw), BF16)
     return comm_call(
-        functools.partial(ffn_backward_kernel, tiles, nz, chained),
+        functools.partial(ffn_backward_kernel, tiles, nz, chained, gate_tiles),
         cid,
         [
-            jax.ShapeDtypeStruct((rows, tiles * tw), BF16),
-            jax.ShapeDtypeStruct((rows, tiles * tw), BF16),
+            wide,
+            wide,
+            jax.ShapeDtypeStruct((tiles, rows, tw), BF16),
             jax.ShapeDtypeStruct((tiles, 8, tw), F32),
             jax.ShapeDtypeStruct((GROUP, block, part), F32),
-            jax.ShapeDtypeStruct((per,) + message, F32),
-        ],
+            jax.ShapeDtypeStruct((part, per * tw), F32),
+            jax.ShapeDtypeStruct((bt.shape[2], max(gate_tiles, 1) * tw), F32),
+        ]
+        + (Chain.landing(nz, per, *message) + gate_landing(nz, gate_tiles, bt) if chained else []),
         [
             pltpu.VMEM(half, BF16),
             pltpu.VMEM(half, BF16),
-            pltpu.VMEM((rows, part), BF16),
+            pltpu.VMEM((part, rows), BF16),
             pltpu.VMEM((2, deep, tw), BF16),
-            pltpu.VMEM((deep, tw), BF16),
             pltpu.VMEM((2, 2, part, tw), BF16),
-            pltpu.VMEM((2, part, tw), BF16),
             pltpu.VMEM((2, 2, rows, tw), BF16),
             pltpu.VMEM((2, rows, tw), BF16),
-            pltpu.VMEM((tiles, rows, tw), BF16),
+            pltpu.VMEM((4, rows, tw), BF16),
             pltpu.VMEM((2, rows, tw), F32),
             pltpu.VMEM((4, rows, tw), BF16),
-            pltpu.VMEM((tiles, rows, tw), BF16),
+            pltpu.VMEM((2, rows, tw), BF16),
             pltpu.VMEM((ring, rows, tw), BF16),
             pltpu.VMEM((GROUP, rows, part), F32),
             pltpu.VMEM((2, GROUP, block, part), BF16),
             pltpu.VMEM((2, GROUP, block, part), BF16),
             pltpu.VMEM((GROUP, block, part), BF16),
             pltpu.VMEM((GROUP, block, part), BF16),
-            DMA((2,)), DMA((2,)), DMA((2, 2)), DMA((2,)), DMA((tiles,)), DMA((tiles,)), DMA((tiles,)), DMA((tiles,)),
-            DMA((tiles,)), DMA((tiles,)), DMA((tiles,)), DMA, DMA, DMA((2, 4)), DMA((2, 4)), DMA((4,)), DMA((4,)),
+            DMA((2,)), DMA((2,)), DMA((2, 2)), DMA((2,)), DMA((2,)), each, each, each, each,
+            each, each, each, DMA, DMA, DMA((2, 4)), DMA((2, 4)), DMA((4,)), DMA((4,)),
         ]
-        + (Chain.scratch(nz, per, *message) if chained else []),
-        [VMEM, ANY, ANY, VMEM, ANY, ANY, ANY],
-        [ANY, ANY, VMEM, VMEM, ANY],
-    )(gf, wd, wgu, gs, gu, hid, hidy)
-
-
-def gate_chain(nz, first, count, seq, me, bt, bty, dg, dgy, out, slabs, halves, slab_sem, scratch):
-    loads = [pltpu.make_async_copy(bt.at[:, seq % 2], halves.at[0], slab_sem.at[2])]
-    loads.append(pltpu.make_async_copy(bty, halves.at[1], slab_sem.at[3]))
-    for i, ref in enumerate((dg, dgy)):
-        loads.append(
-            pltpu.make_async_copy(ref.at[:, pl.ds(first * TILE, count * TILE)], slabs.at[i], slab_sem.at[i])
-        )
-    for copy in loads:
-        copy.start()
-
-    def partial(k, j):
-        cols = pl.ds(pl.multiple_of(j * TILE, 128), TILE)
-        return dot(halves[0, k], slabs[0, :, cols]) + dot(halves[1, k], slabs[1, :, cols])
-
-    def keep(j, stage, sem):
-        return pltpu.make_async_copy(stage, out.at[:, pl.ds(pl.multiple_of(j * TILE, 128), TILE)], sem)
-
-    return Chain(nz, count, seq, me, partial, keep, scratch), loads
-
-
-def gate_scratch(nz, count, bt):
-    rows = bt.shape[3]
-    return [
-        pltpu.VMEM((2, rows, count * TILE), BF16), pltpu.VMEM((2, nz) + bt.shape[2:], BF16), DMA((4,))
-    ] + Chain.scratch(nz, count, bt.shape[2], TILE)
-
-
-def branch_back_kernel(n, tiles, *refs):
+        + (Chain.scratch(nz, per, *message) + gate_scratch(nz, gate_tiles, bt) if chained else []),
+        [VMEM, VMEM, ANY, ANY, VMEM, ANY, ANY, ANY, ANY, ANY],
+        [ANY, ANY, ANY, VMEM, VMEM, ANY, ANY] + [ANY] * (4 if chained else 0),
+    )(gf, gft, levd, lev, gs, gu, hid, hidy, bt, bty)
+
+
+def branch_back_kernel(n, first, tiles, *refs):
     (gsi, mid, raw, cot, g2, g3, scale, wo, q, mixed, mass, own_meta, metas, kv, bt, bty, dg, dgy) = refs[:18]
     dmid, sums, gy, gyy, dq, dkv, gate_o = refs[18:25]
-    (low, gys, gy_all, part, from_core, to_x, from_x, grad, kvs, dkvs, es, er, el, cs, cr, xs, xr, ks, ds, yss, ysr,
-     ows) = refs[25:47]
-    rest = refs[47:]
+    landing = refs[25:27] if tiles else []
+    refs = refs[len(landing) :]
+    (unit, gyt, gys, gy_all, part, from_core, to_x, from_x, grad, kvs, dkvs, es, er, el, cs, cr, xs, xr, ks, ds, yss, ysr,
+     ows) = refs[25:48]
+    rest = refs[48:]
     seq, me, x, c = place_now()
     nz = n // 2
     across = (seq, (1 - x) * 2 + c)
@@ -1663,7 +1782,9 @@
     peers = [(seq, lax.rem(me + d, GROUP)) for d in range(1, GROUP)]
     chain = None
     if tiles:
-        chain, loads = gate_chain(nz, 0, tiles, seq, me, bt, bty, dg, dgy, gate_o, *rest[:3], rest[3:])
+        chain, loads = gate_chain(nz, first, tiles, seq, me, bt, bty, dg, dgy, gate_o, landing, *rest[:3], rest[3:])
+        for load in loads:
+            load.start()
         greet_all(seq, me, nz, peers)
     else:
         greet(peers + [beyond])
@@ -1730,9 +1851,11 @@
     for copy in copies:
         copy.wait_recv()
     own.wait()
-    gy_out = pltpu.make_async_copy(gy_all, gy, ows)
+    fill_unit(unit)
+    gyt[...] = contract_last(unit[...], gy_all[...].reshape(gyt.shape[1], gyt.shape[0])).astype(BF16)
+    gy_out = pltpu.make_async_copy(gyt, gy, ows)
     gy_out.start()
-    swap = remote(gy_all, gyy, yss, ysr, beyond)
+    swap = remote(gyt, gyy, yss, ysr, beyond)
     swap.start()
 
     heads = part.shape[3]
@@ -1822,7 +1945,7 @@
     gy_out.wait()
 
 
-def branch_back(cid, n, tiles, gsi, mid, raw, cot, g2, g3, scale, wo, q, mixed, mass, own_meta, metas, kv, pairs):
+def branch_back(cid, n, first, tiles, gsi, mid, raw, cot, g2, g3, scale, wo, q, mixed, mass, own_meta, metas, kv, pairs):
     bt, bty, dg, dgy = pairs
     own, part = raw.shape[1:]
     rows = q.shape[0]
@@ -1831,19 +1954,21 @@
     gate_rows = bt.shape[2]
     pack = (2, n, 2, own, DH)
     return comm_call(
-        functools.partial(branch_back_kernel, n, tiles),
+        functools.partial(branch_back_kernel, n, first, tiles),
         cid,
         [
             block(F32),
             jax.ShapeDtypeStruct((GROUP, 8, part), F32),
-            block(BF16),
-            block(BF16),
+            jax.ShapeDtypeStruct((part, rows), BF16),
+            jax.ShapeDtypeStruct((part, rows), BF16),
             jax.ShapeDtypeStruct(q.shape, F32),
             jax.ShapeDtypeStruct(kv.shape, BF16),
             jax.ShapeDtypeStruct((gate_rows, max(tiles, 1) * TILE), F32),
-        ],
+        ]
+        + (gate_landing(n // 2, tiles, bt) if tiles else []),
         [
-            pltpu.VMEM((8, 128), BF16),
+            pltpu.VMEM((part, part), BF16),
+            pltpu.VMEM((part, rows), BF16),
             pltpu.VMEM((GROUP, own, part), BF16),
             pltpu.VMEM((GROUP, own, part), BF16),
             pltpu.VMEM((2, 2, rows, heads), BF16),
@@ -1857,13 +1982,15 @@
         ]
         + (gate_scratch(n // 2, tiles, bt) if tiles else []),
         [VMEM] * 13 + [ANY] * 5,
-        [VMEM, VMEM, ANY, ANY, VMEM, ANY, ANY],
+        [VMEM, VMEM, ANY, ANY, VMEM, ANY, ANY] + [ANY] * (2 if tiles else 0),
     )(gsi, mid, raw, cot, g2, g3, scale, wo, q, mixed, mass, own_meta, metas, kv, bt, bty, dg, dgy)
 
 
 def keys_back_kernel(n, first, tiles, *refs):
     (src, dq, q_raw, p_raw, cosine, sine, q_scale, p_scale, wq, wkv, bt, bty, dg, dgy) = refs[:14]
     joined, joined_y, out, sums, gate_o = refs[14:19]
+    landing = refs[19:21]
+    refs = refs[2:]
     (y_got, r_got, l_got, r_out, l_out, moved, back, acc, low, from_core, to_xb, from_x,
      ys, yr, rs, rr, ls, lr, hs, hr, local, jys, jyr, ccs, ccr, cxs, cxr) = refs[19:46]
     slabs, halves, slab_sem, *rest = refs[46:]
@@ -1876,7 +2003,9 @@
     beyond = (z * 2 + 1 - y, me)
     across = (seq, (1 - x) * 2 + c)
     beside = (seq, x * 2 + 1 - c)
-    chain, loads = gate_chain(nz, first, tiles, seq, me, bt, bty, dg, dgy, gate_o, slabs, halves, slab_sem, rest)
+    chain, loads = gate_chain(nz, first, tiles, seq, me, bt, bty, dg, dgy, gate_o, landing, slabs, halves, slab_sem, rest)
+    for load in loads:
+        load.start()
     greet_all(seq, me, nz, [(seq, lax.rem(me + d, GROUP)) for d in range(1, GROUP)])
     rows, width = dq.shape
     deep = acc.shape[1]
@@ -2115,7 +2244,8 @@
             jax.ShapeDtypeStruct((block, deep), F32),
             jax.ShapeDtypeStruct((8, width), F32),
             jax.ShapeDtypeStruct((bt.shape[2], tiles * TILE), F32),
-        ],
+        ]
+        + gate_landing(nz, tiles, bt),
         [
             pltpu.VMEM((nz,) + shape, BF16), chain, chain, chain, chain, pltpu.VMEM(shape, BF16), pltpu.VMEM(shape, BF16),
             pltpu.VMEM((rows, deep), F32),
@@ -2128,41 +2258,44 @@
         ]
         + gate_scratch(nz, tiles, bt),
         [VMEM] * 10 + [ANY] * 4,
-        [VMEM, ANY, VMEM, VMEM, ANY],
+        [VMEM, ANY, VMEM, VMEM, ANY, ANY, ANY],
     )(src, dq, q_raw, p_raw, cosine, sine, q_scale, p_scale, wq, wkv, bt, bty, dg, dgy)
 
 
 def finish_kernel(n, rounds, first, tiles, *refs):
     (whole, part, bt, bty, dg, dgy, ot, oty, gy, gyy, at, aty, joined, joined_y) = refs[:14]
     whole_out, part_out, gate_o, output_o, attention_o = refs[14:19]
+    landing = refs[19:25]
+    refs = refs[6:]
     bufs, gots, mine, theirs, ss, rs = refs[19:25]
     slabs, halves, slab_sem = refs[25:28]
-    gate_refs, output_refs, attention_refs = refs[28:38], refs[38:48], refs[48:58]
-    output_halves, attention_halves, half_sem = refs[58:]
+    gate_refs, output_refs, attention_refs = refs[28:39], refs[39:50], refs[50:61]
+    output_halves, attention_halves, half_sem = refs[61:]
     seq, me, x, c = place_now()
     nz = n // 2
     across = (seq, (1 - x) * 2 + c)
     beside = (seq, x * 2 + 1 - c)
-    gates, loads = gate_chain(nz, first, tiles, seq, me, bt, bty, dg, dgy, gate_o, slabs, halves, slab_sem, gate_refs)
+    gates, loads = gate_chain(nz, first, tiles, seq, me, bt, bty, dg, dgy, gate_o, landing[:2], slabs, halves, slab_sem, gate_refs)
     for i, (ref, to) in enumerate(
         ((ot.at[:, seq % 2], output_halves.at[0]), (oty, output_halves.at[1]),
          (at.at[:, seq % 2], attention_halves.at[0]), (aty, attention_halves.at[1]))
     ):
-        load = pltpu.make_async_copy(ref, to, half_sem.at[i])
+        loads.append(pltpu.make_async_copy(ref, to, half_sem.at[i]))
+    for load in loads:
         load.start()
-        loads.append(load)
     wide = joined.shape[1] // 2
 
     def output_partial(k, j):
-        return dot(output_halves[0, k], gy[...]) + dot(output_halves[1, k], gyy[...])
+        return dot(gy[...], output_halves[0, k]) + dot(gyy[...], output_halves[1, k])
 
     def attention_partial(k, j):
         cols = pl.ds(pl.multiple_of(j * wide, 128), wide)
         return dot(attention_halves[0, k], joined[:, cols]) + dot(attention_halves[1, k], joined_y[:, cols])
 
-    outputs = Chain(
-        nz, 1, seq, me, output_partial, lambda j, stage, sem: pltpu.make_async_copy(stage, output_o, sem), output_refs
-    )
+    def keep_output(j, stage, sem):
+        return pltpu.make_async_copy(stage, output_o, sem)
+
+    outputs = Chain(nz, 1, seq, me, output_partial, keep_output, landing[2:4], output_refs)
     attentions = Chain(
         nz,
         2,
@@ -2172,6 +2305,7 @@
         lambda j, stage, sem: pltpu.make_async_copy(
             stage, attention_o.at[:, pl.ds(pl.multiple_of(j * wide, 128), wide)], sem
         ),
+        landing[4:],
         attention_refs,
     )
     partners = []
@@ -2184,8 +2318,13 @@
     rows = whole.shape[0]
     bufs[0, :rows, :] = whole[...]
     bufs[0, rows:, :] = part[...]
-    work = [(gates, u) for u in range(0, gates.units(), 3)]
-    work += [(outputs, 0), (attentions, 0), (attentions, 3)]
+    queues = [(chain, list(range(0, chain.units(), nz - 1))) for chain in (gates, outputs, attentions)]
+    work = [(gates, u) for u in queues[0][1][:tiles]]
+    rest = [queues[0][1][tiles:], queues[1][1], queues[2][1]]
+    while any(rest):
+        for (chain, _), left in zip(queues, rest):
+            if left:
+                work.append((chain, left.pop(0)))
     at_work = [0]
 
     def beside_work(count):
@@ -2232,7 +2371,7 @@
     nz = n // 2
     rounds = int(math.log2(n))
     rows = whole.shape[0] + part.shape[0]
-    output_rows = ot.shape[2]
+    output_shape = (gy.shape[0], ot.shape[3])
     attention_rows = at.shape[2]
     return comm_call(
         functools.partial(finish_kernel, n, rounds, first, tiles),
@@ -2241,9 +2380,12 @@
             jax.ShapeDtypeStruct(whole.shape, F32),
             jax.ShapeDtypeStruct((GROUP,) + part.shape, F32),
             jax.ShapeDtypeStruct((bt.shape[2], tiles * TILE), F32),
-            jax.ShapeDtypeStruct((output_rows, gy.shape[1]), F32),
+            jax.ShapeDtypeStruct(output_shape, F32),
             jax.ShapeDtypeStruct((attention_rows, joined.shape[1]), F32),
-        ],
+        ]
+        + gate_landing(nz, tiles, bt)
+        + Chain.landing(nz, 1, *output_shape)
+        + Chain.landing(nz, 2, attention_rows, joined.shape[1] // 2),
         [
             pltpu.VMEM((rounds + 1, rows, 128), F32),
             pltpu.VMEM((rounds + 1, rows, 128), F32),
@@ -2253,7 +2395,7 @@
             DMA((rounds + 2,)),
         ]
         + gate_scratch(nz, tiles, bt)
-        + Chain.scratch(nz, 1, output_rows, gy.shape[1])
+        + Chain.scratch(nz, 1, *output_shape)
         + Chain.scratch(nz, 2, attention_rows, joined.shape[1] // 2)
         + [
             pltpu.VMEM((2, nz) + ot.shape[2:], BF16),
@@ -2261,7 +2403,7 @@
             DMA((4,)),
         ],
         [VMEM] * 2 + [ANY] * 6 + [VMEM] * 2 + [ANY] * 2 + [VMEM] * 2,
-        [VMEM, VMEM, ANY, ANY, ANY],
+        [VMEM, VMEM] + [ANY] * 9,
     )(whole, part, bt, bty, dg, dgy, ot, oty, gy, gyy, at, aty, joined, joined_y)
 
 
@@ -2352,7 +2494,7 @@
     )
 
     mixed_low, mixed, mass = attend(n, query, pairs, own_meta, metas)
-    second_input, branch_own, my_middle, mixed_turned, second_turned = branch_forward(
+    second_input, branch_own, my_middle, mixed_slices, second_turned = branch_forward(
         3,
         mixed_low,
         output_code.T,
@@ -2366,7 +2508,9 @@
     columns = gate_up_code.shape[1]
     tiles = columns // TILE
     gate_scales = my_gate_scale.reshape(tiles, 1, TILE)
-    gate_up, hidden, hidden_y, down_blocks, grad_down, down_sums, *riders = ffn_forward(
+    (
+        gate_up, hidden, hidden_y, down_blocks, grad_down, grad_down_turned, down_sums, gate_levels, down_levels, *riders
+    ) = ffn_forward(
         5,
         second_input,
         gate_up_code,
@@ -2375,17 +2519,30 @@
         cot_blocks,
         gain[3].reshape(GROUP, 1, part),
         down_scale.reshape(GROUP, 1, part),
-        [second_turned, mixed_turned, first_turned],
+        [second_turned, mixed_slices, first_turned],
     )
-    second_pair, mixed_pair, first_pair = zip((second_turned, mixed_turned, first_turned), riders)
+    second_pair, mixed_pair, first_pair = zip((second_turned, mixed_slices, first_turned), riders)
     my_down = lax.dynamic_slice_in_dim(down_blocks, me * own, own, 1).astype(F32) * down_scale.reshape(GROUP, 1, part)
     down_inverse = lax.rsqrt(jnp.mean(my_down * my_down, axis=(0, 2), keepdims=True) + EPSILON)
     result = blocks_to_rows((my_middle + my_down * down_inverse * gain[3].reshape(GROUP, 1, part)).astype(BF16))
-    grad_gate_up, grad_gate_up_y, gate_sums, grad_second_input, down_grad = ffn_backward(
-        6, n, grad_down, down_code.T, gate_up_code, gate_scales, gate_up, hidden, hidden_y
+    tiles_zero, tiles_one, tiles_two = (2, 4, 4) if n == 8 else (0, 0, 0)
+    tiles_three = tiles - tiles_zero - tiles_one - tiles_two
+    grad_gate_up, grad_gate_up_y, _, gate_sums, grad_second_input, down_grad, gate_zero, *_ = ffn_backward(
+        6,
+        n,
+        tiles_zero,
+        grad_down,
+        grad_down_turned,
+        down_levels,
+        gate_levels,
+        gate_scales,
+        gate_up,
+        hidden,
+        hidden_y,
+        *second_pair,
     )
     if n == 8:
-        down_grad = down_grad.reshape(-1, part)
+        down_grad = down_grad.T
     else:
         hidden_own = jnp.concatenate(
             [
@@ -2405,11 +2562,10 @@
     gain_four = down_sums[1]
     scale_gate = gate_sums[:, 0, :].reshape(columns) / my_gate_scale
     gate_pairs = second_pair + (grad_gate_up, grad_gate_up_y)
-    tiles_one, tiles_two = (4, 3) if n == 8 else (0, 0)
-    tiles_three = tiles - tiles_one - tiles_two
-    grad_middle, branch_sums, grad_branch, grad_branch_y, grad_query, grad_pairs, gate_one = branch_back(
+    grad_middle, branch_sums, grad_branch, grad_branch_y, grad_query, grad_pairs, gate_one, *_ = branch_back(
         7,
         n,
+        tiles_zero,
         tiles_one,
         grad_second_input,
         my_middle,
@@ -2431,14 +2587,12 @@
     gain_two = branch_sums[:, 0].reshape(width)
     gain_three = branch_sums[:, 1].reshape(width)
     scale_output = branch_sums[:, 2].reshape(width)
-    grad_branch = grad_branch.reshape(rows, part)
-    grad_branch_y = grad_branch_y.reshape(rows, part)
 
     if n == 8:
-        joined, joined_y, grad_first_input, key_sums, gate_two = keys_back(
+        joined, joined_y, grad_first_input, key_sums, gate_two, *_ = keys_back(
             9,
             n,
-            tiles_one,
+            tiles_zero + tiles_one,
             tiles_two,
             grad_pairs,
             grad_query,
@@ -2482,10 +2636,10 @@
     parts = [scale_query, scale_pair, scale_gate, scale_down, gain_four]
     part_rows = lanes(jnp.concatenate(parts), 56)
     if n == 8:
-        whole_total, part_total, gate_three, output_grad, attention_grad = finish(
+        whole_total, part_total, gate_three, output_grad, attention_grad, *_ = finish(
             11,
             n,
-            tiles_one + tiles_two,
+            tiles - tiles_three,
             tiles_three,
             wholes,
             part_rows,
@@ -2493,7 +2647,8 @@
             mixed_pair + (grad_branch, grad_branch_y),
             first_pair + (joined, joined_y),
         )
-        gate_grad = jnp.concatenate([gate_one, gate_two, gate_three], axis=1)
+        output_grad = output_grad.T
+        gate_grad = jnp.concatenate([gate_zero, gate_one, gate_two, gate_three], axis=1)
     else:
         whole_total, part_total = totals(11, n, wholes, part_rows)
 
@@ -2501,7 +2656,7 @@
             return lax.psum_scatter(dot(left.reshape(-1, rows), right), "seq", scatter_dimension=0, tiled=True)
 
         gate_grad = weight_sum(second_turned, grad_gate_up)
-        output_grad = weight_sum(mixed_turned, grad_branch)
+        output_grad = weight_sum(mixed_slices.transpose(0, 1, 3, 2), grad_branch.T)
         attention_grad = weight_sum(first_turned, joined)
     whole_total = whole_total.reshape(-1)
     part_total = part_total.reshape(GROUP, -1)

time: 821 us -> 785 us (0.956)
  Pallas kernels: 768 us -> 729 us
    pallas_call x1, Pallas kernels: 146 us -> 95.2 us  [finish(): comm_call(functools.partial(finish_kernel, n, rounds, first, tiles), cid,...]
    pallas_call x1, Pallas kernels: 105 us -> 124 us  [keys_back(): comm_call(functools.partial(keys_back_kernel, n, first, tiles), cid, [joi...]
where the time goes in v5:
time: 785 us; the launch traced here: 772 us
  Pallas kernels  729 us (93%)
  local copies, waits for them, and re-layouts  30.3 us (4%)
  other arithmetic  11.6 us (1%)
    pallas_call x1, Pallas kernels, ffn_backward(): comm_call(functools.partial(ffn_backward_kernel, tiles, nz, chained, gate...  150 us
    pallas_call x1, Pallas kernels, ffn_forward(): comm_call(functools.partial(ffn_forward_kernel, tiles, count), cid, [jax....  138 us
    pallas_call x1, Pallas kernels, keys_back(): comm_call(functools.partial(keys_back_kernel, n, first, tiles), cid, [joi...  124 us
    pallas_call x1, Pallas kernels, finish(): comm_call(functools.partial(finish_kernel, n, rounds, first, tiles), cid,...  95.2 us
    pallas_call x1, Pallas kernels, front(): comm_call(functools.partial(front_kernel, n), cid, [blocks, blocks, jax.S...  88 us
    pallas_call x1, Pallas kernels, branch_back(): comm_call(functools.partial(branch_back_kernel, n, first, tiles), cid, [b...  80.2 us
    pallas_call x1, Pallas kernels, branch_forward(): comm_call(branch_kernel, cid, [jax.ShapeDtypeStruct((GROUP, rows, part),...  47.5 us

profile of v5, /device:TPU:0, one launch (start us, length us, event | category | flops | bytes accessed | tf_op | source)
XLA Modules:
  0.0 772.0 jit_solution(11790570059526930180)
XLA Ops:
  0.6 0.0 copy-start.6
  0.7 1.4 copy.30
  2.1 1.1 copy.31
  3.2 0.0 copy-done.6
  3.2 0.3 copy.32
  3.5 1.1 copy.33
  4.7 0.6 stack.2.refs_2_
  5.3 0.1 slice_reduce_fusion.4
  5.4 0.7 reshape_squeeze.29.refs_3_
  6.1 0.5 multiply_power_fusion.refs_4_
  6.6 1.3 dynamic_slice.12
  7.9 1.3 dynamic_slice.13
  9.3 88.0 %shard_map.255 = (bf16[4,512,576]{2,1,0:T(8,128)(2,1)}, bf16[4,512,576]{2,1,0:T(8,128)(2,1)}, f32[4,8,128]{2,1,0:T(8,128)}, f32[8,4,8,128]{3,2,1,0:T(8,128)}, bf...) custom-call(bf16[512,576]{1,0:T(8,128)(2,1)} %bitcast.64, ...), custom_call_target="tpu_custom_call" | custom-call | tf_op jit(solution)/shard_map/pallas_call | solution.py:612
  97.3 0.0 copy-start.12
  97.3 6.2 shard_map.256
  103.6 0.7 reshape.117.scale.refs_6_
  104.2 0.7 reshape_squeeze.30.g2.refs_4_
  104.9 0.7 reshape_squeeze.31.g3.refs_5_
  105.6 47.5 %shard_map.257 = (bf16[4,512,576]{2,1,0:T(8,128)(2,1)}, bf16[4,128,576]{2,1,0:T(8,128)(2,1)}, f32[4,128,576]{2,1,0:T(8,128)}, bf16[4,2,512,256]{3,2,1,0:T(8,128)(2,1)}, bf16[4,2,288,512]{3,2,1,0:T(8,128)(2,1)}) custom-call(bf16[512,512]{1,0:T(8,128)(2,1)} %get-tuple-element.71.low, bf16[576,2048]{1,0:T(8,128)(2,1)} %bitcast.59, ...), custom_call_target="tpu_custom_call" | custom-call | tf_op jit(solution)/shard_map/pallas_call | solution.py:775
  153.2 0.1 mul.94
  153.2 0.1 mul.88
  153.3 0.1 dynamic_slice.14
  153.4 0.6 reshape.118.refs_2_.refs_4_
  154.0 0.7 reshape_squeeze.32.refs_5_
  154.7 0.7 reshape.119.refs_6_
  155.4 138.0 %shard_map.258 = (bf16[2,12,512,384]{3,2,1,0:T(8,128)(2,1)}, bf16[12,512,384]{2,1,0:T(8,128)(2,1)}, bf16[12,512,384]{2,1,0:T(8,128)(2,1)}, bf16[4,512,576]{2,1,0...) custom-call(bf16[4,512,576]{2,1,0:T(8,128)(2,1)} %get-tuple-element., ...), custom_call_target="tpu_custom_call" | custom-call | tf_op jit(solution)/shard_map/pallas_call | solution.py:1407
  293.4 1.4 multiply_reduce_fusion
  294.7 1.4 add_convert_fusion
  296.1 0.1 slice_bitcast_fusion.4
  296.2 1.1 concatenate.27
  297.4 149.9 %shard_map.259 = (bf16[512,4608]{1,0:T(8,128)(2,1)}, bf16[512,4608]{1,0:T(8,128)(2,1)}, bf16[12,512,384]{2,1,0:T(8,128)(2,1)}, f32[12,8,384]{2,1,0:T(8,128)}, f3...) custom-call(bf16[512,576]{1,0:T(8,128)(2,1)} %get-tuple-element.80.r, ...), custom_call_target="tpu_custom_call" | custom-call | tf_op jit(solution)/shard_map/pallas_call | solution.py:1729
  447.2 80.2 %shard_map.260 = (f32[4,128,576]{2,1,0:T(8,128)}, f32[4,8,576]{2,1,0:T(8,128)}, bf16[576,512]{1,0:T(8,128)(2,1)}, bf16[576,512]{1,0:T(8,128)(2,1)}, f32[512,512]...) custom-call(f32[4,128,576]{2,1,0:T(8,128)} %get-tuple-element.88.ref, ...), custom_call_target="tpu_custom_call" | custom-call | tf_op jit(solution)/shard_map/pallas_call | solution.py:1956
  527.4 1.4 slice_bitcast_fusion
  528.8 0.5 concatenate.28
  529.3 0.0 copy-start
  529.4 123.7 %shard_map.261 = (bf16[512,1024]{1,0:T(8,128)(2,1)}, bf16[512,1024]{1,0:T(8,128)(2,1)}, f32[128,2304]{1,0:T(8,128)}, f32[8,512]{1,0:T(8,128)}, f32[288,1536]{1,0...) custom-call(bf16[8,2,512,256]{3,2,1,0:T(8,128)(2,1)} %get-tuple-element.95.refs_0_, ...), custom_call_target="tpu_custom_call" | custom-call | tf_op jit(solution)/shard_map/pallas_call | solution.py:2238
  653.1 0.2 fusion.9
  653.3 1.8 fusion.8
  655.1 1.4 fusion.7
  656.5 1.1 slice_reduce_fusion.3
  657.7 0.1 concatenate.32
  657.8 0.1 concatenate.31
  657.8 0.1 concatenate.30
  657.9 0.6 pad_maximum_fusion.1.refs_0_
  658.5 0.8 fusion.12
  659.3 1.0 slice_reduce_fusion
  660.3 0.1 dynamic-slice_divide_fusion
  660.4 0.8 slice_reduce_fusion.8
  661.2 0.1 concatenate.34
  661.3 0.6 pad_bitcast_fusion.refs_1_
  661.9 95.2 %shard_map.262 = (f32[72,128]{1,0:T(8,128)}, f32[4,56,128]{2,1,0:T(8,128)}, f32[288,768]{1,0:T(8,128)}, f32[576,256]{1,0:T(8,128)}, f32[288,1024]{1,0:T(8,128)},...) custom-call(f32[72,128]{1,0:T(8,128)} %pad_maximum_fusion.1.refs_0_,, ...), custom_call_target="tpu_custom_call" | custom-call | tf_op jit(solution)/shard_map/pallas_call | solution.py:2376
  757.2 2.5 fusion.10
  759.7 4.1 pad_maximum_fusion
  763.8 0.6 copy.35
  764.4 0.6 copy.36
  765.0 1.3 slice_bitcast_fusion.9
  766.3 0.7 reshape.124
  767.0 0.1 fusion.11
  767.0 0.7 reshape.125
  767.7 0.1 reshape.126
  767.8 0.8 slice_bitcast_fusion.8
  768.6 0.6 reshape.127
  769.2 0.8 copy.41
  770.0 1.5 copy.42
  (40 shorter events, 0.1 us)
Async XLA Ops:
  0.6 2.6 copy-start.6
  3.2 1.4 copy-start.14
  3.2 1.4 copy-start.13
  3.2 1.4 copy-start.15
  3.2 2.1 copy-start.10
  97.3 6.3 copy-start.12
  105.6 47.6 %copy-start.9 = (f32[2304]{0:T(1024)S(1)}, f32[2304]{0:T(1024)}, u32[]{:S(2)}) copy-start(f32[2304]{0:T(1024)} %param.29) | copy-start | bytes 27652
  105.6 47.7 %copy-start.11 = (f32[18432]{0:T(1024)S(1)}, f32[18432]{0:T(1024)}, u32[]{:S(2)}) copy-start(f32[18432]{0:T(1024)} %param.28) | copy-start | bytes 221188
  155.4 139.3 %copy-start.1 = (f32[4,128,576]{2,1,0:T(8,128)S(1)}, f32[4,128,576]{2,1,0:T(8,128)}, u32[]{:S(2)}) copy-start(f32[4,128,576]{2,1,0:T(8,128)} %get-tuple-element.73.refs_1_) | copy-start | bytes 3538948
  529.3 123.7 %copy-start = (bf16[1,128,2304]{2,1,0:T(8,128)(2,1)S(1)}, bf16[1,128,2304]{2,1,0:T(8,128)(2,1)}, u32[]{:S(2)}) copy-start(bf16[1,128,2304]{2,1,0:T(8,128)(2,1)} %param.16) | copy-start | bytes 1769476
  653.0 2.1 copy-start.2
  661.9 97.7 %copy-start.5 = (f32[288,768]{1,0:T(8,128)S(1)}, f32[288,768]{1,0:T(8,128)}, u32[]{:S(2)}) copy-start(f32[288,768]{1,0:T(8,128)} %get-tuple-element.114) | copy-start | bytes 2654212
  757.2 2.5 copy-start.4
  759.6 4.1 copy-start.8
  759.6 10.4 %copy-start.3 = (f32[576,1152]{1,0:T(8,128)S(1)}, f32[576,1152]{1,0:T(8,128)}, u32[]{:S(2)}) copy-start(f32[576,1152]{1,0:T(8,128)} %get-tuple-element.118) | copy-start | bytes 7962628
  763.7 5.5 copy-start.7

commit v6 on v5

--- a/solution.py
+++ b/solution.py
@@ -118,181 +118,6 @@
         jax.ShapeDtypeStruct((rows, width), dtype),
         [pltpu.VMEM((2, rows, width), BF16), pltpu.VMEM((rows, width), BF16), pltpu.VMEM((rows, width), BF16),
          DMA((2, parts)), DMA((2, parts)), DMA((parts,)), DMA((parts,))],
-        [VMEM],
-        VMEM,
-    )(value)
-
-
-def keys_reduce_kernel(n, src, out, y_got, r_got, l_got, r_out, l_out, moved, ys, yr, rs, rr, ls, lr, hs, hr, local):
-    seq, me, x, c = place_now()
-    y = seq % 2
-    z = seq // 2
-    nz = n // 2
-    right = (seq + 2, me)
-    left = (seq - 2, me)
-    beyond = (z * 2 + 1 - y, me)
-    barrier = pltpu.get_barrier_semaphore()
-    for d in range(1, GROUP):
-        pl.semaphore_signal(barrier, inc=1, device_id=(seq, lax.rem(me + d, GROUP)), device_id_type=MESH)
-    pl.semaphore_signal(barrier, inc=1, device_id=beyond, device_id_type=MESH)
-
-    @pl.when(z > 0)
-    def _():
-        pl.semaphore_signal(barrier, inc=1, device_id=left, device_id_type=MESH)
-
-    @pl.when(z < nz - 1)
-    def _():
-        pl.semaphore_signal(barrier, inc=1, device_id=right, device_id_type=MESH)
-
-    chain = jnp.where(z > 0, 1, 0) + jnp.where(z < nz - 1, 1, 0)
-    pl.semaphore_wait(barrier, GROUP + chain)
-
-    def swap(k):
-        return remote(src.at[k * 2 + 1 - y], y_got.at[k], ys.at[k], yr.at[k], beyond)
-
-    for t in range(1, nz):
-        go_right = z + nz - t
-        go_left = z - nz + t
-
-        @pl.when(go_right < nz)
-        def _():
-            swap(go_right).start()
-
-        @pl.when(go_left >= 0)
-        def _():
-            swap(go_left).start()
-
-    swap(z).start()
-
-    def pair_sum(k, more, to):
-        def body(i, carry):
-            half = i // 2
-            span = pl.ds(pl.multiple_of((i % 2) * 256, 256), 256)
-            total = src[k * 2 + y, half, span, :].astype(F32) + y_got[k, half, span, :].astype(F32)
-            for ref in more:
-                total = total + ref[half, span, :].astype(F32)
-            to[half, span, :] = total.astype(BF16)
-            return carry
-
-        lax.fori_loop(0, 4, body, 0)
-
-    for t in range(1, nz):
-        go_right = z + nz - t
-        go_left = z - nz + t
-
-        @pl.when(go_right < nz)
-        def _():
-            swap(go_right).wait_recv()
-            if t == 1:
-                pair_sum(go_right, [], r_out.at[t - 1])
-            else:
-
-                @pl.when(z > 0)
-                def _():
-                    remote(r_out.at[t - 1], r_got.at[t - 2], rs.at[t - 2], rr.at[t - 2], left).wait_recv()
-                    pair_sum(go_right, [r_got.at[t - 2]], r_out.at[t - 1])
-
-                @pl.when(z == 0)
-                def _():
-                    pair_sum(go_right, [], r_out.at[t - 1])
-
-            remote(r_out.at[t - 1], r_got.at[t - 1], rs.at[t - 1], rr.at[t - 1], right).start()
-
-        @pl.when(go_left >= 0)
-        def _():
-            swap(go_left).wait_recv()
-            if t == 1:
-                pair_sum(go_left, [], l_out.at[t - 1])
-            else:
-
-                @pl.when(z < nz - 1)
-                def _():
-                    remote(l_out.at[t - 1], l_got.at[t - 2], ls.at[t - 2], lr.at[t - 2], right).wait_recv()
-                    pair_sum(go_left, [l_got.at[t - 2]], l_out.at[t - 1])
-
-                @pl.when(z == nz - 1)
-                def _():
-                    pair_sum(go_left, [], l_out.at[t - 1])
-
-            remote(l_out.at[t - 1], l_got.at[t - 1], ls.at[t - 1], lr.at[t - 1], left).start()
-
-    swap(z).wait_recv()
-    last = nz - 2
-
-    def got_left():
-        remote(r_out.at[last], r_got.at[last], rs.at[last], rr.at[last], left).wait_recv()
-
-    def got_right():
-        remote(l_out.at[last], l_got.at[last], ls.at[last], lr.at[last], right).wait_recv()
-
-    @pl.when(z == 0)
-    def _():
-        got_right()
-        pair_sum(z, [l_got.at[last]], moved)
-
-    @pl.when(z == nz - 1)
-    def _():
-        got_left()
-        pair_sum(z, [r_got.at[last]], moved)
-
-    @pl.when((z > 0) & (z < nz - 1))
-    def _():
-        got_left()
-        got_right()
-        pair_sum(z, [r_got.at[last], l_got.at[last]], moved)
-
-    for t in range(2):
-        target = t * 2 + x
-
-        @pl.when(target == me)
-        def _():
-            pltpu.make_async_copy(moved.at[t], out.at[c], local).start()
-
-        @pl.when(target != me)
-        def _():
-            remote(moved.at[t], out.at[c], hs.at[t], hr.at[c], (seq, target)).start()
-
-    for j in range(2):
-        source = c * 2 + j
-
-        @pl.when(source == me)
-        def _():
-            pltpu.make_async_copy(moved.at[0], out.at[j], local).wait()
-
-        @pl.when(source != me)
-        def _():
-            remote(moved.at[0], out.at[j], hs.at[0], hr.at[j], (seq, source)).wait_recv()
-
-    for t in range(2):
-
-        @pl.when(t * 2 + x != me)
-        def _():
-            remote(moved.at[t], out.at[c], hs.at[t], hr.at[c], (seq, t * 2 + x)).wait_send()
-
-    for k in range(nz):
-        swap(k).wait_send()
-    for t in range(1, nz):
-
-        @pl.when(z + nz - t < nz)
-        def _():
-            remote(r_out.at[t - 1], r_got.at[t - 1], rs.at[t - 1], rr.at[t - 1], right).wait_send()
-
-        @pl.when(z - nz + t >= 0)
-        def _():
-            remote(l_out.at[t - 1], l_got.at[t - 1], ls.at[t - 1], lr.at[t - 1], left).wait_send()
-
-
-def keys_reduce(cid, n, value):
-    nz = n // 2
-    shape = value.shape[1:]
-    chain = pltpu.VMEM((nz - 1,) + shape, BF16)
-    return comm_call(
-        functools.partial(keys_reduce_kernel, n),
-        cid,
-        jax.ShapeDtypeStruct(shape, BF16),
-        [pltpu.VMEM((nz,) + shape, BF16), chain, chain, chain, chain, pltpu.VMEM(shape, BF16),
-         DMA((nz,)), DMA((nz,)), DMA((nz - 1,)), DMA((nz - 1,)), DMA((nz - 1,)), DMA((nz - 1,)),
-         DMA((2,)), DMA((2,)), DMA],
         [VMEM],
         VMEM,
     )(value)
@@ -885,8 +710,8 @@
             grad_keys, grad_values = new_keys, new_values
         else:
             grad_keys, grad_values = grad_keys + new_keys, grad_values + new_values
-    dkv_ref[:, 0] = grad_keys.astype(BF16).reshape(n, 128, DH)
-    dkv_ref[:, 1] = grad_values.astype(BF16).reshape(n, 128, DH)
+    dkv_ref[:, :, 0] = grad_keys.astype(BF16).reshape(n // 2, 2, 128, DH)
+    dkv_ref[:, :, 1] = grad_values.astype(BF16).reshape(n // 2, 2, 128, DH)
 
 
 class Chain:
@@ -1439,12 +1264,12 @@
 
 def ffn_backward_kernel(tiles, nz, chained, gate_tiles, *refs):
     gf, gft, levd, lev, gs, gu, hid, hidy, bt, bty = refs[:10]
-    dg_o, dgy_o, xg_o, gsum_o, out, ddown_o, gate_o = refs[10:17]
-    landing = refs[17:21] if chained else []
-    refs = refs[len(landing) + 1 :]
+    dg_o, dgy_o, gsum_o, out, ddown_o, gate_o = refs[10:16]
+    landing = refs[16:20] if chained else []
+    refs = refs[len(landing) :]
     (hh, hy, gfy, wbuf, dbuf, pair, co, cgot, near, sx, xgot, dg, acc, low, from_core, to_xb, from_x,
-     hsem, wsem, dsem, psem, lsem, cs, cr, xs, xr, ys, yr, os, gys, gyr, ccs, ccr, cxs, cxr) = refs[16:51]
-    rest = refs[51:]
+     hsem, wsem, dsem, psem, cs, cr, xs, xr, ys, yr, os, gys, gyr, ccs, ccr, cxs, cxr) = refs[16:50]
+    rest = refs[50:]
     seq, me, x, c = place_now()
     y = seq % 2
     across = (seq, (1 - x) * 2 + c)
@@ -1498,10 +1323,7 @@
         return remote(co.at[t % 2], cgot.at[t % 4], cs.at[t], cr.at[t], beside)
 
     def to_x(t):
-        return remote(sx.at[t % 4], xg_o.at[t], xs.at[t], xr.at[t], across)
-
-    def load_got(t):
-        return pltpu.make_async_copy(xg_o.at[t], xgot.at[t % 2], lsem.at[t % 2])
+        return remote(sx.at[t % 4], xgot.at[t], xs.at[t], xr.at[t], across)
 
     def columns(ref, t):
         return ref.at[:, pl.ds(pl.multiple_of(t * tw, 128), tw)]
@@ -1551,10 +1373,6 @@
 
     is_gate = jnp.where(x == 0, 1.0, 0.0).astype(F32)
 
-    def arrive(t):
-        to_x(t).wait_recv()
-        load_got(t).start()
-
     def own(t):
         load_pair(t).wait()
 
@@ -1563,12 +1381,12 @@
             to_y(t - ring).wait_send()
             keep(t - ring).wait()
 
-        load_got(t).wait()
+        to_x(t).wait_recv()
         scale = gs[t]
         gsum_o[t] = jnp.zeros((8, tw), F32)
 
         def body(span):
-            grad = sx[t % 4, span, :].astype(F32) + xgot[t % 2, span, :].astype(F32)
+            grad = sx[t % 4, span, :].astype(F32) + xgot[t, span, :].astype(F32)
             gate = pair[t % 2, 0, span, :].astype(F32)
             up = pair[t % 2, 1, span, :].astype(F32)
             value, slope = gelu_parts(gate)
@@ -1617,10 +1435,6 @@
         @pl.when((i >= 1) & (i < tiles + 1))
         def _():
             chip(i - 1)
-
-        @pl.when((i >= 2) & (i < tiles + 2))
-        def _():
-            arrive(i - 2)
 
         if chained:
 
@@ -1732,7 +1546,6 @@
         [
             wide,
             wide,
-            jax.ShapeDtypeStruct((tiles, rows, tw), BF16),
             jax.ShapeDtypeStruct((tiles, 8, tw), F32),
             jax.ShapeDtypeStruct((GROUP, block, part), F32),
             jax.ShapeDtypeStruct((part, per * tw), F32),
@@ -1750,30 +1563,31 @@
             pltpu.VMEM((4, rows, tw), BF16),
             pltpu.VMEM((2, rows, tw), F32),
             pltpu.VMEM((4, rows, tw), BF16),
-            pltpu.VMEM((2, rows, tw), BF16),
+            pltpu.VMEM((tiles, rows, tw), BF16),
             pltpu.VMEM((ring, rows, tw), BF16),
             pltpu.VMEM((GROUP, rows, part), F32),
             pltpu.VMEM((2, GROUP, block, part), BF16),
             pltpu.VMEM((2, GROUP, block, part), BF16),
             pltpu.VMEM((GROUP, block, part), BF16),
             pltpu.VMEM((GROUP, block, part), BF16),
-            DMA((2,)), DMA((2,)), DMA((2, 2)), DMA((2,)), DMA((2,)), each, each, each, each,
+            DMA((2,)), DMA((2,)), DMA((2, 2)), DMA((2,)), each, each, each, each,
             each, each, each, DMA, DMA, DMA((2, 4)), DMA((2, 4)), DMA((4,)), DMA((4,)),
         ]
         + (Chain.scratch(nz, per, *message) + gate_scratch(nz, gate_tiles, bt) if chained else []),
         [VMEM, VMEM, ANY, ANY, VMEM, ANY, ANY, ANY, ANY, ANY],
-        [ANY, ANY, ANY, VMEM, VMEM, ANY, ANY] + [ANY] * (4 if chained else 0),
+        [ANY, ANY, VMEM, VMEM, ANY, ANY] + [ANY] * (4 if chained else 0),
     )(gf, gft, levd, lev, gs, gu, hid, hidy, bt, bty)
 
 
 def branch_back_kernel(n, first, tiles, *refs):
     (gsi, mid, raw, cot, g2, g3, scale, wo, q, mixed, mass, own_meta, metas, kv, bt, bty, dg, dgy) = refs[:18]
-    dmid, sums, gy, gyy, dq, dkv, gate_o = refs[18:25]
+    dmid, sums, gy, gyy, dq, dkv, gate_o, dkv_y = refs[18:26]
+    refs = refs[1:]
     landing = refs[25:27] if tiles else []
     refs = refs[len(landing) :]
     (unit, gyt, gys, gy_all, part, from_core, to_x, from_x, grad, kvs, dkvs, es, er, el, cs, cr, xs, xr, ks, ds, yss, ysr,
-     ows) = refs[25:48]
-    rest = refs[48:]
+     ows, pys, pyr) = refs[25:50]
+    rest = refs[50:]
     seq, me, x, c = place_now()
     nz = n // 2
     across = (seq, (1 - x) * 2 + c)
@@ -1899,29 +1713,32 @@
             kv.at[:, :, pl.ds(pl.multiple_of(p * 128, 128), 128)], kvs.at[p % 2], ks.at[p % 2]
         )
 
+    y = seq % 2
+
     def store_pack(p):
         return pltpu.make_async_copy(
-            dkvs.at[p % 2], dkv.at[:, :, pl.ds(pl.multiple_of(p * 128, 128), 128)], ds.at[p % 2]
+            dkvs.at[p, :, y], dkv.at[:, :, pl.ds(pl.multiple_of(p * 128, 128), 128)], ds.at[p]
         )
 
+    def pack_to_y(p):
+        return remote(
+            dkvs.at[p, :, 1 - y], dkv_y.at[:, :, pl.ds(pl.multiple_of(p * 128, 128), 128)], pys.at[p], pyr.at[p], beyond
+        )
+
     base = at[0]
-    each = max(0, units - base) // GROUP
+    each = 1 if units - base >= GROUP else 0
 
     def one_pack(p, carry):
         load_pack(p).wait()
-
-        @pl.when(p >= 2)
-        def _():
-            store_pack(p - 2).wait()
-
         span = pl.ds(pl.multiple_of(p * 128, 128), 128)
         keys = kvs[p % 2, :, 0].reshape(n * 128, DH)
         values = kvs[p % 2, :, 1].reshape(n * 128, DH)
         allowed = masks(n, own_meta.at[pl.ds(p, 1)], metas.at[:, pl.ds(p, 1)])
         back_pack(
             n, keys, values, allowed, q.at[span], grad.at[span], mixed.at[span], mass.at[span], dq.at[span],
-            dkvs.at[p % 2],
+            dkvs.at[p],
         )
+        pack_to_y(p).start()
         store_pack(p).start()
 
         @pl.when(p + 2 < GROUP)
@@ -1939,8 +1756,9 @@
         chain.finish()
     for copy in copies + cores + [over]:
         copy.wait_send()
-    store_pack(2).wait()
-    store_pack(3).wait()
+    for p in js:
+        store_pack(p).wait()
+        pack_to_y(p).wait()
     swap.wait()
     gy_out.wait()
 
@@ -1962,8 +1780,9 @@
             jax.ShapeDtypeStruct((part, rows), BF16),
             jax.ShapeDtypeStruct((part, rows), BF16),
             jax.ShapeDtypeStruct(q.shape, F32),
-            jax.ShapeDtypeStruct(kv.shape, BF16),
+            jax.ShapeDtypeStruct((n // 2,) + kv.shape[1:], BF16),
             jax.ShapeDtypeStruct((gate_rows, max(tiles, 1) * TILE), F32),
+            jax.ShapeDtypeStruct((n // 2,) + kv.shape[1:], BF16),
         ]
         + (gate_landing(n // 2, tiles, bt) if tiles else []),
         [
@@ -1977,30 +1796,32 @@
             pltpu.VMEM((rows, heads), BF16),
             pltpu.VMEM((rows, heads), BF16),
             pltpu.VMEM(pack, BF16),
-            pltpu.VMEM(pack, BF16),
-            DMA((3,)), DMA((3,)), DMA, DMA((2,)), DMA((2,)), DMA, DMA, DMA((2,)), DMA((2,)), DMA, DMA, DMA,
+            pltpu.VMEM((GROUP, n // 2, 2) + pack[2:], BF16),
+            DMA((3,)), DMA((3,)), DMA, DMA((2,)), DMA((2,)), DMA, DMA, DMA((2,)), DMA((GROUP,)), DMA, DMA, DMA,
+            DMA((GROUP,)), DMA((GROUP,)),
         ]
         + (gate_scratch(n // 2, tiles, bt) if tiles else []),
         [VMEM] * 13 + [ANY] * 5,
-        [VMEM, VMEM, ANY, ANY, VMEM, ANY, ANY] + [ANY] * (2 if tiles else 0),
+        [VMEM, VMEM, ANY, ANY, VMEM, ANY, ANY, ANY] + [ANY] * (2 if tiles else 0),
     )(gsi, mid, raw, cot, g2, g3, scale, wo, q, mixed, mass, own_meta, metas, kv, bt, bty, dg, dgy)
 
 
 def keys_back_kernel(n, first, tiles, *refs):
-    (src, dq, q_raw, p_raw, cosine, sine, q_scale, p_scale, wq, wkv, bt, bty, dg, dgy) = refs[:14]
-    joined, joined_y, out, sums, gate_o = refs[14:19]
+    (src, y_got, dq, q_raw, p_raw, cosine, sine, q_scale, p_scale, wq, wkv, tok, dmid, gain, bt, bty, dg, dgy) = refs[:18]
+    refs = refs[4:]
+    joined, joined_y, out, sums, gain_o, gate_o = refs[14:20]
+    refs = refs[1:]
     landing = refs[19:21]
     refs = refs[2:]
-    (y_got, r_got, l_got, r_out, l_out, moved, back, acc, low, from_core, to_xb, from_x,
-     ys, yr, rs, rr, ls, lr, hs, hr, local, jys, jyr, ccs, ccr, cxs, cxr) = refs[19:46]
-    slabs, halves, slab_sem, *rest = refs[46:]
+    (r_got, l_got, r_out, l_out, moved, back, acc, low, from_core, to_xb, from_x,
+     rs, rr, ls, lr, hs, hr, local, jys, jyr, ccs, ccr, cxs, cxr) = refs[19:43]
+    slabs, halves, slab_sem, *rest = refs[43:]
     seq, me, x, c = place_now()
-    y = seq % 2
     z = seq // 2
     nz = n // 2
     right = (seq + 2, me)
     left = (seq - 2, me)
-    beyond = (z * 2 + 1 - y, me)
+    beyond = (seq + 1 - 2 * (seq % 2), me)
     across = (seq, (1 - x) * 2 + c)
     beside = (seq, x * 2 + 1 - c)
     chain, loads = gate_chain(nz, first, tiles, seq, me, bt, bty, dg, dgy, gate_o, landing, slabs, halves, slab_sem, rest)
@@ -2011,48 +1832,14 @@
     deep = acc.shape[1]
     half = DH // 2
 
-    def swap(k):
-        return remote(src.at[k * 2 + 1 - y], y_got.at[k], ys.at[k], yr.at[k], beyond)
-
-    for t in range(1, nz):
-        go_right = z + nz - t
-        go_left = z - nz + t
-
-        @pl.when(go_right < nz)
-        def _():
-            swap(go_right).start()
-
-        @pl.when(go_left >= 0)
-        def _():
-            swap(go_left).start()
-
-    swap(z).start()
     sums[...] = jnp.zeros_like(sums)
-
-    def turn_queries(span):
-        cos = cosine[span, :]
-        sin = sine[span, :]
-        for h in range(2):
-            a = slice(h * DH, h * DH + half)
-            b = slice(h * DH + half, (h + 1) * DH)
-            one = dq[span, a]
-            two = dq[span, b]
-            for cols, full in ((a, one * cos + two * sin), (b, two * cos - one * sin)):
-                sums[0:1, cols] += jnp.sum(q_raw[span, cols] * full, axis=0, keepdims=True)
-                joined[span, cols] = (full * q_scale[:, cols]).astype(BF16)
-
-    strips(rows // 64, 64, turn_queries)
-
-    def query_part(span):
-        acc[span, :] = contract_last(joined[span, :width], wq[...])
-
-    strips(rows // 128, 128, query_part)
+    gain_o[...] = jnp.zeros_like(gain_o)
 
     def pair_sum(k, more, to):
         def body(i, carry):
             part = i // 4
             span = pl.ds(pl.multiple_of((i % 4) * 128, 128), 128)
-            total = src[k * 2 + y, part, span, :].astype(F32) + y_got[k, part, span, :].astype(F32)
+            total = src[k, part, span, :].astype(F32) + y_got[k, part, span, :].astype(F32)
             for ref in more:
                 total = total + ref[part, span, :].astype(F32)
             to[part, span, :] = total.astype(BF16)
@@ -2060,6 +1847,26 @@
 
         lax.fori_loop(0, 8, body, 0)
 
+    def queries():
+        def turn_queries(span):
+            cos = cosine[span, :]
+            sin = sine[span, :]
+            for h in range(2):
+                a = slice(h * DH, h * DH + half)
+                b = slice(h * DH + half, (h + 1) * DH)
+                one = dq[span, a]
+                two = dq[span, b]
+                for cols, full in ((a, one * cos + two * sin), (b, two * cos - one * sin)):
+                    sums[0:1, cols] += jnp.sum(q_raw[span, cols] * full, axis=0, keepdims=True)
+                    joined[span, cols] = (full * q_scale[:, cols]).astype(BF16)
+
+        strips(rows // 64, 64, turn_queries)
+
+        def query_part(span):
+            acc[span, :] = contract_last(joined[span, :width], wq[...])
+
+        strips(rows // 128, 128, query_part)
+
     for load in loads:
         load.wait()
     units = chain.units()
@@ -2075,7 +1882,6 @@
         go_left = z - nz + t
 
         def hop(go, at_end, got, send, ss, sr, to, source):
-            swap(go).wait_recv()
             if t == 1:
                 pair_sum(go, [], send.at[t - 1])
             else:
@@ -2099,9 +1905,10 @@
         def _():
             hop(go_left, z == nz - 1, l_got, l_out, ls, lr, left, right)
 
-        beside_work(1)
-
-    swap(z).wait_recv()
+        beside_work(3)
+        if t == 1:
+            queries()
+
     last = nz - 2
 
     def got_left():
@@ -2137,7 +1944,7 @@
         def _():
             remote(moved.at[t], back.at[c], hs.at[t], hr.at[c], (seq, target)).start()
 
-    beside_work(1)
+    beside_work(3)
     for j in range(2):
         source = c * 2 + j
 
@@ -2201,7 +2008,15 @@
         here = pl.ds(pl.multiple_of((order[1] * 2 + c) * block + k * size, 16), size)
         cores[parts + k].wait_recv()
         sends[k].wait_recv()
-        out[span, :] = acc[here, :] + from_core[1, span, :].astype(F32) + from_x[span, :].astype(F32)
+        grad = acc[here, :] + from_core[1, span, :].astype(F32) + from_x[span, :].astype(F32)
+        value = tok[span, :].astype(F32)
+        inverse = lax.rsqrt(jnp.mean(value * value, axis=1, keepdims=True) + EPSILON)
+        normed = value * inverse
+        scaled = grad * gain[...]
+        out[span, :] = dmid[span, :] + inverse * (
+            scaled - normed * jnp.mean(scaled * normed, axis=1, keepdims=True)
+        )
+        gain_o[0:1, :] += jnp.sum(grad * normed, axis=0, keepdims=True)
 
     for t in range(2):
 
@@ -2209,8 +2024,6 @@
         def _():
             remote(moved.at[t], back.at[c], hs.at[t], hr.at[c], (seq, t * 2 + x)).wait_send()
 
-    for k in range(nz):
-        swap(k).wait_send()
     for t in range(1, nz):
 
         @pl.when(z + nz - t < nz)
@@ -2226,7 +2039,7 @@
     joined_swap.wait()
 
 
-def keys_back(cid, n, first, tiles, src, dq, q_raw, p_raw, cosine, sine, q_scale, p_scale, wq, wkv, pairs):
+def keys_back(cid, n, first, tiles, src, src_y, dq, q_raw, p_raw, cosine, sine, q_scale, p_scale, wq, wkv, tok, dmid, gain, pairs):
     bt, bty, dg, dgy = pairs
     nz = n // 2
     rows, width = dq.shape
@@ -2243,23 +2056,24 @@
             joined,
             jax.ShapeDtypeStruct((block, deep), F32),
             jax.ShapeDtypeStruct((8, width), F32),
+            jax.ShapeDtypeStruct((8, deep), F32),
             jax.ShapeDtypeStruct((bt.shape[2], tiles * TILE), F32),
         ]
         + gate_landing(nz, tiles, bt),
         [
-            pltpu.VMEM((nz,) + shape, BF16), chain, chain, chain, chain, pltpu.VMEM(shape, BF16), pltpu.VMEM(shape, BF16),
+            chain, chain, chain, chain, pltpu.VMEM(shape, BF16), pltpu.VMEM(shape, BF16),
             pltpu.VMEM((rows, deep), F32),
             pltpu.VMEM((2, block, deep), BF16),
             pltpu.VMEM((2, block, deep), BF16),
             pltpu.VMEM((block, deep), BF16),
             pltpu.VMEM((block, deep), BF16),
-            DMA((nz,)), DMA((nz,)), DMA((nz - 1,)), DMA((nz - 1,)), DMA((nz - 1,)), DMA((nz - 1,)),
+            DMA((nz - 1,)), DMA((nz - 1,)), DMA((nz - 1,)), DMA((nz - 1,)),
             DMA((2,)), DMA((2,)), DMA, DMA, DMA, DMA((2, 4)), DMA((2, 4)), DMA((4,)), DMA((4,)),
         ]
         + gate_scratch(nz, tiles, bt),
-        [VMEM] * 10 + [ANY] * 4,
-        [VMEM, ANY, VMEM, VMEM, ANY, ANY, ANY],
-    )(src, dq, q_raw, p_raw, cosine, sine, q_scale, p_scale, wq, wkv, bt, bty, dg, dgy)
+        [VMEM] * 14 + [ANY] * 4,
+        [VMEM, ANY, VMEM, VMEM, VMEM, ANY, ANY, ANY],
+    )(src, src_y, dq, q_raw, p_raw, cosine, sine, q_scale, p_scale, wq, wkv, tok, dmid, gain, bt, bty, dg, dgy)
 
 
 def finish_kernel(n, rounds, first, tiles, *refs):
@@ -2525,9 +2339,9 @@
     my_down = lax.dynamic_slice_in_dim(down_blocks, me * own, own, 1).astype(F32) * down_scale.reshape(GROUP, 1, part)
     down_inverse = lax.rsqrt(jnp.mean(my_down * my_down, axis=(0, 2), keepdims=True) + EPSILON)
     result = blocks_to_rows((my_middle + my_down * down_inverse * gain[3].reshape(GROUP, 1, part)).astype(BF16))
-    tiles_zero, tiles_one, tiles_two = (2, 4, 4) if n == 8 else (0, 0, 0)
+    tiles_zero, tiles_one, tiles_two = (2, 5, 4) if n == 8 else (0, 0, 0)
     tiles_three = tiles - tiles_zero - tiles_one - tiles_two
-    grad_gate_up, grad_gate_up_y, _, gate_sums, grad_second_input, down_grad, gate_zero, *_ = ffn_backward(
+    grad_gate_up, grad_gate_up_y, gate_sums, grad_second_input, down_grad, gate_zero, *_ = ffn_backward(
         6,
         n,
         tiles_zero,
@@ -2562,7 +2376,7 @@
     gain_four = down_sums[1]
     scale_gate = gate_sums[:, 0, :].reshape(columns) / my_gate_scale
     gate_pairs = second_pair + (grad_gate_up, grad_gate_up_y)
-    grad_middle, branch_sums, grad_branch, grad_branch_y, grad_query, grad_pairs, gate_one, *_ = branch_back(
+    grad_middle, branch_sums, grad_branch, grad_branch_y, grad_query, grad_pairs, gate_one, grad_pairs_y, *_ = branch_back(
         7,
         n,
         tiles_zero,
@@ -2589,12 +2403,13 @@
     scale_output = branch_sums[:, 2].reshape(width)
 
     if n == 8:
-        joined, joined_y, grad_first_input, key_sums, gate_two, *_ = keys_back(
+        joined, joined_y, grad_inputs, key_sums, gain_one, gate_two, *_ = keys_back(
             9,
             n,
             tiles_zero + tiles_one,
             tiles_two,
             grad_pairs,
+            grad_pairs_y,
             grad_query,
             query_raw,
             pair_raw,
@@ -2604,15 +2419,26 @@
             my_pair_scale[None],
             query_code,
             key_value_code,
+            tokens[0],
+            grad_middle,
+            gain[0][None],
             gate_pairs,
         )
+        gain_one = gain_one[0]
         scale_query = key_sums[0]
         scale_pair = key_sums[1]
     else:
         is_key = me < 2
         pair_cosine = jnp.where(is_key, cosine, 1.0)
         pair_sine = jnp.where(is_key, sine, 0.0)
-        grad_heads = keys_reduce(9, n, grad_pairs).astype(F32)
+        y = lax.axis_index("seq") % 2
+        both = (grad_pairs.astype(F32) + grad_pairs_y.astype(F32))[:, None]
+        spread = jnp.concatenate([jnp.where(y == 0, both, 0.0), jnp.where(y == 1, both, 0.0)], axis=1)
+        summed = lax.psum_scatter(spread.reshape((n,) + grad_pairs.shape[1:]), "seq", scatter_dimension=0)
+        heads = lax.all_gather(summed, "fsdp")
+        grad_heads = lax.dynamic_index_in_dim(
+            lax.dynamic_slice_in_dim(heads, c * 2, 2, 0), me // 2, 1, keepdims=False
+        )
         grad_query_full = rotate(
             grad_query.reshape(rows, 2, DH), cosine[:, None], -sine[:, None]
         ).reshape(rows, 2 * DH)
@@ -2626,11 +2452,11 @@
         joined = jnp.concatenate([grad_query_low, grad_pair_low], axis=1)
         grad_first_sum = contract_last(grad_query_low, query_code) + contract_last(grad_pair_low, key_value_code)
         grad_first_input = group_reduce(10, grad_first_sum.astype(BF16).reshape(GROUP, own, width), F32)
-    my_inputs = tokens[0].astype(F32)
-    my_inverse = rms_inverse(my_inputs)
-    first = my_inputs * my_inverse
-    gain_one = jnp.sum(grad_first_input * first, axis=0)
-    grad_inputs = grad_middle + norm_back(my_inverse, first, grad_first_input * gain[0])
+        my_inputs = tokens[0].astype(F32)
+        my_inverse = rms_inverse(my_inputs)
+        first = my_inputs * my_inverse
+        gain_one = jnp.sum(grad_first_input * first, axis=0)
+        grad_inputs = grad_middle + norm_back(my_inverse, first, grad_first_input * gain[0])
 
     wholes = lanes(jnp.concatenate([gain_one, gain_two, gain_three, scale_output]), 72)
     parts = [scale_query, scale_pair, scale_gate, scale_down, gain_four]

time: 785 us -> 759 us (0.967)
  Pallas kernels: 729 us -> 705 us
    pallas_call x1, Pallas kernels: 124 us -> 104 us  [keys_back(): comm_call(functools.partial(keys_back_kernel, n, first, tiles), cid, [joi...]
    pallas_call x1, Pallas kernels: 95.2 us -> 80.6 us  [finish(): comm_call(functools.partial(finish_kernel, n, rounds, first, tiles), cid,...]
    pallas_call x1, Pallas kernels: 80.2 us -> 90.9 us  [branch_back(): comm_call(functools.partial(branch_back_kernel, n, first, tiles), cid, [b...]
where the time goes in v6:
time: 759 us; the launch traced here: 747 us
  Pallas kernels  705 us (93%)
  local copies, waits for them, and re-layouts  33.4 us (4%)
  other arithmetic  7.63 us (1%)
    pallas_call x1, Pallas kernels, ffn_backward(): comm_call(functools.partial(ffn_backward_kernel, tiles, nz, chained, gate...  149 us
    pallas_call x1, Pallas kernels, ffn_forward(): comm_call(functools.partial(ffn_forward_kernel, tiles, count), cid, [jax....  138 us
    pallas_call x1, Pallas kernels, keys_back(): comm_call(functools.partial(keys_back_kernel, n, first, tiles), cid, [joi...  104 us
    pallas_call x1, Pallas kernels, branch_back(): comm_call(functools.partial(branch_back_kernel, n, first, tiles), cid, [b...  90.9 us
    pallas_call x1, Pallas kernels, front(): comm_call(functools.partial(front_kernel, n), cid, [blocks, blocks, jax.S...  87.8 us
    pallas_call x1, Pallas kernels, finish(): comm_call(functools.partial(finish_kernel, n, rounds, first, tiles), cid,...  80.6 us
    pallas_call x1, Pallas kernels, branch_forward(): comm_call(branch_kernel, cid, [jax.ShapeDtypeStruct((GROUP, rows, part),...  47.6 us

profile of v6, /device:TPU:0, one launch (start us, length us, event | category | flops | bytes accessed | tf_op | source)
XLA Modules:
  0.0 747.0 jit_solution(5248339010572634338)
XLA Ops:
  0.6 0.0 copy-start.5
  0.7 1.4 copy.36
  2.1 1.1 copy.37
  3.2 0.3 copy.38
  3.5 1.1 copy.39
  4.6 0.0 copy-done.13
  4.6 0.6 stack.2.refs_2_
  5.3 0.6 slice_reduce_fusion.4
  5.9 0.7 reshape_squeeze.34.refs_3_
  6.6 0.5 multiply_power_fusion.refs_4_
  7.1 1.3 dynamic_slice.12
  8.4 1.3 dynamic_slice.13
  9.8 87.8 %shard_map.255 = (bf16[4,512,576]{2,1,0:T(8,128)(2,1)}, bf16[4,512,576]{2,1,0:T(8,128)(2,1)}, f32[4,8,128]{2,1,0:T(8,128)}, f32[8,4,8,128]{3,2,1,0:T(8,128)}, bf...) custom-call(bf16[512,576]{1,0:T(8,128)(2,1)} %bitcast.58, ...), custom_call_target="tpu_custom_call" | custom-call | tf_op jit(solution)/shard_map/pallas_call | solution.py:437
  97.6 0.0 copy-start.12
  97.6 6.2 shard_map.256
  103.9 0.7 reshape.104.scale.refs_6_
  104.5 0.7 reshape_squeeze.35.g2.refs_4_
  105.2 0.7 reshape_squeeze.36.g3.refs_5_
  105.9 47.6 %shard_map.257 = (bf16[4,512,576]{2,1,0:T(8,128)(2,1)}, bf16[4,128,576]{2,1,0:T(8,128)(2,1)}, f32[4,128,576]{2,1,0:T(8,128)}, bf16[4,2,512,256]{3,2,1,0:T(8,128)(2,1)}, bf16[4,2,288,512]{3,2,1,0:T(8,128)(2,1)}) custom-call(bf16[512,512]{1,0:T(8,128)(2,1)} %get-tuple-element.73.low, bf16[576,2048]{1,0:T(8,128)(2,1)} %bitcast.53, ...), custom_call_target="tpu_custom_call" | custom-call | tf_op jit(solution)/shard_map/pallas_call | solution.py:600
  153.5 0.1 mul.53
  153.6 0.1 mul.47
  153.7 0.1 dynamic_slice.14
  153.7 0.6 reshape.105.refs_2_.refs_4_
  154.4 0.7 reshape_squeeze.37.refs_5_
  155.0 0.7 reshape.106.refs_6_
  155.7 137.9 %shard_map.258 = (bf16[2,12,512,384]{3,2,1,0:T(8,128)(2,1)}, bf16[12,512,384]{2,1,0:T(8,128)(2,1)}, bf16[12,512,384]{2,1,0:T(8,128)(2,1)}, bf16[4,512,576]{2,1,0...) custom-call(bf16[4,512,576]{2,1,0:T(8,128)(2,1)} %get-tuple-element., ...), custom_call_target="tpu_custom_call" | custom-call | tf_op jit(solution)/shard_map/pallas_call | solution.py:1232
  293.6 1.4 multiply_reduce_fusion
  295.0 0.0 copy-done
  295.0 1.4 add_convert_fusion
  296.4 0.1 slice_bitcast_fusion.4
  296.4 1.1 concatenate.27
  297.6 149.5 %shard_map.259 = (bf16[512,4608]{1,0:T(8,128)(2,1)}, bf16[512,4608]{1,0:T(8,128)(2,1)}, f32[12,8,384]{2,1,0:T(8,128)}, f32[4,128,576]{2,1,0:T(8,128)}, f32[576,1...) custom-call(bf16[512,576]{1,0:T(8,128)(2,1)} %get-tuple-element.82.r, ...), custom_call_target="tpu_custom_call" | custom-call | tf_op jit(solution)/shard_map/pallas_call | solution.py:1543
  447.1 90.9 %shard_map.260 = (f32[4,128,576]{2,1,0:T(8,128)}, f32[4,8,576]{2,1,0:T(8,128)}, bf16[576,512]{1,0:T(8,128)(2,1)}, bf16[576,512]{1,0:T(8,128)(2,1)}, f32[512,512]...) custom-call(f32[4,128,576]{2,1,0:T(8,128)} %get-tuple-element.90.ref, ...), custom_call_target="tpu_custom_call" | custom-call | tf_op jit(solution)/shard_map/pallas_call | solution.py:1774
  537.9 1.4 slice_bitcast_fusion
  539.3 1.3 concatenate.28.refs_12_
  540.6 104.2 %shard_map.261 = (bf16[512,1024]{1,0:T(8,128)(2,1)}, bf16[512,1024]{1,0:T(8,128)(2,1)}, f32[128,2304]{1,0:T(8,128)}, f32[8,512]{1,0:T(8,128)}, f32[8,2304]{1,0:T...) custom-call(bf16[4,2,512,256]{3,2,1,0:T(8,128)(2,1)} %get-tuple-element.96.refs_0_,, ...), custom_call_target="tpu_custom_call" | custom-call | tf_op jit(solution)/shard_map/pallas_call | solution.py:2051
  644.8 1.1 slice_reduce_fusion.3
  645.9 0.1 concatenate.32
  646.0 0.1 concatenate.31
  646.1 0.1 concatenate.30
  646.2 0.9 slice_reduce_fusion.7
  647.1 0.6 pad_maximum_fusion.1.refs_0_
  647.7 0.8 fusion.2
  648.5 1.0 slice_reduce_fusion
  649.5 0.1 dynamic-slice_divide_fusion
  649.6 0.8 slice_reduce_fusion.8
  650.4 0.1 concatenate.34
  650.5 0.6 pad_bitcast_fusion.refs_1_
  651.1 80.6 %shard_map.262 = (f32[72,128]{1,0:T(8,128)}, f32[4,56,128]{2,1,0:T(8,128)}, f32[288,384]{1,0:T(8,128)}, f32[576,256]{1,0:T(8,128)}, f32[288,1024]{1,0:T(8,128)},...) custom-call(f32[72,128]{1,0:T(8,128)} %pad_maximum_fusion.1.refs_0_,, ...), custom_call_target="tpu_custom_call" | custom-call | tf_op jit(solution)/shard_map/pallas_call | solution.py:2190
  731.7 2.5 fusion
  734.2 0.0 copy-done.3
  734.2 3.6 pad_maximum_fusion
  737.8 0.0 copy-done.7
  737.9 0.6 copy.47
  738.5 0.6 copy.48
  739.1 0.6 slice_bitcast_fusion.9
  739.7 0.7 reshape.111
  740.4 0.1 fusion.1
  740.5 0.7 reshape.112
  741.1 0.1 reshape.113
  741.2 0.6 reshape.114
  741.9 2.4 copy.54
  744.2 0.8 copy.55
  745.0 1.5 copy.56
  (37 shorter events, 0.1 us)
Async XLA Ops:
  0.6 2.6 copy-start.5
  0.7 4.0 copy-start.14
  0.7 3.9 copy-start.13
  0.7 3.9 copy-start.15
  0.7 4.6 copy-start.10
  97.6 6.3 copy-start.12
  105.9 47.7 %copy-start.8 = (f32[2304]{0:T(1024)S(1)}, f32[2304]{0:T(1024)}, u32[]{:S(2)}) copy-start(f32[2304]{0:T(1024)} %param.29) | copy-start | bytes 27652
  105.9 47.8 %copy-start.11 = (f32[18432]{0:T(1024)S(1)}, f32[18432]{0:T(1024)}, u32[]{:S(2)}) copy-start(f32[18432]{0:T(1024)} %param.28) | copy-start | bytes 221188
  155.7 139.2 %copy-start = (f32[4,128,576]{2,1,0:T(8,128)S(1)}, f32[4,128,576]{2,1,0:T(8,128)}, u32[]{:S(2)}) copy-start(f32[4,128,576]{2,1,0:T(8,128)} %get-tuple-element.75.refs_1_) | copy-start | bytes 3538948
  651.1 83.1 %copy-start.3 = (f32[288,1536]{1,0:T(8,128)S(1)}, f32[288,1536]{1,0:T(8,128)}, u32[]{:S(2)}) copy-start(f32[288,1536]{1,0:T(8,128)} %get-tuple-element.120) | copy-start | bytes 5308420
  651.1 83.1 %copy-start.4 = (f32[288,768]{1,0:T(8,128)S(1)}, f32[288,768]{1,0:T(8,128)}, u32[]{:S(2)}) copy-start(f32[288,768]{1,0:T(8,128)} %get-tuple-element.118) | copy-start | bytes 2654212
  731.7 2.5 copy-start.2
  734.2 3.6 copy-start.7
  734.2 4.9 copy-start.9
  737.8 6.4 copy-start.6
  737.8 7.2 copy-start.1

commit v7 on v6

--- a/solution.py
+++ b/solution.py
@@ -938,14 +938,14 @@
     gu_o, hid_o, hidy_o, down_o, gf_o, gft_o, sums_o, lev_o, levd_o = refs[:9]
     refs = refs[9:]
     rider_out, refs = refs[:riders], refs[riders:]
-    (both, hid, unit, wbuf, wlev, dbuf, dlev, acc, downs, wsem, dsem, lsem, ldsem, osem, xs, xr, oks, hs, hr, ks,
+    (both, other, hid, unit, wbuf, wlev, dbuf, dlev, acc, downs, wsem, dsem, lsem, ldsem, osem, xs, xr, oks, hs, hr, ks,
      ys, yr, fs, fr, gxs, gxr, gcs, gcr, gfs, gfr, rs, rr, outs) = refs
     seq, me, x, c = place_now()
     y = seq % 2
     across = (seq, (1 - x) * 2 + c)
     beside = (seq, x * 2 + 1 - c)
     beyond = (seq + 1 - 2 * y, me)
-    rows, tw = both.shape[2:]
+    rows, tw = both.shape[1:]
     part = b.shape[2]
     deep = GROUP * part
     per = tiles // 4
@@ -976,16 +976,13 @@
     fill_unit(unit)
 
     def to_x(t):
-        return remote(both.at[t % 3, x], gu_o.at[x, t], xs.at[t], xr.at[t], across)
-
-    def from_x(t):
-        return remote(both.at[t % 3, x], gu_o.at[1 - x, t], xs.at[t], xr.at[t], across)
+        return remote(both.at[t % 3], other.at[t], xs.at[t], xr.at[t], across)
 
     def keep_own(t):
-        return pltpu.make_async_copy(both.at[t % 3, x], gu_o.at[x, t], oks.at[t])
-
-    def load_other(t):
-        return pltpu.make_async_copy(gu_o.at[1 - x, t], both.at[t % 3, 1 - x], osem.at[t % 2])
+        return pltpu.make_async_copy(both.at[t % 3], gu_o.at[x, t], oks.at[t])
+
+    def keep_other(t):
+        return pltpu.make_async_copy(other.at[t], gu_o.at[1 - x, t], osem.at[t])
 
     def keep_level(t):
         return pltpu.make_async_copy(wlev.at[t % 2], lev_o.at[t], lsem.at[t % 2])
@@ -1036,22 +1033,23 @@
             total = dot(b[0, span, :], wlev[t % 2, 0:part, :])
             for j in range(1, GROUP):
                 total = total + dot(b[j, span, :], wlev[t % 2, j * part : (j + 1) * part, :])
-            both[t % 3, x, span, :] = (total * scale).astype(BF16)
+            both[t % 3, span, :] = (total * scale).astype(BF16)
 
         strips(rows // 256, 256, product)
         to_x(t).start()
         keep_own(t).start()
 
-    def arrive(t):
-        from_x(t).wait_recv()
-        load_other(t).start()
+    is_gate = jnp.where(x == 0, 1.0, 0.0).astype(F32)
 
     def middle(t):
-        load_other(t).wait()
+        to_x(t).wait_recv()
+        keep_other(t).start()
 
         def body(span):
-            gate = both[t % 3, 0, span, :].astype(F32)
-            up = both[t % 3, 1, span, :].astype(F32)
+            mine = both[t % 3, span, :].astype(F32)
+            theirs = other[t, span, :].astype(F32)
+            gate = is_gate * mine + (1.0 - is_gate) * theirs
+            up = is_gate * theirs + (1.0 - is_gate) * mine
             hid[c * tiles + t, span, :] = (gelu_parts(gate)[0] * up).astype(BF16)
 
         strips(rows // 64, 64, body)
@@ -1100,10 +1098,6 @@
         @pl.when(i < tiles)
         def _():
             wide(i)
-
-        @pl.when((i >= 1) & (i < tiles + 1))
-        def _():
-            arrive(i - 1)
 
         @pl.when(i >= 2)
         def _():
@@ -1196,6 +1190,7 @@
 
     def drain(t, carry):
         to_core(t).wait_send()
+        keep_other(t).wait()
 
         @pl.when(for_mine(t))
         def _():
@@ -1245,7 +1240,8 @@
         ]
         + [jax.ShapeDtypeStruct(r.shape[:1] + r.shape[2:], r.dtype) for r in riders],
         [
-            pltpu.VMEM((3, 2, rows, tw), BF16),
+            pltpu.VMEM((3, rows, tw), BF16),
+            pltpu.VMEM((tiles, rows, tw), BF16),
             pltpu.VMEM((2 * tiles, rows, tw), BF16),
             pltpu.VMEM((part, part), BF16),
             pltpu.VMEM((2, deep, tw), BF16),
@@ -1254,7 +1250,7 @@
             pltpu.VMEM((2, 2, part, tw), BF16),
             pltpu.VMEM((rows, part), F32),
             pltpu.VMEM((GROUP, rows, part), BF16),
-            DMA((2,)), DMA((2, 2)), DMA((2,)), DMA((2, 2)), DMA((2,)), each, each, each, each, each, DMA((2, tiles)),
+            DMA((2,)), DMA((2, 2)), DMA((2,)), DMA((2, 2)), each, each, each, each, each, each, DMA((2, tiles)),
             each, each, each, each, four, four, four, four, four, four, DMA((lone, 2)), DMA((lone, 2)), DMA,
         ],
         [VMEM, ANY, VMEM, ANY, VMEM, VMEM, VMEM] + [ANY] * count,

time: 759 us -> 758 us (level)
  no operation moved by 1% of the time
where the time goes in v7:
time: 758 us; the launch traced here: 746 us
  Pallas kernels  703 us (93%)
  local copies, waits for them, and re-layouts  33.4 us (4%)
  other arithmetic  7.63 us (1%)
    pallas_call x1, Pallas kernels, ffn_backward(): comm_call(functools.partial(ffn_backward_kernel, tiles, nz, chained, gate...  150 us
    pallas_call x1, Pallas kernels, ffn_forward(): comm_call(functools.partial(ffn_forward_kernel, tiles, count), cid, [jax....  136 us
    pallas_call x1, Pallas kernels, keys_back(): comm_call(functools.partial(keys_back_kernel, n, first, tiles), cid, [joi...  104 us
    pallas_call x1, Pallas kernels, branch_back(): comm_call(functools.partial(branch_back_kernel, n, first, tiles), cid, [b...  91.1 us
    pallas_call x1, Pallas kernels, front(): comm_call(functools.partial(front_kernel, n), cid, [blocks, blocks, jax.S...  87.8 us
    pallas_call x1, Pallas kernels, finish(): comm_call(functools.partial(finish_kernel, n, rounds, first, tiles), cid,...  80.6 us
    pallas_call x1, Pallas kernels, branch_forward(): comm_call(branch_kernel, cid, [jax.ShapeDtypeStruct((GROUP, rows, part),...  47.6 us

profile of v7, /device:TPU:0, one launch (start us, length us, event | category | flops | bytes accessed | tf_op | source)
XLA Modules:
  0.0 745.6 jit_solution(9326844853688392615)
XLA Ops:
  0.6 0.0 copy-start.5
  0.7 0.0 copy-start.14
  0.7 1.4 copy.36
  2.1 1.1 copy.37
  3.2 0.3 copy.38
  3.5 1.1 copy.39
  4.6 0.0 copy-done.14
  4.6 0.6 stack.2.refs_2_
  5.3 0.6 slice_reduce_fusion.4
  5.9 0.7 reshape_squeeze.34.refs_3_
  6.6 0.5 multiply_power_fusion.refs_4_
  7.1 1.3 dynamic_slice.12
  8.4 1.3 dynamic_slice.13
  9.8 87.8 %shard_map.255 = (bf16[4,512,576]{2,1,0:T(8,128)(2,1)}, bf16[4,512,576]{2,1,0:T(8,128)(2,1)}, f32[4,8,128]{2,1,0:T(8,128)}, f32[8,4,8,128]{3,2,1,0:T(8,128)}, bf...) custom-call(bf16[512,576]{1,0:T(8,128)(2,1)} %bitcast.58, ...), custom_call_target="tpu_custom_call" | custom-call | tf_op jit(solution)/shard_map/pallas_call | solution.py:437
  97.6 0.0 copy-start.12
  97.6 6.2 shard_map.256
  103.9 0.7 reshape.104.scale.refs_6_
  104.5 0.7 reshape_squeeze.35.g2.refs_4_
  105.2 0.7 reshape_squeeze.36.g3.refs_5_
  105.9 47.6 %shard_map.257 = (bf16[4,512,576]{2,1,0:T(8,128)(2,1)}, bf16[4,128,576]{2,1,0:T(8,128)(2,1)}, f32[4,128,576]{2,1,0:T(8,128)}, bf16[4,2,512,256]{3,2,1,0:T(8,128)(2,1)}, bf16[4,2,288,512]{3,2,1,0:T(8,128)(2,1)}) custom-call(bf16[512,512]{1,0:T(8,128)(2,1)} %get-tuple-element.73.low, bf16[576,2048]{1,0:T(8,128)(2,1)} %bitcast.53, ...), custom_call_target="tpu_custom_call" | custom-call | tf_op jit(solution)/shard_map/pallas_call | solution.py:600
  153.5 0.1 mul.53
  153.6 0.1 mul.47
  153.7 0.1 dynamic_slice.14
  153.7 0.6 reshape.105.refs_2_.refs_4_
  154.4 0.7 reshape_squeeze.37.refs_5_
  155.0 0.7 reshape.106.refs_6_
  155.7 136.3 %shard_map.258 = (bf16[2,12,512,384]{3,2,1,0:T(8,128)(2,1)}, bf16[12,512,384]{2,1,0:T(8,128)(2,1)}, bf16[12,512,384]{2,1,0:T(8,128)(2,1)}, bf16[4,512,576]{2,1,0...) custom-call(bf16[4,512,576]{2,1,0:T(8,128)(2,1)} %get-tuple-element., ...), custom_call_target="tpu_custom_call" | custom-call | tf_op jit(solution)/shard_map/pallas_call | solution.py:1227
  292.1 1.4 multiply_reduce_fusion
  293.5 1.4 add_convert_fusion
  294.8 0.1 slice_bitcast_fusion.4
  294.9 1.1 concatenate.27
  296.0 149.6 %shard_map.259 = (bf16[512,4608]{1,0:T(8,128)(2,1)}, bf16[512,4608]{1,0:T(8,128)(2,1)}, f32[12,8,384]{2,1,0:T(8,128)}, f32[4,128,576]{2,1,0:T(8,128)}, f32[576,1...) custom-call(bf16[512,576]{1,0:T(8,128)(2,1)} %get-tuple-element.82.r, ...), custom_call_target="tpu_custom_call" | custom-call | tf_op jit(solution)/shard_map/pallas_call | solution.py:1539
  445.6 91.1 %shard_map.260 = (f32[4,128,576]{2,1,0:T(8,128)}, f32[4,8,576]{2,1,0:T(8,128)}, bf16[576,512]{1,0:T(8,128)(2,1)}, bf16[576,512]{1,0:T(8,128)(2,1)}, f32[512,512]...) custom-call(f32[4,128,576]{2,1,0:T(8,128)} %get-tuple-element.90.ref, ...), custom_call_target="tpu_custom_call" | custom-call | tf_op jit(solution)/shard_map/pallas_call | solution.py:1770
  536.7 1.4 slice_bitcast_fusion
  538.0 1.3 concatenate.28.refs_12_
  539.3 104.1 %shard_map.261 = (bf16[512,1024]{1,0:T(8,128)(2,1)}, bf16[512,1024]{1,0:T(8,128)(2,1)}, f32[128,2304]{1,0:T(8,128)}, f32[8,512]{1,0:T(8,128)}, f32[8,2304]{1,0:T...) custom-call(bf16[4,2,512,256]{3,2,1,0:T(8,128)(2,1)} %get-tuple-element.96.refs_0_,, ...), custom_call_target="tpu_custom_call" | custom-call | tf_op jit(solution)/shard_map/pallas_call | solution.py:2047
  643.4 1.1 slice_reduce_fusion.3
  644.6 0.1 concatenate.32
  644.6 0.1 concatenate.31
  644.7 0.1 concatenate.30
  644.8 0.9 slice_reduce_fusion.7
  645.7 0.6 pad_maximum_fusion.1.refs_0_
  646.4 0.8 fusion.2
  647.2 1.0 slice_reduce_fusion
  648.1 0.1 dynamic-slice_divide_fusion
  648.2 0.8 slice_reduce_fusion.8
  649.0 0.1 concatenate.34
  649.1 0.6 pad_bitcast_fusion.refs_1_
  649.7 80.6 %shard_map.262 = (f32[72,128]{1,0:T(8,128)}, f32[4,56,128]{2,1,0:T(8,128)}, f32[288,384]{1,0:T(8,128)}, f32[576,256]{1,0:T(8,128)}, f32[288,1024]{1,0:T(8,128)},...) custom-call(f32[72,128]{1,0:T(8,128)} %pad_maximum_fusion.1.refs_0_,, ...), custom_call_target="tpu_custom_call" | custom-call | tf_op jit(solution)/shard_map/pallas_call | solution.py:2186
  730.4 2.5 fusion
  732.9 0.0 copy-done.2
  732.9 3.6 pad_maximum_fusion
  736.5 0.0 copy-done.7
  736.6 0.6 copy.47
  737.2 0.6 copy.48
  737.8 0.6 slice_bitcast_fusion.9
  738.4 0.7 reshape.111
  739.0 0.1 fusion.1
  739.1 0.7 reshape.112
  739.8 0.1 reshape.113
  739.9 0.6 reshape.114
  740.5 2.4 copy.54
  742.9 0.8 copy.55
  743.7 1.5 copy.56
  (37 shorter events, 0.1 us)
Async XLA Ops:
  0.6 2.6 copy-start.5
  0.7 4.0 copy-start.14
  0.7 3.9 copy-start.13
  0.7 3.9 copy-start.15
  0.7 4.6 copy-start.10
  97.6 6.3 copy-start.12
  105.9 47.7 %copy-start.8 = (f32[2304]{0:T(1024)S(1)}, f32[2304]{0:T(1024)}, u32[]{:S(2)}) copy-start(f32[2304]{0:T(1024)} %param.29) | copy-start | bytes 27652
  105.9 47.8 %copy-start.11 = (f32[18432]{0:T(1024)S(1)}, f32[18432]{0:T(1024)}, u32[]{:S(2)}) copy-start(f32[18432]{0:T(1024)} %param.28) | copy-start | bytes 221188
  155.7 137.7 %copy-start = (f32[4,128,576]{2,1,0:T(8,128)S(1)}, f32[4,128,576]{2,1,0:T(8,128)}, u32[]{:S(2)}) copy-start(f32[4,128,576]{2,1,0:T(8,128)} %get-tuple-element.75.refs_1_) | copy-start | bytes 3538948
  649.7 83.1 %copy-start.3 = (f32[288,1536]{1,0:T(8,128)S(1)}, f32[288,1536]{1,0:T(8,128)}, u32[]{:S(2)}) copy-start(f32[288,1536]{1,0:T(8,128)} %get-tuple-element.120) | copy-start | bytes 5308420
  649.7 83.1 %copy-start.4 = (f32[288,768]{1,0:T(8,128)S(1)}, f32[288,768]{1,0:T(8,128)}, u32[]{:S(2)}) copy-start(f32[288,768]{1,0:T(8,128)} %get-tuple-element.118) | copy-start | bytes 2654212
  730.4 2.5 copy-start.2
  732.9 3.6 copy-start.7
  732.9 4.9 copy-start.9
  736.5 6.4 copy-start.6
  736.5 7.2 copy-start.1
